TPU v7x, 128 devices: a whole 4x4x4 slice. The times are simulated.
128 devices in a mesh: seq: 16 (over x, y), head: 8 (over z, core).
Axes of the slice: x: 4, y: 4, z: 4, core: 2. Of those that a mesh axis runs over, the one named last changes fastest.
Arguments:
- query: bfloat16 [4096, 4096], P('seq', 'head'), may hold values from -6 to 6
- key: bfloat16 [4096, 4096], P('seq', 'head'), may hold values from -6 to 6
- value: bfloat16 [4096, 4096], P('seq', 'head'), may hold values from -6 to 6
- head_gain: float32 [4096], P('head'), may hold values from 0.1 to 1.9
- out_weight: bfloat16 [4096, 4096], P('head', 'seq'), may hold values from -0.09375 to 0.09375
- stream: bfloat16 [4096, 4096], P(('seq', 'head')), may hold values from -6 to 6
- model_gain: float32 [4096], replicated, may hold values from 0.1 to 1.9
- expert_ids: int32 [4096, 8], P(('seq', 'head')), may hold values from 0 to 127, all different within a row; in each aligned block of 32 rows (0 to 31, 32 to 63, ...) at most 3 rows name the same one
- expert_gates: float32 [4096, 8], P(('seq', 'head')), may hold values from 0.1 to 0.5
- gate_weight: bfloat16 [128, 4096, 768], P(('seq', 'head')), may hold values from -0.09375 to 0.09375
- up_weight: bfloat16 [128, 4096, 768], P(('seq', 'head')), may hold values from -0.09375 to 0.09375
- down_weight: bfloat16 [128, 768, 4096], P(('seq', 'head')), may hold values from -0.21875 to 0.21875
- weight_scales: float32 [128, 3], P(('seq', 'head')), may hold values from 0.6 to 1.6
Outputs:
- layer_out: bfloat16 [4096, 4096], P(('seq', 'head'))
Inputs may be any that keep to these rules, and one draw needn't show every extreme that they name: `expert_ids`: among the 32 tokens of one device (aligned blocks of rows), no expert is named more than 3 times, a bound that some block reaches; the entries of one row differ.
All inputs are finite; a program needn't handle non-finite values.
Results may differ from a plain program's by a relative error of at most 0.013.
Values may be sent and summed in bfloat16 or wider, within the bound.
No kernel may reach another device: no remote copies, remote signals or barrier semaphores. Data moves between devices by JAX's collectives and lax.ppermute only.
A program may use at most 128 MiB of HBM per device.

v0:
```python
import jax
import jax.numpy as jnp
from jax import lax
from jax.sharding import PartitionSpec as P

D = 4096
HD = 128
TOPK = 8


def prefix(part, axis, combine, identity):
    place = lax.axis_index(axis)
    gathered = lax.all_gather(part, axis)
    state = jnp.zeros_like(part) + jnp.asarray(identity, part.dtype)

    def one(lap, state):
        return combine(state, lax.dynamic_index_in_dim(gathered, lap, 0, False))

    return lax.fori_loop(0, place, one, state)


def add_states(earlier, later):
    return earlier + later


def body(
    query,
    key,
    value,
    head_gain,
    out_weight,
    stream,
    model_gain,
    expert_ids,
    expert_gates,
    gate_weight,
    up_weight,
    down_weight,
    weight_scales,
):
    seq_rows = query.shape[0]
    heads_local = head_gain.shape[0] // HD
    query_rows = query.reshape(seq_rows, heads_local, HD)
    key_rows = key.reshape(seq_rows, heads_local, HD)
    value_rows = value.reshape(seq_rows, heads_local, HD)
    scores = jnp.einsum("thd,shd->hts", query_rows, key_rows, preferred_element_type=jnp.float32)
    causal = jnp.tril(jnp.ones((seq_rows, seq_rows), dtype=bool))
    scores = jnp.where(causal[None, :, :], scores, 0.0).astype(jnp.bfloat16)
    local_part = jnp.einsum("hts,shd->thd", scores, value_rows, preferred_element_type=jnp.float32)
    block_state = jnp.einsum(
        "shd,she->hde", key_rows, value_rows, preferred_element_type=jnp.float32
    )
    prior_state = prefix(block_state, "seq", add_states, jnp.zeros_like(block_state))
    earlier_part = jnp.einsum(
        "thd,hde->the",
        query_rows,
        prior_state.astype(jnp.bfloat16),
        preferred_element_type=jnp.float32,
    )
    mixed_heads = local_part + earlier_part
    mean_square = jnp.mean(mixed_heads * mixed_heads, axis=-1, keepdims=True)
    head_normed = (
        mixed_heads * lax.rsqrt(mean_square + 1e-06) * head_gain.reshape(heads_local, HD)
    ).astype(jnp.bfloat16)
    head_normed = head_normed.reshape(seq_rows, heads_local * HD)
    full_out = lax.all_gather(out_weight, "seq", axis=1, tiled=True)
    tok_rows = stream.shape[0]
    attention = lax.psum_scatter(
        jnp.dot(head_normed, full_out, preferred_element_type=jnp.float32),
        "head",
        scatter_dimension=0,
        tiled=True,
    )
    residual_float = (
        (stream.astype(jnp.float32) + attention).astype(jnp.bfloat16).astype(jnp.float32)
    )
    mean_square = jnp.mean(residual_float * residual_float, axis=-1, keepdims=True)
    normed = (residual_float * lax.rsqrt(mean_square + 1e-06) * model_gain).astype(jnp.bfloat16)
    seq_count = lax.axis_size("seq")
    head_count = lax.axis_size("head")
    experts = seq_count * head_count
    capacity = 3 * tok_rows * TOPK // (2 * experts)
    flat_ids = expert_ids.reshape(-1)
    onehot = (flat_ids[:, None] == jnp.arange(experts, dtype=jnp.int32)[None, :]).astype(jnp.int32)
    earlier_count = jnp.cumsum(onehot, axis=0) - onehot
    slot_index = jnp.sum(earlier_count * onehot, axis=1)
    target = flat_ids * capacity + slot_index
    source_rows = jnp.broadcast_to(normed[:, None, :], (tok_rows, TOPK, D)).reshape(
        tok_rows * TOPK, D
    )
    outgoing = jnp.zeros((experts * capacity, D), jnp.bfloat16).at[target].set(source_rows)
    outgoing = outgoing.reshape(experts, capacity, D)
    scale_row = weight_scales[0]
    slot_rows = lax.all_to_all(outgoing, ("seq", "head"), split_axis=0, concat_axis=0, tiled=True)
    gate_part = (
        jnp.einsum("smd,df->smf", slot_rows, gate_weight[0], preferred_element_type=jnp.float32)
        * scale_row[0]
    )
    up_part = (
        jnp.einsum("smd,df->smf", slot_rows, up_weight[0], preferred_element_type=jnp.float32)
        * scale_row[1]
    )
    act = (jax.nn.silu(gate_part) * up_part).astype(jnp.bfloat16)
    produced = (
        jnp.einsum("smf,fd->smd", act, down_weight[0], preferred_element_type=jnp.float32)
        * scale_row[2]
    )
    computed = produced.astype(jnp.bfloat16)
    results = lax.all_to_all(computed, ("seq", "head"), split_axis=0, concat_axis=0, tiled=True)
    gathered = results.reshape(experts * capacity, D)[target].reshape(tok_rows, TOPK, D)
    expert_mix = jnp.sum(gathered.astype(jnp.float32) * expert_gates[:, :, None], axis=1)
    return (residual_float + expert_mix).astype(jnp.bfloat16)


def solution(mesh):
    return jax.shard_map(
        body,
        mesh=mesh,
        in_specs=(
            P("seq", "head"),
            P("seq", "head"),
            P("seq", "head"),
            P("head"),
            P("head", "seq"),
            P(("seq", "head"), None),
            P(),
            P(("seq", "head"), None),
            P(("seq", "head"), None),
            P(("seq", "head"), None, None),
            P(("seq", "head"), None, None),
            P(("seq", "head"), None, None),
            P(("seq", "head"), None),
        ),
        out_specs=P(("seq", "head"), None),
        check_vma=False,
    )
```

profile of v0, /device:TPU:1, one launch (start us, length us, event | category | flops | bytes accessed | tf_op | source)
XLA Modules:
  0.0 346.8 jit_solution(17948770530914740345)
XLA Ops:
  6.5 1.1 copy.50
  7.7 1.9 fusion.46
  9.6 0.7 all-gather.4.cloned.1.call-update
  10.4 53.9 %all-gather.6.cloned.1.call-done = f32[64,128,128]{2,1,0:T(8,128)} async-done(((f32[4,128,128]{2,1,0:T(8,128)}), f32[64,128,128]{2,1,0:T(8,128)}) %all-gather.6.cloned.1.call-update) | async-done | bytes 4194320 | tf_op jit(solution)/shard_map/all_gather | solution.py:13
  65.3 57.4 %all-gather.4.cloned.1.call-done = bf16[512,4096]{1,0:T(8,128)(2,1)} async-done(((bf16[512,256]{1,0:T(8,128)(2,1)}), bf16[512,4096]{1,0:T(8,128)(2,1)}) %all-gather.4.cloned.1.call-update) | async-done | bytes 4194320 | tf_op jit(solution)/shard_map/all_gather | solution.py:66
  122.7 5.4 %fusion.66 = f32[256,4096]{1,0:T(8,128)} fusion(bf16[256,512]{0,1:T(8,128)(2,1)S(1)} %bitcast.95, bf16[512,4096]{1,0:T(8,128)(2,1)} %all-gather.4.cloned.1.call-done), kind=kOutput, calls=%fused_computation.68 | convolution fusion | flops 1073741824 | bytes 8650752 | tf_op jit(solution)/shard_map/dot_general | solution.py:69
  128.2 0.7 copy-done.6
  129.9 34.0 %reduce-scatter.2.cloned.1.call-done = f32[32,4096]{1,0:T(8,128)} async-done(((f32[256,4096]{1,0:T(8,128)}), f32[32,4096]{1,0:T(8,128)}) %reduce-scatter.2.cloned.1.call-update) | async-done | bytes 524304 | tf_op jit(solution)/shard_map/reduce_scatter | solution.py:68
  163.9 1.2 fusion.39
  165.1 0.8 fusion.41
  166.0 4.8 %scatter_custom_fusion = bf16[384,4096]{1,0:T(8,128)(2,1)S(1)} fusion(s32[256]{0:T(256)S(1)} %bitcast.103, bf16[]{:T(256)} %constant.40.clone.1, bf16[32,4096]{1,0:T(8,128)(2,1)} %fusion.41), kind=kCustom, calls=%fused_computation.14 | custom fusion | bytes 3407874 | tf_op jit(solution)/shard_map/scatter | solution.py:91
  170.8 4.5 %reshape.109 = bf16[128,3,4096]{2,1,0:T(4,128)(2,1)} reshape(bf16[384,4096]{1,0:T(8,128)(2,1)S(1)} %scatter_custom_fusion) | data formatting | bytes 6291456 | tf_op jit(solution)/shard_map/reshape | solution.py:92
  175.3 10.5 %all-to-all-start = ((bf16[128,3,4096]{2,1,0:T(4,128)(2,1)}), bf16[128,3,4096]{2,1,0:T(4,128)(2,1)}, u32[]{:S(2)}, u32[]{:S(2)}) async-start(bf16[128,3,4096]{2,1,0:T(4,128)(2,1)} %reshape.109), calls=%async_computation.1 | async-start | bytes 8388608 | tf_op jit(solution)/shard_map/all_to_all | solution.py:94
  186.4 52.1 %all-to-all-done = bf16[128,3,4096]{2,1,0:T(4,128)(2,1)} async-done(((bf16[128,3,4096]{2,1,0:T(4,128)(2,1)}), bf16[128,3,4096]{2,1,0:T(4,128)(2,1)}, u32[]{:S(2)}, u32[]{:S(2)}) %all-to-all-start) | async-done | bytes 3145760 | tf_op jit(solution)/shard_map/all_to_all | solution.py:94
  238.6 11.5 %fusion.14 = f32[128,3,768]{2,0,1:T(8,128)S(1)} fusion(bf16[1,4096,768]{2,1,0:T(8,128)(2,1)} %param.24, bf16[128,3,4096]{2,1,0:T(4,128)(2,1)} %all-to-all-done, f32[]{:T(128)} %bitcast.14), kind=kOutput, calls=%fused_computation.17 | convolution fusion | flops 2416214016 | bytes 10616836 | tf_op jit(solution)/shard_map/smd,df->smf/dot_general | solution.py:96
  250.2 8.8 %fusion.29 = bf16[128,3,768]{2,0,1:T(8,128)(2,1)S(1)} fusion(bf16[1,4096,768]{2,1,0:T(8,128)(2,1)S(1)} %bitcast.107, bf16[128,3,4096]{2,1,0:T(4,128)(2,1)} %all-to-all-done, f32[128,3,768]{2,0,1:T(8,128)S(1)} %fusion.14, f32[]{:T(128)} %bitcast.17), kind=kOutput, calls=%fused_computation.21 | convolution fusion | flops 2417983488 | bytes 11206660 | tf_op jit(solution)/shard_map/smd,df->smf/dot_general | solution.py:100
  259.0 3.7 %multiply_convert_fusion = bf16[128,3,4096]{2,0,1:T(8,128)(2,1)S(1)} fusion(bf16[128,3,768]{2,0,1:T(8,128)(2,1)S(1)} %fusion.29, bf16[1,768,4096]{2,1,0:T(8,128)(2,1)S(1)} %bitcast.109, f32[]{:T(128)} %bitcast.20), kind=kOutput, calls=%fused_computation.9 | convolution fusion | flops 2419064832 | bytes 10027012 | tf_op jit(solution)/shard_map/smf,fd->smd/dot_general | solution.py:105
  262.7 4.7 %copy.47 = bf16[128,3,4096]{2,1,0:T(4,128)(2,1)} copy(bf16[128,3,4096]{2,0,1:T(8,128)(2,1)S(1)} %multiply_convert_fusion) | data formatting | bytes 6291456 | tf_op jit(solution)/shard_map/convert_element_type | solution.py:108
  267.4 5.8 %all-to-all-start.1 = ((bf16[128,3,4096]{2,1,0:T(4,128)(2,1)}), bf16[128,3,4096]{2,1,0:T(4,128)(2,1)}, u32[]{:S(2)}, u32[]{:S(2)}) async-start(bf16[128,3,4096]{2,1,0:T(4,128)(2,1)} %copy.47), calls=%async_computation.2 | async-start | bytes 8388608 | tf_op jit(solution)/shard_map/all_to_all | solution.py:109
  273.3 52.8 %all-to-all-done.1 = bf16[128,3,4096]{2,1,0:T(4,128)(2,1)} async-done(((bf16[128,3,4096]{2,1,0:T(4,128)(2,1)}), bf16[128,3,4096]{2,1,0:T(4,128)(2,1)}, u32[]{:S(2)}, u32[]{:S(2)}) %all-to-all-start.1) | async-done | bytes 3145760 | tf_op jit(solution)/shard_map/all_to_all | solution.py:109
  326.1 6.0 %reshape.110 = bf16[384,4096]{1,0:T(8,128)(2,1)S(1)} reshape(bf16[128,3,4096]{2,1,0:T(4,128)(2,1)} %all-to-all-done.1) | data formatting | bytes 6291456 | tf_op jit(solution)/shard_map/reshape | solution.py:110
  332.1 3.2 gather_fusion
  335.3 3.2 fusion.8
  338.5 1.7 fusion.42
  (61 shorter events, 2.8 us)
Async XLA Ops:
  6.5 57.8 %copy-start = (bf16[256,512]{1,0:T(8,128)(2,1)S(1)}, bf16[256,512]{1,0:T(8,128)(2,1)}, u32[]{:S(2)}) copy-start(bf16[256,512]{1,0:T(8,128)(2,1)} %param.15) | copy-start | bytes 786436
  6.5 57.8 %all-gather.6.cloned.1.call-start = ((), (), s32[]{:S(2)}) async-start(), calls=%async_computation.5 | async-start | bytes 4456448 | tf_op jit(solution)/shard_map/all_gather | solution.py:13
  9.5 55.1 %copy-start.3 = (bf16[256,512]{1,0:T(8,128)(2,1)S(1)}, bf16[256,512]{1,0:T(8,128)(2,1)}, u32[]{:S(2)}) copy-start(bf16[256,512]{1,0:T(8,128)(2,1)} %param.17) | copy-start | bytes 786436
  9.6 113.2 %all-gather.4.cloned.1.call-start = ((), (), s32[]{:S(2)}) async-start(), calls=%async_computation.3 | async-start | bytes 4456448 | tf_op jit(solution)/shard_map/all_gather | solution.py:66
  10.3 153.6 %reduce-scatter.2.cloned.1.call-start = ((), (), s32[]{:S(2)}) async-start(), calls=%async_computation.4 | async-start | bytes 4718592 | tf_op jit(solution)/shard_map/reduce_scatter | solution.py:68
  64.3 0.8 copy-start.9
  128.2 0.7 copy-start.6
  128.2 35.7 %copy-start.4 = (bf16[32,4096]{1,0:T(8,128)(2,1)S(1)}, bf16[32,4096]{1,0:T(8,128)(2,1)}, u32[]{:S(2)}) copy-start(bf16[32,4096]{1,0:T(8,128)(2,1)} %param.20) | copy-start | bytes 786436
  128.2 37.0 %copy-start.5 = (f32[4096]{0:T(1024)S(1)}, f32[4096]{0:T(1024)}, u32[]{:S(2)}) copy-start(f32[4096]{0:T(1024)} %param.21) | copy-start | bytes 49156
  165.1 10.2 %copy-start.2 = (bf16[32,4096]{1,0:T(8,128)(2,1)}, bf16[32,4096]{1,0:T(8,128)(2,1)S(1)}, u32[]{:S(2)}) copy-start(bf16[32,4096]{1,0:T(8,128)(2,1)S(1)} %get-tuple-element.38) | copy-start | bytes 786436
  175.3 10.5 %copy-start.7 = (f32[1,3]{1,0:T(1,128)S(1)}, f32[1,3]{1,0:T(1,128)}, u32[]{:S(2)}) copy-start(f32[1,3]{1,0:T(1,128)} %param.27) | copy-start | bytes 40
  175.3 74.8 %slice-start = ((s8[6291456]{0:T(1024)(128)(4,1)}), s8[2097152]{0:T(1024)(128)(4,1)S(1)}, s32[]{:S(2)}) async-start(s8[6291456]{0:T(1024)(128)(4,1)} %bitcast.106), calls=%async_computation.6 | async-start | bytes 4194304
  175.3 63.2 %all-to-all-start = ((bf16[128,3,4096]{2,1,0:T(4,128)(2,1)}), bf16[128,3,4096]{2,1,0:T(4,128)(2,1)}, u32[]{:S(2)}, u32[]{:S(2)}) async-start(bf16[128,3,4096]{2,1,0:T(4,128)(2,1)} %reshape.109), calls=%async_computation.1 | async-start | bytes 8388608 | tf_op jit(solution)/shard_map/all_to_all | solution.py:94
  238.6 11.6 %slice-start.1 = ((s8[6291456]{0:T(1024)(128)(4,1)}), s8[4194304]{0:T(1024)(128)(4,1)S(1)}, s32[]{:S(2)}) async-start(s8[6291456]{0:T(1024)(128)(4,1)} %bitcast.106), calls=%async_computation.7 | async-start | bytes 8388608
  238.6 20.4 %slice-start.2 = ((s8[6291456]{0:T(1024)(128)(4,1)}), s8[4194304]{0:T(1024)(128)(4,1)S(1)}, s32[]{:S(2)}) async-start(s8[6291456]{0:T(1024)(128)(4,1)} %bitcast.108), calls=%async_computation.8 | async-start | bytes 8388608
  250.2 8.8 %slice-start.3 = ((s8[6291456]{0:T(1024)(128)(4,1)}), s8[2097152]{0:T(1024)(128)(4,1)S(1)}, s32[]{:S(2)}) async-start(s8[6291456]{0:T(1024)(128)(4,1)} %bitcast.108), calls=%async_computation.9 | async-start | bytes 4194304
  267.4 5.8 %copy-start.8 = (f32[32,8]{0,1:T(8,128)S(1)}, f32[32,8]{0,1:T(8,128)}, u32[]{:S(2)}) copy-start(f32[32,8]{0,1:T(8,128)} %param.23) | copy-start | bytes 3076
  267.4 58.7 %all-to-all-start.1 = ((bf16[128,3,4096]{2,1,0:T(4,128)(2,1)}), bf16[128,3,4096]{2,1,0:T(4,128)(2,1)}, u32[]{:S(2)}, u32[]{:S(2)}) async-start(bf16[128,3,4096]{2,1,0:T(4,128)(2,1)} %copy.47), calls=%async_computation.2 | async-start | bytes 8388608 | tf_op jit(solution)/shard_map/all_to_all | solution.py:109
  332.1 8.1 %copy-start.1 = (bf16[256,512]{1,0:T(8,128)(2,1)S(1)}, bf16[256,512]{1,0:T(8,128)(2,1)}, u32[]{:S(2)}) copy-start(bf16[256,512]{1,0:T(8,128)(2,1)} %param.15) | copy-start | bytes 786436
Sparse Core Ops, SparseCore 0:
  9.7 54.5 all-gather.5
  66.4 56.2 all-gather.3
  128.3 35.5 reduce-scatter.1
where the time goes:
time: 348 us; the launch traced here: 347 us
  waiting for transfers between devices  251 us (72%)
  matrix products  32.1 us (9%)
  local copies, waits for them, and re-layouts  26.2 us (8%)
  starting transfers between devices  16.4 us (5%)
  between operations  13.4 us (4%)
  other arithmetic  7.63 us (2%)
    all_gather x1, waiting for transfers between devices, body(): full_out = lax.all_gather(out_weight, 'seq', axis=1, tiled=True)  57.4 us
    all_gather x1, waiting for transfers between devices, prefix(): gathered = lax.all_gather(part, axis)  53.9 us
    all_to_all x1, waiting for transfers between devices, body(): lax.all_to_all(computed, ('seq', 'head'), split_axis=0, concat_axis=0, ti...  52.8 us
    all_to_all x1, waiting for transfers between devices, body(): lax.all_to_all(outgoing, ('seq', 'head'), split_axis=0, concat_axis=0, ti...  52.1 us
    reduce_scatter x1, waiting for transfers between devices, body(): lax.psum_scatter(jnp.dot(head_normed, full_out, preferred_element_type=jn...  34 us
    dot_general x1, matrix products, body(): jnp.einsum('smd,df->smf', slot_rows, gate_weight[0], preferred_element_ty...  11.5 us
    all_to_all x1, starting transfers between devices, body(): lax.all_to_all(outgoing, ('seq', 'head'), split_axis=0, concat_axis=0, ti...  10.5 us
    dot_general x1, matrix products, body(): jnp.einsum('smd,df->smf', slot_rows, up_weight[0], preferred_element_type...  8.77 us
  transfers between devices with their start and end apart: 5, of which 5 were waited for; matrix products, arithmetic and copies ran while one was open for 1% of the time, Pallas kernels for 0%

commit v1 on v0

v1 whole, which is shorter than its diff:
```python
import jax
import jax.numpy as jnp
from jax import lax
from jax.sharding import PartitionSpec as P

D = 4096
HD = 128
TOPK = 8
CAP = 3
NX, NY, NZ, NC = 4, 4, 4, 2
BF = jnp.bfloat16
F32 = jnp.float32


def shift_x(a, d):
    pairs = [(x * NY + y, (x + d) % NX * NY + y) for x in range(NX) for y in range(NY)]
    return lax.ppermute(a, "seq", pairs)


def shift_y(a, d):
    pairs = [(x * NY + y, x * NY + (y + d) % NY) for x in range(NX) for y in range(NY)]
    return lax.ppermute(a, "seq", pairs)


def shift_z(a, d):
    pairs = [(z * NC + c, (z + d) % NZ * NC + c) for z in range(NZ) for c in range(NC)]
    return lax.ppermute(a, "head", pairs)


def swap_core(a):
    pairs = [(z * NC + c, z * NC + 1 - c) for z in range(NZ) for c in range(NC)]
    return lax.ppermute(a, "head", pairs)


def earlier_states(block_state, x, y):
    own = block_state.astype(BF)
    total = block_state
    before = jnp.zeros_like(block_state)
    for d in range(1, NY):
        got = shift_y(own, d).astype(F32)
        total = total + got
        before = before + jnp.where(y >= d, got, 0.0)
    total = total.astype(BF)
    for d in range(1, NX):
        before = before + jnp.where(x >= d, shift_x(total, d).astype(F32), 0.0)
    return before


def sum_heads(partial, z, c):
    rows = partial.reshape(NZ, NC, -1, partial.shape[-1])
    first = c == 0
    keep = jnp.where(first, rows[:, 0], rows[:, 1])
    give = jnp.where(first, rows[:, 1], rows[:, 0]).astype(BF)
    pair = keep + swap_core(give).astype(F32)
    total = lax.dynamic_index_in_dim(pair, z, 0, False)
    low = pair.astype(BF)
    for d in range(1, NZ):
        total = total + shift_z(lax.dynamic_index_in_dim(low, (z + d) % NZ, 0, False), d).astype(F32)
    return total


def body(
    query,
    key,
    value,
    head_gain,
    out_weight,
    stream,
    model_gain,
    expert_ids,
    expert_gates,
    gate_weight,
    up_weight,
    down_weight,
    weight_scales,
):
    seq = lax.axis_index("seq")
    head = lax.axis_index("head")
    x, y, z, c = seq // NY, seq % NY, head // NC, head % NC
    seq_rows = query.shape[0]
    tok_rows = stream.shape[0]
    heads_local = head_gain.shape[0] // HD
    experts = lax.axis_size("seq") * lax.axis_size("head")
    slots = experts * CAP

    full_out = lax.all_gather(out_weight, "seq", axis=1, tiled=True)

    query_rows = query.reshape(seq_rows, heads_local, HD)
    key_rows = key.reshape(seq_rows, heads_local, HD)
    value_rows = value.reshape(seq_rows, heads_local, HD)
    block_state = jnp.einsum("shd,she->hde", key_rows, value_rows, preferred_element_type=F32)
    prior_state = earlier_states(block_state, x, y)
    scores = jnp.einsum("thd,shd->hts", query_rows, key_rows, preferred_element_type=F32)
    causal = jnp.tril(jnp.ones((seq_rows, seq_rows), dtype=bool))
    scores = jnp.where(causal[None, :, :], scores, 0.0).astype(BF)
    local_part = jnp.einsum("hts,shd->thd", scores, value_rows, preferred_element_type=F32)
    earlier_part = jnp.einsum(
        "thd,hde->the", query_rows, prior_state.astype(BF), preferred_element_type=F32
    )
    mixed_heads = local_part + earlier_part
    mean_square = jnp.mean(mixed_heads * mixed_heads, axis=-1, keepdims=True)
    head_normed = (
        mixed_heads * lax.rsqrt(mean_square + 1e-06) * head_gain.reshape(heads_local, HD)
    ).astype(BF)
    head_normed = head_normed.reshape(seq_rows, heads_local * HD)

    flat_ids = expert_ids.reshape(-1)
    n = flat_ids.shape[0]
    at = jnp.arange(n, dtype=jnp.int32)
    same = (flat_ids[:, None] == flat_ids[None, :]) & (at[None, :] < at[:, None])
    slot_index = jnp.sum(same.astype(jnp.int32), axis=1)
    target = (flat_ids * CAP + slot_index).reshape(tok_rows, TOPK)
    chosen = target[:, :, None] == jnp.arange(slots, dtype=jnp.int32)[None, None, :]
    place = jnp.any(chosen, axis=1).astype(BF)
    gates = jnp.sum(jnp.where(chosen, expert_gates[:, :, None], 0.0), axis=1)
    gates_high = gates.astype(BF)
    gates_low = (gates - gates_high.astype(F32)).astype(BF)
    gates_two = jnp.concatenate([gates_high, gates_low], axis=0)

    partial = jnp.dot(head_normed, full_out, preferred_element_type=F32)
    attention = sum_heads(partial, z, c)
    residual_float = (stream.astype(F32) + attention).astype(BF).astype(F32)
    mean_square = jnp.mean(residual_float * residual_float, axis=-1, keepdims=True)
    normed = (residual_float * lax.rsqrt(mean_square + 1e-06) * model_gain).astype(BF)

    outgoing = jnp.einsum("ts,td->sd", place, normed, preferred_element_type=F32).astype(BF)
    lanes = 128
    message = outgoing.reshape(experts, CAP * D // lanes, lanes)
    arrived = lax.all_to_all(message, ("seq", "head"), split_axis=0, concat_axis=0, tiled=True)
    slot_rows = arrived.reshape(slots, D)
    scale_row = weight_scales[0]
    gate_part = jnp.dot(slot_rows, gate_weight[0], preferred_element_type=F32) * scale_row[0]
    up_part = jnp.dot(slot_rows, up_weight[0], preferred_element_type=F32) * scale_row[1]
    act = (jax.nn.silu(gate_part) * up_part).astype(BF)
    produced = jnp.dot(act, down_weight[0], preferred_element_type=F32) * scale_row[2]
    message = produced.astype(BF).reshape(experts, CAP * D // lanes, lanes)
    results = lax.all_to_all(message, ("seq", "head"), split_axis=0, concat_axis=0, tiled=True)
    results = results.reshape(slots, D)
    both = jnp.dot(gates_two, results, preferred_element_type=F32)
    expert_mix = both[:tok_rows] + both[tok_rows:]
    return (residual_float + expert_mix).astype(BF)


def solution(mesh):
    token = P(("seq", "head"), None)
    expert = P(("seq", "head"), None, None)
    return jax.shard_map(
        body,
        mesh=mesh,
        in_specs=(
            P("seq", "head"),
            P("seq", "head"),
            P("seq", "head"),
            P("head"),
            P("head", "seq"),
            token,
            P(),
            token,
            token,
            expert,
            expert,
            expert,
            token,
        ),
        out_specs=token,
        check_vma=False,
    )
```

time: 348 us -> 247 us (0.71)
  waiting for transfers between devices: 251 us -> 146 us
  starting transfers between devices: 16.4 us -> 29.7 us
  local copies, waits for them, and re-layouts: 26.2 us -> 21 us
    all_gather x1 -> x0, waiting for transfers between devices: 53.9 us -> none  [prefix(): gathered = lax.all_gather(part, axis)]
    reduce_scatter x1 -> x0, waiting for transfers between devices: 34 us -> none  [body(): lax.psum_scatter(jnp.dot(head_normed, full_out, preferred_element_type=jn...]
    ppermute x0 -> x10, waiting for transfers between devices: none -> 22.6 us  [the longest x3 10.4 us: shift_z(): return lax.ppermute(a, 'head', pairs)]
    all_to_all x2, waiting for transfers between devices: 105 us -> 82.8 us  [body(): lax.all_to_all(message, ('seq', 'head'), split_axis=0, concat_axis=0, til...]
    all_gather x1, waiting for transfers between devices: 57.4 us -> 39.6 us  [body(): full_out = lax.all_gather(out_weight, 'seq', axis=1, tiled=True)]
    ppermute x0 -> x10, starting transfers between devices: none -> 17.4 us  [the longest x3 5.88 us: shift_y(): return lax.ppermute(a, 'seq', pairs)]
    reshape x2 -> x4, local copies, waits for them, and re-layouts: 10.4 us -> 15.9 us  [the longest x1 5.87 us: body(): message = produced.astype(BF).reshape(experts, CAP * D // lanes, lanes)]
    scatter x1 -> x0, local copies, waits for them, and re-layouts: 4.84 us -> none  [body(): jnp.zeros((experts * capacity, D), jnp.bfloat16).at[target].set(source_rows)]
  transfers between devices with their start and end apart: 5 -> 13, of which waited for: 5 -> 11; matrix products, arithmetic and copies ran while one was open for 1% -> 2% of each run, Pallas kernels for 0% -> 0%
where the time goes in v1:
time: 247 us
  waiting for transfers between devices  146 us (59%)
  matrix products  31.8 us (13%)
  starting transfers between devices  29.7 us (12%)
  local copies, waits for them, and re-layouts  21 us (9%)
  between operations  13.6 us (6%)
  other arithmetic  4.65 us (2%)
    all_to_all x2, waiting for transfers between devices, body(): lax.all_to_all(message, ('seq', 'head'), split_axis=0, concat_axis=0, til...  82.8 us
    all_gather x1, waiting for transfers between devices, body(): full_out = lax.all_gather(out_weight, 'seq', axis=1, tiled=True)  39.6 us
    dot_general x1, matrix products, body(): jnp.dot(act, down_weight[0], preferred_element_type=F32) * scale_row[2]  14.5 us
    all_to_all x2, starting transfers between devices, body(): lax.all_to_all(message, ('seq', 'head'), split_axis=0, concat_axis=0, til...  12.4 us
    ppermute x3, waiting for transfers between devices, shift_z(): return lax.ppermute(a, 'head', pairs)  10.4 us
    dot_general x1, matrix products, body(): jnp.dot(slot_rows, gate_weight[0], preferred_element_type=F32)  8.15 us
    ppermute x3, starting transfers between devices, shift_y(): return lax.ppermute(a, 'seq', pairs)  5.88 us
    reshape x1, local copies, waits for them, and re-layouts, body(): message = produced.astype(BF).reshape(experts, CAP * D // lanes, lanes)  5.87 us
  transfers between devices with their start and end apart: 13, of which 11 were waited for; matrix products, arithmetic and copies ran while one was open for 2% of the time, Pallas kernels for 0%

profile of v1, /device:TPU:1, one launch (start us, length us, event | category | flops | bytes accessed | tf_op | source)
XLA Modules:
  0.0 246.5 jit_solution(13957495050865137763)
XLA Ops:
  8.6 2.2 collective-permute-start
  10.8 2.6 %collective-permute-start.1 = (bf16[4,128,128]{2,1,0:T(8,128)(2,1)S(1)}, bf16[4,128,128]{2,1,0:T(8,128)(2,1)S(1)}, u32[]{:S(2)}, u32[]{:S(2)}) collective-permute-start(bf16[4,128,128]{2,1,0:T(8,128)(2,1)S(1)} %get-tuple-element.17), channel_id=1, source_target_pairs={{0,16},{8,24},{16,0},{24,8},{32,48},{40,56},{48,32},{56,40},{64,80... | collective-permute-start | bytes 393224 | tf_op jit(solution)/shard_map/ppermute | solution.py:22
  15.3 3.8 %collective-permute-done.1 = bf16[4,128,128]{2,1,0:T(8,128)(2,1)S(1)} collective-permute-done((bf16[4,128,128]{2,1,0:T(8,128)(2,1)S(1)}, bf16[4,128,128]{2,1,0:T(8,128)(2,1)S(1)}, u32[]{:S(2)}, u32[]{:S(2)}) %collective-permute-start.1) | collective-permute-done | bytes 131104 | tf_op jit(solution)/shard_map/ppermute | solution.py:22
  20.5 2.5 collective-permute-start.4
  24.3 3.8 %collective-permute-done.4 = bf16[4,128,128]{2,1,0:T(8,128)(2,1)S(1)} collective-permute-done((bf16[4,128,128]{2,1,0:T(8,128)(2,1)S(1)}, bf16[4,128,128]{2,1,0:T(8,128)(2,1)S(1)}, u32[]{:S(2)}, u32[]{:S(2)}) %collective-permute-start.4) | collective-permute-done | bytes 131104 | tf_op jit(solution)/shard_map/ppermute | solution.py:17
  32.1 39.6 %all-gather.2.cloned.1.call-done = bf16[512,4096]{1,0:T(8,128)(2,1)} async-done(((bf16[512,256]{1,0:T(8,128)(2,1)}), bf16[512,4096]{1,0:T(8,128)(2,1)}) %all-gather.2.cloned.1.call-update) | async-done | bytes 4194320 | tf_op jit(solution)/shard_map/all_gather | solution.py:86
  71.7 3.4 %fusion.8 = f32[4,2,32,4096]{3,2,1,0:T(8,128)S(1)} fusion(bf16[4,2,32,512]{3,2,1,0:T(8,128)(2,1)S(1)} %dot_general.36, bf16[512,4096]{1,0:T(8,128)(2,1)} %all-gather.2.cloned.1.call-done), kind=kOutput, calls=%fused_computation.8 | convolution fusion | flops 1073741824 | bytes 8650752 | tf_op jit(solution)/shard_map/dot_general | solution.py:120
  75.1 1.9 copy-done.1
  79.3 1.8 collective-permute-done.6
  81.2 2.6 %fusion.83 = (bf16[4,32,4096]{2,1,0:T(8,128)(2,1)S(1)}, f32[4,32,4096]{2,1,0:T(8,128)S(1)}) fusion(bf16[4,32,4096]{2,1,0:T(8,128)(2,1)S(1)} %collective-permute-done.6, f32[4,2,32,4096]{3,2,1,0:T(8,128)} %copy-done.1, pred[]{:T(512)S(6)} %eq.37), kind=kLoop, calls=%fused_computation.97 | loop fusion | flops 2097152 | bytes 8388609 | tf_op jit(solution)/shard_map/convert_element_type | solution.py:56
  85.2 2.6 %collective-permute-start.8 = (bf16[32,4096]{1,0:T(8,128)(2,1)S(1)}, bf16[32,4096]{1,0:T(8,128)(2,1)S(1)}, u32[]{:S(2)}, u32[]{:S(2)}) collective-permute-start(bf16[32,4096]{1,0:T(8,128)(2,1)S(1)} %get-tuple-element.13), channel_id=1, source_target_pairs={{0,4},{1,5},{2,6},{3,7},{4,0},{5,1},{6,2},{7,3},{8,12},{9,13},{10,... | collective-permute-start | bytes 786440 | tf_op jit(solution)/shard_map/ppermute | solution.py:27
  89.1 3.6 %collective-permute-done.7 = bf16[32,4096]{1,0:T(8,128)(2,1)S(1)} collective-permute-done((bf16[32,4096]{1,0:T(8,128)(2,1)S(1)}, bf16[32,4096]{1,0:T(8,128)(2,1)S(1)}, u32[]{:S(2)}, u32[]{:S(2)}) %collective-permute-start.7) | collective-permute-done | bytes 262176 | tf_op jit(solution)/shard_map/ppermute | solution.py:27
  92.6 6.8 %collective-permute-done.8 = bf16[32,4096]{1,0:T(8,128)(2,1)S(1)} collective-permute-done((bf16[32,4096]{1,0:T(8,128)(2,1)S(1)}, bf16[32,4096]{1,0:T(8,128)(2,1)S(1)}, u32[]{:S(2)}, u32[]{:S(2)}) %collective-permute-start.8) | collective-permute-done | bytes 262176 | tf_op jit(solution)/shard_map/ppermute | solution.py:27
  101.5 3.4 %reshape.74 = bf16[128,96,128]{2,1,0:T(8,128)(2,1)} reshape(bf16[384,4096]{1,0:T(8,128)(2,1)S(1)} %convolution_convert_fusion) | data formatting | bytes 6291456 | tf_op jit(solution)/shard_map/reshape | solution.py:128
  104.9 7.7 %all-to-all-start = ((bf16[128,96,128]{2,1,0:T(8,128)(2,1)}), bf16[128,96,128]{2,1,0:T(8,128)(2,1)S(1)}, u32[]{:S(2)}, u32[]{:S(2)}) async-start(bf16[128,96,128]{2,1,0:T(8,128)(2,1)} %reshape.74), calls=%async_computation | async-start | bytes 6291456 | tf_op jit(solution)/shard_map/all_to_all | solution.py:129
  113.3 41.2 %all-to-all-done = bf16[128,96,128]{2,1,0:T(8,128)(2,1)S(1)} async-done(((bf16[128,96,128]{2,1,0:T(8,128)(2,1)}), bf16[128,96,128]{2,1,0:T(8,128)(2,1)S(1)}, u32[]{:S(2)}, u32[]{:S(2)}) %all-to-all-start) | async-done | bytes 3145760 | tf_op jit(solution)/shard_map/all_to_all | solution.py:129
  154.4 3.3 %reshape.75 = bf16[384,4096]{1,0:T(8,128)(2,1)} reshape(bf16[128,96,128]{2,1,0:T(8,128)(2,1)S(1)} %all-to-all-done) | data formatting | bytes 6291456 | tf_op jit(solution)/shard_map/reshape | solution.py:130
  157.8 8.1 %fusion.12 = f32[384,768]{1,0:T(8,128)} fusion(bf16[384,4096]{1,0:T(8,128)(2,1)} %reshape.75, bf16[1,4096,768]{2,1,0:T(8,128)(2,1)} %param.22, f32[]{:T(128)} %bitcast.15), kind=kOutput, calls=%fused_computation.14 | convolution fusion | flops 2416214016 | bytes 10616836 | tf_op jit(solution)/shard_map/dot_general | solution.py:132
  165.9 14.5 %multiply_convert_fusion = bf16[384,4096]{1,0:T(8,128)(2,1)} fusion(bf16[1,768,4096]{2,1,0:T(8,128)(2,1)} %param.24, f32[]{:T(128)} %bitcast.19, bf16[384,4096]{1,0:T(8,128)(2,1)S(1)} %copy-done.2, bf16[1,4096,768]{2,1,0:T(8,128)(2,1)} %param.23, f32[384,768]{1,0:T(8,128)} %fusion.12, f32[]{:T(128)} %bitcast.17), kind=kOutput, calls=%fused_computation.6 | convolution fusion | flops 4837048320 | bytes 20054024 | tf_op jit(solution)/shard_map/dot_general | solution.py:135
  180.4 5.9 %reshape.76 = bf16[128,96,128]{2,1,0:T(8,128)(2,1)} reshape(bf16[384,4096]{1,0:T(8,128)(2,1)} %multiply_convert_fusion) | data formatting | bytes 6291456 | tf_op jit(solution)/shard_map/reshape | solution.py:136
  186.3 4.7 %all-to-all-start.1 = ((bf16[128,96,128]{2,1,0:T(8,128)(2,1)}), bf16[128,96,128]{2,1,0:T(8,128)(2,1)S(1)}, u32[]{:S(2)}, u32[]{:S(2)}) async-start(bf16[128,96,128]{2,1,0:T(8,128)(2,1)} %reshape.76), calls=%async_computation.1 | async-start | bytes 6291456 | tf_op jit(solution)/shard_map/all_to_all | solution.py:137
  191.3 41.7 %all-to-all-done.1 = bf16[128,96,128]{2,1,0:T(8,128)(2,1)S(1)} async-done(((bf16[128,96,128]{2,1,0:T(8,128)(2,1)}), bf16[128,96,128]{2,1,0:T(8,128)(2,1)S(1)}, u32[]{:S(2)}, u32[]{:S(2)}) %all-to-all-start.1) | async-done | bytes 3145760 | tf_op jit(solution)/shard_map/all_to_all | solution.py:137
  233.0 3.3 %reshape.77 = bf16[384,4096]{1,0:T(8,128)(2,1)} reshape(bf16[128,96,128]{2,1,0:T(8,128)(2,1)S(1)} %all-to-all-done.1) | data formatting | bytes 6291456 | tf_op jit(solution)/shard_map/reshape | solution.py:138
  236.3 2.6 %fusion.74 = f32[64,4096]{1,0:T(8,128)S(1)} fusion(bf16[384,4096]{1,0:T(8,128)(2,1)} %reshape.77, bf16[32,384]{1,0:T(8,128)(2,1)S(1)} %get-tuple-element.5, bf16[32,384]{1,0:T(8,128)(2,1)S(1)} %get-tuple-element.6), kind=kOutput, calls=%fused_computation.85 | convolution fusion | flops 201424896 | bytes 4243456 | tf_op jit(solution)/shard_map/dot_general | solution.py:139
  (62 shorter events, 19.2 us)
Async XLA Ops:
  6.5 1.8 copy-start
  6.5 24.6 %copy-start.11 = (bf16[256,512]{1,0:T(8,128)(2,1)S(1)}, bf16[256,512]{1,0:T(8,128)(2,1)}, u32[]{:S(2)}) copy-start(bf16[256,512]{1,0:T(8,128)(2,1)} %param.13) | copy-start | bytes 786436
  6.5 65.1 %all-gather.2.cloned.1.call-start = ((), (), s32[]{:S(2)}) async-start(), calls=%async_computation.2 | async-start | bytes 4456448 | tf_op jit(solution)/shard_map/all_gather | solution.py:86
  7.3 24.4 %copy-start.10 = (f32[512]{0:T(512)S(1)}, f32[512]{0:T(512)}, u32[]{:S(2)}) copy-start(f32[512]{0:T(512)} %param.16) | copy-start | bytes 6148
  8.6 6.7 %collective-permute-start = (bf16[4,128,128]{2,1,0:T(8,128)(2,1)S(1)}, bf16[4,128,128]{2,1,0:T(8,128)(2,1)S(1)}, u32[]{:S(2)}, u32[]{:S(2)}) collective-permute-start(bf16[4,128,128]{2,1,0:T(8,128)(2,1)S(1)} %get-tuple-element.17), channel_id=1, source_target_pairs={{0,8},{8,16},{16,24},{24,0},{32,40},{40,48},{48,56},{56,32},{64,72... | collective-permute-start | bytes 393224 | tf_op jit(solution)/shard_map/ppermute | solution.py:22
  10.8 8.3 %collective-permute-start.1 = (bf16[4,128,128]{2,1,0:T(8,128)(2,1)S(1)}, bf16[4,128,128]{2,1,0:T(8,128)(2,1)S(1)}, u32[]{:S(2)}, u32[]{:S(2)}) collective-permute-start(bf16[4,128,128]{2,1,0:T(8,128)(2,1)S(1)} %get-tuple-element.17), channel_id=1, source_target_pairs={{0,16},{8,24},{16,0},{24,8},{32,48},{40,56},{48,32},{56,40},{64,80... | collective-permute-start | bytes 393224 | tf_op jit(solution)/shard_map/ppermute | solution.py:22
  13.4 5.7 %collective-permute-start.2 = (bf16[4,128,128]{2,1,0:T(8,128)(2,1)S(1)}, bf16[4,128,128]{2,1,0:T(8,128)(2,1)S(1)}, u32[]{:S(2)}, u32[]{:S(2)}) collective-permute-start(bf16[4,128,128]{2,1,0:T(8,128)(2,1)S(1)} %get-tuple-element.17), channel_id=1, source_target_pairs={{0,24},{8,0},{16,8},{24,16},{32,56},{40,32},{48,40},{56,48},{64,88... | collective-permute-start | bytes 393224 | tf_op jit(solution)/shard_map/ppermute | solution.py:22
  19.2 5.1 %collective-permute-start.3 = (bf16[4,128,128]{2,1,0:T(8,128)(2,1)S(1)}, bf16[4,128,128]{2,1,0:T(8,128)(2,1)S(1)}, u32[]{:S(2)}, u32[]{:S(2)}) collective-permute-start(bf16[4,128,128]{2,1,0:T(8,128)(2,1)S(1)} %fusion.50), channel_id=1, source_target_pairs={{0,32},{8,40},{16,48},{24,56},{32,64},{40,72},{48,80},{56,88},{64,... | collective-permute-start | bytes 393224 | tf_op jit(solution)/shard_map/ppermute | solution.py:17
  20.5 7.6 %collective-permute-start.4 = (bf16[4,128,128]{2,1,0:T(8,128)(2,1)S(1)}, bf16[4,128,128]{2,1,0:T(8,128)(2,1)S(1)}, u32[]{:S(2)}, u32[]{:S(2)}) collective-permute-start(bf16[4,128,128]{2,1,0:T(8,128)(2,1)S(1)} %fusion.50), channel_id=1, source_target_pairs={{0,64},{8,72},{16,80},{24,88},{32,96},{40,104},{48,112},{56,120},{... | collective-permute-start | bytes 393224 | tf_op jit(solution)/shard_map/ppermute | solution.py:17
  22.9 6.9 %collective-permute-start.5 = (bf16[4,128,128]{2,1,0:T(8,128)(2,1)S(1)}, bf16[4,128,128]{2,1,0:T(8,128)(2,1)S(1)}, u32[]{:S(2)}, u32[]{:S(2)}) collective-permute-start(bf16[4,128,128]{2,1,0:T(8,128)(2,1)S(1)} %fusion.50), channel_id=1, source_target_pairs={{0,96},{8,104},{16,112},{24,120},{32,0},{40,8},{48,16},{56,24},{64... | collective-permute-start | bytes 393224 | tf_op jit(solution)/shard_map/ppermute | solution.py:17
  75.1 1.9 copy-start.1
  77.1 1.8 copy-start.8
  77.3 3.9 %collective-permute-start.6 = (bf16[4,32,4096]{2,1,0:T(8,128)(2,1)S(1)}, bf16[4,32,4096]{2,1,0:T(8,128)(2,1)S(1)}, u32[]{:S(2)}, u32[]{:S(2)}) collective-permute-start(bf16[4,32,4096]{2,1,0:T(8,128)(2,1)S(1)} %fusion.28), channel_id=1, source_target_pairs={{0,1},{1,0},{2,3},{3,2},{4,5},{5,4},{6,7},{7,6},{8,9},{9,8},{10,11... | collective-permute-start | bytes 3145736 | tf_op jit(solution)/shard_map/ppermute | solution.py:32
  79.3 20.1 %copy-start.5 = (bf16[32,4096]{1,0:T(8,128)(2,1)S(1)}, bf16[32,4096]{1,0:T(8,128)(2,1)}, u32[]{:S(2)}) copy-start(bf16[32,4096]{1,0:T(8,128)(2,1)} %param.18) | copy-start | bytes 786436
  83.8 16.7 %copy-start.6 = (f32[4096]{0:T(1024)S(1)}, f32[4096]{0:T(1024)}, u32[]{:S(2)}) copy-start(f32[4096]{0:T(1024)} %param.19) | copy-start | bytes 49156
  83.8 8.8 %collective-permute-start.7 = (bf16[32,4096]{1,0:T(8,128)(2,1)S(1)}, bf16[32,4096]{1,0:T(8,128)(2,1)S(1)}, u32[]{:S(2)}, u32[]{:S(2)}) collective-permute-start(bf16[32,4096]{1,0:T(8,128)(2,1)S(1)} %get-tuple-element.11), channel_id=1, source_target_pairs={{0,2},{1,3},{2,4},{3,5},{4,6},{5,7},{6,0},{7,1},{8,10},{9,11},{10,... | collective-permute-start | bytes 786440 | tf_op jit(solution)/shard_map/ppermute | solution.py:27
  85.2 14.2 %collective-permute-start.8 = (bf16[32,4096]{1,0:T(8,128)(2,1)S(1)}, bf16[32,4096]{1,0:T(8,128)(2,1)S(1)}, u32[]{:S(2)}, u32[]{:S(2)}) collective-permute-start(bf16[32,4096]{1,0:T(8,128)(2,1)S(1)} %get-tuple-element.13), channel_id=1, source_target_pairs={{0,4},{1,5},{2,6},{3,7},{4,0},{5,1},{6,2},{7,3},{8,12},{9,13},{10,... | collective-permute-start | bytes 786440 | tf_op jit(solution)/shard_map/ppermute | solution.py:27
  87.8 11.7 %collective-permute-start.9 = (bf16[32,4096]{1,0:T(8,128)(2,1)S(1)}, bf16[32,4096]{1,0:T(8,128)(2,1)S(1)}, u32[]{:S(2)}, u32[]{:S(2)}) collective-permute-start(bf16[32,4096]{1,0:T(8,128)(2,1)S(1)} %get-tuple-element.12), channel_id=1, source_target_pairs={{0,6},{1,7},{2,0},{3,1},{4,2},{5,3},{6,4},{7,5},{8,14},{9,15},{10,... | collective-permute-start | bytes 786440 | tf_op jit(solution)/shard_map/ppermute | solution.py:27
  104.9 7.7 %copy-start.7 = (f32[1,3]{1,0:T(1,128)S(1)}, f32[1,3]{1,0:T(1,128)}, u32[]{:S(2)}) copy-start(f32[1,3]{1,0:T(1,128)} %param.25) | copy-start | bytes 40
  104.9 49.5 %all-to-all-start = ((bf16[128,96,128]{2,1,0:T(8,128)(2,1)}), bf16[128,96,128]{2,1,0:T(8,128)(2,1)S(1)}, u32[]{:S(2)}, u32[]{:S(2)}) async-start(bf16[128,96,128]{2,1,0:T(8,128)(2,1)} %reshape.74), calls=%async_computation | async-start | bytes 6291456 | tf_op jit(solution)/shard_map/all_to_all | solution.py:129
  157.8 8.2 %copy-start.2 = (bf16[384,4096]{1,0:T(8,128)(2,1)S(1)}, bf16[384,4096]{1,0:T(8,128)(2,1)}, u32[]{:S(2)}) copy-start(bf16[384,4096]{1,0:T(8,128)(2,1)} %reshape.75) | copy-start | bytes 9437188
  186.3 4.7 %copy-start.9 = (f32[32,8]{0,1:T(8,128)S(1)}, f32[32,8]{0,1:T(8,128)}, u32[]{:S(2)}) copy-start(f32[32,8]{0,1:T(8,128)} %param.21) | copy-start | bytes 3076
  186.3 46.7 %all-to-all-start.1 = ((bf16[128,96,128]{2,1,0:T(8,128)(2,1)}), bf16[128,96,128]{2,1,0:T(8,128)(2,1)S(1)}, u32[]{:S(2)}, u32[]{:S(2)}) async-start(bf16[128,96,128]{2,1,0:T(8,128)(2,1)} %reshape.76), calls=%async_computation.1 | async-start | bytes 6291456 | tf_op jit(solution)/shard_map/all_to_all | solution.py:137
  236.3 2.6 %copy-start.4 = (bf16[32,4096]{1,0:T(8,128)(2,1)S(1)}, bf16[32,4096]{1,0:T(8,128)(2,1)}, u32[]{:S(2)}) copy-start(bf16[32,4096]{1,0:T(8,128)(2,1)} %copy-done.3) | copy-start | bytes 786436
  (1 other events, 0.7 us)
Sparse Core Ops, SparseCore 0:
  9.5 62.1 all-gather.1

commit v2 on v1

--- a/solution.py
+++ b/solution.py
@@ -1,25 +1,17 @@
 import jax
 import jax.numpy as jnp
 from jax import lax
+from jax.experimental import pallas as pl
+from jax.experimental.pallas import tpu as pltpu
 from jax.sharding import PartitionSpec as P
 
 D = 4096
 HD = 128
 TOPK = 8
 CAP = 3
-NX, NY, NZ, NC = 4, 4, 4, 2
+NZ, NC = 4, 2
 BF = jnp.bfloat16
 F32 = jnp.float32
-
-
-def shift_x(a, d):
-    pairs = [(x * NY + y, (x + d) % NX * NY + y) for x in range(NX) for y in range(NY)]
-    return lax.ppermute(a, "seq", pairs)
-
-
-def shift_y(a, d):
-    pairs = [(x * NY + y, x * NY + (y + d) % NY) for x in range(NX) for y in range(NY)]
-    return lax.ppermute(a, "seq", pairs)
 
 
 def shift_z(a, d):
@@ -32,18 +24,15 @@
     return lax.ppermute(a, "head", pairs)
 
 
-def earlier_states(block_state, x, y):
-    own = block_state.astype(BF)
-    total = block_state
-    before = jnp.zeros_like(block_state)
-    for d in range(1, NY):
-        got = shift_y(own, d).astype(F32)
-        total = total + got
-        before = before + jnp.where(y >= d, got, 0.0)
-    total = total.astype(BF)
-    for d in range(1, NX):
-        before = before + jnp.where(x >= d, shift_x(total, d).astype(F32), 0.0)
-    return before
+def earlier_states(block_state, seq):
+    blocks = lax.axis_size("seq")
+    parts = block_state.reshape(blocks, -1, HD)
+    got = lax.all_to_all(parts, "seq", split_axis=0, concat_axis=0, tiled=True)
+    sums = [jnp.zeros_like(got[0])]
+    for block in range(blocks - 1):
+        sums.append(sums[-1] + got[block])
+    back = lax.all_to_all(jnp.stack(sums).astype(BF), "seq", split_axis=0, concat_axis=0, tiled=True)
+    return back.reshape(block_state.shape)
 
 
 def sum_heads(partial, z, c):
@@ -57,6 +46,53 @@
     for d in range(1, NZ):
         total = total + shift_z(lax.dynamic_index_in_dim(low, (z + d) % NZ, 0, False), d).astype(F32)
     return total
+
+
+WIDE = 256
+OUT = 1024
+
+
+def expert_kernel(scale, rows, gate, up, down, out, act):
+    step = pl.program_id(0)
+    wide = act.shape[0]
+
+    @pl.when(step < wide)
+    def _():
+        x = rows[...]
+        gate_part = jnp.dot(x, gate[...], preferred_element_type=F32) * scale[0, 0]
+        up_part = jnp.dot(x, up[...], preferred_element_type=F32) * scale[0, 1]
+        act[step] = (gate_part / (1.0 + jnp.exp(-gate_part)) * up_part).astype(BF)
+
+    @pl.when(step >= wide)
+    def _():
+        total = jnp.dot(act[0], down[0:WIDE], preferred_element_type=F32)
+        for j in range(1, wide):
+            total += jnp.dot(act[j], down[j * WIDE : (j + 1) * WIDE], preferred_element_type=F32)
+        out[...] = (total * scale[0, 2]).astype(BF)
+
+
+def run_expert(scale, rows, gate, up, down):
+    count, depth = rows.shape
+    hidden = gate.shape[1]
+    wide = hidden // WIDE
+    return pl.pallas_call(
+        expert_kernel,
+        out_shape=jax.ShapeDtypeStruct((count, depth), BF),
+        grid=(wide + depth // OUT,),
+        in_specs=[
+            pl.BlockSpec(memory_space=pltpu.SMEM),
+            pl.BlockSpec((count, depth), lambda i: (0, 0)),
+            pl.BlockSpec((depth, WIDE), lambda i: (0, jnp.minimum(i, wide - 1))),
+            pl.BlockSpec((depth, WIDE), lambda i: (0, jnp.minimum(i, wide - 1))),
+            pl.BlockSpec((hidden, OUT), lambda i: (0, jnp.maximum(i - wide, 0))),
+        ],
+        out_specs=pl.BlockSpec((count, OUT), lambda i: (0, jnp.maximum(i - wide, 0))),
+        scratch_shapes=[pltpu.VMEM((wide, count, WIDE), BF)],
+        compiler_params=pltpu.CompilerParams(vmem_limit_bytes=40 << 20),
+        cost_estimate=pl.CostEstimate(
+            flops=6 * count * depth * hidden, bytes_accessed=6 * depth * hidden, transcendentals=count * hidden
+        ),
+    )(scale, rows, gate, up, down)
 
 
 def body(
@@ -76,7 +112,7 @@
 ):
     seq = lax.axis_index("seq")
     head = lax.axis_index("head")
-    x, y, z, c = seq // NY, seq % NY, head // NC, head % NC
+    z, c = head // NC, head % NC
     seq_rows = query.shape[0]
     tok_rows = stream.shape[0]
     heads_local = head_gain.shape[0] // HD
@@ -89,13 +125,13 @@
     key_rows = key.reshape(seq_rows, heads_local, HD)
     value_rows = value.reshape(seq_rows, heads_local, HD)
     block_state = jnp.einsum("shd,she->hde", key_rows, value_rows, preferred_element_type=F32)
-    prior_state = earlier_states(block_state, x, y)
+    prior_state = earlier_states(block_state, seq)
     scores = jnp.einsum("thd,shd->hts", query_rows, key_rows, preferred_element_type=F32)
     causal = jnp.tril(jnp.ones((seq_rows, seq_rows), dtype=bool))
     scores = jnp.where(causal[None, :, :], scores, 0.0).astype(BF)
     local_part = jnp.einsum("hts,shd->thd", scores, value_rows, preferred_element_type=F32)
     earlier_part = jnp.einsum(
-        "thd,hde->the", query_rows, prior_state.astype(BF), preferred_element_type=F32
+        "thd,hde->the", query_rows, prior_state, preferred_element_type=F32
     )
     mixed_heads = local_part + earlier_part
     mean_square = jnp.mean(mixed_heads * mixed_heads, axis=-1, keepdims=True)
@@ -128,12 +164,8 @@
     message = outgoing.reshape(experts, CAP * D // lanes, lanes)
     arrived = lax.all_to_all(message, ("seq", "head"), split_axis=0, concat_axis=0, tiled=True)
     slot_rows = arrived.reshape(slots, D)
-    scale_row = weight_scales[0]
-    gate_part = jnp.dot(slot_rows, gate_weight[0], preferred_element_type=F32) * scale_row[0]
-    up_part = jnp.dot(slot_rows, up_weight[0], preferred_element_type=F32) * scale_row[1]
-    act = (jax.nn.silu(gate_part) * up_part).astype(BF)
-    produced = jnp.dot(act, down_weight[0], preferred_element_type=F32) * scale_row[2]
-    message = produced.astype(BF).reshape(experts, CAP * D // lanes, lanes)
+    produced = run_expert(weight_scales, slot_rows, gate_weight[0], up_weight[0], down_weight[0])
+    message = produced.reshape(experts, CAP * D // lanes, lanes)
     results = lax.all_to_all(message, ("seq", "head"), split_axis=0, concat_axis=0, tiled=True)
     results = results.reshape(slots, D)
     both = jnp.dot(gates_two, results, preferred_element_type=F32)

time: 247 us -> 240 us (0.972)
  waiting for transfers between devices: 146 us -> 91.6 us
  blocking collectives: 0 us -> 49.6 us
  matrix products: 31.8 us -> 9.7 us
  Pallas kernels: 0 us -> 12.5 us
  other arithmetic: 4.65 us -> 13 us
  starting transfers between devices: 29.7 us -> 22.5 us
  local copies, waits for them, and re-layouts: 21 us -> 26.8 us
    all_to_all x0 -> x1, blocking collectives: none -> 49.6 us  [body(): lax.all_to_all(message, ('seq', 'head'), split_axis=0, concat_axis=0, til...]
    all_to_all x2 -> x1, waiting for transfers between devices: 82.8 us -> 41.7 us  [body(): lax.all_to_all(message, ('seq', 'head'), split_axis=0, concat_axis=0, til...]
    dot_general x3 -> x1, matrix products: 24 us -> 0.26 us  [body(): jnp.einsum('thd,hde->the', query_rows, prior_state, preferred_element_typ...]
    all_gather x1, waiting for transfers between devices: 39.6 us -> 23.4 us  [body(): full_out = lax.all_gather(out_weight, 'seq', axis=1, tiled=True)]
    all_to_all x0 -> x2, waiting for transfers between devices: none -> 13.6 us  [the longest x1 6.86 us: earlier_states(): got = lax.all_to_all(parts, 'seq', split_axis=0, concat_axis=0, tiled=True)]
    pallas_call x0 -> x1, Pallas kernels: none -> 12.5 us  [run_expert(): pl.pallas_call(expert_kernel, out_shape=jax.ShapeDtypeStruct((count, dept...]
    all_to_all x0 -> x2, starting transfers between devices: none -> 11.1 us  [the longest x1 7.58 us: earlier_states(): got = lax.all_to_all(parts, 'seq', split_axis=0, concat_axis=0, tiled=True)]
    ppermute x6 -> x0, starting transfers between devices: 10.7 us -> none  [the longest x3 5.88 us: shift_y(): return lax.ppermute(a, 'seq', pairs)]
  transfers between devices with their start and end apart: 13 -> 8, of which waited for: 11 -> 7; matrix products, arithmetic and copies ran while one was open for 2% -> 6% of each run, Pallas kernels for 0% -> 0%
where the time goes in v2:
time: 240 us; the launch traced here: 239 us
  waiting for transfers between devices  91.6 us (38%)
  blocking collectives  49.6 us (21%)
  local copies, waits for them, and re-layouts  26.8 us (11%)
  starting transfers between devices  22.5 us (9%)
  between operations  13.7 us (6%)
  other arithmetic  13 us (5%)
  Pallas kernels  12.5 us (5%)
  matrix products  9.7 us (4%)
    all_to_all x1, blocking collectives, body(): lax.all_to_all(message, ('seq', 'head'), split_axis=0, concat_axis=0, til...  49.6 us
    all_to_all x1, waiting for transfers between devices, body(): lax.all_to_all(message, ('seq', 'head'), split_axis=0, concat_axis=0, til...  41.7 us
    all_gather x1, waiting for transfers between devices, body(): full_out = lax.all_gather(out_weight, 'seq', axis=1, tiled=True)  23.4 us
    pallas_call x1, Pallas kernels, run_expert(): pl.pallas_call(expert_kernel, out_shape=jax.ShapeDtypeStruct((count, dept...  12.5 us
    ppermute x3, waiting for transfers between devices, shift_z(): return lax.ppermute(a, 'head', pairs)  10.4 us
    unnamed x30, local copies, waits for them, and re-layouts  8.44 us
    unnamed x13, other arithmetic  7.8 us
    all_to_all x1, starting transfers between devices, earlier_states(): got = lax.all_to_all(parts, 'seq', split_axis=0, concat_axis=0, tiled=True)  7.58 us
  transfers between devices with their start and end apart: 8, of which 7 were waited for; matrix products, arithmetic and copies ran while one was open for 6% of the time, Pallas kernels for 0%

profile of v2, /device:TPU:1, one launch (start us, length us, event | category | flops | bytes accessed | tf_op | source)
XLA Modules:
  0.0 239.4 jit_solution(10632460798656275408)
XLA Ops:
  8.4 1.9 fusion.22
  10.2 7.6 %all-to-all-start = ((f32[16,32,128]{2,1,0:T(8,128)}), f32[16,32,128]{2,1,0:T(8,128)S(1)}, u32[]{:S(2)}, u32[]{:S(2)}) async-start(f32[16,32,128]{2,1,0:T(8,128)} %bitcast.1), calls=%async_computation | async-start | bytes 524288 | tf_op jit(solution)/shard_map/all_to_all | solution.py:30
  18.4 6.9 %all-to-all-done = f32[16,32,128]{2,1,0:T(8,128)S(1)} async-done(((f32[16,32,128]{2,1,0:T(8,128)}), f32[16,32,128]{2,1,0:T(8,128)S(1)}, u32[]{:S(2)}, u32[]{:S(2)}) %all-to-all-start) | async-done | bytes 262176 | tf_op jit(solution)/shard_map/all_to_all | solution.py:30
  34.3 3.6 %all-to-all-start.1 = ((bf16[16,32,128]{2,1,0:T(8,128)(2,1)}), bf16[16,32,128]{2,1,0:T(8,128)(2,1)S(1)}, u32[]{:S(2)}, u32[]{:S(2)}) async-start(bf16[16,32,128]{2,1,0:T(8,128)(2,1)} %constant_dynamic-update-slice_fusion), calls=%async_computation.1 | async-start | bytes 262144 | tf_op jit(solution)/shard_map/all_to_all | solution.py:34
  37.9 6.7 %all-to-all-done.1 = bf16[16,32,128]{2,1,0:T(8,128)(2,1)S(1)} async-done(((bf16[16,32,128]{2,1,0:T(8,128)(2,1)}), bf16[16,32,128]{2,1,0:T(8,128)(2,1)S(1)}, u32[]{:S(2)}, u32[]{:S(2)}) %all-to-all-start.1) | async-done | bytes 131104 | tf_op jit(solution)/shard_map/all_to_all | solution.py:34
  45.8 23.4 %all-gather.2.cloned.1.call-done = bf16[512,4096]{1,0:T(8,128)(2,1)} async-done(((bf16[512,256]{1,0:T(8,128)(2,1)}), bf16[512,4096]{1,0:T(8,128)(2,1)}) %all-gather.2.cloned.1.call-update) | async-done | bytes 4194320 | tf_op jit(solution)/shard_map/all_gather | solution.py:122
  69.2 3.4 %fusion = f32[4,2,32,4096]{3,2,1,0:T(8,128)S(1)} fusion(bf16[4,2,32,512]{3,2,1,0:T(8,128)(2,1)S(1)} %dot_general.27, bf16[512,4096]{1,0:T(8,128)(2,1)} %all-gather.2.cloned.1.call-done), kind=kOutput, calls=%fused_computation.1 | convolution fusion | flops 1073741824 | bytes 8650752 | tf_op jit(solution)/shard_map/dot_general | solution.py:156
  72.7 1.9 copy-done.4
  74.8 1.6 collective-permute-start
  76.9 1.8 collective-permute-done
  78.7 2.6 %fusion.43 = (bf16[4,32,4096]{2,1,0:T(8,128)(2,1)S(1)}, f32[4,32,4096]{2,1,0:T(8,128)S(1)}) fusion(bf16[4,32,4096]{2,1,0:T(8,128)(2,1)S(1)} %collective-permute-done, f32[4,2,32,4096]{3,2,1,0:T(8,128)} %copy-done.4, pred[]{:T(512)S(6)} %eq.36), kind=kLoop, calls=%fused_computation.94 | loop fusion | flops 2097152 | bytes 8388609 | tf_op jit(solution)/shard_map/convert_element_type | solution.py:45
  82.8 2.6 %collective-permute-start.2 = (bf16[32,4096]{1,0:T(8,128)(2,1)S(1)}, bf16[32,4096]{1,0:T(8,128)(2,1)S(1)}, u32[]{:S(2)}, u32[]{:S(2)}) collective-permute-start(bf16[32,4096]{1,0:T(8,128)(2,1)S(1)} %get-tuple-element.23), channel_id=1, source_target_pairs={{0,4},{1,5},{2,6},{3,7},{4,0},{5,1},{6,2},{7,3},{8,12},{9,13},{10,... | collective-permute-start | bytes 786440 | tf_op jit(solution)/shard_map/ppermute | solution.py:19
  86.6 3.6 %collective-permute-done.1 = bf16[32,4096]{1,0:T(8,128)(2,1)S(1)} collective-permute-done((bf16[32,4096]{1,0:T(8,128)(2,1)S(1)}, bf16[32,4096]{1,0:T(8,128)(2,1)S(1)}, u32[]{:S(2)}, u32[]{:S(2)}) %collective-permute-start.1) | collective-permute-done | bytes 262176 | tf_op jit(solution)/shard_map/ppermute | solution.py:19
  90.3 6.8 %collective-permute-done.2 = bf16[32,4096]{1,0:T(8,128)(2,1)S(1)} collective-permute-done((bf16[32,4096]{1,0:T(8,128)(2,1)S(1)}, bf16[32,4096]{1,0:T(8,128)(2,1)S(1)}, u32[]{:S(2)}, u32[]{:S(2)}) %collective-permute-start.2) | collective-permute-done | bytes 262176 | tf_op jit(solution)/shard_map/ppermute | solution.py:19
  99.1 3.4 %reshape.76 = bf16[128,96,128]{2,1,0:T(8,128)(2,1)} reshape(bf16[384,4096]{1,0:T(8,128)(2,1)S(1)} %convolution_convert_fusion) | data formatting | bytes 6291456 | tf_op jit(solution)/shard_map/reshape | solution.py:164
  102.5 49.6 %all_to_all.20 = bf16[128,96,128]{2,1,0:T(8,128)(2,1)} all-to-all(bf16[128,96,128]{2,1,0:T(8,128)(2,1)} %reshape.76), channel_id=1, replica_groups=mesh['seq'=16,'head'=8] {'seq','head'}, dimensions={0} | all-to-all | bytes 6291456 | tf_op jit(solution)/shard_map/all_to_all | solution.py:165
  152.1 4.1 %reshape.77.rows = bf16[384,4096]{1,0:T(8,128)(2,1)S(1)} reshape(bf16[128,96,128]{2,1,0:T(8,128)(2,1)} %all_to_all.20) | data formatting | bytes 6291456 | tf_op jit(solution)/shard_map/reshape | solution.py:166
  156.3 2.8 %copy-done.2 = bf16[1,4096,768]{2,1,0:T(8,128)(2,1)S(1)} copy-done((bf16[1,4096,768]{2,1,0:T(8,128)(2,1)S(1)}, bf16[1,4096,768]{2,1,0:T(8,128)(2,1)}, u32[]{:S(2)}) %copy-start.2) | copy-done | bytes 6291480
  159.1 12.5 %shard_map.127 = bf16[384,4096]{1,0:T(8,128)(2,1)S(1)} custom-call(f32[1,3]{1,0:T(1,128)S(1)} %copy-done.3, bf16[384,4096]{1,0:T(8,128)(2,1)S(1)} %reshape.77.rows, bf16[4096,768]{1,0:T(8,128)(2,1)S(1)} %bitcast.94, bf16[4096,768]{1,0:T(8,128)(2,1)} %bitcast.99, bf16[768,4096]{1,0:T(8,128)(2,1)} %bitcast.100), custom_call_target="tpu_custom_call" | custom-call | flops 7247757312 | bytes 18874368 | tf_op jit(solution)/shard_map/pallas_call | solution.py:78
  173.3 5.9 %reshape.78 = bf16[128,96,128]{2,1,0:T(8,128)(2,1)} reshape(bf16[384,4096]{1,0:T(8,128)(2,1)} %copy-done.1) | data formatting | bytes 6291456 | tf_op jit(solution)/shard_map/reshape | solution.py:168
  179.2 4.7 %all-to-all-start.3 = ((bf16[128,96,128]{2,1,0:T(8,128)(2,1)}), bf16[128,96,128]{2,1,0:T(8,128)(2,1)S(1)}, u32[]{:S(2)}, u32[]{:S(2)}) async-start(bf16[128,96,128]{2,1,0:T(8,128)(2,1)} %reshape.78), calls=%async_computation.3 | async-start | bytes 6291456 | tf_op jit(solution)/shard_map/all_to_all | solution.py:169
  184.1 41.7 %all-to-all-done.3 = bf16[128,96,128]{2,1,0:T(8,128)(2,1)S(1)} async-done(((bf16[128,96,128]{2,1,0:T(8,128)(2,1)}), bf16[128,96,128]{2,1,0:T(8,128)(2,1)S(1)}, u32[]{:S(2)}, u32[]{:S(2)}) %all-to-all-start.3) | async-done | bytes 3145760 | tf_op jit(solution)/shard_map/all_to_all | solution.py:169
  225.8 3.3 %reshape.79 = bf16[384,4096]{1,0:T(8,128)(2,1)} reshape(bf16[128,96,128]{2,1,0:T(8,128)(2,1)S(1)} %all-to-all-done.3) | data formatting | bytes 6291456 | tf_op jit(solution)/shard_map/reshape | solution.py:170
  229.1 2.6 %fusion.35 = f32[64,4096]{1,0:T(8,128)S(1)} fusion(bf16[384,4096]{1,0:T(8,128)(2,1)} %reshape.79, bf16[32,384]{1,0:T(8,128)(2,1)S(1)} %get-tuple-element.5, bf16[32,384]{1,0:T(8,128)(2,1)S(1)} %get-tuple-element.6), kind=kOutput, calls=%fused_computation.52 | convolution fusion | flops 201424896 | bytes 4243456 | tf_op jit(solution)/shard_map/dot_general | solution.py:171
  (68 shorter events, 20.7 us)
Async XLA Ops:
  6.5 38.0 %copy-start = (bf16[256,512]{1,0:T(8,128)(2,1)S(1)}, bf16[256,512]{1,0:T(8,128)(2,1)}, u32[]{:S(2)}) copy-start(bf16[256,512]{1,0:T(8,128)(2,1)} %param.13) | copy-start | bytes 786436
  6.5 38.3 %copy-start.7 = (bf16[256,512]{1,0:T(8,128)(2,1)S(1)}, bf16[256,512]{1,0:T(8,128)(2,1)}, u32[]{:S(2)}) copy-start(bf16[256,512]{1,0:T(8,128)(2,1)} %param.15) | copy-start | bytes 786436
  6.5 38.8 %copy-start.12 = (f32[512]{0:T(512)S(1)}, f32[512]{0:T(512)}, u32[]{:S(2)}) copy-start(f32[512]{0:T(512)} %param.16) | copy-start | bytes 6148
  6.5 62.7 %all-gather.2.cloned.1.call-start = ((), (), s32[]{:S(2)}) async-start(), calls=%async_computation.4 | async-start | bytes 4456448 | tf_op jit(solution)/shard_map/all_gather | solution.py:122
  10.2 15.0 %all-to-all-start = ((f32[16,32,128]{2,1,0:T(8,128)}), f32[16,32,128]{2,1,0:T(8,128)S(1)}, u32[]{:S(2)}, u32[]{:S(2)}) async-start(f32[16,32,128]{2,1,0:T(8,128)} %bitcast.1), calls=%async_computation | async-start | bytes 524288 | tf_op jit(solution)/shard_map/all_to_all | solution.py:30
  34.3 10.3 %all-to-all-start.1 = ((bf16[16,32,128]{2,1,0:T(8,128)(2,1)}), bf16[16,32,128]{2,1,0:T(8,128)(2,1)S(1)}, u32[]{:S(2)}, u32[]{:S(2)}) async-start(bf16[16,32,128]{2,1,0:T(8,128)(2,1)} %constant_dynamic-update-slice_fusion), calls=%async_computation.1 | async-start | bytes 262144 | tf_op jit(solution)/shard_map/all_to_all | solution.py:34
  72.7 1.9 copy-start.4
  74.6 1.8 copy-start.10
  74.8 3.9 %collective-permute-start = (bf16[4,32,4096]{2,1,0:T(8,128)(2,1)S(1)}, bf16[4,32,4096]{2,1,0:T(8,128)(2,1)S(1)}, u32[]{:S(2)}, u32[]{:S(2)}) collective-permute-start(bf16[4,32,4096]{2,1,0:T(8,128)(2,1)S(1)} %fusion.8), channel_id=1, source_target_pairs={{0,1},{1,0},{2,3},{3,2},{4,5},{5,4},{6,7},{7,6},{8,9},{9,8},{10,11... | collective-permute-start | bytes 3145736 | tf_op jit(solution)/shard_map/ppermute | solution.py:24
  76.9 20.1 %copy-start.8 = (bf16[32,4096]{1,0:T(8,128)(2,1)S(1)}, bf16[32,4096]{1,0:T(8,128)(2,1)}, u32[]{:S(2)}) copy-start(bf16[32,4096]{1,0:T(8,128)(2,1)} %param.18) | copy-start | bytes 786436
  81.3 16.7 %copy-start.9 = (f32[4096]{0:T(1024)S(1)}, f32[4096]{0:T(1024)}, u32[]{:S(2)}) copy-start(f32[4096]{0:T(1024)} %param.19) | copy-start | bytes 49156
  81.4 8.9 %collective-permute-start.1 = (bf16[32,4096]{1,0:T(8,128)(2,1)S(1)}, bf16[32,4096]{1,0:T(8,128)(2,1)S(1)}, u32[]{:S(2)}, u32[]{:S(2)}) collective-permute-start(bf16[32,4096]{1,0:T(8,128)(2,1)S(1)} %get-tuple-element.21), channel_id=1, source_target_pairs={{0,2},{1,3},{2,4},{3,5},{4,6},{5,7},{6,0},{7,1},{8,10},{9,11},{10,... | collective-permute-start | bytes 786440 | tf_op jit(solution)/shard_map/ppermute | solution.py:19
  82.8 14.2 %collective-permute-start.2 = (bf16[32,4096]{1,0:T(8,128)(2,1)S(1)}, bf16[32,4096]{1,0:T(8,128)(2,1)S(1)}, u32[]{:S(2)}, u32[]{:S(2)}) collective-permute-start(bf16[32,4096]{1,0:T(8,128)(2,1)S(1)} %get-tuple-element.23), channel_id=1, source_target_pairs={{0,4},{1,5},{2,6},{3,7},{4,0},{5,1},{6,2},{7,3},{8,12},{9,13},{10,... | collective-permute-start | bytes 786440 | tf_op jit(solution)/shard_map/ppermute | solution.py:19
  85.4 11.7 %collective-permute-start.3 = (bf16[32,4096]{1,0:T(8,128)(2,1)S(1)}, bf16[32,4096]{1,0:T(8,128)(2,1)S(1)}, u32[]{:S(2)}, u32[]{:S(2)}) collective-permute-start(bf16[32,4096]{1,0:T(8,128)(2,1)S(1)} %get-tuple-element.22), channel_id=1, source_target_pairs={{0,6},{1,7},{2,0},{3,1},{4,2},{5,3},{6,4},{7,5},{8,14},{9,15},{10,... | collective-permute-start | bytes 786440 | tf_op jit(solution)/shard_map/ppermute | solution.py:19
  97.3 0.7 copy-start.5
  152.1 4.2 %copy-start.3 = (f32[1,3]{1,0:T(1,128)S(1)}, f32[1,3]{1,0:T(1,128)}, u32[]{:S(2)}) copy-start(f32[1,3]{1,0:T(1,128)} %scale.1) | copy-start | bytes 40
  156.3 2.8 %copy-start.2 = (bf16[1,4096,768]{2,1,0:T(8,128)(2,1)S(1)}, bf16[1,4096,768]{2,1,0:T(8,128)(2,1)}, u32[]{:S(2)}) copy-start(bf16[1,4096,768]{2,1,0:T(8,128)(2,1)} %param.22) | copy-start | bytes 18874372
  171.6 1.7 copy-start.1
  179.2 4.7 %copy-start.11 = (f32[32,8]{0,1:T(8,128)S(1)}, f32[32,8]{0,1:T(8,128)}, u32[]{:S(2)}) copy-start(f32[32,8]{0,1:T(8,128)} %param.21) | copy-start | bytes 3076
  179.2 46.7 %all-to-all-start.3 = ((bf16[128,96,128]{2,1,0:T(8,128)(2,1)}), bf16[128,96,128]{2,1,0:T(8,128)(2,1)S(1)}, u32[]{:S(2)}, u32[]{:S(2)}) async-start(bf16[128,96,128]{2,1,0:T(8,128)(2,1)} %reshape.78), calls=%async_computation.3 | async-start | bytes 6291456 | tf_op jit(solution)/shard_map/all_to_all | solution.py:169
  229.1 2.6 %copy-start.6 = (bf16[32,4096]{1,0:T(8,128)(2,1)S(1)}, bf16[32,4096]{1,0:T(8,128)(2,1)}, u32[]{:S(2)}) copy-start(bf16[32,4096]{1,0:T(8,128)(2,1)} %copy-done.5) | copy-start | bytes 786436
Sparse Core Ops, SparseCore 0:
  9.5 59.6 all-gather.1

commit v3 on v1

v3 whole, which is shorter than its diff:
```python
import functools

import jax
import jax.numpy as jnp
from jax import lax
from jax.experimental import pallas as pl
from jax.experimental.pallas import tpu as pltpu
from jax.sharding import PartitionSpec as P

D = 4096
HD = 128
TOPK = 8
CAP = 3
NX, NY, NZ, NC = 4, 4, 4, 2
LANES = 128
HALF = D // 2
BLOCKS = HALF // LANES
WIDE = 256
BF = jnp.bfloat16
F32 = jnp.float32


def from_x(a, d):
    pairs = [((x + d) % NX * NY + y, x * NY + y) for x in range(NX) for y in range(NY)]
    return lax.ppermute(a, "seq", pairs)


def from_y(a, d):
    pairs = [(x * NY + (y + d) % NY, x * NY + y) for x in range(NX) for y in range(NY)]
    return lax.ppermute(a, "seq", pairs)


def to_z(a, d):
    pairs = [(z * NC + c, (z + d) % NZ * NC + c) for z in range(NZ) for c in range(NC)]
    return lax.ppermute(a, "head", pairs)


def swap_core(a):
    pairs = [(z * NC + c, z * NC + 1 - c) for z in range(NZ) for c in range(NC)]
    return lax.ppermute(a, "head", pairs)


def earlier_states(block_state):
    blocks = lax.axis_size("seq")
    parts = block_state.reshape(blocks, -1, HD)
    got = lax.all_to_all(parts, "seq", split_axis=0, concat_axis=0, tiled=True)
    at = jnp.arange(blocks)
    earlier = (at[None, :] < at[:, None])[:, :, None, None]
    sums = jnp.sum(jnp.where(earlier, got[None], 0.0), axis=1).astype(BF)
    back = lax.all_to_all(sums, "seq", split_axis=0, concat_axis=0, tiled=True)
    return back.reshape(block_state.shape)


def gather_weight(weight):
    first, second = weight[:, :LANES], weight[:, LANES:]
    line_y = [first] + [from_y(first, d) for d in range(1, NY)]
    line_x = [second] + [from_x(second, d) for d in range(1, NX)]
    line_y = jnp.concatenate(line_y, axis=1)
    line_x = jnp.concatenate(line_x, axis=1)
    first = [line_y] + [from_x(line_y, d) for d in range(1, NX)]
    second = [line_x] + [from_y(line_x, d) for d in range(1, NY)]
    return first, second


def sum_pair(partial, c):
    rows = partial.reshape(NZ, NC, -1, partial.shape[-1])
    first = c == 0
    keep = jnp.where(first, rows[:, 0], rows[:, 1])
    give = jnp.where(first, rows[:, 1], rows[:, 0]).astype(BF)
    return keep + swap_core(give).astype(F32)


def spread_z(pair, z):
    own = lax.dynamic_index_in_dim(pair, z, 0, False)
    low = pair.astype(BF)
    return own, [to_z(lax.dynamic_index_in_dim(low, (z + d) % NZ, 0, False), d) for d in range(1, NZ)]


def place_kernel(half, pos, target, own, one, two, three, stream, res, message):
    tok = own.shape[0]
    x, y = pos[0], pos[1]
    for j in range(BLOCKS):
        lanes = slice(j * LANES, (j + 1) * LANES)
        if half == 0:
            block = (x + j // NY) % NX * NY + (y + j % NY) % NY
        else:
            block = (x + j % NX) % NX * NY + (y + j // NX) % NY
        at = pl.multiple_of(block * 2 * LANES + half * LANES, LANES)
        total = (
            own[:, lanes]
            + one[:, lanes].astype(F32)
            + two[:, lanes].astype(F32)
            + three[:, lanes].astype(F32)
            + stream[:, pl.ds(at, LANES)].astype(F32)
        )
        res[:, pl.ds(block, 1), :] = total.astype(BF).astype(F32)[:, None, :]
    message[...] = jnp.zeros_like(message)

    def one_token(t, carry):
        row = res[t].astype(BF)
        for k in range(TOPK):
            message[target[t, k]] = row
        return carry

    lax.fori_loop(0, tok, one_token, 0)


def place(half, pos, target, own, parts, stream, slots):
    tok = own.shape[0]
    smem = pl.BlockSpec(memory_space=pltpu.SMEM)
    vmem = pl.BlockSpec(memory_space=pltpu.VMEM)
    return pl.pallas_call(
        functools.partial(place_kernel, half),
        out_shape=(
            jax.ShapeDtypeStruct((tok, BLOCKS, LANES), F32),
            jax.ShapeDtypeStruct((slots, BLOCKS, LANES), BF),
        ),
        in_specs=[smem, smem] + [vmem] * 5,
        out_specs=(vmem, vmem),
        compiler_params=pltpu.CompilerParams(vmem_limit_bytes=16 << 20),
        cost_estimate=pl.CostEstimate(flops=1 << 20, bytes_accessed=3 << 20, transcendentals=0),
    )(pos, target, own, *parts, stream)


def first_kernel(rows, gain, gate, up, gate_out, up_out, squares, scaled):
    @pl.when(pl.program_id(0) == 0)
    def _():
        x = rows[...].astype(F32)
        squares[...] = jnp.broadcast_to(jnp.sum(x * x, axis=1, keepdims=True), squares.shape)
        scaled[...] = (x * gain[...]).astype(BF)

    x = scaled[...]
    gate_out[...] = jnp.dot(x, gate[...].reshape(HALF, WIDE), preferred_element_type=F32)
    up_out[...] = jnp.dot(x, up[...].reshape(HALF, WIDE), preferred_element_type=F32)


def second_kernel(scale, rows, gain, gate, up, gate_in, up_in, squares, act, scaled, factor):
    @pl.when(pl.program_id(0) == 0)
    def _():
        x = rows[...].astype(F32)
        total = squares[...] + jnp.sum(x * x, axis=1, keepdims=True)
        factor[...] = lax.rsqrt(total * (1.0 / D) + 1e-06)
        scaled[...] = (x * gain[...]).astype(BF)

    x = scaled[...]
    by_row = factor[:, :1]
    gate_part = jnp.dot(x, gate[...].reshape(HALF, WIDE), preferred_element_type=F32) + gate_in[...]
    up_part = jnp.dot(x, up[...].reshape(HALF, WIDE), preferred_element_type=F32) + up_in[...]
    gate_part = gate_part * (by_row * scale[0, 0])
    up_part = up_part * (by_row * scale[0, 1])
    act[...] = (gate_part / (1.0 + jnp.exp(-gate_part)) * up_part).astype(BF)


def hidden_half(half, rows, gain, gate, up, rest=None):
    count, hidden = rows.shape[0], gate.shape[1]
    gate = gate.reshape(BLOCKS, 2, LANES, hidden)
    up = up.reshape(BLOCKS, 2, LANES, hidden)
    weight = pl.BlockSpec((BLOCKS, None, LANES, WIDE), lambda i: (0, half, 0, i))
    part = pl.BlockSpec((count, WIDE), lambda i: (0, i))
    row = pl.BlockSpec((count, HALF), lambda i: (0, 0))
    one = pl.BlockSpec((1, HALF), lambda i: (0, 0))
    narrow = pl.BlockSpec((count, LANES), lambda i: (0, 0))
    scratch = [pltpu.VMEM((count, HALF), BF)]
    common = dict(
        grid=(hidden // WIDE,),
        compiler_params=pltpu.CompilerParams(vmem_limit_bytes=24 << 20),
        cost_estimate=pl.CostEstimate(
            flops=4 * count * HALF * hidden, bytes_accessed=4 * HALF * hidden, transcendentals=0
        ),
    )
    if rest is None:
        sums = jax.ShapeDtypeStruct((count, hidden), F32)
        return pl.pallas_call(
            first_kernel,
            out_shape=(sums, sums, jax.ShapeDtypeStruct((count, LANES), F32)),
            in_specs=[row, one, weight, weight],
            out_specs=(part, part, narrow),
            scratch_shapes=scratch,
            **common,
        )(rows, gain, gate, up)
    scale, gate_in, up_in, squares = rest
    return pl.pallas_call(
        second_kernel,
        out_shape=jax.ShapeDtypeStruct((count, hidden), BF),
        in_specs=[pl.BlockSpec(memory_space=pltpu.SMEM), row, one, weight, weight, part, part, narrow],
        out_specs=part,
        scratch_shapes=scratch + [pltpu.VMEM((count, LANES), F32)],
        **common,
    )(scale, rows, gain, gate, up, gate_in, up_in, squares)


def down_kernel(scale, act, one, two, three, four, out):
    weight = jnp.concatenate([one[...], two[...], three[...], four[...]], axis=1)
    total = jnp.dot(act[...], weight, preferred_element_type=F32)
    out[...] = (total * scale[0, 2]).astype(BF)


def down_half(half, scale, act, down):
    count, hidden = act.shape
    group = 4

    def columns(g):
        return pl.BlockSpec((hidden, LANES), lambda i: (0, 2 * (group * i + g) + half))

    return pl.pallas_call(
        down_kernel,
        out_shape=jax.ShapeDtypeStruct((count, HALF), BF),
        grid=(BLOCKS // group,),
        in_specs=[pl.BlockSpec(memory_space=pltpu.SMEM), pl.BlockSpec((count, hidden), lambda i: (0, 0))]
        + [columns(g) for g in range(group)],
        out_specs=pl.BlockSpec((count, group * LANES), lambda i: (0, i)),
        compiler_params=pltpu.CompilerParams(vmem_limit_bytes=16 << 20),
        cost_estimate=pl.CostEstimate(
            flops=2 * count * HALF * hidden, bytes_accessed=2 * HALF * hidden, transcendentals=0
        ),
    )(scale, act, down, down, down, down)


def mix_kernel(last, target, gates, results, res, *rest):
    tok = res.shape[0]
    mixed = rest[-1]

    def one_token(t, carry):
        total = res[t]
        add = gates[t, 0] * results[target[t, 0]].astype(F32)
        for k in range(1, TOPK):
            add += gates[t, k] * results[target[t, k]].astype(F32)
        mixed[t] = total + add
        return carry

    lax.fori_loop(0, tok, one_token, 0)
    if last:
        first, out = rest[0], rest[1]
        for block in range(BLOCKS):
            at = block * 2 * LANES
            out[:, at : at + LANES] = first[:, block, :].astype(BF)
            out[:, at + LANES : at + 2 * LANES] = mixed[:, block, :].astype(BF)


def mix(target, gates, results, res, first=None):
    tok = res.shape[0]
    smem = pl.BlockSpec(memory_space=pltpu.SMEM)
    vmem = pl.BlockSpec(memory_space=pltpu.VMEM)
    last = first is not None
    shape = jax.ShapeDtypeStruct((tok, D), BF) if last else jax.ShapeDtypeStruct(res.shape, F32)
    return pl.pallas_call(
        functools.partial(mix_kernel, last),
        out_shape=shape,
        in_specs=[smem, smem, vmem, vmem] + [vmem] * last,
        out_specs=vmem,
        scratch_shapes=[pltpu.VMEM(res.shape, F32)] * last,
        compiler_params=pltpu.CompilerParams(vmem_limit_bytes=16 << 20),
        cost_estimate=pl.CostEstimate(flops=1 << 20, bytes_accessed=3 << 20, transcendentals=0),
    )(target, gates, results, res, *([first] if last else []))


def body(
    query,
    key,
    value,
    head_gain,
    out_weight,
    stream,
    model_gain,
    expert_ids,
    expert_gates,
    gate_weight,
    up_weight,
    down_weight,
    weight_scales,
):
    seq = lax.axis_index("seq")
    head = lax.axis_index("head")
    x, y, z, c = seq // NY, seq % NY, head // NC, head % NC
    pos = jnp.stack([x, y]).astype(jnp.int32)
    seq_rows = query.shape[0]
    tok_rows = stream.shape[0]
    heads_local = head_gain.shape[0] // HD
    experts = lax.axis_size("seq") * lax.axis_size("head")
    slots = experts * CAP

    pieces = gather_weight(out_weight)

    query_rows = query.reshape(seq_rows, heads_local, HD)
    key_rows = key.reshape(seq_rows, heads_local, HD)
    value_rows = value.reshape(seq_rows, heads_local, HD)
    block_state = jnp.einsum("shd,she->hde", key_rows, value_rows, preferred_element_type=F32)
    prior_state = earlier_states(block_state)
    scores = jnp.einsum("thd,shd->hts", query_rows, key_rows, preferred_element_type=F32)
    causal = jnp.tril(jnp.ones((seq_rows, seq_rows), dtype=bool))
    scores = jnp.where(causal[None, :, :], scores, 0.0).astype(BF)
    local_part = jnp.einsum("hts,shd->thd", scores, value_rows, preferred_element_type=F32)
    earlier_part = jnp.einsum("thd,hde->the", query_rows, prior_state, preferred_element_type=F32)
    mixed_heads = local_part + earlier_part
    mean_square = jnp.mean(mixed_heads * mixed_heads, axis=-1, keepdims=True)
    head_normed = (
        mixed_heads * lax.rsqrt(mean_square + 1e-06) * head_gain.reshape(heads_local, HD)
    ).astype(BF)
    head_normed = head_normed.reshape(seq_rows, heads_local * HD)

    flat_ids = expert_ids.reshape(-1)
    at = jnp.arange(flat_ids.shape[0], dtype=jnp.int32)
    same = (flat_ids[:, None] == flat_ids[None, :]) & (at[None, :] < at[:, None])
    slot_index = jnp.sum(same.astype(jnp.int32), axis=1)
    target = (flat_ids * CAP + slot_index).reshape(tok_rows, TOPK)
    gains = model_gain.reshape(BLOCKS, 2, LANES)

    def exchange(rows):
        message = rows.reshape(experts, CAP * BLOCKS, LANES)
        got = lax.all_to_all(message, ("seq", "head"), split_axis=0, concat_axis=0, tiled=True)
        return got.reshape(slots, BLOCKS, LANES)

    residual, arrived = [], []
    source = head_normed
    for half in range(2):
        partial = jnp.concatenate(
            [jnp.dot(source, piece, preferred_element_type=F32) for piece in pieces[half]], axis=1
        )
        pair = sum_pair(partial, c)
        if half == 0:
            source, pair = lax.optimization_barrier((source, pair))
        own, parts = spread_z(pair, z)
        res, message = place(half, pos, target, own, parts, stream, slots)
        residual.append(res)
        arrived.append(exchange(message).reshape(slots, HALF))

    rest = None
    for half in range(2):
        gain = gains[:, half].reshape(1, HALF)
        rest = hidden_half(half, arrived[half], gain, gate_weight[0], up_weight[0], rest)
        if half == 0:
            rest = (weight_scales, *rest)
    act = rest
    first = None
    for half in range(2):
        produced = down_half(half, weight_scales, act, down_weight[0])
        results = exchange(produced.reshape(slots, BLOCKS, LANES))
        first = mix(target, expert_gates, results, residual[half], first)
    return first


def solution(mesh):
    token = P(("seq", "head"), None)
    expert = P(("seq", "head"), None, None)
    return jax.shard_map(
        body,
        mesh=mesh,
        in_specs=(
            P("seq", "head"),
            P("seq", "head"),
            P("seq", "head"),
            P("head"),
            P("head", "seq"),
            token,
            P(),
            token,
            token,
            expert,
            expert,
            expert,
            token,
        ),
        out_specs=token,
        check_vma=False,
    )
```

time: 247 us -> 252 us (1.020)
  waiting for transfers between devices: 146 us -> 101 us
  starting transfers between devices: 29.7 us -> 69.6 us
  Pallas kernels: 0 us -> 25.9 us
  matrix products: 31.8 us -> 7.59 us
  local copies, waits for them, and re-layouts: 21 us -> 39 us
  between operations: 13.6 us -> 0.6 us
  other arithmetic: 4.65 us -> 7.57 us
    all_gather x1 -> x0, waiting for transfers between devices: 39.6 us -> none  [body(): full_out = lax.all_gather(out_weight, 'seq', axis=1, tiled=True)]
    all_to_all x2 -> x6, waiting for transfers between devices: 82.8 us -> 50.3 us  [the longest x4 48.7 us: exchange(): lax.all_to_all(message, ('seq', 'head'), split_axis=0, concat_axis=0, til...]
    ppermute x9 -> x18, waiting for transfers between devices: 20.7 us -> 48.7 us  [the longest x6 20.5 us: to_z(): return lax.ppermute(a, 'head', pairs)]
    dot_general x6 -> x9, matrix products: 31.1 us -> 3.81 us  [the longest x8 3.55 us: body(): jnp.dot(source, piece, preferred_element_type=F32)]
    pallas_call x0 -> x8, Pallas kernels: none -> 25.9 us  [the longest x2 6.64 us: down_half(): pl.pallas_call(down_kernel, out_shape=jax.ShapeDtypeStruct((count, HALF),...]
    all_to_all x2 -> x6, starting transfers between devices: 12.4 us -> 37.3 us  [the longest x4 26.1 us: exchange(): lax.all_to_all(message, ('seq', 'head'), split_axis=0, concat_axis=0, til...]
    unnamed x26 -> x50, local copies, waits for them, and re-layouts: 2.82 us -> 26.7 us
    reshape x4 -> x0, local copies, waits for them, and re-layouts: 15.9 us -> none  [the longest x1 5.87 us: body(): message = produced.astype(BF).reshape(experts, CAP * D // lanes, lanes)]
  transfers between devices with their start and end apart: 13 -> 26, of which waited for: 11 -> 13; matrix products, arithmetic and copies ran while one was open for 2% -> 8% of each run, Pallas kernels for 0% -> 5%
where the time goes in v3:
time: 252 us; the launch traced here: 251 us
  waiting for transfers between devices  101 us (40%)
  starting transfers between devices  69.6 us (28%)
  local copies, waits for them, and re-layouts  39 us (15%)
  Pallas kernels  25.9 us (10%)
  matrix products  7.59 us (3%)
  other arithmetic  7.57 us (3%)
    all_to_all x4, waiting for transfers between devices, exchange(): lax.all_to_all(message, ('seq', 'head'), split_axis=0, concat_axis=0, til...  48.7 us
    unnamed x50, local copies, waits for them, and re-layouts  26.7 us
    all_to_all x4, starting transfers between devices, exchange(): lax.all_to_all(message, ('seq', 'head'), split_axis=0, concat_axis=0, til...  26.1 us
    ppermute x6, waiting for transfers between devices, to_z(): return lax.ppermute(a, 'head', pairs)  20.5 us
    ppermute x6, waiting for transfers between devices, from_y(): return lax.ppermute(a, 'seq', pairs)  14.7 us
    ppermute x6, waiting for transfers between devices, from_x(): return lax.ppermute(a, 'seq', pairs)  13.5 us
    ppermute x6, starting transfers between devices, from_y(): return lax.ppermute(a, 'seq', pairs)  9.6 us
    ppermute x6, starting transfers between devices, from_x(): return lax.ppermute(a, 'seq', pairs)  9.31 us
  transfers between devices with their start and end apart: 26, of which 13 were waited for; matrix products, arithmetic and copies ran while one was open for 8% of the time, Pallas kernels for 5%

profile of v3, /device:TPU:1, one launch (start us, length us, event | category | flops | bytes accessed | tf_op | source)
XLA Modules:
  0.0 250.8 jit_solution(18372593163161449749)
XLA Ops:
  3.0 7.7 %all-to-all-start = ((f32[16,32,128]{2,1,0:T(8,128)}), f32[16,32,128]{2,1,0:T(8,128)S(1)}, u32[]{:S(2)}, u32[]{:S(2)}) async-start(f32[16,32,128]{2,1,0:T(8,128)} %bitcast.3), calls=%async_computation | async-start | bytes 524288 | tf_op jit(solution)/shard_map/all_to_all | solution.py:46
  22.9 3.5 %all-to-all-start.1 = ((bf16[16,32,128]{2,1,0:T(8,128)(2,1)}), bf16[16,32,128]{2,1,0:T(8,128)(2,1)S(1)}, u32[]{:S(2)}, u32[]{:S(2)}) async-start(bf16[16,32,128]{2,1,0:T(8,128)(2,1)} %select_reduce_fusion), calls=%async_computation.1 | async-start | bytes 262144 | tf_op jit(solution)/shard_map/all_to_all | solution.py:50
  37.2 3.2 %collective-permute-done.5 = bf16[512,512]{1,0:T(8,128)(2,1)} collective-permute-done((bf16[512,512]{1,0:T(8,128)(2,1)S(1)}, bf16[512,512]{1,0:T(8,128)(2,1)}, u32[]{:S(2)}, u32[]{:S(2)}) %collective-permute-start.5) | collective-permute-done | bytes 524320 | tf_op jit(solution)/shard_map/ppermute | solution.py:25
  42.3 9.5 %collective-permute-done.4 = bf16[512,512]{1,0:T(8,128)(2,1)S(1)} collective-permute-done((bf16[512,512]{1,0:T(8,128)(2,1)S(1)}, bf16[512,512]{1,0:T(8,128)(2,1)S(1)}, u32[]{:S(2)}, u32[]{:S(2)}) %collective-permute-start.4) | collective-permute-done | bytes 524320 | tf_op jit(solution)/shard_map/ppermute | solution.py:25
  54.3 3.2 %collective-permute-start.6 = (bf16[4,32,2048]{2,1,0:T(8,128)(2,1)}, bf16[4,32,2048]{2,1,0:T(8,128)(2,1)}, u32[]{:S(2)}, u32[]{:S(2)}) collective-permute-start(bf16[4,32,2048]{2,1,0:T(8,128)(2,1)} %fusion.4), channel_id=1, source_target_pairs={{0,1},{1,0},{2,3},{3,2},{4,5},{5,4},{6,7},{7,6},{8,9},{9,8},{10,11... | collective-permute-start | bytes 1572872 | tf_op jit(solution)/shard_map/ppermute | solution.py:40
  65.3 3.8 %collective-permute-start.19 = (bf16[32,2048]{1,0:T(8,128)(2,1)S(1)}, bf16[32,2048]{1,0:T(8,128)(2,1)S(1)}, u32[]{:S(2)}, u32[]{:S(2)}) collective-permute-start(bf16[32,2048]{1,0:T(8,128)(2,1)S(1)} %get-tuple-element.25), channel_id=1, source_target_pairs={{0,6},{1,7},{2,0},{3,1},{4,2},{5,3},{6,4},{7,5},{8,14},{9,15},{10,... | collective-permute-start | bytes 393224 | tf_op jit(solution)/shard_map/ppermute | solution.py:35
  69.4 4.5 %collective-permute-done.12 = bf16[512,512]{1,0:T(8,128)(2,1)S(1)} collective-permute-done((bf16[512,512]{1,0:T(8,128)(2,1)S(1)}, bf16[512,512]{1,0:T(8,128)(2,1)S(1)}, u32[]{:S(2)}, u32[]{:S(2)}) %collective-permute-start.12) | collective-permute-done | bytes 524320 | tf_op jit(solution)/shard_map/ppermute | solution.py:30
  75.9 10.2 %collective-permute-done.11 = bf16[512,512]{1,0:T(8,128)(2,1)S(1)} collective-permute-done((bf16[512,512]{1,0:T(8,128)(2,1)S(1)}, bf16[512,512]{1,0:T(8,128)(2,1)S(1)}, u32[]{:S(2)}, u32[]{:S(2)}) %collective-permute-start.11) | collective-permute-done | bytes 524320 | tf_op jit(solution)/shard_map/ppermute | solution.py:30
  87.7 2.9 %shard_map.128 = (f32[32,16,128]{2,1,0:T(8,128)S(1)}, bf16[384,16,128]{2,1,0:T(8,128)(2,1)}) custom-call(s32[2]{0:T(128)S(1)} %pad_add_fusion.pos, s32[32,8]{1,0:T(8,128)S(1)} %multiply_add_fusion.target, f32[32,2048]{1,0:T(8,128)S(1)} %dynamic-slice_bitcast_fusion.own, bf16[32,2048]{1,0:T(8,128)(2,1)S(1)} %collective-permute-done.17.one, ...), custom_call_target="tpu_custom_call" | custom-call | flops 1048576 | bytes 3145728 | tf_op jit(solution)/shard_map/pallas_call | solution.py:112
  91.3 10.4 %all-to-all-start.3 = ((bf16[128,48,128]{2,1,0:T(8,128)(2,1)}), bf16[128,48,128]{2,1,0:T(8,128)(2,1)}, u32[]{:S(2)}, u32[]{:S(2)}) async-start(bf16[128,48,128]{2,1,0:T(8,128)(2,1)} %bitcast.27), calls=%async_computation.3 | async-start | bytes 3145728 | tf_op jit(solution)/shard_map/all_to_all | solution.py:310
  108.3 15.7 %collective-permute-done.16.three = bf16[32,2048]{1,0:T(8,128)(2,1)S(1)} collective-permute-done((bf16[32,2048]{1,0:T(8,128)(2,1)S(1)}, bf16[32,2048]{1,0:T(8,128)(2,1)S(1)}, u32[]{:S(2)}, u32[]{:S(2)}) %collective-permute-start.16) | collective-permute-done | bytes 131104 | tf_op jit(solution)/shard_map/ppermute | solution.py:35
  128.8 3.0 %shard_map.127 = (f32[32,16,128]{2,1,0:T(8,128)S(1)}, bf16[384,16,128]{2,1,0:T(8,128)(2,1)}) custom-call(s32[2]{0:T(128)S(1)} %pad_add_fusion.pos, s32[32,8]{1,0:T(8,128)S(1)} %multiply_add_fusion.target, f32[32,2048]{1,0:T(8,128)S(1)} %dynamic-slice_bitcast_fusion.1.own, bf16[32,2048]{1,0:T(8,128)(2,1)S(1)} %collective-permute-done.14.one, ...), custom_call_target="tpu_custom_call" | custom-call | flops 1048576 | bytes 3145728 | tf_op jit(solution)/shard_map/pallas_call | solution.py:112
  132.5 6.5 %all-to-all-start.2 = ((bf16[128,48,128]{2,1,0:T(8,128)(2,1)}), bf16[128,48,128]{2,1,0:T(8,128)(2,1)}, u32[]{:S(2)}, u32[]{:S(2)}) async-start(bf16[128,48,128]{2,1,0:T(8,128)(2,1)} %bitcast.18), calls=%async_computation.2 | async-start | bytes 3145728 | tf_op jit(solution)/shard_map/all_to_all | solution.py:310
  147.1 4.1 %shard_map.129 = (f32[384,768]{1,0:T(8,128)S(1)}, f32[384,768]{1,0:T(8,128)S(1)}, f32[384,128]{1,0:T(8,128)S(1)}) custom-call(bf16[384,2048]{1,0:T(8,128)(2,1)S(1)} %reshape_reshape.13.rows, f32[1,2048]{1,0:T(1,128)S(1)} %get-tuple-element.33.gain, bf16[16,2,128,768]{3,2,1,0:T(8,128)(2,1)S(1)} %bitcast.143, bf16[16,2,128,768]{3,2,1,0:T(8,128)(2,1)S(1)} %bitcast.145), custom_call_target="tpu_custom_call" | custom-call | flops 2415919104 | bytes 6291456 | tf_op jit(solution)/shard_map/pallas_call | solution.py:173
  152.3 11.3 %all-to-all-done.2 = bf16[128,48,128]{2,1,0:T(8,128)(2,1)} async-done(((bf16[128,48,128]{2,1,0:T(8,128)(2,1)}), bf16[128,48,128]{2,1,0:T(8,128)(2,1)}, u32[]{:S(2)}, u32[]{:S(2)}) %all-to-all-start.2) | async-done | bytes 1572896 | tf_op jit(solution)/shard_map/all_to_all | solution.py:310
  173.0 4.7 %shard_map.130.act = bf16[384,768]{1,0:T(8,128)(2,1)S(1)} custom-call(f32[1,3]{1,0:T(1,128)S(1)} %copy-done.18, bf16[384,2048]{1,0:T(8,128)(2,1)S(1)} %reshape_reshape.12.rows, f32[1,2048]{1,0:T(1,128)S(1)} %get-tuple-element.34.gain, bf16[16,2,128,768]{3,2,1,0:T(8,128)(2,1)S(1)} %bitcast.144, bf16[16,2,128,768]{3,2,1,0:T(8,128)(2,1)S(1)} %bitcast.146, ...), custom_call_target="tpu_custom_call" | custom-call | flops 2415919104 | bytes 6291456 | tf_op jit(solution)/shard_map/pallas_call | solution.py:182
  177.7 2.8 %copy-done.1 = bf16[1,768,4096]{2,1,0:T(8,128)(2,1)S(1)} copy-done((bf16[1,768,4096]{2,1,0:T(8,128)(2,1)S(1)}, bf16[1,768,4096]{2,1,0:T(8,128)(2,1)}, u32[]{:S(2)}) %copy-start.1) | copy-done | bytes 6291480
  180.5 3.3 %shard_map.132 = bf16[384,2048]{1,0:T(8,128)(2,1)S(1)} custom-call(f32[1,3]{1,0:T(1,128)S(1)} %copy-done.18, bf16[384,768]{1,0:T(8,128)(2,1)S(1)} %shard_map.130.act, bf16[768,4096]{1,0:T(8,128)(2,1)S(1)} %bitcast.135, bf16[768,4096]{1,0:T(8,128)(2,1)S(1)} %bitcast.136, bf16[768,4096]{1,0:T(8,128)(2,1)S(1)} %bitcast.137, bf16[768,4096]{1,0:T(8,128)(2,1)S(1)} %bitcast.138), custom_call_target="tpu_custom_call" | custom-call | flops 1207959552 | bytes 3145728 | tf_op jit(solution)/shard_map/pallas_call | solution.py:205
  186.7 4.6 %all-to-all-start.5 = ((bf16[128,48,128]{2,1,0:T(8,128)(2,1)}), bf16[128,48,128]{2,1,0:T(8,128)(2,1)S(1)}, u32[]{:S(2)}, u32[]{:S(2)}) async-start(bf16[128,48,128]{2,1,0:T(8,128)(2,1)} %reshape_reshape.15), calls=%async_computation.5 | async-start | bytes 3145728 | tf_op jit(solution)/shard_map/all_to_all | solution.py:310
  195.2 3.3 %shard_map.131 = bf16[384,2048]{1,0:T(8,128)(2,1)S(1)} custom-call(f32[1,3]{1,0:T(1,128)S(1)} %copy-done.18, bf16[384,768]{1,0:T(8,128)(2,1)S(1)} %copy-done.8, bf16[768,4096]{1,0:T(8,128)(2,1)S(1)} %bitcast.139, bf16[768,4096]{1,0:T(8,128)(2,1)S(1)} %bitcast.140, bf16[768,4096]{1,0:T(8,128)(2,1)S(1)} %bitcast.141, bf16[768,4096]{1,0:T(8,128)(2,1)S(1)} %bitcast.142), custom_call_target="tpu_custom_call" | custom-call | flops 1207959552 | bytes 3145728 | tf_op jit(solution)/shard_map/pallas_call | solution.py:205
  200.7 15.7 %all-to-all-done.5 = bf16[128,48,128]{2,1,0:T(8,128)(2,1)S(1)} async-done(((bf16[128,48,128]{2,1,0:T(8,128)(2,1)}), bf16[128,48,128]{2,1,0:T(8,128)(2,1)S(1)}, u32[]{:S(2)}, u32[]{:S(2)}) %all-to-all-start.5) | async-done | bytes 1572896 | tf_op jit(solution)/shard_map/all_to_all | solution.py:310
  216.4 4.6 %all-to-all-start.4 = ((bf16[128,48,128]{2,1,0:T(8,128)(2,1)}), bf16[128,48,128]{2,1,0:T(8,128)(2,1)S(1)}, u32[]{:S(2)}, u32[]{:S(2)}) async-start(bf16[128,48,128]{2,1,0:T(8,128)(2,1)} %reshape_reshape.14), calls=%async_computation.4 | async-start | bytes 3145728 | tf_op jit(solution)/shard_map/all_to_all | solution.py:310
  224.4 21.6 %all-to-all-done.4 = bf16[128,48,128]{2,1,0:T(8,128)(2,1)S(1)} async-done(((bf16[128,48,128]{2,1,0:T(8,128)(2,1)}), bf16[128,48,128]{2,1,0:T(8,128)(2,1)S(1)}, u32[]{:S(2)}, u32[]{:S(2)}) %all-to-all-start.4) | async-done | bytes 1572896 | tf_op jit(solution)/shard_map/all_to_all | solution.py:310
  247.9 2.9 %shard_map.134 = bf16[32,4096]{1,0:T(8,128)(2,1)} custom-call(s32[32,8]{1,0:T(8,128)S(1)} %multiply_add_fusion.target, f32[32,8]{1,0:T(8,128)S(1)} %copy.52.gates, bf16[384,16,128]{2,1,0:T(8,128)(2,1)S(1)} %bitcast.148, f32[32,16,128]{2,1,0:T(8,128)S(1)} %copy-done.15, f32[32,16,128]{2,1,0:T(8,128)S(1)} %copy-done.13), custom_call_target="tpu_custom_call" | custom-call | flops 1048576 | bytes 3145728 | tf_op jit(solution)/shard_map/pallas_call | solution.py:246
  (127 shorter events, 87.1 us)
Async XLA Ops:
  3.0 18.7 %all-to-all-start = ((f32[16,32,128]{2,1,0:T(8,128)}), f32[16,32,128]{2,1,0:T(8,128)S(1)}, u32[]{:S(2)}, u32[]{:S(2)}) async-start(f32[16,32,128]{2,1,0:T(8,128)} %bitcast.3), calls=%async_computation | async-start | bytes 524288 | tf_op jit(solution)/shard_map/all_to_all | solution.py:46
  11.7 46.3 %collective-permute-start.9 = (bf16[512,128]{1,0:T(8,128)(2,1)S(1)}, bf16[512,128]{1,0:T(8,128)(2,1)}, u32[]{:S(2)}, u32[]{:S(2)}) collective-permute-start(bf16[512,128]{1,0:T(8,128)(2,1)S(1)} %get-tuple-element.31), channel_id=1, source_target_pairs={{96,0},{104,8},{112,16},{120,24},{0,32},{8,40},{16,48},{24,56},{32... | collective-permute-start | bytes 393224 | tf_op jit(solution)/shard_map/ppermute | solution.py:25
  13.2 44.9 %collective-permute-start.8 = (bf16[512,128]{1,0:T(8,128)(2,1)S(1)}, bf16[512,128]{1,0:T(8,128)(2,1)}, u32[]{:S(2)}, u32[]{:S(2)}) collective-permute-start(bf16[512,128]{1,0:T(8,128)(2,1)S(1)} %get-tuple-element.31), channel_id=1, source_target_pairs={{64,0},{72,8},{80,16},{88,24},{96,32},{104,40},{112,48},{120,56},{... | collective-permute-start | bytes 393224 | tf_op jit(solution)/shard_map/ppermute | solution.py:25
  15.6 10.9 %collective-permute-start.2 = (bf16[512,128]{1,0:T(8,128)(2,1)S(1)}, bf16[512,128]{1,0:T(8,128)(2,1)S(1)}, u32[]{:S(2)}, u32[]{:S(2)}) collective-permute-start(bf16[512,128]{1,0:T(8,128)(2,1)S(1)} %get-tuple-element.32), channel_id=1, source_target_pairs={{24,0},{0,8},{8,16},{16,24},{56,32},{32,40},{40,48},{48,56},{88,64... | collective-permute-start | bytes 393224 | tf_op jit(solution)/shard_map/ppermute | solution.py:30
  16.7 9.7 %collective-permute-start.1 = (bf16[512,128]{1,0:T(8,128)(2,1)S(1)}, bf16[512,128]{1,0:T(8,128)(2,1)S(1)}, u32[]{:S(2)}, u32[]{:S(2)}) collective-permute-start(bf16[512,128]{1,0:T(8,128)(2,1)S(1)} %get-tuple-element.32), channel_id=1, source_target_pairs={{16,0},{24,8},{0,16},{8,24},{48,32},{56,40},{32,48},{40,56},{80,64... | collective-permute-start | bytes 393224 | tf_op jit(solution)/shard_map/ppermute | solution.py:30
  22.9 10.2 %all-to-all-start.1 = ((bf16[16,32,128]{2,1,0:T(8,128)(2,1)}), bf16[16,32,128]{2,1,0:T(8,128)(2,1)S(1)}, u32[]{:S(2)}, u32[]{:S(2)}) async-start(bf16[16,32,128]{2,1,0:T(8,128)(2,1)} %select_reduce_fusion), calls=%async_computation.1 | async-start | bytes 262144 | tf_op jit(solution)/shard_map/all_to_all | solution.py:50
  26.6 13.8 %collective-permute-start.5 = (bf16[512,512]{1,0:T(8,128)(2,1)S(1)}, bf16[512,512]{1,0:T(8,128)(2,1)}, u32[]{:S(2)}, u32[]{:S(2)}) collective-permute-start(bf16[512,512]{1,0:T(8,128)(2,1)S(1)} %pad_maximum_fusion.2), channel_id=1, source_target_pairs={{96,0},{104,8},{112,16},{120,24},{0,32},{8,40},{16,48},{24,56},{32... | collective-permute-start | bytes 1572872 | tf_op jit(solution)/shard_map/ppermute | solution.py:25
  27.9 23.9 %collective-permute-start.4 = (bf16[512,512]{1,0:T(8,128)(2,1)S(1)}, bf16[512,512]{1,0:T(8,128)(2,1)S(1)}, u32[]{:S(2)}, u32[]{:S(2)}) collective-permute-start(bf16[512,512]{1,0:T(8,128)(2,1)S(1)} %pad_maximum_fusion.2), channel_id=1, source_target_pairs={{64,0},{72,8},{80,16},{88,24},{96,32},{104,40},{112,48},{120,56},{... | collective-permute-start | bytes 1572872 | tf_op jit(solution)/shard_map/ppermute | solution.py:25
  30.3 22.6 %collective-permute-start.3 = (bf16[512,512]{1,0:T(8,128)(2,1)S(1)}, bf16[512,512]{1,0:T(8,128)(2,1)S(1)}, u32[]{:S(2)}, u32[]{:S(2)}) collective-permute-start(bf16[512,512]{1,0:T(8,128)(2,1)S(1)} %pad_maximum_fusion.2), channel_id=1, source_target_pairs={{32,0},{40,8},{48,16},{56,24},{64,32},{72,40},{80,48},{88,56},{96,... | collective-permute-start | bytes 1572872 | tf_op jit(solution)/shard_map/ppermute | solution.py:25
  40.4 17.7 %collective-permute-start.7 = (bf16[512,128]{1,0:T(8,128)(2,1)S(1)}, bf16[512,128]{1,0:T(8,128)(2,1)S(1)}, u32[]{:S(2)}, u32[]{:S(2)}) collective-permute-start(bf16[512,128]{1,0:T(8,128)(2,1)S(1)} %get-tuple-element.31), channel_id=1, source_target_pairs={{32,0},{40,8},{48,16},{56,24},{64,32},{72,40},{80,48},{88,56},{96,... | collective-permute-start | bytes 393224 | tf_op jit(solution)/shard_map/ppermute | solution.py:25
  54.3 9.6 %collective-permute-start.6 = (bf16[4,32,2048]{2,1,0:T(8,128)(2,1)}, bf16[4,32,2048]{2,1,0:T(8,128)(2,1)}, u32[]{:S(2)}, u32[]{:S(2)}) collective-permute-start(bf16[4,32,2048]{2,1,0:T(8,128)(2,1)} %fusion.4), channel_id=1, source_target_pairs={{0,1},{1,0},{2,3},{3,2},{4,5},{5,4},{6,7},{7,6},{8,9},{9,8},{10,11... | collective-permute-start | bytes 1572872 | tf_op jit(solution)/shard_map/ppermute | solution.py:40
  59.1 14.8 %collective-permute-start.12 = (bf16[512,512]{1,0:T(8,128)(2,1)S(1)}, bf16[512,512]{1,0:T(8,128)(2,1)S(1)}, u32[]{:S(2)}, u32[]{:S(2)}) collective-permute-start(bf16[512,512]{1,0:T(8,128)(2,1)S(1)} %pad_maximum_fusion.3), channel_id=1, source_target_pairs={{24,0},{0,8},{8,16},{16,24},{56,32},{32,40},{40,48},{48,56},{88,64... | collective-permute-start | bytes 1572872 | tf_op jit(solution)/shard_map/ppermute | solution.py:30
  60.3 25.7 %collective-permute-start.11 = (bf16[512,512]{1,0:T(8,128)(2,1)S(1)}, bf16[512,512]{1,0:T(8,128)(2,1)S(1)}, u32[]{:S(2)}, u32[]{:S(2)}) collective-permute-start(bf16[512,512]{1,0:T(8,128)(2,1)S(1)} %pad_maximum_fusion.3), channel_id=1, source_target_pairs={{16,0},{24,8},{0,16},{8,24},{48,32},{56,40},{32,48},{40,56},{80,64... | collective-permute-start | bytes 1572872 | tf_op jit(solution)/shard_map/ppermute | solution.py:30
  62.7 23.6 %collective-permute-start.10 = (bf16[512,512]{1,0:T(8,128)(2,1)S(1)}, bf16[512,512]{1,0:T(8,128)(2,1)S(1)}, u32[]{:S(2)}, u32[]{:S(2)}) collective-permute-start(bf16[512,512]{1,0:T(8,128)(2,1)S(1)} %pad_maximum_fusion.3), channel_id=1, source_target_pairs={{8,0},{16,8},{24,16},{0,24},{40,32},{48,40},{56,48},{32,56},{72,64... | collective-permute-start | bytes 1572872 | tf_op jit(solution)/shard_map/ppermute | solution.py:30
  65.3 21.7 %collective-permute-start.19 = (bf16[32,2048]{1,0:T(8,128)(2,1)S(1)}, bf16[32,2048]{1,0:T(8,128)(2,1)S(1)}, u32[]{:S(2)}, u32[]{:S(2)}) collective-permute-start(bf16[32,2048]{1,0:T(8,128)(2,1)S(1)} %get-tuple-element.25), channel_id=1, source_target_pairs={{0,6},{1,7},{2,0},{3,1},{4,2},{5,3},{6,4},{7,5},{8,14},{9,15},{10,... | collective-permute-start | bytes 393224 | tf_op jit(solution)/shard_map/ppermute | solution.py:35
  69.1 17.9 %collective-permute-start.18 = (bf16[32,2048]{1,0:T(8,128)(2,1)S(1)}, bf16[32,2048]{1,0:T(8,128)(2,1)S(1)}, u32[]{:S(2)}, u32[]{:S(2)}) collective-permute-start(bf16[32,2048]{1,0:T(8,128)(2,1)S(1)} %get-tuple-element.26), channel_id=1, source_target_pairs={{0,4},{1,5},{2,6},{3,7},{4,0},{5,1},{6,2},{7,3},{8,12},{9,13},{10,... | collective-permute-start | bytes 393224 | tf_op jit(solution)/shard_map/ppermute | solution.py:35
  73.9 13.1 %collective-permute-start.17 = (bf16[32,2048]{1,0:T(8,128)(2,1)S(1)}, bf16[32,2048]{1,0:T(8,128)(2,1)S(1)}, u32[]{:S(2)}, u32[]{:S(2)}) collective-permute-start(bf16[32,2048]{1,0:T(8,128)(2,1)S(1)} %get-tuple-element.27), channel_id=1, source_target_pairs={{0,2},{1,3},{2,4},{3,5},{4,6},{5,7},{6,0},{7,1},{8,10},{9,11},{10,... | collective-permute-start | bytes 393224 | tf_op jit(solution)/shard_map/ppermute | solution.py:35
  91.3 41.2 %all-to-all-start.3 = ((bf16[128,48,128]{2,1,0:T(8,128)(2,1)}), bf16[128,48,128]{2,1,0:T(8,128)(2,1)}, u32[]{:S(2)}, u32[]{:S(2)}) async-start(bf16[128,48,128]{2,1,0:T(8,128)(2,1)} %bitcast.27), calls=%async_computation.3 | async-start | bytes 3145728 | tf_op jit(solution)/shard_map/all_to_all | solution.py:310
  104.8 19.2 %collective-permute-start.16 = (bf16[32,2048]{1,0:T(8,128)(2,1)S(1)}, bf16[32,2048]{1,0:T(8,128)(2,1)S(1)}, u32[]{:S(2)}, u32[]{:S(2)}) collective-permute-start(bf16[32,2048]{1,0:T(8,128)(2,1)S(1)} %get-tuple-element.28), channel_id=1, source_target_pairs={{0,6},{1,7},{2,0},{3,1},{4,2},{5,3},{6,4},{7,5},{8,14},{9,15},{10,... | collective-permute-start | bytes 393224 | tf_op jit(solution)/shard_map/ppermute | solution.py:35
  107.4 19.1 %collective-permute-start.15 = (bf16[32,2048]{1,0:T(8,128)(2,1)S(1)}, bf16[32,2048]{1,0:T(8,128)(2,1)S(1)}, u32[]{:S(2)}, u32[]{:S(2)}) collective-permute-start(bf16[32,2048]{1,0:T(8,128)(2,1)S(1)} %get-tuple-element.29), channel_id=1, source_target_pairs={{0,4},{1,5},{2,6},{3,7},{4,0},{5,1},{6,2},{7,3},{8,12},{9,13},{10,... | collective-permute-start | bytes 393224 | tf_op jit(solution)/shard_map/ppermute | solution.py:35
  107.7 21.1 %collective-permute-start.14 = (bf16[32,2048]{1,0:T(8,128)(2,1)S(1)}, bf16[32,2048]{1,0:T(8,128)(2,1)S(1)}, u32[]{:S(2)}, u32[]{:S(2)}) collective-permute-start(bf16[32,2048]{1,0:T(8,128)(2,1)S(1)} %get-tuple-element.30), channel_id=1, source_target_pairs={{0,2},{1,3},{2,4},{3,5},{4,6},{5,7},{6,0},{7,1},{8,10},{9,11},{10,... | collective-permute-start | bytes 393224 | tf_op jit(solution)/shard_map/ppermute | solution.py:35
  132.5 31.1 %all-to-all-start.2 = ((bf16[128,48,128]{2,1,0:T(8,128)(2,1)}), bf16[128,48,128]{2,1,0:T(8,128)(2,1)}, u32[]{:S(2)}, u32[]{:S(2)}) async-start(bf16[128,48,128]{2,1,0:T(8,128)(2,1)} %bitcast.18), calls=%async_computation.2 | async-start | bytes 3145728 | tf_op jit(solution)/shard_map/all_to_all | solution.py:310
  186.7 29.6 %all-to-all-start.5 = ((bf16[128,48,128]{2,1,0:T(8,128)(2,1)}), bf16[128,48,128]{2,1,0:T(8,128)(2,1)S(1)}, u32[]{:S(2)}, u32[]{:S(2)}) async-start(bf16[128,48,128]{2,1,0:T(8,128)(2,1)} %reshape_reshape.15), calls=%async_computation.5 | async-start | bytes 3145728 | tf_op jit(solution)/shard_map/all_to_all | solution.py:310
  216.4 29.6 %all-to-all-start.4 = ((bf16[128,48,128]{2,1,0:T(8,128)(2,1)}), bf16[128,48,128]{2,1,0:T(8,128)(2,1)S(1)}, u32[]{:S(2)}, u32[]{:S(2)}) async-start(bf16[128,48,128]{2,1,0:T(8,128)(2,1)} %reshape_reshape.14), calls=%async_computation.4 | async-start | bytes 3145728 | tf_op jit(solution)/shard_map/all_to_all | solution.py:310
  (26 other events, 190.0 us)

commit v4 on v2

v4 whole, which is shorter than its diff:
```python
import jax
import jax.numpy as jnp
from jax import lax
from jax.experimental import pallas as pl
from jax.experimental.pallas import tpu as pltpu
from jax.sharding import PartitionSpec as P

D = 4096
HD = 128
TOPK = 8
CAP = 3
NX, NY, NZ, NC = 4, 4, 4, 2
LANES = 128
BLOCKS = D // LANES
WIDE = 256
OUT = 1024
BF = jnp.bfloat16
F32 = jnp.float32


SMEM = pl.BlockSpec(memory_space=pltpu.SMEM)
VMEM = pl.BlockSpec(memory_space=pltpu.VMEM)


def params(mib):
    return pltpu.CompilerParams(vmem_limit_bytes=mib << 20)


def cost(flops, size):
    return pl.CostEstimate(flops=flops, bytes_accessed=size, transcendentals=0)


def to_x(a, d):
    pairs = [(x * NY + y, (x + d) % NX * NY + y) for x in range(NX) for y in range(NY)]
    return lax.ppermute(a, "seq", pairs)


def to_y(a, d):
    pairs = [(x * NY + y, x * NY + (y + d) % NY) for x in range(NX) for y in range(NY)]
    return lax.ppermute(a, "seq", pairs)


def to_z(a, d):
    pairs = [(z * NC + c, (z + d) % NZ * NC + c) for z in range(NZ) for c in range(NC)]
    return lax.ppermute(a, "head", pairs)


def swap_core(a):
    pairs = [(z * NC + c, z * NC + 1 - c) for z in range(NZ) for c in range(NC)]
    return lax.ppermute(a, "head", pairs)


def mixed_kernel(pos, query, before, one, two, three, local, gain, out):
    heads = before.shape[0]
    masks = [jnp.where(pos[0] >= d, 1.0, 0.0) for d in (1, 2, 3)]
    for h in range(heads):
        lanes = slice(h * HD, (h + 1) * HD)
        prior = before[h]
        for mask, got in zip(masks, (one, two, three)):
            prior += mask * got[h].astype(F32)
        mixed = local[:, lanes] + jnp.dot(query[:, lanes], prior.astype(BF), preferred_element_type=F32)
        mean_square = jnp.mean(mixed * mixed, axis=-1, keepdims=True)
        out[:, lanes] = (mixed * lax.rsqrt(mean_square + 1e-06) * gain[:, lanes]).astype(BF)


def mixed_heads(pos, query, before, totals, local, gain):
    return pl.pallas_call(
        mixed_kernel,
        out_shape=jax.ShapeDtypeStruct(query.shape, BF),
        in_specs=[SMEM] + [VMEM] * 7,
        out_specs=VMEM,
        compiler_params=params(16),
        cost_estimate=cost(1 << 25, 2 << 20),
    )(pos, query, before, *totals, local, gain)


def project_kernel(pos, *refs):
    tokens, weights, (keep, give, rows) = refs[:NX], refs[NX : NX + NY], refs[NX + NY :]
    tok, wide = keep.shape[1], weights[0].shape[1]
    mine = pl.multiple_of(pos[3] * tok, tok)
    other = pl.multiple_of(tok - pos[3] * tok, tok)
    for dx in range(NX):
        for dy in range(NY):
            rows[:, dy * wide : (dy + 1) * wide] = jnp.dot(
                tokens[dx][...], weights[dy][...], preferred_element_type=F32
            )
        for z in range(NZ):
            keep[dx * NZ + z] = rows[pl.ds(z * NC * tok + mine, tok), :]
            give[dx * NZ + z] = rows[pl.ds(z * NC * tok + other, tok), :].astype(BF)


def project(pos, tokens, weights, tok):
    wide = NY * weights[0].shape[1]
    shape = (NX * NZ, tok, wide)
    count, depth = tokens[0].shape
    return pl.pallas_call(
        project_kernel,
        out_shape=(jax.ShapeDtypeStruct(shape, F32), jax.ShapeDtypeStruct(shape, BF)),
        in_specs=[SMEM] + [VMEM] * (NX + NY),
        out_specs=(VMEM, VMEM),
        scratch_shapes=[pltpu.VMEM((count, wide), F32)],
        compiler_params=params(24),
        cost_estimate=cost(2 * NX * count * depth * wide, 5 << 20),
    )(pos, *tokens, *weights)


def pair_kernel(pos, keep, got, own, one, two, three):
    z = pos[2]
    for dx in range(NX):
        at = dx * NZ + z
        own[dx] = keep[at] + got[at].astype(F32)
        for d, out in ((1, one), (2, two), (3, three)):
            at = dx * NZ + lax.rem(z + d, NZ)
            out[dx] = (keep[at] + got[at].astype(F32)).astype(BF)


def pair_sums(pos, keep, got):
    shape = (NX, *keep.shape[1:])
    low = jax.ShapeDtypeStruct(shape, BF)
    return pl.pallas_call(
        pair_kernel,
        out_shape=(jax.ShapeDtypeStruct(shape, F32), low, low, low),
        in_specs=[SMEM, VMEM, VMEM],
        out_specs=(VMEM,) * 4,
        compiler_params=params(16),
        cost_estimate=cost(1 << 20, 5 << 20),
    )(pos, keep, got)


def place_kernel(pos, target, own, one, two, three, stream, gain, res, message, total, scaled):
    tok = own.shape[0]
    wide = 2 * LANES
    x, y = pos[0], pos[1]
    squares = jnp.zeros((tok, LANES), F32)
    places = []
    for dx, part in enumerate((own, one, two, three)):
        for dy in range(NY):
            seq = lax.rem(x + NX - dx, NX) * NY + lax.rem(y + dy, NY)
            at = pl.multiple_of(seq * wide, wide)
            value = part[:, dy * wide : (dy + 1) * wide].astype(F32) + stream[:, pl.ds(at, wide)].astype(F32)
            value = value.astype(BF).astype(F32)
            j = dx * NY + dy
            total[:, j * wide : (j + 1) * wide] = value
            for half in range(2):
                cut = value[:, half * LANES : (half + 1) * LANES]
                squares += cut * cut
                res[:, pl.ds(seq * 2 + half, 1), :] = cut[:, None, :]
            places.append((j, seq, at))
    factor = lax.rsqrt(jnp.sum(squares, axis=1, keepdims=True) * (1.0 / D) + 1e-06)
    for j, seq, at in places:
        value = total[:, j * wide : (j + 1) * wide] * factor * gain[:, pl.ds(at, wide)]
        for half in range(2):
            scaled[:, pl.ds(seq * 2 + half, 1), :] = value[:, half * LANES : (half + 1) * LANES][:, None, :]
    message[...] = jnp.zeros_like(message)

    def one_token(t, carry):
        row = scaled[t].astype(BF)
        for k in range(TOPK):
            message[target[t, k]] = row
        return carry

    lax.fori_loop(0, tok, one_token, 0)


def place(pos, target, parts, stream, gain, slots):
    tok = stream.shape[0]
    return pl.pallas_call(
        place_kernel,
        out_shape=(
            jax.ShapeDtypeStruct((tok, BLOCKS, LANES), F32),
            jax.ShapeDtypeStruct((slots, BLOCKS, LANES), BF),
        ),
        in_specs=[SMEM, SMEM] + [VMEM] * 6,
        out_specs=(VMEM, VMEM),
        scratch_shapes=[pltpu.VMEM((tok, D), F32), pltpu.VMEM((tok, BLOCKS, LANES), F32)],
        compiler_params=params(24),
        cost_estimate=cost(1 << 20, 5 << 20),
    )(pos, target, *parts, stream, gain)


def expert_kernel(scale, rows, gate, up, down, out, act):
    step = pl.program_id(0)
    wide = act.shape[0]

    @pl.when(step < wide)
    def _():
        x = rows[...]
        gate_part = jnp.dot(x, gate[...], preferred_element_type=F32) * scale[0, 0]
        up_part = jnp.dot(x, up[...], preferred_element_type=F32) * scale[0, 1]
        act[step] = (gate_part / (1.0 + jnp.exp(-gate_part)) * up_part).astype(BF)

    @pl.when(step >= wide)
    def _():
        total = jnp.dot(act[0], down[0:WIDE], preferred_element_type=F32)
        for j in range(1, wide):
            total += jnp.dot(act[j], down[j * WIDE : (j + 1) * WIDE], preferred_element_type=F32)
        out[...] = (total * scale[0, 2]).astype(BF)


def run_expert(scale, rows, gate, up, down):
    count, depth = rows.shape
    hidden = gate.shape[1]
    wide = hidden // WIDE
    return pl.pallas_call(
        expert_kernel,
        out_shape=jax.ShapeDtypeStruct((count, depth), BF),
        grid=(wide + depth // OUT,),
        in_specs=[
            pl.BlockSpec(memory_space=pltpu.SMEM),
            pl.BlockSpec((count, depth), lambda i: (0, 0)),
            pl.BlockSpec((depth, WIDE), lambda i: (0, jnp.minimum(i, wide - 1))),
            pl.BlockSpec((depth, WIDE), lambda i: (0, jnp.minimum(i, wide - 1))),
            pl.BlockSpec((hidden, OUT), lambda i: (0, jnp.maximum(i - wide, 0))),
        ],
        out_specs=pl.BlockSpec((count, OUT), lambda i: (0, jnp.maximum(i - wide, 0))),
        scratch_shapes=[pltpu.VMEM((wide, count, WIDE), BF)],
        compiler_params=pltpu.CompilerParams(vmem_limit_bytes=60 << 20),
        cost_estimate=pl.CostEstimate(
            flops=6 * count * depth * hidden, bytes_accessed=6 * depth * hidden, transcendentals=count * hidden
        ),
    )(scale, rows, gate, up, down)


def mix_kernel(target, gates, results, res, out, mixed):
    tok = res.shape[0]

    def one_token(t, carry):
        add = gates[t, 0] * results[target[t, 0]].astype(F32)
        for k in range(1, TOPK):
            add += gates[t, k] * results[target[t, k]].astype(F32)
        mixed[t] = res[t] + add
        return carry

    lax.fori_loop(0, tok, one_token, 0)
    for block in range(BLOCKS):
        out[:, block * LANES : (block + 1) * LANES] = mixed[:, block, :].astype(BF)


def mix(target, gates, results, res):
    tok = res.shape[0]
    return pl.pallas_call(
        mix_kernel,
        out_shape=jax.ShapeDtypeStruct((tok, D), BF),
        in_specs=[SMEM, SMEM, VMEM, VMEM],
        out_specs=VMEM,
        scratch_shapes=[pltpu.VMEM(res.shape, F32)],
        compiler_params=params(16),
        cost_estimate=cost(1 << 20, 4 << 20),
    )(target, gates, results, res)


def body(
    query,
    key,
    value,
    head_gain,
    out_weight,
    stream,
    model_gain,
    expert_ids,
    expert_gates,
    gate_weight,
    up_weight,
    down_weight,
    weight_scales,
):
    seq = lax.axis_index("seq")
    head = lax.axis_index("head")
    x, y, z, c = seq // NY, seq % NY, head // NC, head % NC
    pos = jnp.stack([x, y, z, c]).astype(jnp.int32)
    seq_rows = query.shape[0]
    tok_rows = stream.shape[0]
    heads_local = head_gain.shape[0] // HD
    experts = lax.axis_size("seq") * lax.axis_size("head")
    slots = experts * CAP

    query_rows = query.reshape(seq_rows, heads_local, HD)
    key_rows = key.reshape(seq_rows, heads_local, HD)
    value_rows = value.reshape(seq_rows, heads_local, HD)
    block_state = jnp.einsum("shd,she->hde", key_rows, value_rows, preferred_element_type=F32)
    low = block_state.astype(BF)
    line, before = block_state, jnp.zeros_like(block_state)
    for d in range(1, NY):
        got = to_y(low, d).astype(F32)
        line = line + got
        before = before + jnp.where(y >= d, got, 0.0)
    low = line.astype(BF)
    totals = [to_x(low, d) for d in range(1, NX)]
    weights = [out_weight] + [to_y(out_weight, NY - d) for d in range(1, NY)]

    scores = jnp.einsum("thd,shd->hts", query_rows, key_rows, preferred_element_type=F32)
    causal = jnp.tril(jnp.ones((seq_rows, seq_rows), dtype=bool))
    scores = jnp.where(causal[None, :, :], scores, 0.0).astype(BF)
    local_part = jnp.einsum("hts,shd->thd", scores, value_rows, preferred_element_type=F32)
    local_part = local_part.reshape(seq_rows, heads_local * HD)
    head_normed = mixed_heads(pos, query, before, totals, local_part, head_gain[None])

    flat_ids = expert_ids.reshape(-1)
    at = jnp.arange(flat_ids.shape[0], dtype=jnp.int32)
    same = (flat_ids[:, None] == flat_ids[None, :]) & (at[None, :] < at[:, None])
    slot_index = jnp.sum(same.astype(jnp.int32), axis=1)
    target = (flat_ids * CAP + slot_index).reshape(tok_rows, TOPK)

    def exchange(rows):
        message = rows.reshape(experts, CAP * BLOCKS, LANES)
        got = lax.all_to_all(message, ("seq", "head"), split_axis=0, concat_axis=0, tiled=True)
        return got.reshape(slots, BLOCKS, LANES)

    tokens = [head_normed] + [to_x(head_normed, NX - d) for d in range(1, NX)]
    keep, give = project(pos, tokens, weights, tok_rows)
    own, *low = pair_sums(pos, keep, swap_core(give))
    for d in range(1, NZ):
        own = own + to_z(low[d - 1], d).astype(F32)
    parts = [own[0]] + [to_x(own[d].astype(BF), d) for d in range(1, NX)]
    res, message = place(pos, target, parts, stream, model_gain[None], slots)
    slot_rows = exchange(message).reshape(slots, D)
    produced = run_expert(weight_scales, slot_rows, gate_weight[0], up_weight[0], down_weight[0])
    results = exchange(produced.reshape(slots, BLOCKS, LANES))
    return mix(target, expert_gates, results, res)


def solution(mesh):
    token = P(("seq", "head"), None)
    expert = P(("seq", "head"), None, None)
    return jax.shard_map(
        body,
        mesh=mesh,
        in_specs=(
            P("seq", "head"),
            P("seq", "head"),
            P("seq", "head"),
            P("head"),
            P("head", "seq"),
            token,
            P(),
            token,
            token,
            expert,
            expert,
            expert,
            token,
        ),
        out_specs=token,
        check_vma=False,
    )
```

time: 240 us -> 205 us (0.85)
  waiting for transfers between devices: 91.6 us -> 74.4 us
  Pallas kernels: 12.5 us -> 27.3 us
  between operations: 13.7 us -> 0.22 us
  local copies, waits for them, and re-layouts: 26.8 us -> 14.6 us
  other arithmetic: 13 us -> 1.6 us
  starting transfers between devices: 22.5 us -> 31.8 us
  matrix products: 9.7 us -> 1.69 us
  blocking collectives: 49.6 us -> 52.6 us
    all_gather x1 -> x0, waiting for transfers between devices: 23.4 us -> none  [body(): full_out = lax.all_gather(out_weight, 'seq', axis=1, tiled=True)]
    ppermute x3 -> x18, waiting for transfers between devices: 10.4 us -> 30.1 us  [the longest x9 15.1 us: to_x(): return lax.ppermute(a, 'seq', pairs)]
    ppermute x3 -> x18, starting transfers between devices: 5.04 us -> 24.3 us  [the longest x9 10 us: to_x(): return lax.ppermute(a, 'seq', pairs)]
    reshape x5 -> x2, local copies, waits for them, and re-layouts: 17.8 us -> 1.35 us  [the longest x1 1.15 us: body(): value_rows = value.reshape(seq_rows, heads_local, HD)]
    all_to_all x3 -> x1, waiting for transfers between devices: 55.2 us -> 41.9 us  [exchange(): lax.all_to_all(message, ('seq', 'head'), split_axis=0, concat_axis=0, til...]
    pallas_call x0 -> x5, Pallas kernels: none -> 11.3 us  [the longest x1 3.1 us: mix(): pl.pallas_call(mix_kernel, out_shape=jax.ShapeDtypeStruct((tok, D), BF),...]
    all_to_all x3 -> x1, starting transfers between devices: 15.8 us -> 4.67 us  [exchange(): lax.all_to_all(message, ('seq', 'head'), split_axis=0, concat_axis=0, til...]
    another operation x0 -> x2, local copies, waits for them, and re-layouts: none -> 9.25 us  [the longest x1 5.89 us: exchange(): message = rows.reshape(experts, CAP * BLOCKS, LANES)]
  transfers between devices with their start and end apart: 8 -> 20, of which waited for: 7 -> 14; matrix products, arithmetic and copies ran while one was open for 6% -> 1% of each run, Pallas kernels for 0% -> 0%
where the time goes in v4:
time: 205 us; the launch traced here: 204 us
  waiting for transfers between devices  74.4 us (36%)
  blocking collectives  52.6 us (26%)
  starting transfers between devices  31.8 us (16%)
  Pallas kernels  27.3 us (13%)
  local copies, waits for them, and re-layouts  14.6 us (7%)
    all_to_all x1, blocking collectives, exchange(): lax.all_to_all(message, ('seq', 'head'), split_axis=0, concat_axis=0, til...  52.6 us
    all_to_all x1, waiting for transfers between devices, exchange(): lax.all_to_all(message, ('seq', 'head'), split_axis=0, concat_axis=0, til...  41.9 us
    pallas_call x1, Pallas kernels, run_expert(): pl.pallas_call(expert_kernel, out_shape=jax.ShapeDtypeStruct((count, dept...  16 us
    ppermute x9, waiting for transfers between devices, to_x(): return lax.ppermute(a, 'seq', pairs)  15.1 us
    ppermute x3, waiting for transfers between devices, to_z(): return lax.ppermute(a, 'head', pairs)  10.9 us
    ppermute x9, starting transfers between devices, to_x(): return lax.ppermute(a, 'seq', pairs)  10 us
    ppermute x6, starting transfers between devices, to_y(): return lax.ppermute(a, 'seq', pairs)  8.66 us
    another operation x1, local copies, waits for them, and re-layouts, exchange(): message = rows.reshape(experts, CAP * BLOCKS, LANES)  5.89 us
  transfers between devices with their start and end apart: 20, of which 14 were waited for; matrix products, arithmetic and copies ran while one was open for 1% of the time, Pallas kernels for 0%

profile of v4, /device:TPU:1, one launch (start us, length us, event | category | flops | bytes accessed | tf_op | source)
XLA Modules:
  0.0 204.2 jit_solution(13783437302135686510)
XLA Ops:
  1.5 2.2 %collective-permute-start = (bf16[4,128,128]{2,1,0:T(8,128)(2,1)S(1)}, bf16[4,128,128]{2,1,0:T(8,128)(2,1)S(1)}, u32[]{:S(2)}, u32[]{:S(2)}) collective-permute-start(bf16[4,128,128]{2,1,0:T(8,128)(2,1)S(1)} %get-tuple-element.28), channel_id=1, source_target_pairs={{0,8},{8,16},{16,24},{24,0},{32,40},{40,48},{48,56},{56,32},{64,72... | collective-permute-start | bytes 393224 | tf_op jit(solution)/shard_map/ppermute | solution.py:40
  3.7 2.6 %collective-permute-start.1 = (bf16[4,128,128]{2,1,0:T(8,128)(2,1)S(1)}, bf16[4,128,128]{2,1,0:T(8,128)(2,1)S(1)}, u32[]{:S(2)}, u32[]{:S(2)}) collective-permute-start(bf16[4,128,128]{2,1,0:T(8,128)(2,1)S(1)} %get-tuple-element.28), channel_id=1, source_target_pairs={{0,16},{8,24},{16,0},{24,8},{32,48},{40,56},{48,32},{56,40},{64,80... | collective-permute-start | bytes 393224 | tf_op jit(solution)/shard_map/ppermute | solution.py:40
  8.2 3.8 %collective-permute-done.1 = bf16[4,128,128]{2,1,0:T(8,128)(2,1)S(1)} collective-permute-done((bf16[4,128,128]{2,1,0:T(8,128)(2,1)S(1)}, bf16[4,128,128]{2,1,0:T(8,128)(2,1)S(1)}, u32[]{:S(2)}, u32[]{:S(2)}) %collective-permute-start.1) | collective-permute-done | bytes 131104 | tf_op jit(solution)/shard_map/ppermute | solution.py:40
  13.4 2.4 %collective-permute-start.4 = (bf16[4,128,128]{2,1,0:T(8,128)(2,1)S(1)}, bf16[4,128,128]{2,1,0:T(8,128)(2,1)S(1)}, u32[]{:S(2)}, u32[]{:S(2)}) collective-permute-start(bf16[4,128,128]{2,1,0:T(8,128)(2,1)S(1)} %get-tuple-element.23), channel_id=1, source_target_pairs={{0,64},{8,72},{16,80},{24,88},{32,96},{40,104},{48,112},{56,120},{... | collective-permute-start | bytes 393224 | tf_op jit(solution)/shard_map/ppermute | solution.py:35
  18.8 2.2 %collective-permute-start.9 = (bf16[512,256]{1,0:T(8,128)(2,1)S(1)}, bf16[512,256]{1,0:T(8,128)(2,1)S(1)}, u32[]{:S(2)}, u32[]{:S(2)}) collective-permute-start(bf16[512,256]{1,0:T(8,128)(2,1)S(1)} %copy-done.8), channel_id=1, source_target_pairs={{0,24},{8,0},{16,8},{24,16},{32,56},{40,32},{48,40},{56,48},{64,88... | collective-permute-start | bytes 786440 | tf_op jit(solution)/shard_map/ppermute | solution.py:40
  24.3 3.2 %collective-permute-done.6.refs_1_ = bf16[256,512]{1,0:T(8,128)(2,1)S(1)} collective-permute-done((bf16[256,512]{1,0:T(8,128)(2,1)S(1)}, bf16[256,512]{1,0:T(8,128)(2,1)S(1)}, u32[]{:S(2)}, u32[]{:S(2)}) %collective-permute-start.6) | collective-permute-done | bytes 262176 | tf_op jit(solution)/shard_map/ppermute | solution.py:35
  27.5 2.6 %collective-permute-done.7.refs_2_ = bf16[256,512]{1,0:T(8,128)(2,1)S(1)} collective-permute-done((bf16[256,512]{1,0:T(8,128)(2,1)S(1)}, bf16[256,512]{1,0:T(8,128)(2,1)S(1)}, u32[]{:S(2)}, u32[]{:S(2)}) %collective-permute-start.7) | collective-permute-done | bytes 262176 | tf_op jit(solution)/shard_map/ppermute | solution.py:35
  30.2 6.2 %collective-permute-done.8.refs_3_ = bf16[256,512]{1,0:T(8,128)(2,1)S(1)} collective-permute-done((bf16[256,512]{1,0:T(8,128)(2,1)S(1)}, bf16[256,512]{1,0:T(8,128)(2,1)S(1)}, u32[]{:S(2)}, u32[]{:S(2)}) %collective-permute-start.8) | collective-permute-done | bytes 262176 | tf_op jit(solution)/shard_map/ppermute | solution.py:35
  36.4 2.9 %shard_map.128 = (f32[16,32,1024]{2,1,0:T(8,128)S(1)}, bf16[16,32,1024]{2,1,0:T(8,128)(2,1)}) custom-call(s32[4]{0:T(128)S(1)} %pad_add_fusion.pos, bf16[256,512]{1,0:T(8,128)(2,1)S(1)} %shard_map.127.refs_0_, bf16[256,512]{1,0:T(8,128)(2,1)S(1)} %collective-permute-done.6.refs_1_, bf16[256,512]{1,0:T(8,128)(2,1)S(1)} %collective-permute-done.7.refs_2_, ...), custom_call_target="tpu_custom_call" | custom-call | flops 1073741824 | bytes 5242880 | tf_op jit(solution)/shard_map/pallas_call | solution.py:96
  39.3 2.8 %collective-permute-start.12 = (bf16[16,32,1024]{2,1,0:T(8,128)(2,1)}, bf16[16,32,1024]{2,1,0:T(8,128)(2,1)S(1)}, u32[]{:S(2)}, u32[]{:S(2)}) collective-permute-start(bf16[16,32,1024]{2,1,0:T(8,128)(2,1)} %get-tuple-element.14), channel_id=1, source_target_pairs={{0,1},{1,0},{2,3},{3,2},{4,5},{5,4},{6,7},{7,6},{8,9},{9,8},{10,11... | collective-permute-start | bytes 3145736 | tf_op jit(solution)/shard_map/ppermute | solution.py:50
  42.3 2.3 %collective-permute-done.12.got = bf16[16,32,1024]{2,1,0:T(8,128)(2,1)S(1)} collective-permute-done((bf16[16,32,1024]{2,1,0:T(8,128)(2,1)}, bf16[16,32,1024]{2,1,0:T(8,128)(2,1)S(1)}, u32[]{:S(2)}, u32[]{:S(2)}) %collective-permute-start.12) | collective-permute-done | bytes 1048608 | tf_op jit(solution)/shard_map/ppermute | solution.py:50
  46.9 1.6 collective-permute-start.13
  48.6 3.3 %collective-permute-start.14 = (bf16[4,32,1024]{2,1,0:T(8,128)(2,1)}, bf16[4,32,1024]{2,1,0:T(8,128)(2,1)S(1)}, u32[]{:S(2)}, u32[]{:S(2)}) collective-permute-start(bf16[4,32,1024]{2,1,0:T(8,128)(2,1)} %get-tuple-element.17), channel_id=1, source_target_pairs={{0,4},{1,5},{2,6},{3,7},{4,0},{5,1},{6,2},{7,3},{8,12},{9,13},{10,... | collective-permute-start | bytes 786440 | tf_op jit(solution)/shard_map/ppermute | solution.py:45
  52.9 4.4 %collective-permute-done.13 = bf16[4,32,1024]{2,1,0:T(8,128)(2,1)S(1)} collective-permute-done((bf16[4,32,1024]{2,1,0:T(8,128)(2,1)}, bf16[4,32,1024]{2,1,0:T(8,128)(2,1)S(1)}, u32[]{:S(2)}, u32[]{:S(2)}) %collective-permute-start.13) | collective-permute-done | bytes 262176 | tf_op jit(solution)/shard_map/ppermute | solution.py:45
  57.3 6.5 %collective-permute-done.14 = bf16[4,32,1024]{2,1,0:T(8,128)(2,1)S(1)} collective-permute-done((bf16[4,32,1024]{2,1,0:T(8,128)(2,1)}, bf16[4,32,1024]{2,1,0:T(8,128)(2,1)S(1)}, u32[]{:S(2)}, u32[]{:S(2)}) %collective-permute-start.14) | collective-permute-done | bytes 262176 | tf_op jit(solution)/shard_map/ppermute | solution.py:45
  67.9 1.9 collective-permute-done.16.one
  71.9 2.8 %shard_map.130 = (f32[32,32,128]{2,1,0:T(8,128)S(1)}, bf16[384,32,128]{2,1,0:T(8,128)(2,1)S(1)}) custom-call(s32[4]{0:T(128)S(1)} %pad_add_fusion.pos, s32[32,8]{1,0:T(8,128)S(1)} %multiply_add_fusion.target, f32[32,1024]{1,0:T(8,128)S(1)} %slice_bitcast_fusion.own, bf16[32,1024]{1,0:T(8,128)(2,1)S(1)} %collective-permute-done.16.one, ...), custom_call_target="tpu_custom_call" | custom-call | flops 1048576 | bytes 5242880 | tf_op jit(solution)/shard_map/pallas_call | solution.py:167
  75.5 52.6 %all_to_all.10 = bf16[128,96,128]{2,1,0:T(8,128)(2,1)S(1)} all-to-all(bf16[128,96,128]{2,1,0:T(8,128)(2,1)S(1)} %bitcast.51), channel_id=1, replica_groups=mesh['seq'=16,'head'=8] {'seq','head'}, dimensions={0} | all-to-all | bytes 6291456 | tf_op jit(solution)/shard_map/all_to_all | solution.py:306
  128.1 3.4 %reshape_reshape.6.rows = bf16[384,4096]{1,0:T(8,128)(2,1)} reshape(bf16[128,96,128]{2,1,0:T(8,128)(2,1)S(1)} %all_to_all.10) | data formatting | bytes 6291456 | tf_op jit(solution)/shard_map/reshape;reshape | solution.py:316
  131.5 16.0 %shard_map.131 = bf16[384,4096]{1,0:T(8,128)(2,1)} custom-call(f32[1,3]{1,0:T(1,128)} %scale.1, bf16[384,4096]{1,0:T(8,128)(2,1)} %reshape_reshape.6.rows, bf16[4096,768]{1,0:T(8,128)(2,1)} %bitcast.57, bf16[4096,768]{1,0:T(8,128)(2,1)} %bitcast.58, bf16[768,4096]{1,0:T(8,128)(2,1)} %bitcast.59), custom_call_target="tpu_custom_call" | custom-call | flops 7247757312 | bytes 18874368 | tf_op jit(solution)/shard_map/pallas_call | solution.py:204
  147.5 5.9 %reshape_reshape.7 = bf16[128,96,128]{2,1,0:T(8,128)(2,1)} reshape(bf16[384,4096]{1,0:T(8,128)(2,1)} %shard_map.131) | data formatting | bytes 6291456 | tf_op jit(solution)/shard_map/reshape;reshape | solution.py:305
  153.4 4.7 %all-to-all-start.1 = ((bf16[128,96,128]{2,1,0:T(8,128)(2,1)}), bf16[128,96,128]{2,1,0:T(8,128)(2,1)S(1)}, u32[]{:S(2)}, u32[]{:S(2)}) async-start(bf16[128,96,128]{2,1,0:T(8,128)(2,1)} %reshape_reshape.7), calls=%async_computation.1 | async-start | bytes 6291456 | tf_op jit(solution)/shard_map/all_to_all | solution.py:306
  158.1 41.9 %all-to-all-done.1 = bf16[128,96,128]{2,1,0:T(8,128)(2,1)S(1)} async-done(((bf16[128,96,128]{2,1,0:T(8,128)(2,1)}), bf16[128,96,128]{2,1,0:T(8,128)(2,1)S(1)}, u32[]{:S(2)}, u32[]{:S(2)}) %all-to-all-start.1) | async-done | bytes 3145760 | tf_op jit(solution)/shard_map/all_to_all | solution.py:306
  201.1 3.1 %shard_map.132 = bf16[32,4096]{1,0:T(8,128)(2,1)} custom-call(s32[32,8]{1,0:T(8,128)S(1)} %multiply_add_fusion.target, f32[32,8]{1,0:T(8,128)S(1)} %copy.35.gates, bf16[384,32,128]{2,1,0:T(8,128)(2,1)S(1)} %bitcast.50, f32[32,32,128]{2,1,0:T(8,128)S(1)} %copy-done.2), custom_call_target="tpu_custom_call" | custom-call | flops 1048576 | bytes 4194304 | tf_op jit(solution)/shard_map/pallas_call | solution.py:241
  (63 shorter events, 22.5 us)
Async XLA Ops:
  0.0 21.0 %copy-start.4 = (bf16[256,512]{1,0:T(8,128)(2,1)S(1)}, bf16[256,512]{1,0:T(8,128)(2,1)}, u32[]{:S(2)}) copy-start(bf16[256,512]{1,0:T(8,128)(2,1)} %query.1) | copy-start | bytes 786436
  0.0 21.0 %copy-start.7 = (f32[512]{0:T(512)S(1)}, f32[512]{0:T(512)}, u32[]{:S(2)}) copy-start(f32[512]{0:T(512)} %param.16) | copy-start | bytes 6148
  1.5 6.7 %collective-permute-start = (bf16[4,128,128]{2,1,0:T(8,128)(2,1)S(1)}, bf16[4,128,128]{2,1,0:T(8,128)(2,1)S(1)}, u32[]{:S(2)}, u32[]{:S(2)}) collective-permute-start(bf16[4,128,128]{2,1,0:T(8,128)(2,1)S(1)} %get-tuple-element.28), channel_id=1, source_target_pairs={{0,8},{8,16},{16,24},{24,0},{32,40},{40,48},{48,56},{56,32},{64,72... | collective-permute-start | bytes 393224 | tf_op jit(solution)/shard_map/ppermute | solution.py:40
  3.7 8.3 %collective-permute-start.1 = (bf16[4,128,128]{2,1,0:T(8,128)(2,1)S(1)}, bf16[4,128,128]{2,1,0:T(8,128)(2,1)S(1)}, u32[]{:S(2)}, u32[]{:S(2)}) collective-permute-start(bf16[4,128,128]{2,1,0:T(8,128)(2,1)S(1)} %get-tuple-element.28), channel_id=1, source_target_pairs={{0,16},{8,24},{16,0},{24,8},{32,48},{40,56},{48,32},{56,40},{64,80... | collective-permute-start | bytes 393224 | tf_op jit(solution)/shard_map/ppermute | solution.py:40
  6.3 5.7 %collective-permute-start.2 = (bf16[4,128,128]{2,1,0:T(8,128)(2,1)S(1)}, bf16[4,128,128]{2,1,0:T(8,128)(2,1)S(1)}, u32[]{:S(2)}, u32[]{:S(2)}) collective-permute-start(bf16[4,128,128]{2,1,0:T(8,128)(2,1)S(1)} %get-tuple-element.28), channel_id=1, source_target_pairs={{0,24},{8,0},{16,8},{24,16},{32,56},{40,32},{48,40},{56,48},{64,88... | collective-permute-start | bytes 393224 | tf_op jit(solution)/shard_map/ppermute | solution.py:40
  7.3 16.8 %collective-permute-start.10 = (bf16[512,256]{1,0:T(8,128)(2,1)}, bf16[512,256]{1,0:T(8,128)(2,1)S(1)}, u32[]{:S(2)}, u32[]{:S(2)}) collective-permute-start(bf16[512,256]{1,0:T(8,128)(2,1)} %refs_4_.1), channel_id=1, source_target_pairs={{0,16},{8,24},{16,0},{24,8},{32,48},{40,56},{48,32},{56,40},{64,80... | collective-permute-start | bytes 786440 | tf_op jit(solution)/shard_map/ppermute | solution.py:40
  7.6 16.7 %collective-permute-start.11 = (bf16[512,256]{1,0:T(8,128)(2,1)}, bf16[512,256]{1,0:T(8,128)(2,1)S(1)}, u32[]{:S(2)}, u32[]{:S(2)}) collective-permute-start(bf16[512,256]{1,0:T(8,128)(2,1)} %refs_4_.1), channel_id=1, source_target_pairs={{0,8},{8,16},{16,24},{24,0},{32,40},{40,48},{48,56},{56,32},{64,72... | collective-permute-start | bytes 786440 | tf_op jit(solution)/shard_map/ppermute | solution.py:40
  12.1 6.7 %collective-permute-start.3 = (bf16[4,128,128]{2,1,0:T(8,128)(2,1)S(1)}, bf16[4,128,128]{2,1,0:T(8,128)(2,1)S(1)}, u32[]{:S(2)}, u32[]{:S(2)}) collective-permute-start(bf16[4,128,128]{2,1,0:T(8,128)(2,1)S(1)} %get-tuple-element.23), channel_id=1, source_target_pairs={{0,32},{8,40},{16,48},{24,56},{32,64},{40,72},{48,80},{56,88},{64,... | collective-permute-start | bytes 393224 | tf_op jit(solution)/shard_map/ppermute | solution.py:35
  13.4 7.6 %collective-permute-start.4 = (bf16[4,128,128]{2,1,0:T(8,128)(2,1)S(1)}, bf16[4,128,128]{2,1,0:T(8,128)(2,1)S(1)}, u32[]{:S(2)}, u32[]{:S(2)}) collective-permute-start(bf16[4,128,128]{2,1,0:T(8,128)(2,1)S(1)} %get-tuple-element.23), channel_id=1, source_target_pairs={{0,64},{8,72},{16,80},{24,88},{32,96},{40,104},{48,112},{56,120},{... | collective-permute-start | bytes 393224 | tf_op jit(solution)/shard_map/ppermute | solution.py:35
  15.8 5.1 %collective-permute-start.5 = (bf16[4,128,128]{2,1,0:T(8,128)(2,1)S(1)}, bf16[4,128,128]{2,1,0:T(8,128)(2,1)S(1)}, u32[]{:S(2)}, u32[]{:S(2)}) collective-permute-start(bf16[4,128,128]{2,1,0:T(8,128)(2,1)S(1)} %get-tuple-element.23), channel_id=1, source_target_pairs={{0,96},{8,104},{16,112},{24,120},{32,0},{40,8},{48,16},{56,24},{64... | collective-permute-start | bytes 393224 | tf_op jit(solution)/shard_map/ppermute | solution.py:35
  18.4 23.6 %copy-start.9 = (s32[32,8]{0,1:T(8,128)S(1)}, s32[32,8]{0,1:T(8,128)}, u32[]{:S(2)}) copy-start(s32[32,8]{0,1:T(8,128)} %param.20) | copy-start | bytes 3076
  18.8 5.6 %collective-permute-start.9 = (bf16[512,256]{1,0:T(8,128)(2,1)S(1)}, bf16[512,256]{1,0:T(8,128)(2,1)S(1)}, u32[]{:S(2)}, u32[]{:S(2)}) collective-permute-start(bf16[512,256]{1,0:T(8,128)(2,1)S(1)} %copy-done.8), channel_id=1, source_target_pairs={{0,24},{8,0},{16,8},{24,16},{32,56},{40,32},{48,40},{56,48},{64,88... | collective-permute-start | bytes 786440 | tf_op jit(solution)/shard_map/ppermute | solution.py:40
  21.9 5.6 %collective-permute-start.6 = (bf16[256,512]{1,0:T(8,128)(2,1)S(1)}, bf16[256,512]{1,0:T(8,128)(2,1)S(1)}, u32[]{:S(2)}, u32[]{:S(2)}) collective-permute-start(bf16[256,512]{1,0:T(8,128)(2,1)S(1)} %shard_map.127.refs_0_), channel_id=1, source_target_pairs={{0,96},{8,104},{16,112},{24,120},{32,0},{40,8},{48,16},{56,24},{64... | collective-permute-start | bytes 786440 | tf_op jit(solution)/shard_map/ppermute | solution.py:35
  23.3 6.8 %collective-permute-start.7 = (bf16[256,512]{1,0:T(8,128)(2,1)S(1)}, bf16[256,512]{1,0:T(8,128)(2,1)S(1)}, u32[]{:S(2)}, u32[]{:S(2)}) collective-permute-start(bf16[256,512]{1,0:T(8,128)(2,1)S(1)} %shard_map.127.refs_0_), channel_id=1, source_target_pairs={{0,64},{8,72},{16,80},{24,88},{32,96},{40,104},{48,112},{56,120},{... | collective-permute-start | bytes 786440 | tf_op jit(solution)/shard_map/ppermute | solution.py:35
  24.1 12.2 %collective-permute-start.8 = (bf16[256,512]{1,0:T(8,128)(2,1)S(1)}, bf16[256,512]{1,0:T(8,128)(2,1)S(1)}, u32[]{:S(2)}, u32[]{:S(2)}) collective-permute-start(bf16[256,512]{1,0:T(8,128)(2,1)S(1)} %shard_map.127.refs_0_), channel_id=1, source_target_pairs={{0,32},{8,40},{16,48},{24,56},{32,64},{40,72},{48,80},{56,88},{64,... | collective-permute-start | bytes 786440 | tf_op jit(solution)/shard_map/ppermute | solution.py:35
  39.3 31.7 %copy-start.6 = (f32[4096]{0:T(1024)S(1)}, f32[4096]{0:T(1024)}, u32[]{:S(2)}) copy-start(f32[4096]{0:T(1024)} %param.19) | copy-start | bytes 49156
  39.3 5.3 %collective-permute-start.12 = (bf16[16,32,1024]{2,1,0:T(8,128)(2,1)}, bf16[16,32,1024]{2,1,0:T(8,128)(2,1)S(1)}, u32[]{:S(2)}, u32[]{:S(2)}) collective-permute-start(bf16[16,32,1024]{2,1,0:T(8,128)(2,1)} %get-tuple-element.14), channel_id=1, source_target_pairs={{0,1},{1,0},{2,3},{3,2},{4,5},{5,4},{6,7},{7,6},{8,9},{9,8},{10,11... | collective-permute-start | bytes 3145736 | tf_op jit(solution)/shard_map/ppermute | solution.py:50
  46.9 10.3 %collective-permute-start.13 = (bf16[4,32,1024]{2,1,0:T(8,128)(2,1)}, bf16[4,32,1024]{2,1,0:T(8,128)(2,1)S(1)}, u32[]{:S(2)}, u32[]{:S(2)}) collective-permute-start(bf16[4,32,1024]{2,1,0:T(8,128)(2,1)} %get-tuple-element.16), channel_id=1, source_target_pairs={{0,2},{1,3},{2,4},{3,5},{4,6},{5,7},{6,0},{7,1},{8,10},{9,11},{10,... | collective-permute-start | bytes 786440 | tf_op jit(solution)/shard_map/ppermute | solution.py:45
  48.6 15.2 %collective-permute-start.14 = (bf16[4,32,1024]{2,1,0:T(8,128)(2,1)}, bf16[4,32,1024]{2,1,0:T(8,128)(2,1)S(1)}, u32[]{:S(2)}, u32[]{:S(2)}) collective-permute-start(bf16[4,32,1024]{2,1,0:T(8,128)(2,1)} %get-tuple-element.17), channel_id=1, source_target_pairs={{0,4},{1,5},{2,6},{3,7},{4,0},{5,1},{6,2},{7,3},{8,12},{9,13},{10,... | collective-permute-start | bytes 786440 | tf_op jit(solution)/shard_map/ppermute | solution.py:45
  51.9 11.9 %collective-permute-start.15 = (bf16[4,32,1024]{2,1,0:T(8,128)(2,1)}, bf16[4,32,1024]{2,1,0:T(8,128)(2,1)S(1)}, u32[]{:S(2)}, u32[]{:S(2)}) collective-permute-start(bf16[4,32,1024]{2,1,0:T(8,128)(2,1)} %get-tuple-element.18), channel_id=1, source_target_pairs={{0,6},{1,7},{2,0},{3,1},{4,2},{5,3},{6,4},{7,5},{8,14},{9,15},{10,... | collective-permute-start | bytes 786440 | tf_op jit(solution)/shard_map/ppermute | solution.py:45
  65.0 4.9 %collective-permute-start.16 = (bf16[32,1024]{1,0:T(8,128)(2,1)S(1)}, bf16[32,1024]{1,0:T(8,128)(2,1)S(1)}, u32[]{:S(2)}, u32[]{:S(2)}) collective-permute-start(bf16[32,1024]{1,0:T(8,128)(2,1)S(1)} %get-tuple-element.27), channel_id=1, source_target_pairs={{0,32},{8,40},{16,48},{24,56},{32,64},{40,72},{48,80},{56,88},{64,... | collective-permute-start | bytes 196616 | tf_op jit(solution)/shard_map/ppermute | solution.py:35
  65.1 5.2 %collective-permute-start.17 = (bf16[32,1024]{1,0:T(8,128)(2,1)S(1)}, bf16[32,1024]{1,0:T(8,128)(2,1)S(1)}, u32[]{:S(2)}, u32[]{:S(2)}) collective-permute-start(bf16[32,1024]{1,0:T(8,128)(2,1)S(1)} %get-tuple-element.26), channel_id=1, source_target_pairs={{0,64},{8,72},{16,80},{24,88},{32,96},{40,104},{48,112},{56,120},{... | collective-permute-start | bytes 196616 | tf_op jit(solution)/shard_map/ppermute | solution.py:35
  66.6 4.3 %collective-permute-start.18 = (bf16[32,1024]{1,0:T(8,128)(2,1)S(1)}, bf16[32,1024]{1,0:T(8,128)(2,1)S(1)}, u32[]{:S(2)}, u32[]{:S(2)}) collective-permute-start(bf16[32,1024]{1,0:T(8,128)(2,1)S(1)} %get-tuple-element.25), channel_id=1, source_target_pairs={{0,96},{8,104},{16,112},{24,120},{32,0},{40,8},{48,16},{56,24},{64... | collective-permute-start | bytes 196616 | tf_op jit(solution)/shard_map/ppermute | solution.py:35
  153.4 46.7 %all-to-all-start.1 = ((bf16[128,96,128]{2,1,0:T(8,128)(2,1)}), bf16[128,96,128]{2,1,0:T(8,128)(2,1)S(1)}, u32[]{:S(2)}, u32[]{:S(2)}) async-start(bf16[128,96,128]{2,1,0:T(8,128)(2,1)} %reshape_reshape.7), calls=%async_computation.1 | async-start | bytes 6291456 | tf_op jit(solution)/shard_map/all_to_all | solution.py:306
  (7 other events, 28.2 us)

commit v5 on v4

v5 whole, which is shorter than its diff:
```python
import jax
import jax.numpy as jnp
from jax import lax
from jax.experimental import pallas as pl
from jax.experimental.pallas import tpu as pltpu
from jax.sharding import PartitionSpec as P

D = 4096
HD = 128
TOPK = 8
CAP = 3
AXES = ("x", "y", "z", "c")
NX, NY, NZ, NC = 4, 4, 4, 2
LANES = 128
BLOCKS = D // LANES
DEEP = 512
OUT = 1024
BF = jnp.bfloat16
F32 = jnp.float32


SMEM = pl.BlockSpec(memory_space=pltpu.SMEM)
VMEM = pl.BlockSpec(memory_space=pltpu.VMEM)


def params(mib):
    return pltpu.CompilerParams(vmem_limit_bytes=mib << 20)


def cost(flops, size):
    return pl.CostEstimate(flops=flops, bytes_accessed=size, transcendentals=0)


def shift(a, axis, d):
    n = lax.axis_size(axis)
    return lax.ppermute(a, axis, [(i, (i + d) % n) for i in range(n)])


def gather_line(a, axis):
    n = lax.axis_size(axis)
    return [a] + [shift(a, axis, n - d) for d in range(1, n)]


def mixed_kernel(pos, query, before, one, two, three, local, gain, out):
    heads = before.shape[0]
    masks = [jnp.where(pos[0] >= d, 1.0, 0.0) for d in (1, 2, 3)]
    for h in range(heads):
        lanes = slice(h * HD, (h + 1) * HD)
        prior = before[h]
        for mask, got in zip(masks, (one, two, three)):
            prior += mask * got[h].astype(F32)
        mixed = local[:, lanes] + jnp.dot(query[:, lanes], prior.astype(BF), preferred_element_type=F32)
        mean_square = jnp.mean(mixed * mixed, axis=-1, keepdims=True)
        out[:, lanes] = (mixed * lax.rsqrt(mean_square + 1e-06) * gain[:, lanes]).astype(BF)


def mixed_heads(pos, query, before, totals, local, gain):
    return pl.pallas_call(
        mixed_kernel,
        out_shape=jax.ShapeDtypeStruct(query.shape, BF),
        in_specs=[SMEM] + [VMEM] * 7,
        out_specs=VMEM,
        compiler_params=params(16),
        cost_estimate=cost(1 << 25, 2 << 20),
    )(pos, query, before, *totals, local, gain)


def project_kernel(pos, *refs):
    tokens, weights, (keep, give, rows) = refs[:NX], refs[NX : NX + NY], refs[NX + NY :]
    tok, wide = keep.shape[1], weights[0].shape[1]
    mine = pl.multiple_of(pos[3] * tok, tok)
    other = pl.multiple_of(tok - pos[3] * tok, tok)
    for dx in range(NX):
        for dy in range(NY):
            rows[:, dy * wide : (dy + 1) * wide] = jnp.dot(
                tokens[dx][...], weights[dy][...], preferred_element_type=F32
            )
        for z in range(NZ):
            keep[dx * NZ + z] = rows[pl.ds(z * NC * tok + mine, tok), :]
            give[dx * NZ + z] = rows[pl.ds(z * NC * tok + other, tok), :].astype(BF)


def project(pos, tokens, weights, tok):
    wide = NY * weights[0].shape[1]
    shape = (NX * NZ, tok, wide)
    count, depth = tokens[0].shape
    return pl.pallas_call(
        project_kernel,
        out_shape=(jax.ShapeDtypeStruct(shape, F32), jax.ShapeDtypeStruct(shape, BF)),
        in_specs=[SMEM] + [VMEM] * (NX + NY),
        out_specs=(VMEM, VMEM),
        scratch_shapes=[pltpu.VMEM((count, wide), F32)],
        compiler_params=params(24),
        cost_estimate=cost(2 * NX * count * depth * wide, 5 << 20),
    )(pos, *tokens, *weights)


def pair_kernel(pos, keep, got, own, one, two, three):
    z = pos[2]
    for dx in range(NX):
        at = dx * NZ + z
        own[dx] = keep[at] + got[at].astype(F32)
        for d, out in ((1, one), (2, two), (3, three)):
            at = dx * NZ + lax.rem(z + d, NZ)
            out[dx] = (keep[at] + got[at].astype(F32)).astype(BF)


def pair_sums(pos, keep, got):
    shape = (NX, *keep.shape[1:])
    low = jax.ShapeDtypeStruct(shape, BF)
    return pl.pallas_call(
        pair_kernel,
        out_shape=(jax.ShapeDtypeStruct(shape, F32), low, low, low),
        in_specs=[SMEM, VMEM, VMEM],
        out_specs=(VMEM,) * 4,
        compiler_params=params(16),
        cost_estimate=cost(1 << 20, 5 << 20),
    )(pos, keep, got)


def quarter_kernel(pos, own, one, two, three, *refs):
    stream, out = refs[:NX], refs[NX]
    wide = 2 * LANES
    y = pos[1]
    for dx in range(NX):
        for dy in range(NY):
            lanes = slice(dy * wide, (dy + 1) * wide)
            at = pl.multiple_of(lax.rem(y + dy, NY) * wide, wide)
            total = (
                own[dx, :, lanes]
                + one[dx, :, lanes].astype(F32)
                + two[dx, :, lanes].astype(F32)
                + three[dx, :, lanes].astype(F32)
                + stream[dx][:, pl.ds(at, wide)].astype(F32)
            )
            out[dx, :, pl.ds(at, wide)] = total.astype(BF)


def quarter(pos, own, parts, stream):
    return pl.pallas_call(
        quarter_kernel,
        out_shape=jax.ShapeDtypeStruct(own.shape, BF),
        in_specs=[SMEM] + [VMEM] * (NZ + NX),
        out_specs=VMEM,
        compiler_params=params(16),
        cost_estimate=cost(1 << 20, 3 << 20),
    )(pos, own, *parts, *stream)


def norm_kernel(pos, *refs):
    quarters, gain, normed, res = refs[:NX], refs[NX], refs[NX + 1], refs[NX + 2]
    tok, wide = quarters[0].shape[1:]
    x = pos[0]
    at = [pl.multiple_of(lax.rem(x + d, NX) * wide, wide) for d in range(NX)]
    for b in range(NX):
        values = [quarters[d][(b - d) % NX].astype(F32) for d in range(NX)]
        squares = values[0] * values[0]
        for value in values[1:]:
            squares += value * value
        factor = lax.rsqrt(jnp.sum(squares, axis=1, keepdims=True) * (1.0 / D) + 1e-06)
        for d in range(NX):
            lanes = pl.ds(at[d], wide)
            normed[b * tok : (b + 1) * tok, lanes] = (values[d] * factor * gain[:, lanes]).astype(BF)
            if b == 0:
                res[:, lanes] = values[d].astype(BF)


def norm(pos, quarters, gain):
    tok = quarters[0].shape[1]
    return pl.pallas_call(
        norm_kernel,
        out_shape=(jax.ShapeDtypeStruct((NX * tok, D), BF), jax.ShapeDtypeStruct((tok, D), BF)),
        in_specs=[SMEM] + [VMEM] * (NX + 1),
        out_specs=(VMEM, VMEM),
        compiler_params=params(16),
        cost_estimate=cost(1 << 21, 3 << 20),
    )(pos, *quarters, gain)


def place_kernel(where, own, other, message):
    tokens = own.shape[0]
    for j in range(0, D, OUT):
        lanes = slice(j, j + OUT)
        total = jnp.dot(where[:, :tokens], own[:, lanes], preferred_element_type=F32)
        total += jnp.dot(where[:, tokens:], other[:, lanes], preferred_element_type=F32)
        message[:, lanes] = total.astype(BF)


def place(where, own, other):
    return pl.pallas_call(
        place_kernel,
        out_shape=jax.ShapeDtypeStruct((where.shape[0], D), BF),
        in_specs=[VMEM] * 3,
        out_specs=VMEM,
        compiler_params=params(16),
        cost_estimate=cost(2 * where.shape[0] * where.shape[1] * D, 5 << 20),
    )(where, own, other)


def expert_kernel(scale, rows, gate, up, down, out, x, wg, wu, wd, gates, ups, act, part, done, in_sem, down_sem, out_sem):
    depth, hidden = wg.shape
    groups = OUT // LANES
    loads, downs, stores = [], [], []
    for i, j in enumerate(range(0, depth, DEEP)):
        at = pl.ds(j, DEEP)
        for k, (source, into) in enumerate(((rows, x), (gate, wg), (up, wu))):
            view = (source.at[:, at], into.at[:, at]) if k == 0 else (source.at[at], into.at[at])
            loads.append(pltpu.make_async_copy(*view, in_sem.at[3 * i + k]))
            loads[-1].start()
    for i, j in enumerate(range(0, depth, OUT)):
        at = pl.ds(j, OUT)
        downs.append(pltpu.make_async_copy(down.at[:, at], wd.at[:, at], down_sem.at[i]))
        downs[-1].start()
    for i, j in enumerate(range(0, depth, DEEP)):
        for load in loads[3 * i : 3 * i + 3]:
            load.wait()
        cut = x[:, j : j + DEEP]
        gate_part = jnp.dot(cut, wg[j : j + DEEP], preferred_element_type=F32)
        up_part = jnp.dot(cut, wu[j : j + DEEP], preferred_element_type=F32)
        if i == 0:
            gates[...] = gate_part
            ups[...] = up_part
        else:
            gates[...] += gate_part
            ups[...] += up_part
    gate_part = gates[...] * scale[0, 0]
    act[...] = (gate_part / (1.0 + jnp.exp(-gate_part)) * (ups[...] * scale[0, 1])).astype(BF)
    for i, j in enumerate(range(0, depth, OUT)):
        downs[i].wait()
        total = jnp.dot(act[...], wd[:, j : j + OUT], preferred_element_type=F32) * scale[0, 2]
        for g in range(groups):
            part[:, g, :] = total[:, g * LANES : (g + 1) * LANES]
        at = pl.ds(i * groups, groups)
        done[:, i * groups : (i + 1) * groups, :] = part[...].astype(BF)
        stores.append(pltpu.make_async_copy(done.at[:, at, :], out.at[:, at, :], out_sem.at[i]))
        stores[-1].start()
    for store in stores:
        store.wait()


def run_expert(scale, rows, gate, up, down):
    count, depth = rows.shape
    hidden = gate.shape[1]
    anywhere = pl.BlockSpec(memory_space=pl.ANY)
    return pl.pallas_call(
        expert_kernel,
        out_shape=jax.ShapeDtypeStruct((count, BLOCKS, LANES), BF),
        in_specs=[SMEM] + [anywhere] * 4,
        out_specs=anywhere,
        scratch_shapes=[
            pltpu.VMEM((count, depth), BF),
            pltpu.VMEM((depth, hidden), BF),
            pltpu.VMEM((depth, hidden), BF),
            pltpu.VMEM((hidden, depth), BF),
            pltpu.VMEM((count, hidden), F32),
            pltpu.VMEM((count, hidden), F32),
            pltpu.VMEM((count, hidden), BF),
            pltpu.VMEM((count, OUT // LANES, LANES), F32),
            pltpu.VMEM((count, BLOCKS, LANES), BF),
            pltpu.SemaphoreType.DMA((3 * depth // DEEP,)),
            pltpu.SemaphoreType.DMA((depth // OUT,)),
            pltpu.SemaphoreType.DMA((depth // OUT,)),
        ],
        compiler_params=params(58),
        cost_estimate=cost(6 * count * depth * hidden, 6 * depth * hidden),
    )(scale, rows, gate, up, down)


def mix_kernel(target, gates, results, res, out, mixed):
    tok = res.shape[0]

    def one_token(t, carry):
        add = gates[t, 0] * results[target[t, 0]].astype(F32)
        for k in range(1, TOPK):
            add += gates[t, k] * results[target[t, k]].astype(F32)
        mixed[t] = add
        return carry

    lax.fori_loop(0, tok, one_token, 0)
    for block in range(BLOCKS):
        lanes = slice(block * LANES, (block + 1) * LANES)
        out[:, lanes] = (res[:, lanes].astype(F32) + mixed[:, block, :]).astype(BF)


def mix(target, gates, results, res):
    tok = res.shape[0]
    return pl.pallas_call(
        mix_kernel,
        out_shape=jax.ShapeDtypeStruct((tok, D), BF),
        in_specs=[SMEM, SMEM, VMEM, VMEM],
        out_specs=VMEM,
        scratch_shapes=[pltpu.VMEM((tok, BLOCKS, LANES), F32)],
        compiler_params=params(16),
        cost_estimate=cost(1 << 20, 4 << 20),
    )(target, gates, results, res)


def body(
    query,
    key,
    value,
    head_gain,
    out_weight,
    stream,
    model_gain,
    expert_ids,
    expert_gates,
    gate_weight,
    up_weight,
    down_weight,
    weight_scales,
):
    x, y, z, c = [lax.axis_index(axis) for axis in AXES]
    pos = jnp.stack([x, y, z, c]).astype(jnp.int32)
    seq_rows = query.shape[0]
    tok_rows = stream.shape[0]
    heads_local = head_gain.shape[0] // HD
    experts = NX * NY * NZ * NC
    slots = experts * CAP

    query_rows = query.reshape(seq_rows, heads_local, HD)
    key_rows = key.reshape(seq_rows, heads_local, HD)
    value_rows = value.reshape(seq_rows, heads_local, HD)
    block_state = jnp.einsum("shd,she->hde", key_rows, value_rows, preferred_element_type=F32)
    low = block_state.astype(BF)
    line, before = block_state, jnp.zeros_like(block_state)
    for d in range(1, NY):
        got = shift(low, "y", d).astype(F32)
        line = line + got
        before = before + jnp.where(y >= d, got, 0.0)
    low = line.astype(BF)
    totals = [shift(low, "x", d) for d in range(1, NX)]
    weights = gather_line(out_weight, "y")

    scores = jnp.einsum("thd,shd->hts", query_rows, key_rows, preferred_element_type=F32)
    causal = jnp.tril(jnp.ones((seq_rows, seq_rows), dtype=bool))
    scores = jnp.where(causal[None, :, :], scores, 0.0).astype(BF)
    local_part = jnp.einsum("hts,shd->thd", scores, value_rows, preferred_element_type=F32)
    local_part = local_part.reshape(seq_rows, heads_local * HD)
    head_normed = mixed_heads(pos, query, before, totals, local_part, head_gain[None])

    flat_ids = expert_ids.reshape(-1)
    at = jnp.arange(flat_ids.shape[0], dtype=jnp.int32)
    same = (flat_ids[:, None] == flat_ids[None, :]) & (at[None, :] < at[:, None])
    slot_index = jnp.sum(same.astype(jnp.int32), axis=1)
    target = (flat_ids * CAP + slot_index).reshape(tok_rows, TOPK)

    head_normed, weights = lax.optimization_barrier((head_normed, weights))
    tokens = gather_line(head_normed, "x")
    keep, give = project(pos, tokens, weights, tok_rows)
    own, *low = pair_sums(pos, keep, shift(give, "c", 1))
    parts = [shift(low[d - 1], "z", d) for d in range(1, NZ)]
    own, target, stream = lax.optimization_barrier((own, target, stream))
    line_target = jnp.concatenate(gather_line(target.T, "x"), axis=1)
    line_target = jnp.concatenate([line_target, shift(line_target, "c", 1)], axis=1)
    token = jnp.arange(NC * NX * tok_rows, dtype=jnp.int32)
    piece = token // tok_rows
    token_block = (c + piece // NX) % NC * NX + (x + piece % NX) % NX
    row = jnp.arange(slots, dtype=jnp.int32)
    plane = row // (NC * NX * CAP)
    row_block = row // CAP % (NC * NX)
    wanted = ((x * NY * NZ + plane) * NC + c) * CAP + row % CAP
    where = jnp.any(line_target[:, None, :] == wanted[None, :, None], axis=0)
    where = (where & (token_block[None, :] == row_block[:, None])).astype(BF)
    back = target // CAP
    back = (back % (NY * NZ * NC) * NX + back // (NY * NZ * NC)) * CAP + target % CAP

    wide = D // NX
    stream_parts = [
        lax.dynamic_slice_in_dim(stream, (x + NX - d) % NX * wide, wide, axis=1) for d in range(NX)
    ]
    stream_parts = stream_parts[:1] + [shift(stream_parts[d], "x", NX - d) for d in range(1, NX)]

    residual = quarter(pos, own, parts, stream_parts)
    quarters = gather_line(residual, "x")
    quarters, where, back = lax.optimization_barrier((quarters, where, back))
    normed, res = norm(pos, quarters, model_gain[None])
    message = place(where, normed, shift(normed, "c", 1))
    slot_rows = lax.all_to_all(
        message.reshape(NY * NZ, -1, D), ("y", "z"), split_axis=0, concat_axis=0, tiled=True
    ).reshape(slots, D)
    produced = run_expert(weight_scales, slot_rows, gate_weight[0], up_weight[0], down_weight[0])
    results = lax.all_to_all(
        produced.reshape(experts, CAP * BLOCKS, LANES), ("y", "z", "c", "x"), split_axis=0, concat_axis=0, tiled=True
    )
    return mix(back, expert_gates, results.reshape(slots, BLOCKS, LANES), res)


def solution(mesh):
    chips = jax.sharding.Mesh(mesh.devices.reshape(NX, NY, NZ, NC), AXES)
    seq, head = AXES[:2], AXES[2:]
    token = P(AXES, None)
    expert = P(AXES, None, None)
    return jax.shard_map(
        body,
        mesh=chips,
        in_specs=(
            P(seq, head),
            P(seq, head),
            P(seq, head),
            P(head),
            P(head, seq),
            token,
            P(),
            token,
            token,
            expert,
            expert,
            expert,
            token,
        ),
        out_specs=token,
        check_vma=False,
    )
```

time: 205 us -> 213 us (1.039)
  waiting for transfers between devices: 74.4 us -> 90.4 us
  starting transfers between devices: 31.8 us -> 41.2 us
  blocking collectives: 52.6 us -> 43.3 us
  local copies, waits for them, and re-layouts: 14.6 us -> 7.65 us
    ppermute x19 -> x27, waiting for transfers between devices: 32.5 us -> 48.1 us  [shift(): return lax.ppermute(a, axis, [(i, (i + d) % n) for i in range(n)])]
    another operation x2 -> x0, local copies, waits for them, and re-layouts: 9.25 us -> none  [the longest x1 5.89 us: exchange(): message = rows.reshape(experts, CAP * BLOCKS, LANES)]
    all_to_all x1, blocking collectives: 52.6 us -> 43.3 us  [body(): lax.all_to_all(message.reshape(NY * NZ, -1, D), ('y', 'z'), split_axis=0,...]
    ppermute x19 -> x27, starting transfers between devices: 27.2 us -> 35.6 us  [shift(): return lax.ppermute(a, axis, [(i, (i + d) % n) for i in range(n)])]
    unnamed x24 -> x32, local copies, waits for them, and re-layouts: 3.77 us -> 5.79 us
    pallas_call x2 -> x4, Pallas kernels: 18.8 us -> 19.8 us  [the longest x1 16.3 us: run_expert(): pl.pallas_call(expert_kernel, out_shape=jax.ShapeDtypeStruct((count, BLOC...]
  transfers between devices with their start and end apart: 20 -> 28, of which waited for: 14 -> 15; matrix products, arithmetic and copies ran while one was open for 1% -> 2% of each run, Pallas kernels for 0% -> 0%
where the time goes in v5:
time: 213 us
  waiting for transfers between devices  90.4 us (42%)
  blocking collectives  43.3 us (20%)
  starting transfers between devices  41.2 us (19%)
  Pallas kernels  27.2 us (13%)
  local copies, waits for them, and re-layouts  7.65 us (4%)
    ppermute x27, waiting for transfers between devices, shift(): return lax.ppermute(a, axis, [(i, (i + d) % n) for i in range(n)])  48.1 us
    all_to_all x1, blocking collectives, body(): lax.all_to_all(message.reshape(NY * NZ, -1, D), ('y', 'z'), split_axis=0,...  43.3 us
    all_to_all x1, waiting for transfers between devices, body(): lax.all_to_all(produced.reshape(experts, CAP * BLOCKS, LANES), ('y', 'z',...  42.3 us
    ppermute x27, starting transfers between devices, shift(): return lax.ppermute(a, axis, [(i, (i + d) % n) for i in range(n)])  35.6 us
    pallas_call x1, Pallas kernels, run_expert(): pl.pallas_call(expert_kernel, out_shape=jax.ShapeDtypeStruct((count, BLOC...  16.3 us
    unnamed x32, local copies, waits for them, and re-layouts  5.79 us
    all_to_all x1, starting transfers between devices, body(): lax.all_to_all(produced.reshape(experts, CAP * BLOCKS, LANES), ('y', 'z',...  5.57 us
  transfers between devices with their start and end apart: 28, of which 15 were waited for; matrix products, arithmetic and copies ran while one was open for 2% of the time, Pallas kernels for 0%

profile of v5, /device:TPU:1, one launch (start us, length us, event | category | flops | bytes accessed | tf_op | source)
XLA Modules:
  0.0 212.8 jit_solution(3019946447473556066)
XLA Ops:
  1.5 2.2 %collective-permute-start = (bf16[4,128,128]{2,1,0:T(8,128)(2,1)S(1)}, bf16[4,128,128]{2,1,0:T(8,128)(2,1)S(1)}, u32[]{:S(2)}, u32[]{:S(2)}) collective-permute-start(bf16[4,128,128]{2,1,0:T(8,128)(2,1)S(1)} %get-tuple-element.55), channel_id=1, source_target_pairs={{0,8},{8,16},{16,24},{24,0},{1,9},{9,17},{17,25},{25,1},{2,10},{10... | collective-permute-start | bytes 393224 | tf_op jit(solution)/shard_map/ppermute | solution.py:36
  3.7 2.6 %collective-permute-start.1 = (bf16[4,128,128]{2,1,0:T(8,128)(2,1)S(1)}, bf16[4,128,128]{2,1,0:T(8,128)(2,1)S(1)}, u32[]{:S(2)}, u32[]{:S(2)}) collective-permute-start(bf16[4,128,128]{2,1,0:T(8,128)(2,1)S(1)} %get-tuple-element.55), channel_id=1, source_target_pairs={{0,16},{8,24},{16,0},{24,8},{1,17},{9,25},{17,1},{25,9},{2,18},{10... | collective-permute-start | bytes 393224 | tf_op jit(solution)/shard_map/ppermute | solution.py:36
  8.2 3.8 %collective-permute-done.1 = bf16[4,128,128]{2,1,0:T(8,128)(2,1)S(1)} collective-permute-done((bf16[4,128,128]{2,1,0:T(8,128)(2,1)S(1)}, bf16[4,128,128]{2,1,0:T(8,128)(2,1)S(1)}, u32[]{:S(2)}, u32[]{:S(2)}) %collective-permute-start.1) | collective-permute-done | bytes 131104 | tf_op jit(solution)/shard_map/ppermute | solution.py:36
  13.4 2.1 %collective-permute-start.6 = (bf16[512,256]{1,0:T(8,128)(2,1)}, bf16[512,256]{1,0:T(8,128)(2,1)S(1)}, u32[]{:S(2)}, u32[]{:S(2)}) collective-permute-start(bf16[512,256]{1,0:T(8,128)(2,1)} %refs_4_), channel_id=1, source_target_pairs={{0,24},{8,0},{16,8},{24,16},{1,25},{9,1},{17,9},{25,17},{2,26},{10... | collective-permute-start | bytes 786440 | tf_op jit(solution)/shard_map/ppermute | solution.py:36
  16.2 2.5 %collective-permute-start.4 = (bf16[4,128,128]{2,1,0:T(8,128)(2,1)S(1)}, bf16[4,128,128]{2,1,0:T(8,128)(2,1)S(1)}, u32[]{:S(2)}, u32[]{:S(2)}) collective-permute-start(bf16[4,128,128]{2,1,0:T(8,128)(2,1)S(1)} %get-tuple-element.49), channel_id=1, source_target_pairs={{0,64},{32,96},{64,0},{96,32},{1,65},{33,97},{65,1},{97,33},{2,66}... | collective-permute-start | bytes 393224 | tf_op jit(solution)/shard_map/ppermute | solution.py:36
  23.9 7.2 %collective-permute-done.8.refs_7_ = bf16[512,256]{1,0:T(8,128)(2,1)S(1)} collective-permute-done((bf16[512,256]{1,0:T(8,128)(2,1)}, bf16[512,256]{1,0:T(8,128)(2,1)S(1)}, u32[]{:S(2)}, u32[]{:S(2)}) %collective-permute-start.8) | collective-permute-done | bytes 262176 | tf_op jit(solution)/shard_map/ppermute | solution.py:36
  31.1 2.5 %collective-permute-start.10 = (bf16[256,512]{1,0:T(8,128)(2,1)S(1)}, bf16[256,512]{1,0:T(8,128)(2,1)S(1)}, u32[]{:S(2)}, u32[]{:S(2)}) collective-permute-start(bf16[256,512]{1,0:T(8,128)(2,1)S(1)} %shard_map.127.refs_0_), channel_id=1, source_target_pairs={{0,64},{32,96},{64,0},{96,32},{1,65},{33,97},{65,1},{97,33},{2,66}... | collective-permute-start | bytes 786440 | tf_op jit(solution)/shard_map/ppermute | solution.py:36
  33.5 2.7 %collective-permute-start.9 = (bf16[256,512]{1,0:T(8,128)(2,1)S(1)}, bf16[256,512]{1,0:T(8,128)(2,1)S(1)}, u32[]{:S(2)}, u32[]{:S(2)}) collective-permute-start(bf16[256,512]{1,0:T(8,128)(2,1)S(1)} %shard_map.127.refs_0_), channel_id=1, source_target_pairs={{0,96},{32,0},{64,32},{96,64},{1,97},{33,1},{65,33},{97,65},{2,98}... | collective-permute-start | bytes 786440 | tf_op jit(solution)/shard_map/ppermute | solution.py:36
  36.2 3.8 %collective-permute-done.10.refs_2_ = bf16[256,512]{1,0:T(8,128)(2,1)S(1)} collective-permute-done((bf16[256,512]{1,0:T(8,128)(2,1)S(1)}, bf16[256,512]{1,0:T(8,128)(2,1)S(1)}, u32[]{:S(2)}, u32[]{:S(2)}) %collective-permute-start.10) | collective-permute-done | bytes 262176 | tf_op jit(solution)/shard_map/ppermute | solution.py:36
  40.0 6.4 %collective-permute-done.11.refs_3_ = bf16[256,512]{1,0:T(8,128)(2,1)S(1)} collective-permute-done((bf16[256,512]{1,0:T(8,128)(2,1)S(1)}, bf16[256,512]{1,0:T(8,128)(2,1)S(1)}, u32[]{:S(2)}, u32[]{:S(2)}) %collective-permute-start.11) | collective-permute-done | bytes 262176 | tf_op jit(solution)/shard_map/ppermute | solution.py:36
  46.4 2.9 %shard_map.128 = (f32[16,32,1024]{2,1,0:T(8,128)S(1)}, bf16[16,32,1024]{2,1,0:T(8,128)(2,1)}) custom-call(s32[4]{0:T(128)S(1)} %pad_add_fusion.1.pos, bf16[256,512]{1,0:T(8,128)(2,1)S(1)} %shard_map.127.refs_0_, bf16[256,512]{1,0:T(8,128)(2,1)S(1)} %collective-permute-done.9.refs_1_, bf16[256,512]{1,0:T(8,128)(2,1)S(1)} %collective-permute-done.10.refs_2_, ...), custom_call_target="tpu_custom_call" | custom-call | flops 1073741824 | bytes 5242880 | tf_op jit(solution)/shard_map/pallas_call | solution.py:87
  50.3 2.0 collective-permute-done.12.got
  59.1 2.7 %collective-permute-start.16 = (bf16[32,1024]{1,0:T(8,128)(2,1)S(1)}, bf16[32,1024]{1,0:T(8,128)(2,1)S(1)}, u32[]{:S(2)}, u32[]{:S(2)}) collective-permute-start(bf16[32,1024]{1,0:T(8,128)(2,1)S(1)} %get-tuple-element.53), channel_id=1, source_target_pairs={{0,96},{32,0},{64,32},{96,64},{1,97},{33,1},{65,33},{97,65},{2,98}... | collective-permute-start | bytes 196616 | tf_op jit(solution)/shard_map/ppermute | solution.py:36
  63.4 3.3 %collective-permute-start.14 = (bf16[4,32,1024]{2,1,0:T(8,128)(2,1)}, bf16[4,32,1024]{2,1,0:T(8,128)(2,1)S(1)}, u32[]{:S(2)}, u32[]{:S(2)}) collective-permute-start(bf16[4,32,1024]{2,1,0:T(8,128)(2,1)} %copy-done.10), channel_id=1, source_target_pairs={{0,4},{2,6},{4,0},{6,2},{1,5},{3,7},{5,1},{7,3},{8,12},{10,14},{12... | collective-permute-start | bytes 786440 | tf_op jit(solution)/shard_map/ppermute | solution.py:36
  67.7 2.4 %collective-permute-start.25 = (s32[8,128]{1,0:T(8,128)S(1)}, s32[8,128]{1,0:T(8,128)S(1)}, u32[]{:S(2)}, u32[]{:S(2)}) collective-permute-start(s32[8,128]{1,0:T(8,128)S(1)} %pad_add_fusion), channel_id=1, source_target_pairs={{0,1},{1,0},{2,3},{3,2},{4,5},{5,4},{6,7},{7,6},{8,9},{9,8},{10,11... | collective-permute-start | bytes 12296 | tf_op jit(solution)/shard_map/ppermute | solution.py:36
  71.4 4.4 %collective-permute-done.17.refs_2_ = bf16[32,1024]{1,0:T(8,128)(2,1)S(1)} collective-permute-done((bf16[32,1024]{1,0:T(8,128)(2,1)S(1)}, bf16[32,1024]{1,0:T(8,128)(2,1)S(1)}, u32[]{:S(2)}, u32[]{:S(2)}) %collective-permute-start.17) | collective-permute-done | bytes 65568 | tf_op jit(solution)/shard_map/ppermute | solution.py:36
  81.5 3.6 %collective-permute-done.19.refs_1_ = bf16[4,32,1024]{2,1,0:T(8,128)(2,1)S(1)} collective-permute-done((bf16[4,32,1024]{2,1,0:T(8,128)(2,1)S(1)}, bf16[4,32,1024]{2,1,0:T(8,128)(2,1)S(1)}, u32[]{:S(2)}, u32[]{:S(2)}) %collective-permute-start.19) | collective-permute-done | bytes 262176 | tf_op jit(solution)/shard_map/ppermute | solution.py:36
  87.0 8.0 %collective-permute-done.21.refs_3_ = bf16[4,32,1024]{2,1,0:T(8,128)(2,1)S(1)} collective-permute-done((bf16[4,32,1024]{2,1,0:T(8,128)(2,1)S(1)}, bf16[4,32,1024]{2,1,0:T(8,128)(2,1)S(1)}, u32[]{:S(2)}, u32[]{:S(2)}) %collective-permute-start.21) | collective-permute-done | bytes 262176 | tf_op jit(solution)/shard_map/ppermute | solution.py:36
  97.3 2.3 %collective-permute-done.26.other = bf16[128,4096]{1,0:T(8,128)(2,1)S(1)} collective-permute-done((bf16[128,4096]{1,0:T(8,128)(2,1)S(1)}, bf16[128,4096]{1,0:T(8,128)(2,1)S(1)}, u32[]{:S(2)}, u32[]{:S(2)}) %collective-permute-start.26) | collective-permute-done | bytes 1048608 | tf_op jit(solution)/shard_map/ppermute | solution.py:36
  101.4 43.3 %all_to_all.10 = bf16[16,24,4096]{2,1,0:T(8,128)(2,1)} all-to-all(bf16[16,24,4096]{2,1,0:T(8,128)(2,1)S(1)} %bitcast.46), channel_id=1, replica_groups=mesh['x'=4,'y'=4,'z'=4,'c'=2] {'y','z'}, dimensions={0} | all-to-all | bytes 6291456 | tf_op jit(solution)/shard_map/all_to_all | solution.py:379
  144.7 16.3 %shard_map.133 = bf16[384,32,128]{2,1,0:T(8,128)(2,1)} custom-call(f32[1,3]{1,0:T(1,128)} %scale.1, bf16[384,4096]{1,0:T(8,128)(2,1)} %bitcast.50, bf16[4096,768]{1,0:T(8,128)(2,1)} %bitcast.58, bf16[4096,768]{1,0:T(8,128)(2,1)} %bitcast.59, bf16[768,4096]{1,0:T(8,128)(2,1)} %bitcast.60), custom_call_target="tpu_custom_call" | custom-call | flops 7247757312 | bytes 18874368 | tf_op jit(solution)/shard_map/pallas_call | solution.py:245
  161.1 5.6 %all-to-all-start.1 = ((bf16[128,96,128]{2,1,0:T(8,128)(2,1)}), bf16[128,96,128]{2,1,0:T(8,128)(2,1)S(1)}, u32[]{:S(2)}, u32[]{:S(2)}) async-start(bf16[128,96,128]{2,1,0:T(8,128)(2,1)} %bitcast.49), calls=%async_computation.1 | async-start | bytes 6291456 | tf_op jit(solution)/shard_map/all_to_all | solution.py:383
  166.7 42.3 %all-to-all-done.1 = bf16[128,96,128]{2,1,0:T(8,128)(2,1)S(1)} async-done(((bf16[128,96,128]{2,1,0:T(8,128)(2,1)}), bf16[128,96,128]{2,1,0:T(8,128)(2,1)S(1)}, u32[]{:S(2)}, u32[]{:S(2)}) %all-to-all-start.1) | async-done | bytes 3145760 | tf_op jit(solution)/shard_map/all_to_all | solution.py:383
  209.9 2.9 %shard_map.134 = bf16[32,4096]{1,0:T(8,128)(2,1)} custom-call(s32[32,8]{1,0:T(8,128)S(1)} %fusion.22.target, f32[32,8]{1,0:T(8,128)S(1)} %copy.62.gates, bf16[384,32,128]{2,1,0:T(8,128)(2,1)S(1)} %bitcast.45, bf16[32,4096]{1,0:T(8,128)(2,1)S(1)} %copy-done.4), custom_call_target="tpu_custom_call" | custom-call | flops 1048576 | bytes 4194304 | tf_op jit(solution)/shard_map/pallas_call | solution.py:287
  (97 shorter events, 34.8 us)
Async XLA Ops:
  1.5 6.7 %collective-permute-start = (bf16[4,128,128]{2,1,0:T(8,128)(2,1)S(1)}, bf16[4,128,128]{2,1,0:T(8,128)(2,1)S(1)}, u32[]{:S(2)}, u32[]{:S(2)}) collective-permute-start(bf16[4,128,128]{2,1,0:T(8,128)(2,1)S(1)} %get-tuple-element.55), channel_id=1, source_target_pairs={{0,8},{8,16},{16,24},{24,0},{1,9},{9,17},{17,25},{25,1},{2,10},{10... | collective-permute-start | bytes 393224 | tf_op jit(solution)/shard_map/ppermute | solution.py:36
  3.7 8.3 %collective-permute-start.1 = (bf16[4,128,128]{2,1,0:T(8,128)(2,1)S(1)}, bf16[4,128,128]{2,1,0:T(8,128)(2,1)S(1)}, u32[]{:S(2)}, u32[]{:S(2)}) collective-permute-start(bf16[4,128,128]{2,1,0:T(8,128)(2,1)S(1)} %get-tuple-element.55), channel_id=1, source_target_pairs={{0,16},{8,24},{16,0},{24,8},{1,17},{9,25},{17,1},{25,9},{2,18},{10... | collective-permute-start | bytes 393224 | tf_op jit(solution)/shard_map/ppermute | solution.py:36
  6.3 5.7 %collective-permute-start.2 = (bf16[4,128,128]{2,1,0:T(8,128)(2,1)S(1)}, bf16[4,128,128]{2,1,0:T(8,128)(2,1)S(1)}, u32[]{:S(2)}, u32[]{:S(2)}) collective-permute-start(bf16[4,128,128]{2,1,0:T(8,128)(2,1)S(1)} %get-tuple-element.55), channel_id=1, source_target_pairs={{0,24},{8,0},{16,8},{24,16},{1,25},{9,1},{17,9},{25,17},{2,26},{10... | collective-permute-start | bytes 393224 | tf_op jit(solution)/shard_map/ppermute | solution.py:36
  12.1 6.7 %collective-permute-start.3 = (bf16[4,128,128]{2,1,0:T(8,128)(2,1)S(1)}, bf16[4,128,128]{2,1,0:T(8,128)(2,1)S(1)}, u32[]{:S(2)}, u32[]{:S(2)}) collective-permute-start(bf16[4,128,128]{2,1,0:T(8,128)(2,1)S(1)} %get-tuple-element.49), channel_id=1, source_target_pairs={{0,32},{32,64},{64,96},{96,0},{1,33},{33,65},{65,97},{97,1},{2,34}... | collective-permute-start | bytes 393224 | tf_op jit(solution)/shard_map/ppermute | solution.py:36
  13.4 10.5 %collective-permute-start.6 = (bf16[512,256]{1,0:T(8,128)(2,1)}, bf16[512,256]{1,0:T(8,128)(2,1)S(1)}, u32[]{:S(2)}, u32[]{:S(2)}) collective-permute-start(bf16[512,256]{1,0:T(8,128)(2,1)} %refs_4_), channel_id=1, source_target_pairs={{0,24},{8,0},{16,8},{24,16},{1,25},{9,1},{17,9},{25,17},{2,26},{10... | collective-permute-start | bytes 786440 | tf_op jit(solution)/shard_map/ppermute | solution.py:36
  15.5 8.3 %collective-permute-start.7 = (bf16[512,256]{1,0:T(8,128)(2,1)}, bf16[512,256]{1,0:T(8,128)(2,1)S(1)}, u32[]{:S(2)}, u32[]{:S(2)}) collective-permute-start(bf16[512,256]{1,0:T(8,128)(2,1)} %refs_4_), channel_id=1, source_target_pairs={{0,16},{8,24},{16,0},{24,8},{1,17},{9,25},{17,1},{25,9},{2,18},{10... | collective-permute-start | bytes 786440 | tf_op jit(solution)/shard_map/ppermute | solution.py:36
  16.2 14.9 %collective-permute-start.8 = (bf16[512,256]{1,0:T(8,128)(2,1)}, bf16[512,256]{1,0:T(8,128)(2,1)S(1)}, u32[]{:S(2)}, u32[]{:S(2)}) collective-permute-start(bf16[512,256]{1,0:T(8,128)(2,1)} %refs_4_), channel_id=1, source_target_pairs={{0,8},{8,16},{16,24},{24,0},{1,9},{9,17},{17,25},{25,1},{2,10},{10... | collective-permute-start | bytes 786440 | tf_op jit(solution)/shard_map/ppermute | solution.py:36
  16.2 5.4 %collective-permute-start.4 = (bf16[4,128,128]{2,1,0:T(8,128)(2,1)S(1)}, bf16[4,128,128]{2,1,0:T(8,128)(2,1)S(1)}, u32[]{:S(2)}, u32[]{:S(2)}) collective-permute-start(bf16[4,128,128]{2,1,0:T(8,128)(2,1)S(1)} %get-tuple-element.49), channel_id=1, source_target_pairs={{0,64},{32,96},{64,0},{96,32},{1,65},{33,97},{65,1},{97,33},{2,66}... | collective-permute-start | bytes 393224 | tf_op jit(solution)/shard_map/ppermute | solution.py:36
  31.1 8.9 %collective-permute-start.10 = (bf16[256,512]{1,0:T(8,128)(2,1)S(1)}, bf16[256,512]{1,0:T(8,128)(2,1)S(1)}, u32[]{:S(2)}, u32[]{:S(2)}) collective-permute-start(bf16[256,512]{1,0:T(8,128)(2,1)S(1)} %shard_map.127.refs_0_), channel_id=1, source_target_pairs={{0,64},{32,96},{64,0},{96,32},{1,65},{33,97},{65,1},{97,33},{2,66}... | collective-permute-start | bytes 786440 | tf_op jit(solution)/shard_map/ppermute | solution.py:36
  33.5 12.9 %collective-permute-start.11 = (bf16[256,512]{1,0:T(8,128)(2,1)S(1)}, bf16[256,512]{1,0:T(8,128)(2,1)S(1)}, u32[]{:S(2)}, u32[]{:S(2)}) collective-permute-start(bf16[256,512]{1,0:T(8,128)(2,1)S(1)} %shard_map.127.refs_0_), channel_id=1, source_target_pairs={{0,32},{32,64},{64,96},{96,0},{1,33},{33,65},{65,97},{97,1},{2,34}... | collective-permute-start | bytes 786440 | tf_op jit(solution)/shard_map/ppermute | solution.py:36
  33.5 12.9 %collective-permute-start.9 = (bf16[256,512]{1,0:T(8,128)(2,1)S(1)}, bf16[256,512]{1,0:T(8,128)(2,1)S(1)}, u32[]{:S(2)}, u32[]{:S(2)}) collective-permute-start(bf16[256,512]{1,0:T(8,128)(2,1)S(1)} %shard_map.127.refs_0_), channel_id=1, source_target_pairs={{0,96},{32,0},{64,32},{96,64},{1,97},{33,1},{65,33},{97,65},{2,98}... | collective-permute-start | bytes 786440 | tf_op jit(solution)/shard_map/ppermute | solution.py:36
  56.0 7.4 %collective-permute-start.22 = (s32[8,32]{0,1:T(8,128)S(1)}, s32[8,32]{0,1:T(8,128)S(1)}, u32[]{:S(2)}, u32[]{:S(2)}) collective-permute-start(s32[8,32]{0,1:T(8,128)S(1)} %bitcast.54), channel_id=1, source_target_pairs={{0,96},{32,0},{64,32},{96,64},{1,97},{33,1},{65,33},{97,65},{2,98}... | collective-permute-start | bytes 3080 | tf_op jit(solution)/shard_map/ppermute | solution.py:36
  57.4 9.3 %collective-permute-start.23 = (s32[8,32]{0,1:T(8,128)S(1)}, s32[8,32]{0,1:T(8,128)S(1)}, u32[]{:S(2)}, u32[]{:S(2)}) collective-permute-start(s32[8,32]{0,1:T(8,128)S(1)} %bitcast.55), channel_id=1, source_target_pairs={{0,64},{32,96},{64,0},{96,32},{1,65},{33,97},{65,1},{97,33},{2,66}... | collective-permute-start | bytes 3080 | tf_op jit(solution)/shard_map/ppermute | solution.py:36
  59.0 8.6 %collective-permute-start.24 = (s32[8,32]{0,1:T(8,128)S(1)}, s32[8,32]{0,1:T(8,128)S(1)}, u32[]{:S(2)}, u32[]{:S(2)}) collective-permute-start(s32[8,32]{0,1:T(8,128)S(1)} %bitcast.56), channel_id=1, source_target_pairs={{0,32},{32,64},{64,96},{96,0},{1,33},{33,65},{65,97},{97,1},{2,34}... | collective-permute-start | bytes 3080 | tf_op jit(solution)/shard_map/ppermute | solution.py:36
  59.1 12.1 %collective-permute-start.16 = (bf16[32,1024]{1,0:T(8,128)(2,1)S(1)}, bf16[32,1024]{1,0:T(8,128)(2,1)S(1)}, u32[]{:S(2)}, u32[]{:S(2)}) collective-permute-start(bf16[32,1024]{1,0:T(8,128)(2,1)S(1)} %get-tuple-element.53), channel_id=1, source_target_pairs={{0,96},{32,0},{64,32},{96,64},{1,97},{33,1},{65,33},{97,65},{2,98}... | collective-permute-start | bytes 196616 | tf_op jit(solution)/shard_map/ppermute | solution.py:36
  61.8 15.8 %collective-permute-start.13 = (bf16[4,32,1024]{2,1,0:T(8,128)(2,1)}, bf16[4,32,1024]{2,1,0:T(8,128)(2,1)S(1)}, u32[]{:S(2)}, u32[]{:S(2)}) collective-permute-start(bf16[4,32,1024]{2,1,0:T(8,128)(2,1)} %copy-done.11), channel_id=1, source_target_pairs={{0,2},{2,4},{4,6},{6,0},{1,3},{3,5},{5,7},{7,1},{8,10},{10,12},{12... | collective-permute-start | bytes 786440 | tf_op jit(solution)/shard_map/ppermute | solution.py:36
  63.4 14.2 %collective-permute-start.14 = (bf16[4,32,1024]{2,1,0:T(8,128)(2,1)}, bf16[4,32,1024]{2,1,0:T(8,128)(2,1)S(1)}, u32[]{:S(2)}, u32[]{:S(2)}) collective-permute-start(bf16[4,32,1024]{2,1,0:T(8,128)(2,1)} %copy-done.10), channel_id=1, source_target_pairs={{0,4},{2,6},{4,0},{6,2},{1,5},{3,7},{5,1},{7,3},{8,12},{10,14},{12... | collective-permute-start | bytes 786440 | tf_op jit(solution)/shard_map/ppermute | solution.py:36
  66.8 10.8 %collective-permute-start.15 = (bf16[4,32,1024]{2,1,0:T(8,128)(2,1)}, bf16[4,32,1024]{2,1,0:T(8,128)(2,1)S(1)}, u32[]{:S(2)}, u32[]{:S(2)}) collective-permute-start(bf16[4,32,1024]{2,1,0:T(8,128)(2,1)} %copy-done.9), channel_id=1, source_target_pairs={{0,6},{2,0},{4,2},{6,4},{1,7},{3,1},{5,3},{7,5},{8,14},{10,8},{12,... | collective-permute-start | bytes 786440 | tf_op jit(solution)/shard_map/ppermute | solution.py:36
  70.9 4.9 %collective-permute-start.17 = (bf16[32,1024]{1,0:T(8,128)(2,1)S(1)}, bf16[32,1024]{1,0:T(8,128)(2,1)S(1)}, u32[]{:S(2)}, u32[]{:S(2)}) collective-permute-start(bf16[32,1024]{1,0:T(8,128)(2,1)S(1)} %get-tuple-element.52), channel_id=1, source_target_pairs={{0,64},{32,96},{64,0},{96,32},{1,65},{33,97},{65,1},{97,33},{2,66}... | collective-permute-start | bytes 196616 | tf_op jit(solution)/shard_map/ppermute | solution.py:36
  71.1 6.5 %collective-permute-start.18 = (bf16[32,1024]{1,0:T(8,128)(2,1)S(1)}, bf16[32,1024]{1,0:T(8,128)(2,1)S(1)}, u32[]{:S(2)}, u32[]{:S(2)}) collective-permute-start(bf16[32,1024]{1,0:T(8,128)(2,1)S(1)} %get-tuple-element.51), channel_id=1, source_target_pairs={{0,32},{32,64},{64,96},{96,0},{1,33},{33,65},{65,97},{97,1},{2,34}... | collective-permute-start | bytes 196616 | tf_op jit(solution)/shard_map/ppermute | solution.py:36
  79.4 5.7 %collective-permute-start.19 = (bf16[4,32,1024]{2,1,0:T(8,128)(2,1)S(1)}, bf16[4,32,1024]{2,1,0:T(8,128)(2,1)S(1)}, u32[]{:S(2)}, u32[]{:S(2)}) collective-permute-start(bf16[4,32,1024]{2,1,0:T(8,128)(2,1)S(1)} %shard_map.130.refs_0_), channel_id=1, source_target_pairs={{0,96},{32,0},{64,32},{96,64},{1,97},{33,1},{65,33},{97,65},{2,98}... | collective-permute-start | bytes 786440 | tf_op jit(solution)/shard_map/ppermute | solution.py:36
  79.8 7.2 %collective-permute-start.20 = (bf16[4,32,1024]{2,1,0:T(8,128)(2,1)S(1)}, bf16[4,32,1024]{2,1,0:T(8,128)(2,1)S(1)}, u32[]{:S(2)}, u32[]{:S(2)}) collective-permute-start(bf16[4,32,1024]{2,1,0:T(8,128)(2,1)S(1)} %shard_map.130.refs_0_), channel_id=1, source_target_pairs={{0,64},{32,96},{64,0},{96,32},{1,65},{33,97},{65,1},{97,33},{2,66}... | collective-permute-start | bytes 786440 | tf_op jit(solution)/shard_map/ppermute | solution.py:36
  80.2 14.8 %collective-permute-start.21 = (bf16[4,32,1024]{2,1,0:T(8,128)(2,1)S(1)}, bf16[4,32,1024]{2,1,0:T(8,128)(2,1)S(1)}, u32[]{:S(2)}, u32[]{:S(2)}) collective-permute-start(bf16[4,32,1024]{2,1,0:T(8,128)(2,1)S(1)} %shard_map.130.refs_0_), channel_id=1, source_target_pairs={{0,32},{32,64},{64,96},{96,0},{1,33},{33,65},{65,97},{97,1},{2,34}... | collective-permute-start | bytes 786440 | tf_op jit(solution)/shard_map/ppermute | solution.py:36
  161.1 47.9 %all-to-all-start.1 = ((bf16[128,96,128]{2,1,0:T(8,128)(2,1)}), bf16[128,96,128]{2,1,0:T(8,128)(2,1)S(1)}, u32[]{:S(2)}, u32[]{:S(2)}) async-start(bf16[128,96,128]{2,1,0:T(8,128)(2,1)} %bitcast.49), calls=%async_computation.1 | async-start | bytes 6291456 | tf_op jit(solution)/shard_map/all_to_all | solution.py:383
  (19 other events, 198.7 us)

commit v6 on v5

--- a/solution.py
+++ b/solution.py
@@ -177,8 +177,23 @@
     )(pos, *quarters, gain)
 
 
-def place_kernel(where, own, other, message):
-    tokens = own.shape[0]
+def place_kernel(pos, *refs):
+    targets, (own, other, message, where) = refs[:NX], refs[NX:]
+    x, c = pos[0], pos[3]
+    tok = targets[0].shape[1]
+    slots, tokens = where.shape[0], own.shape[0]
+    row = lax.broadcasted_iota(jnp.int32, (slots, tok), 0)
+    block = row // CAP % (NC * NX)
+    wanted = ((x * NY * NZ + row // (NC * NX * CAP)) * NC + c) * CAP + row % CAP
+    for core in range(NC):
+        for d in range(NX):
+            mine = block == lax.rem(c + core, NC) * NX + lax.rem(x + d, NX)
+            found = jnp.zeros((slots, tok), jnp.bool_)
+            for k in range(TOPK):
+                at = core * TOPK + k
+                found |= targets[d][at : at + 1, :] == wanted
+            piece = core * NX + d
+            where[:, piece * tok : (piece + 1) * tok] = jnp.where(mine & found, 1.0, 0.0).astype(BF)
     for j in range(0, D, OUT):
         lanes = slice(j, j + OUT)
         total = jnp.dot(where[:, :tokens], own[:, lanes], preferred_element_type=F32)
@@ -186,15 +201,17 @@
         message[:, lanes] = total.astype(BF)
 
 
-def place(where, own, other):
+def place(pos, targets, own, other):
+    slots = NX * NY * NZ * NC * CAP
     return pl.pallas_call(
         place_kernel,
-        out_shape=jax.ShapeDtypeStruct((where.shape[0], D), BF),
-        in_specs=[VMEM] * 3,
+        out_shape=jax.ShapeDtypeStruct((slots, D), BF),
+        in_specs=[SMEM] + [VMEM] * (NX + 2),
         out_specs=VMEM,
-        compiler_params=params(16),
-        cost_estimate=cost(2 * where.shape[0] * where.shape[1] * D, 5 << 20),
-    )(where, own, other)
+        scratch_shapes=[pltpu.VMEM((slots, 2 * own.shape[0]), BF)],
+        compiler_params=params(16),
+        cost_estimate=cost(4 * slots * own.shape[0] * D, 5 << 20),
+    )(pos, *targets, own, other)
 
 
 def expert_kernel(scale, rows, gate, up, down, out, x, wg, wu, wd, gates, ups, act, part, done, in_sem, down_sem, out_sem):
@@ -345,37 +362,27 @@
     slot_index = jnp.sum(same.astype(jnp.int32), axis=1)
     target = (flat_ids * CAP + slot_index).reshape(tok_rows, TOPK)
 
-    head_normed, weights = lax.optimization_barrier((head_normed, weights))
-    tokens = gather_line(head_normed, "x")
-    keep, give = project(pos, tokens, weights, tok_rows)
-    own, *low = pair_sums(pos, keep, shift(give, "c", 1))
-    parts = [shift(low[d - 1], "z", d) for d in range(1, NZ)]
-    own, target, stream = lax.optimization_barrier((own, target, stream))
-    line_target = jnp.concatenate(gather_line(target.T, "x"), axis=1)
-    line_target = jnp.concatenate([line_target, shift(line_target, "c", 1)], axis=1)
-    token = jnp.arange(NC * NX * tok_rows, dtype=jnp.int32)
-    piece = token // tok_rows
-    token_block = (c + piece // NX) % NC * NX + (x + piece % NX) % NX
-    row = jnp.arange(slots, dtype=jnp.int32)
-    plane = row // (NC * NX * CAP)
-    row_block = row // CAP % (NC * NX)
-    wanted = ((x * NY * NZ + plane) * NC + c) * CAP + row % CAP
-    where = jnp.any(line_target[:, None, :] == wanted[None, :, None], axis=0)
-    where = (where & (token_block[None, :] == row_block[:, None])).astype(BF)
-    back = target // CAP
-    back = (back % (NY * NZ * NC) * NX + back // (NY * NZ * NC)) * CAP + target % CAP
-
+    both = jnp.concatenate([target.T, shift(target.T, "c", 1)], axis=0)
     wide = D // NX
     stream_parts = [
         lax.dynamic_slice_in_dim(stream, (x + NX - d) % NX * wide, wide, axis=1) for d in range(NX)
     ]
+    back = target // CAP
+    back = (back % (NY * NZ * NC) * NX + back // (NY * NZ * NC)) * CAP + target % CAP
+    head_normed, both, stream_parts, back = lax.optimization_barrier((head_normed, both, stream_parts, back))
+
+    keep, give = project(pos, gather_line(head_normed, "x"), weights, tok_rows)
+    own, *low = pair_sums(pos, keep, shift(give, "c", 1))
+    parts = [shift(low[d - 1], "z", d) for d in range(1, NZ)]
+    parts[0], stream_parts = lax.optimization_barrier((parts[0], stream_parts))
     stream_parts = stream_parts[:1] + [shift(stream_parts[d], "x", NX - d) for d in range(1, NX)]
-
     residual = quarter(pos, own, parts, stream_parts)
     quarters = gather_line(residual, "x")
-    quarters, where, back = lax.optimization_barrier((quarters, where, back))
+    quarters[1], both = lax.optimization_barrier((quarters[1], both))
+    targets = gather_line(both, "x")
+    quarters[3], targets = lax.optimization_barrier((quarters[3], targets))
     normed, res = norm(pos, quarters, model_gain[None])
-    message = place(where, normed, shift(normed, "c", 1))
+    message = place(pos, targets, normed, shift(normed, "c", 1))
     slot_rows = lax.all_to_all(
         message.reshape(NY * NZ, -1, D), ("y", "z"), split_axis=0, concat_axis=0, tiled=True
     ).reshape(slots, D)

time: 213 us -> 205 us (0.962)
  waiting for transfers between devices: 90.4 us -> 80.8 us
  starting transfers between devices: 41.2 us -> 46.2 us
  local copies, waits for them, and re-layouts: 7.65 us -> 4.98 us
    ppermute x27, waiting for transfers between devices: 48.1 us -> 38.7 us  [shift(): return lax.ppermute(a, axis, [(i, (i + d) % n) for i in range(n)])]
    ppermute x27, starting transfers between devices: 35.6 us -> 39.7 us  [shift(): return lax.ppermute(a, axis, [(i, (i + d) % n) for i in range(n)])]
    unnamed x32 -> x22, local copies, waits for them, and re-layouts: 5.79 us -> 2.52 us
  transfers between devices with their start and end apart: 28 -> 28, of which waited for: 15 -> 16; matrix products, arithmetic and copies ran while one was open for 2% -> 2% of each run, Pallas kernels for 0% -> 0%
where the time goes in v6:
time: 205 us
  waiting for transfers between devices  80.8 us (39%)
  starting transfers between devices  46.2 us (23%)
  blocking collectives  42 us (20%)
  Pallas kernels  28.1 us (14%)
  local copies, waits for them, and re-layouts  4.98 us (2%)
    all_to_all x1, waiting for transfers between devices, body(): lax.all_to_all(produced.reshape(experts, CAP * BLOCKS, LANES), ('y', 'z',...  42.1 us
    all_to_all x1, blocking collectives, body(): lax.all_to_all(message.reshape(NY * NZ, -1, D), ('y', 'z'), split_axis=0,...  42 us
    ppermute x27, starting transfers between devices, shift(): return lax.ppermute(a, axis, [(i, (i + d) % n) for i in range(n)])  39.7 us
    ppermute x27, waiting for transfers between devices, shift(): return lax.ppermute(a, axis, [(i, (i + d) % n) for i in range(n)])  38.7 us
    pallas_call x1, Pallas kernels, run_expert(): pl.pallas_call(expert_kernel, out_shape=jax.ShapeDtypeStruct((count, BLOC...  16.4 us
    all_to_all x1, starting transfers between devices, body(): lax.all_to_all(produced.reshape(experts, CAP * BLOCKS, LANES), ('y', 'z',...  6.48 us
  transfers between devices with their start and end apart: 28, of which 16 were waited for; matrix products, arithmetic and copies ran while one was open for 2% of the time, Pallas kernels for 0%

profile of v6, /device:TPU:1, one launch (start us, length us, event | category | flops | bytes accessed | tf_op | source)
XLA Modules:
  0.0 204.6 jit_solution(18223704152376156536)
XLA Ops:
  1.5 2.2 %collective-permute-start = (bf16[4,128,128]{2,1,0:T(8,128)(2,1)S(1)}, bf16[4,128,128]{2,1,0:T(8,128)(2,1)S(1)}, u32[]{:S(2)}, u32[]{:S(2)}) collective-permute-start(bf16[4,128,128]{2,1,0:T(8,128)(2,1)S(1)} %get-tuple-element.67), channel_id=1, source_target_pairs={{0,8},{8,16},{16,24},{24,0},{1,9},{9,17},{17,25},{25,1},{2,10},{10... | collective-permute-start | bytes 393224 | tf_op jit(solution)/shard_map/ppermute | solution.py:36
  3.7 2.6 %collective-permute-start.1 = (bf16[4,128,128]{2,1,0:T(8,128)(2,1)S(1)}, bf16[4,128,128]{2,1,0:T(8,128)(2,1)S(1)}, u32[]{:S(2)}, u32[]{:S(2)}) collective-permute-start(bf16[4,128,128]{2,1,0:T(8,128)(2,1)S(1)} %get-tuple-element.67), channel_id=1, source_target_pairs={{0,16},{8,24},{16,0},{24,8},{1,17},{9,25},{17,1},{25,9},{2,18},{10... | collective-permute-start | bytes 393224 | tf_op jit(solution)/shard_map/ppermute | solution.py:36
  13.8 2.5 %collective-permute-start.4 = (bf16[4,128,128]{2,1,0:T(8,128)(2,1)S(1)}, bf16[4,128,128]{2,1,0:T(8,128)(2,1)S(1)}, u32[]{:S(2)}, u32[]{:S(2)}) collective-permute-start(bf16[4,128,128]{2,1,0:T(8,128)(2,1)S(1)} %get-tuple-element.59), channel_id=1, source_target_pairs={{0,64},{32,96},{64,0},{96,32},{1,65},{33,97},{65,1},{97,33},{2,66}... | collective-permute-start | bytes 393224 | tf_op jit(solution)/shard_map/ppermute | solution.py:36
  17.7 2.3 %collective-permute-start.11 = (bf16[512,256]{1,0:T(8,128)(2,1)S(1)}, bf16[512,256]{1,0:T(8,128)(2,1)S(1)}, u32[]{:S(2)}, u32[]{:S(2)}) collective-permute-start(bf16[512,256]{1,0:T(8,128)(2,1)S(1)} %copy-done.6), channel_id=1, source_target_pairs={{0,16},{8,24},{16,0},{24,8},{1,17},{9,25},{17,1},{25,9},{2,18},{10... | collective-permute-start | bytes 786440 | tf_op jit(solution)/shard_map/ppermute | solution.py:36
  22.3 3.0 %collective-permute-start.7 = (bf16[256,512]{1,0:T(8,128)(2,1)S(1)}, bf16[256,512]{1,0:T(8,128)(2,1)S(1)}, u32[]{:S(2)}, u32[]{:S(2)}) collective-permute-start(bf16[256,512]{1,0:T(8,128)(2,1)S(1)} %shard_map.127.refs_0_), channel_id=1, source_target_pairs={{0,96},{32,0},{64,32},{96,64},{1,97},{33,1},{65,33},{97,65},{2,98}... | collective-permute-start | bytes 786440 | tf_op jit(solution)/shard_map/ppermute | solution.py:36
  26.0 5.3 %collective-permute-done.12.refs_7_ = bf16[512,256]{1,0:T(8,128)(2,1)S(1)} collective-permute-done((bf16[512,256]{1,0:T(8,128)(2,1)S(1)}, bf16[512,256]{1,0:T(8,128)(2,1)S(1)}, u32[]{:S(2)}, u32[]{:S(2)}) %collective-permute-start.12) | collective-permute-done | bytes 262176 | tf_op jit(solution)/shard_map/ppermute | solution.py:36
  32.8 7.2 %collective-permute-done.9.refs_3_ = bf16[256,512]{1,0:T(8,128)(2,1)S(1)} collective-permute-done((bf16[256,512]{1,0:T(8,128)(2,1)S(1)}, bf16[256,512]{1,0:T(8,128)(2,1)S(1)}, u32[]{:S(2)}, u32[]{:S(2)}) %collective-permute-start.9) | collective-permute-done | bytes 262176 | tf_op jit(solution)/shard_map/ppermute | solution.py:36
  40.0 2.0 shard_map.128
  42.9 2.3 %collective-permute-done.13.got = bf16[16,32,1024]{2,1,0:T(8,128)(2,1)S(1)} collective-permute-done((bf16[16,32,1024]{2,1,0:T(8,128)(2,1)S(1)}, bf16[16,32,1024]{2,1,0:T(8,128)(2,1)S(1)}, u32[]{:S(2)}, u32[]{:S(2)}) %collective-permute-start.13) | collective-permute-done | bytes 1048608 | tf_op jit(solution)/shard_map/ppermute | solution.py:36
  45.9 1.7 collective-permute-start.14
  47.6 3.3 %collective-permute-start.15 = (bf16[4,32,1024]{2,1,0:T(8,128)(2,1)S(1)}, bf16[4,32,1024]{2,1,0:T(8,128)(2,1)S(1)}, u32[]{:S(2)}, u32[]{:S(2)}) collective-permute-start(bf16[4,32,1024]{2,1,0:T(8,128)(2,1)S(1)} %get-tuple-element.43), channel_id=1, source_target_pairs={{0,4},{2,6},{4,0},{6,2},{1,5},{3,7},{5,1},{7,3},{8,12},{10,14},{12... | collective-permute-start | bytes 786440 | tf_op jit(solution)/shard_map/ppermute | solution.py:36
  51.7 4.4 %collective-permute-done.14.one = bf16[4,32,1024]{2,1,0:T(8,128)(2,1)S(1)} collective-permute-done((bf16[4,32,1024]{2,1,0:T(8,128)(2,1)S(1)}, bf16[4,32,1024]{2,1,0:T(8,128)(2,1)S(1)}, u32[]{:S(2)}, u32[]{:S(2)}) %collective-permute-start.14) | collective-permute-done | bytes 262176 | tf_op jit(solution)/shard_map/ppermute | solution.py:36
  57.6 5.0 %collective-permute-done.15.two = bf16[4,32,1024]{2,1,0:T(8,128)(2,1)S(1)} collective-permute-done((bf16[4,32,1024]{2,1,0:T(8,128)(2,1)S(1)}, bf16[4,32,1024]{2,1,0:T(8,128)(2,1)S(1)}, u32[]{:S(2)}, u32[]{:S(2)}) %collective-permute-start.15) | collective-permute-done | bytes 262176 | tf_op jit(solution)/shard_map/ppermute | solution.py:36
  66.0 3.3 %collective-permute-done.21.refs_1_ = bf16[4,32,1024]{2,1,0:T(8,128)(2,1)S(1)} collective-permute-done((bf16[4,32,1024]{2,1,0:T(8,128)(2,1)S(1)}, bf16[4,32,1024]{2,1,0:T(8,128)(2,1)S(1)}, u32[]{:S(2)}, u32[]{:S(2)}) %collective-permute-start.21) | collective-permute-done | bytes 262176 | tf_op jit(solution)/shard_map/ppermute | solution.py:36
  69.3 2.9 %collective-permute-start.22 = (s32[16,32]{0,1:T(8,128)S(1)}, s32[16,32]{0,1:T(8,128)S(1)}, u32[]{:S(2)}, u32[]{:S(2)}) collective-permute-start(s32[16,32]{0,1:T(8,128)S(1)} %pad_add_fusion), channel_id=1, source_target_pairs={{0,96},{32,0},{64,32},{96,64},{1,97},{33,1},{65,33},{97,65},{2,98}... | collective-permute-start | bytes 6152 | tf_op jit(solution)/shard_map/ppermute | solution.py:36
  76.8 2.3 %collective-permute-done.24 = s32[16,32]{0,1:T(8,128)S(1)} collective-permute-done((s32[16,32]{0,1:T(8,128)S(1)}, s32[16,32]{0,1:T(8,128)S(1)}, u32[]{:S(2)}, u32[]{:S(2)}) %collective-permute-start.24) | collective-permute-done | bytes 2080 | tf_op jit(solution)/shard_map/ppermute | solution.py:36
  80.8 7.0 %collective-permute-start.26 = (bf16[128,4096]{1,0:T(8,128)(2,1)S(1)}, bf16[128,4096]{1,0:T(8,128)(2,1)S(1)}, u32[]{:S(2)}, u32[]{:S(2)}) collective-permute-start(bf16[128,4096]{1,0:T(8,128)(2,1)S(1)} %get-tuple-element.57.refs_4_), channel_id=1, source_target_pairs={{0,1},{1,0},{2,3},{3,2},{4,5},{5,4},{6,7},{7,6},{8,9},{9,8},{10,11... | collective-permute-start | bytes 3145736 | tf_op jit(solution)/shard_map/ppermute | solution.py:36
  88.1 2.0 collective-permute-done.26.refs_5_
  90.1 3.5 %shard_map.132 = bf16[384,4096]{1,0:T(8,128)(2,1)S(1)} custom-call(s32[4]{0:T(128)S(1)} %pad_add_fusion.1.pos, s32[16,32]{1,0:T(8,128)S(1)} %copy.43.refs_0_, s32[16,32]{1,0:T(8,128)S(1)} %copy.44.refs_1_, s32[16,32]{1,0:T(8,128)S(1)} %copy.45.refs_2_, s32[16,32]{1,0:T(8,128)S(1)} %copy.46.refs_3_, bf16[128,4096]{1,0:T(8,128)(2,1)S(1)} %get-tuple-element.57.refs_4_, ...), custom_call_target="tpu_custom_call" | custom-call | flops 805306368 | bytes 5242880 | tf_op jit(solution)/shard_map/pallas_call | solution.py:206
  93.7 42.0 %all_to_all.10 = bf16[16,24,4096]{2,1,0:T(8,128)(2,1)} all-to-all(bf16[16,24,4096]{2,1,0:T(8,128)(2,1)S(1)} %bitcast.47), channel_id=1, replica_groups=mesh['x'=4,'y'=4,'z'=4,'c'=2] {'y','z'}, dimensions={0} | all-to-all | bytes 6291456 | tf_op jit(solution)/shard_map/all_to_all | solution.py:386
  135.7 16.4 %shard_map.133 = bf16[384,32,128]{2,1,0:T(8,128)(2,1)} custom-call(f32[1,3]{1,0:T(1,128)} %scale.1, bf16[384,4096]{1,0:T(8,128)(2,1)} %bitcast.51, bf16[4096,768]{1,0:T(8,128)(2,1)} %bitcast.55, bf16[4096,768]{1,0:T(8,128)(2,1)} %bitcast.56, bf16[768,4096]{1,0:T(8,128)(2,1)} %bitcast.57), custom_call_target="tpu_custom_call" | custom-call | flops 7247757312 | bytes 18874368 | tf_op jit(solution)/shard_map/pallas_call | solution.py:262
  152.1 6.5 %all-to-all-start.1 = ((bf16[128,96,128]{2,1,0:T(8,128)(2,1)}), bf16[128,96,128]{2,1,0:T(8,128)(2,1)S(1)}, u32[]{:S(2)}, u32[]{:S(2)}) async-start(bf16[128,96,128]{2,1,0:T(8,128)(2,1)} %bitcast.50), calls=%async_computation.1 | async-start | bytes 6291456 | tf_op jit(solution)/shard_map/all_to_all | solution.py:390
  158.6 42.1 %all-to-all-done.1 = bf16[128,96,128]{2,1,0:T(8,128)(2,1)S(1)} async-done(((bf16[128,96,128]{2,1,0:T(8,128)(2,1)}), bf16[128,96,128]{2,1,0:T(8,128)(2,1)S(1)}, u32[]{:S(2)}, u32[]{:S(2)}) %all-to-all-start.1) | async-done | bytes 3145760 | tf_op jit(solution)/shard_map/all_to_all | solution.py:390
  201.7 2.9 %shard_map.134 = bf16[32,4096]{1,0:T(8,128)(2,1)} custom-call(s32[32,8]{1,0:T(8,128)S(1)} %get-tuple-element.32.target, f32[32,8]{1,0:T(8,128)S(1)} %copy.47.gates, bf16[384,32,128]{2,1,0:T(8,128)(2,1)S(1)} %bitcast.46, bf16[32,4096]{1,0:T(8,128)(2,1)S(1)} %copy-done.2), custom_call_target="tpu_custom_call" | custom-call | flops 1048576 | bytes 4194304 | tf_op jit(solution)/shard_map/pallas_call | solution.py:304
  (80 shorter events, 29.6 us)
Async XLA Ops:
  1.5 10.9 %collective-permute-start = (bf16[4,128,128]{2,1,0:T(8,128)(2,1)S(1)}, bf16[4,128,128]{2,1,0:T(8,128)(2,1)S(1)}, u32[]{:S(2)}, u32[]{:S(2)}) collective-permute-start(bf16[4,128,128]{2,1,0:T(8,128)(2,1)S(1)} %get-tuple-element.67), channel_id=1, source_target_pairs={{0,8},{8,16},{16,24},{24,0},{1,9},{9,17},{17,25},{25,1},{2,10},{10... | collective-permute-start | bytes 393224 | tf_op jit(solution)/shard_map/ppermute | solution.py:36
  3.7 8.7 %collective-permute-start.1 = (bf16[4,128,128]{2,1,0:T(8,128)(2,1)S(1)}, bf16[4,128,128]{2,1,0:T(8,128)(2,1)S(1)}, u32[]{:S(2)}, u32[]{:S(2)}) collective-permute-start(bf16[4,128,128]{2,1,0:T(8,128)(2,1)S(1)} %get-tuple-element.67), channel_id=1, source_target_pairs={{0,16},{8,24},{16,0},{24,8},{1,17},{9,25},{17,1},{25,9},{2,18},{10... | collective-permute-start | bytes 393224 | tf_op jit(solution)/shard_map/ppermute | solution.py:36
  6.3 6.1 %collective-permute-start.2 = (bf16[4,128,128]{2,1,0:T(8,128)(2,1)S(1)}, bf16[4,128,128]{2,1,0:T(8,128)(2,1)S(1)}, u32[]{:S(2)}, u32[]{:S(2)}) collective-permute-start(bf16[4,128,128]{2,1,0:T(8,128)(2,1)S(1)} %get-tuple-element.67), channel_id=1, source_target_pairs={{0,24},{8,0},{16,8},{24,16},{1,25},{9,1},{17,9},{25,17},{2,26},{10... | collective-permute-start | bytes 393224 | tf_op jit(solution)/shard_map/ppermute | solution.py:36
  8.6 9.1 %collective-permute-start.6 = (s32[8,32]{0,1:T(8,128)S(1)}, s32[8,32]{0,1:T(8,128)S(1)}, u32[]{:S(2)}, u32[]{:S(2)}) collective-permute-start(s32[8,32]{0,1:T(8,128)S(1)} %get-tuple-element.66), channel_id=1, source_target_pairs={{0,1},{1,0},{2,3},{3,2},{4,5},{5,4},{6,7},{7,6},{8,9},{9,8},{10,11... | collective-permute-start | bytes 3080 | tf_op jit(solution)/shard_map/ppermute | solution.py:36
  10.2 15.2 %collective-permute-start.10 = (bf16[512,256]{1,0:T(8,128)(2,1)}, bf16[512,256]{1,0:T(8,128)(2,1)S(1)}, u32[]{:S(2)}, u32[]{:S(2)}) collective-permute-start(bf16[512,256]{1,0:T(8,128)(2,1)} %refs_4_.1), channel_id=1, source_target_pairs={{0,24},{8,0},{16,8},{24,16},{1,25},{9,1},{17,9},{25,17},{2,26},{10... | collective-permute-start | bytes 786440 | tf_op jit(solution)/shard_map/ppermute | solution.py:36
  12.5 7.5 %collective-permute-start.3 = (bf16[4,128,128]{2,1,0:T(8,128)(2,1)S(1)}, bf16[4,128,128]{2,1,0:T(8,128)(2,1)S(1)}, u32[]{:S(2)}, u32[]{:S(2)}) collective-permute-start(bf16[4,128,128]{2,1,0:T(8,128)(2,1)S(1)} %get-tuple-element.59), channel_id=1, source_target_pairs={{0,32},{32,64},{64,96},{96,0},{1,33},{33,65},{65,97},{97,1},{2,34}... | collective-permute-start | bytes 393224 | tf_op jit(solution)/shard_map/ppermute | solution.py:36
  13.8 7.3 %collective-permute-start.4 = (bf16[4,128,128]{2,1,0:T(8,128)(2,1)S(1)}, bf16[4,128,128]{2,1,0:T(8,128)(2,1)S(1)}, u32[]{:S(2)}, u32[]{:S(2)}) collective-permute-start(bf16[4,128,128]{2,1,0:T(8,128)(2,1)S(1)} %get-tuple-element.59), channel_id=1, source_target_pairs={{0,64},{32,96},{64,0},{96,32},{1,65},{33,97},{65,1},{97,33},{2,66}... | collective-permute-start | bytes 393224 | tf_op jit(solution)/shard_map/ppermute | solution.py:36
  17.7 8.3 %collective-permute-start.11 = (bf16[512,256]{1,0:T(8,128)(2,1)S(1)}, bf16[512,256]{1,0:T(8,128)(2,1)S(1)}, u32[]{:S(2)}, u32[]{:S(2)}) collective-permute-start(bf16[512,256]{1,0:T(8,128)(2,1)S(1)} %copy-done.6), channel_id=1, source_target_pairs={{0,16},{8,24},{16,0},{24,8},{1,17},{9,25},{17,1},{25,9},{2,18},{10... | collective-permute-start | bytes 786440 | tf_op jit(solution)/shard_map/ppermute | solution.py:36
  20.0 11.3 %collective-permute-start.12 = (bf16[512,256]{1,0:T(8,128)(2,1)S(1)}, bf16[512,256]{1,0:T(8,128)(2,1)S(1)}, u32[]{:S(2)}, u32[]{:S(2)}) collective-permute-start(bf16[512,256]{1,0:T(8,128)(2,1)S(1)} %copy-done.6), channel_id=1, source_target_pairs={{0,8},{8,16},{16,24},{24,0},{1,9},{9,17},{17,25},{25,1},{2,10},{10... | collective-permute-start | bytes 786440 | tf_op jit(solution)/shard_map/ppermute | solution.py:36
  22.3 10.3 %collective-permute-start.7 = (bf16[256,512]{1,0:T(8,128)(2,1)S(1)}, bf16[256,512]{1,0:T(8,128)(2,1)S(1)}, u32[]{:S(2)}, u32[]{:S(2)}) collective-permute-start(bf16[256,512]{1,0:T(8,128)(2,1)S(1)} %shard_map.127.refs_0_), channel_id=1, source_target_pairs={{0,96},{32,0},{64,32},{96,64},{1,97},{33,1},{65,33},{97,65},{2,98}... | collective-permute-start | bytes 786440 | tf_op jit(solution)/shard_map/ppermute | solution.py:36
  25.3 7.5 %collective-permute-start.8 = (bf16[256,512]{1,0:T(8,128)(2,1)S(1)}, bf16[256,512]{1,0:T(8,128)(2,1)S(1)}, u32[]{:S(2)}, u32[]{:S(2)}) collective-permute-start(bf16[256,512]{1,0:T(8,128)(2,1)S(1)} %shard_map.127.refs_0_), channel_id=1, source_target_pairs={{0,64},{32,96},{64,0},{96,32},{1,65},{33,97},{65,1},{97,33},{2,66}... | collective-permute-start | bytes 786440 | tf_op jit(solution)/shard_map/ppermute | solution.py:36
  25.3 14.7 %collective-permute-start.9 = (bf16[256,512]{1,0:T(8,128)(2,1)S(1)}, bf16[256,512]{1,0:T(8,128)(2,1)S(1)}, u32[]{:S(2)}, u32[]{:S(2)}) collective-permute-start(bf16[256,512]{1,0:T(8,128)(2,1)S(1)} %shard_map.127.refs_0_), channel_id=1, source_target_pairs={{0,32},{32,64},{64,96},{96,0},{1,33},{33,65},{65,97},{97,1},{2,34}... | collective-permute-start | bytes 786440 | tf_op jit(solution)/shard_map/ppermute | solution.py:36
  45.9 10.2 %collective-permute-start.14 = (bf16[4,32,1024]{2,1,0:T(8,128)(2,1)S(1)}, bf16[4,32,1024]{2,1,0:T(8,128)(2,1)S(1)}, u32[]{:S(2)}, u32[]{:S(2)}) collective-permute-start(bf16[4,32,1024]{2,1,0:T(8,128)(2,1)S(1)} %get-tuple-element.37), channel_id=1, source_target_pairs={{0,2},{2,4},{4,6},{6,0},{1,3},{3,5},{5,7},{7,1},{8,10},{10,12},{12... | collective-permute-start | bytes 786440 | tf_op jit(solution)/shard_map/ppermute | solution.py:36
  47.6 15.0 %collective-permute-start.15 = (bf16[4,32,1024]{2,1,0:T(8,128)(2,1)S(1)}, bf16[4,32,1024]{2,1,0:T(8,128)(2,1)S(1)}, u32[]{:S(2)}, u32[]{:S(2)}) collective-permute-start(bf16[4,32,1024]{2,1,0:T(8,128)(2,1)S(1)} %get-tuple-element.43), channel_id=1, source_target_pairs={{0,4},{2,6},{4,0},{6,2},{1,5},{3,7},{5,1},{7,3},{8,12},{10,14},{12... | collective-permute-start | bytes 786440 | tf_op jit(solution)/shard_map/ppermute | solution.py:36
  50.9 11.7 %collective-permute-start.16 = (bf16[4,32,1024]{2,1,0:T(8,128)(2,1)S(1)}, bf16[4,32,1024]{2,1,0:T(8,128)(2,1)S(1)}, u32[]{:S(2)}, u32[]{:S(2)}) collective-permute-start(bf16[4,32,1024]{2,1,0:T(8,128)(2,1)S(1)} %get-tuple-element.44), channel_id=1, source_target_pairs={{0,6},{2,0},{4,2},{6,4},{1,7},{3,1},{5,3},{7,5},{8,14},{10,8},{12,... | collective-permute-start | bytes 786440 | tf_op jit(solution)/shard_map/ppermute | solution.py:36
  56.1 6.5 %collective-permute-start.17 = (bf16[32,1024]{1,0:T(8,128)(2,1)S(1)}, bf16[32,1024]{1,0:T(8,128)(2,1)S(1)}, u32[]{:S(2)}, u32[]{:S(2)}) collective-permute-start(bf16[32,1024]{1,0:T(8,128)(2,1)S(1)} %copy-done.8), channel_id=1, source_target_pairs={{0,96},{32,0},{64,32},{96,64},{1,97},{33,1},{65,33},{97,65},{2,98}... | collective-permute-start | bytes 196616 | tf_op jit(solution)/shard_map/ppermute | solution.py:36
  56.8 5.9 %collective-permute-start.19 = (bf16[32,1024]{1,0:T(8,128)(2,1)S(1)}, bf16[32,1024]{1,0:T(8,128)(2,1)S(1)}, u32[]{:S(2)}, u32[]{:S(2)}) collective-permute-start(bf16[32,1024]{1,0:T(8,128)(2,1)S(1)} %get-tuple-element.48), channel_id=1, source_target_pairs={{0,32},{32,64},{64,96},{96,0},{1,33},{33,65},{65,97},{97,1},{2,34}... | collective-permute-start | bytes 196616 | tf_op jit(solution)/shard_map/ppermute | solution.py:36
  63.3 6.0 %collective-permute-start.21 = (bf16[4,32,1024]{2,1,0:T(8,128)(2,1)S(1)}, bf16[4,32,1024]{2,1,0:T(8,128)(2,1)S(1)}, u32[]{:S(2)}, u32[]{:S(2)}) collective-permute-start(bf16[4,32,1024]{2,1,0:T(8,128)(2,1)S(1)} %shard_map.130.refs_0_), channel_id=1, source_target_pairs={{0,96},{32,0},{64,32},{96,64},{1,97},{33,1},{65,33},{97,65},{2,98}... | collective-permute-start | bytes 786440 | tf_op jit(solution)/shard_map/ppermute | solution.py:36
  64.7 9.1 %collective-permute-start.20 = (bf16[4,32,1024]{2,1,0:T(8,128)(2,1)S(1)}, bf16[4,32,1024]{2,1,0:T(8,128)(2,1)S(1)}, u32[]{:S(2)}, u32[]{:S(2)}) collective-permute-start(bf16[4,32,1024]{2,1,0:T(8,128)(2,1)S(1)} %shard_map.130.refs_0_), channel_id=1, source_target_pairs={{0,32},{32,64},{64,96},{96,0},{1,33},{33,65},{65,97},{97,1},{2,34}... | collective-permute-start | bytes 786440 | tf_op jit(solution)/shard_map/ppermute | solution.py:36
  64.9 14.3 %collective-permute-start.25 = (bf16[4,32,1024]{2,1,0:T(8,128)(2,1)S(1)}, bf16[4,32,1024]{2,1,0:T(8,128)(2,1)S(1)}, u32[]{:S(2)}, u32[]{:S(2)}) collective-permute-start(bf16[4,32,1024]{2,1,0:T(8,128)(2,1)S(1)} %shard_map.130.refs_0_), channel_id=1, source_target_pairs={{0,64},{32,96},{64,0},{96,32},{1,65},{33,97},{65,1},{97,33},{2,66}... | collective-permute-start | bytes 786440 | tf_op jit(solution)/shard_map/ppermute | solution.py:36
  69.3 6.0 %collective-permute-start.22 = (s32[16,32]{0,1:T(8,128)S(1)}, s32[16,32]{0,1:T(8,128)S(1)}, u32[]{:S(2)}, u32[]{:S(2)}) collective-permute-start(s32[16,32]{0,1:T(8,128)S(1)} %pad_add_fusion), channel_id=1, source_target_pairs={{0,96},{32,0},{64,32},{96,64},{1,97},{33,1},{65,33},{97,65},{2,98}... | collective-permute-start | bytes 6152 | tf_op jit(solution)/shard_map/ppermute | solution.py:36
  72.2 6.9 %collective-permute-start.24 = (s32[16,32]{0,1:T(8,128)S(1)}, s32[16,32]{0,1:T(8,128)S(1)}, u32[]{:S(2)}, u32[]{:S(2)}) collective-permute-start(s32[16,32]{0,1:T(8,128)S(1)} %pad_add_fusion), channel_id=1, source_target_pairs={{0,32},{32,64},{64,96},{96,0},{1,33},{33,65},{65,97},{97,1},{2,34}... | collective-permute-start | bytes 6152 | tf_op jit(solution)/shard_map/ppermute | solution.py:36
  80.8 9.3 %collective-permute-start.26 = (bf16[128,4096]{1,0:T(8,128)(2,1)S(1)}, bf16[128,4096]{1,0:T(8,128)(2,1)S(1)}, u32[]{:S(2)}, u32[]{:S(2)}) collective-permute-start(bf16[128,4096]{1,0:T(8,128)(2,1)S(1)} %get-tuple-element.57.refs_4_), channel_id=1, source_target_pairs={{0,1},{1,0},{2,3},{3,2},{4,5},{5,4},{6,7},{7,6},{8,9},{9,8},{10,11... | collective-permute-start | bytes 3145736 | tf_op jit(solution)/shard_map/ppermute | solution.py:36
  152.1 48.7 %all-to-all-start.1 = ((bf16[128,96,128]{2,1,0:T(8,128)(2,1)}), bf16[128,96,128]{2,1,0:T(8,128)(2,1)S(1)}, u32[]{:S(2)}, u32[]{:S(2)}) async-start(bf16[128,96,128]{2,1,0:T(8,128)(2,1)} %bitcast.50), calls=%async_computation.1 | async-start | bytes 6291456 | tf_op jit(solution)/shard_map/all_to_all | solution.py:390
  (14 other events, 171.2 us)

commit v7 on v6

--- a/solution.py
+++ b/solution.py
@@ -177,23 +177,41 @@
     )(pos, *quarters, gain)
 
 
-def place_kernel(pos, *refs):
-    targets, (own, other, message, where) = refs[:NX], refs[NX:]
+def places_kernel(pos, *refs):
+    parts, where = refs[:NX], refs[NX]
     x, c = pos[0], pos[3]
-    tok = targets[0].shape[1]
-    slots, tokens = where.shape[0], own.shape[0]
+    slots, tok = where.shape[0], parts[0].shape[0]
     row = lax.broadcasted_iota(jnp.int32, (slots, tok), 0)
     block = row // CAP % (NC * NX)
     wanted = ((x * NY * NZ + row // (NC * NX * CAP)) * NC + c) * CAP + row % CAP
-    for core in range(NC):
-        for d in range(NX):
+    wanted = wanted.astype(F32)
+    for d in range(NX):
+        choice = parts[d][:, D // NX :].astype(F32).T
+        for core in range(NC):
+            at = 2 * core * TOPK
+            target = choice[at : at + TOPK] * CAP + choice[at + TOPK : at + 2 * TOPK]
             mine = block == lax.rem(c + core, NC) * NX + lax.rem(x + d, NX)
             found = jnp.zeros((slots, tok), jnp.bool_)
             for k in range(TOPK):
-                at = core * TOPK + k
-                found |= targets[d][at : at + 1, :] == wanted
+                found |= target[k : k + 1] == wanted
             piece = core * NX + d
             where[:, piece * tok : (piece + 1) * tok] = jnp.where(mine & found, 1.0, 0.0).astype(BF)
+
+
+def find_places(pos, parts):
+    slots, tokens = NX * NY * NZ * NC * CAP, NC * NX * parts[0].shape[0]
+    return pl.pallas_call(
+        places_kernel,
+        out_shape=jax.ShapeDtypeStruct((slots, tokens), BF),
+        in_specs=[SMEM] + [VMEM] * NX,
+        out_specs=VMEM,
+        compiler_params=params(8),
+        cost_estimate=cost(1 << 21, 1 << 18),
+    )(pos, *parts)
+
+
+def place_kernel(where, own, other, message):
+    tokens = own.shape[0]
     for j in range(0, D, OUT):
         lanes = slice(j, j + OUT)
         total = jnp.dot(where[:, :tokens], own[:, lanes], preferred_element_type=F32)
@@ -201,17 +219,15 @@
         message[:, lanes] = total.astype(BF)
 
 
-def place(pos, targets, own, other):
-    slots = NX * NY * NZ * NC * CAP
+def place(where, own, other):
     return pl.pallas_call(
         place_kernel,
-        out_shape=jax.ShapeDtypeStruct((slots, D), BF),
-        in_specs=[SMEM] + [VMEM] * (NX + 2),
+        out_shape=jax.ShapeDtypeStruct((where.shape[0], D), BF),
+        in_specs=[VMEM] * 3,
         out_specs=VMEM,
-        scratch_shapes=[pltpu.VMEM((slots, 2 * own.shape[0]), BF)],
-        compiler_params=params(16),
-        cost_estimate=cost(4 * slots * own.shape[0] * D, 5 << 20),
-    )(pos, *targets, own, other)
+        compiler_params=params(16),
+        cost_estimate=cost(2 * where.shape[0] * where.shape[1] * D, 5 << 20),
+    )(where, own, other)
 
 
 def expert_kernel(scale, rows, gate, up, down, out, x, wg, wu, wd, gates, ups, act, part, done, in_sem, down_sem, out_sem):
@@ -242,15 +258,18 @@
             ups[...] += up_part
     gate_part = gates[...] * scale[0, 0]
     act[...] = (gate_part / (1.0 + jnp.exp(-gate_part)) * (ups[...] * scale[0, 1])).astype(BF)
+    for load in downs:
+        load.wait()
     for i, j in enumerate(range(0, depth, OUT)):
-        downs[i].wait()
         total = jnp.dot(act[...], wd[:, j : j + OUT], preferred_element_type=F32) * scale[0, 2]
+        two, first = i // 2, i % 2 * groups
         for g in range(groups):
-            part[:, g, :] = total[:, g * LANES : (g + 1) * LANES]
-        at = pl.ds(i * groups, groups)
-        done[:, i * groups : (i + 1) * groups, :] = part[...].astype(BF)
-        stores.append(pltpu.make_async_copy(done.at[:, at, :], out.at[:, at, :], out_sem.at[i]))
-        stores[-1].start()
+            part[two % 2, :, first + g, :] = total[:, g * LANES : (g + 1) * LANES]
+        if first:
+            at = pl.ds(two * 2 * groups, 2 * groups)
+            done[:, at, :] = part[two % 2].astype(BF)
+            stores.append(pltpu.make_async_copy(done.at[:, at, :], out.at[:, at, :], out_sem.at[two]))
+            stores[-1].start()
     for store in stores:
         store.wait()
 
@@ -272,11 +291,11 @@
             pltpu.VMEM((count, hidden), F32),
             pltpu.VMEM((count, hidden), F32),
             pltpu.VMEM((count, hidden), BF),
-            pltpu.VMEM((count, OUT // LANES, LANES), F32),
+            pltpu.VMEM((2, count, 2 * OUT // LANES, LANES), F32),
             pltpu.VMEM((count, BLOCKS, LANES), BF),
             pltpu.SemaphoreType.DMA((3 * depth // DEEP,)),
             pltpu.SemaphoreType.DMA((depth // OUT,)),
-            pltpu.SemaphoreType.DMA((depth // OUT,)),
+            pltpu.SemaphoreType.DMA((depth // (2 * OUT),)),
         ],
         compiler_params=params(58),
         cost_estimate=cost(6 * count * depth * hidden, 6 * depth * hidden),
@@ -362,14 +381,19 @@
     slot_index = jnp.sum(same.astype(jnp.int32), axis=1)
     target = (flat_ids * CAP + slot_index).reshape(tok_rows, TOPK)
 
-    both = jnp.concatenate([target.T, shift(target.T, "c", 1)], axis=0)
+    own_choice = jnp.concatenate([expert_ids, slot_index.reshape(tok_rows, TOPK)], axis=1).astype(BF)
+    choice = jnp.concatenate([own_choice, shift(own_choice, "c", 1)], axis=1)
+    choice = jnp.pad(choice, ((0, 0), (0, LANES - choice.shape[1])))
     wide = D // NX
     stream_parts = [
-        lax.dynamic_slice_in_dim(stream, (x + NX - d) % NX * wide, wide, axis=1) for d in range(NX)
+        jnp.concatenate(
+            [lax.dynamic_slice_in_dim(stream, (x + NX - d) % NX * wide, wide, axis=1), choice], axis=1
+        )
+        for d in range(NX)
     ]
     back = target // CAP
     back = (back % (NY * NZ * NC) * NX + back // (NY * NZ * NC)) * CAP + target % CAP
-    head_normed, both, stream_parts, back = lax.optimization_barrier((head_normed, both, stream_parts, back))
+    head_normed, stream_parts, back = lax.optimization_barrier((head_normed, stream_parts, back))
 
     keep, give = project(pos, gather_line(head_normed, "x"), weights, tok_rows)
     own, *low = pair_sums(pos, keep, shift(give, "c", 1))
@@ -378,11 +402,10 @@
     stream_parts = stream_parts[:1] + [shift(stream_parts[d], "x", NX - d) for d in range(1, NX)]
     residual = quarter(pos, own, parts, stream_parts)
     quarters = gather_line(residual, "x")
-    quarters[1], both = lax.optimization_barrier((quarters[1], both))
-    targets = gather_line(both, "x")
-    quarters[3], targets = lax.optimization_barrier((quarters[3], targets))
+    where = find_places(pos, stream_parts)
+    quarters[3], where = lax.optimization_barrier((quarters[3], where))
     normed, res = norm(pos, quarters, model_gain[None])
-    message = place(pos, targets, normed, shift(normed, "c", 1))
+    message = place(where, normed, shift(normed, "c", 1))
     slot_rows = lax.all_to_all(
         message.reshape(NY * NZ, -1, D), ("y", "z"), split_axis=0, concat_axis=0, tiled=True
     ).reshape(slots, D)

time: 205 us -> 202 us (0.985)
  starting transfers between devices: 46.2 us -> 37.9 us
  blocking collectives: 42 us -> 46.4 us
  waiting for transfers between devices: 80.8 us -> 83.3 us
    ppermute x27 -> x24, starting transfers between devices: 39.7 us -> 30.9 us  [shift(): return lax.ppermute(a, axis, [(i, (i + d) % n) for i in range(n)])]
    all_to_all x1, blocking collectives: 42 us -> 46.4 us  [body(): lax.all_to_all(message.reshape(NY * NZ, -1, D), ('y', 'z'), split_axis=0,...]
    ppermute x27 -> x24, waiting for transfers between devices: 38.7 us -> 41.2 us  [shift(): return lax.ppermute(a, axis, [(i, (i + d) % n) for i in range(n)])]
  transfers between devices with their start and end apart: 28 -> 25, of which waited for: 16 -> 13; matrix products, arithmetic and copies ran while one was open for 2% -> 2% of each run, Pallas kernels for 0% -> 2%
where the time goes in v7:
time: 202 us
  waiting for transfers between devices  83.3 us (41%)
  blocking collectives  46.4 us (23%)
  starting transfers between devices  37.9 us (19%)
  Pallas kernels  27.7 us (14%)
  local copies, waits for them, and re-layouts  4.07 us (2%)
    all_to_all x1, blocking collectives, body(): lax.all_to_all(message.reshape(NY * NZ, -1, D), ('y', 'z'), split_axis=0,...  46.4 us
    all_to_all x1, waiting for transfers between devices, body(): lax.all_to_all(produced.reshape(experts, CAP * BLOCKS, LANES), ('y', 'z',...  42.1 us
    ppermute x24, waiting for transfers between devices, shift(): return lax.ppermute(a, axis, [(i, (i + d) % n) for i in range(n)])  41.2 us
    ppermute x24, starting transfers between devices, shift(): return lax.ppermute(a, axis, [(i, (i + d) % n) for i in range(n)])  30.9 us
    pallas_call x1, Pallas kernels, run_expert(): pl.pallas_call(expert_kernel, out_shape=jax.ShapeDtypeStruct((count, BLOC...  15.6 us
    all_to_all x1, starting transfers between devices, body(): lax.all_to_all(produced.reshape(experts, CAP * BLOCKS, LANES), ('y', 'z',...  7 us
  transfers between devices with their start and end apart: 25, of which 13 were waited for; matrix products, arithmetic and copies ran while one was open for 2% of the time, Pallas kernels for 2%

profile of v7, /device:TPU:1, one launch (start us, length us, event | category | flops | bytes accessed | tf_op | source)
XLA Modules:
  0.0 202.0 jit_solution(1067642583531956891)
XLA Ops:
  1.5 2.2 %collective-permute-start = (bf16[4,128,128]{2,1,0:T(8,128)(2,1)S(1)}, bf16[4,128,128]{2,1,0:T(8,128)(2,1)S(1)}, u32[]{:S(2)}, u32[]{:S(2)}) collective-permute-start(bf16[4,128,128]{2,1,0:T(8,128)(2,1)S(1)} %get-tuple-element.60), channel_id=1, source_target_pairs={{0,8},{8,16},{16,24},{24,0},{1,9},{9,17},{17,25},{25,1},{2,10},{10... | collective-permute-start | bytes 393224 | tf_op jit(solution)/shard_map/ppermute | solution.py:36
  3.7 2.6 %collective-permute-start.1 = (bf16[4,128,128]{2,1,0:T(8,128)(2,1)S(1)}, bf16[4,128,128]{2,1,0:T(8,128)(2,1)S(1)}, u32[]{:S(2)}, u32[]{:S(2)}) collective-permute-start(bf16[4,128,128]{2,1,0:T(8,128)(2,1)S(1)} %get-tuple-element.60), channel_id=1, source_target_pairs={{0,16},{8,24},{16,0},{24,8},{1,17},{9,25},{17,1},{25,9},{2,18},{10... | collective-permute-start | bytes 393224 | tf_op jit(solution)/shard_map/ppermute | solution.py:36
  12.0 2.3 %collective-permute-start.11 = (bf16[512,256]{1,0:T(8,128)(2,1)S(1)}, bf16[512,256]{1,0:T(8,128)(2,1)S(1)}, u32[]{:S(2)}, u32[]{:S(2)}) collective-permute-start(bf16[512,256]{1,0:T(8,128)(2,1)S(1)} %copy-done.6), channel_id=1, source_target_pairs={{0,16},{8,24},{16,0},{24,8},{1,17},{9,25},{17,1},{25,9},{2,18},{10... | collective-permute-start | bytes 786440 | tf_op jit(solution)/shard_map/ppermute | solution.py:36
  15.8 2.4 %collective-permute-start.4 = (bf16[4,128,128]{2,1,0:T(8,128)(2,1)S(1)}, bf16[4,128,128]{2,1,0:T(8,128)(2,1)S(1)}, u32[]{:S(2)}, u32[]{:S(2)}) collective-permute-start(bf16[4,128,128]{2,1,0:T(8,128)(2,1)S(1)} %get-tuple-element.47), channel_id=1, source_target_pairs={{0,64},{32,96},{64,0},{96,32},{1,65},{33,97},{65,1},{97,33},{2,66}... | collective-permute-start | bytes 393224 | tf_op jit(solution)/shard_map/ppermute | solution.py:36
  20.2 3.8 %collective-permute-done.4.two = bf16[4,128,128]{2,1,0:T(8,128)(2,1)S(1)} collective-permute-done((bf16[4,128,128]{2,1,0:T(8,128)(2,1)S(1)}, bf16[4,128,128]{2,1,0:T(8,128)(2,1)S(1)}, u32[]{:S(2)}, u32[]{:S(2)}) %collective-permute-start.4) | collective-permute-done | bytes 131104 | tf_op jit(solution)/shard_map/ppermute | solution.py:36
  25.0 2.2 %collective-permute-start.7 = (bf16[256,512]{1,0:T(8,128)(2,1)S(1)}, bf16[256,512]{1,0:T(8,128)(2,1)S(1)}, u32[]{:S(2)}, u32[]{:S(2)}) collective-permute-start(bf16[256,512]{1,0:T(8,128)(2,1)S(1)} %shard_map.127.refs_0_), channel_id=1, source_target_pairs={{0,96},{32,0},{64,32},{96,64},{1,97},{33,1},{65,33},{97,65},{2,98}... | collective-permute-start | bytes 786440 | tf_op jit(solution)/shard_map/ppermute | solution.py:36
  28.0 4.1 %collective-permute-done.7.refs_1_ = bf16[256,512]{1,0:T(8,128)(2,1)S(1)} collective-permute-done((bf16[256,512]{1,0:T(8,128)(2,1)S(1)}, bf16[256,512]{1,0:T(8,128)(2,1)S(1)}, u32[]{:S(2)}, u32[]{:S(2)}) %collective-permute-start.7) | collective-permute-done | bytes 262176 | tf_op jit(solution)/shard_map/ppermute | solution.py:36
  32.1 2.8 %collective-permute-done.8.refs_2_ = bf16[256,512]{1,0:T(8,128)(2,1)S(1)} collective-permute-done((bf16[256,512]{1,0:T(8,128)(2,1)S(1)}, bf16[256,512]{1,0:T(8,128)(2,1)S(1)}, u32[]{:S(2)}, u32[]{:S(2)}) %collective-permute-start.8) | collective-permute-done | bytes 262176 | tf_op jit(solution)/shard_map/ppermute | solution.py:36
  34.9 7.6 %collective-permute-done.9.refs_3_ = bf16[256,512]{1,0:T(8,128)(2,1)S(1)} collective-permute-done((bf16[256,512]{1,0:T(8,128)(2,1)S(1)}, bf16[256,512]{1,0:T(8,128)(2,1)S(1)}, u32[]{:S(2)}, u32[]{:S(2)}) %collective-permute-start.9) | collective-permute-done | bytes 262176 | tf_op jit(solution)/shard_map/ppermute | solution.py:36
  45.1 2.3 %collective-permute-done.13.got = bf16[16,32,1024]{2,1,0:T(8,128)(2,1)S(1)} collective-permute-done((bf16[16,32,1024]{2,1,0:T(8,128)(2,1)S(1)}, bf16[16,32,1024]{2,1,0:T(8,128)(2,1)S(1)}, u32[]{:S(2)}, u32[]{:S(2)}) %collective-permute-start.13) | collective-permute-done | bytes 1048608 | tf_op jit(solution)/shard_map/ppermute | solution.py:36
  49.8 3.3 %collective-permute-start.15 = (bf16[4,32,1024]{2,1,0:T(8,128)(2,1)S(1)}, bf16[4,32,1024]{2,1,0:T(8,128)(2,1)S(1)}, u32[]{:S(2)}, u32[]{:S(2)}) collective-permute-start(bf16[4,32,1024]{2,1,0:T(8,128)(2,1)S(1)} %get-tuple-element.37), channel_id=1, source_target_pairs={{0,4},{2,6},{4,0},{6,2},{1,5},{3,7},{5,1},{7,3},{8,12},{10,14},{12... | collective-permute-start | bytes 786440 | tf_op jit(solution)/shard_map/ppermute | solution.py:36
  53.8 4.5 %collective-permute-done.14.one = bf16[4,32,1024]{2,1,0:T(8,128)(2,1)S(1)} collective-permute-done((bf16[4,32,1024]{2,1,0:T(8,128)(2,1)S(1)}, bf16[4,32,1024]{2,1,0:T(8,128)(2,1)S(1)}, u32[]{:S(2)}, u32[]{:S(2)}) %collective-permute-start.14) | collective-permute-done | bytes 262176 | tf_op jit(solution)/shard_map/ppermute | solution.py:36
  60.0 4.8 %collective-permute-done.15.two = bf16[4,32,1024]{2,1,0:T(8,128)(2,1)S(1)} collective-permute-done((bf16[4,32,1024]{2,1,0:T(8,128)(2,1)S(1)}, bf16[4,32,1024]{2,1,0:T(8,128)(2,1)S(1)}, u32[]{:S(2)}, u32[]{:S(2)}) %collective-permute-start.15) | collective-permute-done | bytes 262176 | tf_op jit(solution)/shard_map/ppermute | solution.py:36
  65.6 2.7 %collective-permute-start.21 = (bf16[4,32,1024]{2,1,0:T(8,128)(2,1)S(1)}, bf16[4,32,1024]{2,1,0:T(8,128)(2,1)S(1)}, u32[]{:S(2)}, u32[]{:S(2)}) collective-permute-start(bf16[4,32,1024]{2,1,0:T(8,128)(2,1)S(1)} %shard_map.130.refs_0_), channel_id=1, source_target_pairs={{0,96},{32,0},{64,32},{96,64},{1,97},{33,1},{65,33},{97,65},{2,98}... | collective-permute-start | bytes 786440 | tf_op jit(solution)/shard_map/ppermute | solution.py:36
  68.3 2.1 %shard_map.131.where = bf16[384,256]{1,0:T(8,128)(2,1)S(1)} custom-call(s32[4]{0:T(128)S(1)} %pad_add_fusion.pos, bf16[32,1152]{1,0:T(8,128)(2,1)S(1)} %get-tuple-element.39.refs_0_, bf16[32,1152]{1,0:T(8,128)(2,1)S(1)} %collective-permute-done.17.refs_1_, bf16[32,1152]{1,0:T(8,128)(2,1)S(1)} %collective-permute-done.18.refs_2_, ...), custom_call_target="tpu_custom_call" | custom-call | flops 2097152 | bytes 262144 | tf_op jit(solution)/shard_map/pallas_call | solution.py:203
  70.4 2.2 %collective-permute-done.20.refs_3_ = bf16[4,32,1024]{2,1,0:T(8,128)(2,1)S(1)} collective-permute-done((bf16[4,32,1024]{2,1,0:T(8,128)(2,1)S(1)}, bf16[4,32,1024]{2,1,0:T(8,128)(2,1)S(1)}, u32[]{:S(2)}, u32[]{:S(2)}) %collective-permute-start.20) | collective-permute-done | bytes 262176 | tf_op jit(solution)/shard_map/ppermute | solution.py:36
  73.7 4.9 %collective-permute-done.22.refs_2_ = bf16[4,32,1024]{2,1,0:T(8,128)(2,1)S(1)} collective-permute-done((bf16[4,32,1024]{2,1,0:T(8,128)(2,1)S(1)}, bf16[4,32,1024]{2,1,0:T(8,128)(2,1)S(1)}, u32[]{:S(2)}, u32[]{:S(2)}) %collective-permute-start.22) | collective-permute-done | bytes 262176 | tf_op jit(solution)/shard_map/ppermute | solution.py:36
  80.3 2.6 %collective-permute-start.23 = (bf16[128,4096]{1,0:T(8,128)(2,1)S(1)}, bf16[128,4096]{1,0:T(8,128)(2,1)S(1)}, u32[]{:S(2)}, u32[]{:S(2)}) collective-permute-start(bf16[128,4096]{1,0:T(8,128)(2,1)S(1)} %get-tuple-element.45.own), channel_id=1, source_target_pairs={{0,1},{1,0},{2,3},{3,2},{4,5},{5,4},{6,7},{7,6},{8,9},{9,8},{10,11... | collective-permute-start | bytes 3145736 | tf_op jit(solution)/shard_map/ppermute | solution.py:36
  82.9 2.3 %collective-permute-done.23.other = bf16[128,4096]{1,0:T(8,128)(2,1)S(1)} collective-permute-done((bf16[128,4096]{1,0:T(8,128)(2,1)S(1)}, bf16[128,4096]{1,0:T(8,128)(2,1)S(1)}, u32[]{:S(2)}, u32[]{:S(2)}) %collective-permute-start.23) | collective-permute-done | bytes 1048608 | tf_op jit(solution)/shard_map/ppermute | solution.py:36
  86.9 46.4 %all_to_all.10 = bf16[16,24,4096]{2,1,0:T(8,128)(2,1)} all-to-all(bf16[16,24,4096]{2,1,0:T(8,128)(2,1)S(1)} %bitcast.45), channel_id=1, replica_groups=mesh['x'=4,'y'=4,'z'=4,'c'=2] {'y','z'}, dimensions={0} | all-to-all | bytes 6291456 | tf_op jit(solution)/shard_map/all_to_all | solution.py:409
  133.3 15.6 %shard_map.134 = bf16[384,32,128]{2,1,0:T(8,128)(2,1)} custom-call(f32[1,3]{1,0:T(1,128)} %scale.1, bf16[384,4096]{1,0:T(8,128)(2,1)} %bitcast.49, bf16[4096,768]{1,0:T(8,128)(2,1)} %bitcast.53, bf16[4096,768]{1,0:T(8,128)(2,1)} %bitcast.54, bf16[768,4096]{1,0:T(8,128)(2,1)} %bitcast.55), custom_call_target="tpu_custom_call" | custom-call | flops 7247757312 | bytes 18874368 | tf_op jit(solution)/shard_map/pallas_call | solution.py:281
  148.9 7.0 %all-to-all-start.1 = ((bf16[128,96,128]{2,1,0:T(8,128)(2,1)}), bf16[128,96,128]{2,1,0:T(8,128)(2,1)S(1)}, u32[]{:S(2)}, u32[]{:S(2)}) async-start(bf16[128,96,128]{2,1,0:T(8,128)(2,1)} %bitcast.48), calls=%async_computation.1 | async-start | bytes 6291456 | tf_op jit(solution)/shard_map/all_to_all | solution.py:413
  156.0 42.1 %all-to-all-done.1 = bf16[128,96,128]{2,1,0:T(8,128)(2,1)S(1)} async-done(((bf16[128,96,128]{2,1,0:T(8,128)(2,1)}), bf16[128,96,128]{2,1,0:T(8,128)(2,1)S(1)}, u32[]{:S(2)}, u32[]{:S(2)}) %all-to-all-start.1) | async-done | bytes 3145760 | tf_op jit(solution)/shard_map/all_to_all | solution.py:413
  199.1 2.9 %shard_map.135 = bf16[32,4096]{1,0:T(8,128)(2,1)} custom-call(s32[32,8]{1,0:T(8,128)S(1)} %get-tuple-element.26.target, f32[32,8]{1,0:T(8,128)S(1)} %copy.38.gates, bf16[384,32,128]{2,1,0:T(8,128)(2,1)S(1)} %bitcast.44, bf16[32,4096]{1,0:T(8,128)(2,1)S(1)} %copy-done.2), custom_call_target="tpu_custom_call" | custom-call | flops 1048576 | bytes 4194304 | tf_op jit(solution)/shard_map/pallas_call | solution.py:323
  (71 shorter events, 26.0 us)
Async XLA Ops:
  1.5 12.9 %collective-permute-start = (bf16[4,128,128]{2,1,0:T(8,128)(2,1)S(1)}, bf16[4,128,128]{2,1,0:T(8,128)(2,1)S(1)}, u32[]{:S(2)}, u32[]{:S(2)}) collective-permute-start(bf16[4,128,128]{2,1,0:T(8,128)(2,1)S(1)} %get-tuple-element.60), channel_id=1, source_target_pairs={{0,8},{8,16},{16,24},{24,0},{1,9},{9,17},{17,25},{25,1},{2,10},{10... | collective-permute-start | bytes 393224 | tf_op jit(solution)/shard_map/ppermute | solution.py:36
  3.7 10.7 %collective-permute-start.1 = (bf16[4,128,128]{2,1,0:T(8,128)(2,1)S(1)}, bf16[4,128,128]{2,1,0:T(8,128)(2,1)S(1)}, u32[]{:S(2)}, u32[]{:S(2)}) collective-permute-start(bf16[4,128,128]{2,1,0:T(8,128)(2,1)S(1)} %get-tuple-element.60), channel_id=1, source_target_pairs={{0,16},{8,24},{16,0},{24,8},{1,17},{9,25},{17,1},{25,9},{2,18},{10... | collective-permute-start | bytes 393224 | tf_op jit(solution)/shard_map/ppermute | solution.py:36
  6.3 8.1 %collective-permute-start.2 = (bf16[4,128,128]{2,1,0:T(8,128)(2,1)S(1)}, bf16[4,128,128]{2,1,0:T(8,128)(2,1)S(1)}, u32[]{:S(2)}, u32[]{:S(2)}) collective-permute-start(bf16[4,128,128]{2,1,0:T(8,128)(2,1)S(1)} %get-tuple-element.60), channel_id=1, source_target_pairs={{0,24},{8,0},{16,8},{24,16},{1,25},{9,1},{17,9},{25,17},{2,26},{10... | collective-permute-start | bytes 393224 | tf_op jit(solution)/shard_map/ppermute | solution.py:36
  8.6 3.4 %collective-permute-start.6 = (bf16[32,16]{1,0:T(8,128)(2,1)S(1)}, bf16[32,16]{1,0:T(8,128)(2,1)S(1)}, u32[]{:S(2)}, u32[]{:S(2)}) collective-permute-start(bf16[32,16]{1,0:T(8,128)(2,1)S(1)} %pad_maximum_fusion.4), channel_id=1, source_target_pairs={{0,1},{1,0},{2,3},{3,2},{4,5},{5,4},{6,7},{7,6},{8,9},{9,8},{10,11... | collective-permute-start | bytes 3080 | tf_op jit(solution)/shard_map/ppermute | solution.py:36
  10.2 17.8 %collective-permute-start.10 = (bf16[512,256]{1,0:T(8,128)(2,1)}, bf16[512,256]{1,0:T(8,128)(2,1)S(1)}, u32[]{:S(2)}, u32[]{:S(2)}) collective-permute-start(bf16[512,256]{1,0:T(8,128)(2,1)} %refs_4_.1), channel_id=1, source_target_pairs={{0,24},{8,0},{16,8},{24,16},{1,25},{9,1},{17,9},{25,17},{2,26},{10... | collective-permute-start | bytes 786440 | tf_op jit(solution)/shard_map/ppermute | solution.py:36
  12.0 16.0 %collective-permute-start.11 = (bf16[512,256]{1,0:T(8,128)(2,1)S(1)}, bf16[512,256]{1,0:T(8,128)(2,1)S(1)}, u32[]{:S(2)}, u32[]{:S(2)}) collective-permute-start(bf16[512,256]{1,0:T(8,128)(2,1)S(1)} %copy-done.6), channel_id=1, source_target_pairs={{0,16},{8,24},{16,0},{24,8},{1,17},{9,25},{17,1},{25,9},{2,18},{10... | collective-permute-start | bytes 786440 | tf_op jit(solution)/shard_map/ppermute | solution.py:36
  14.5 5.7 %collective-permute-start.3 = (bf16[4,128,128]{2,1,0:T(8,128)(2,1)S(1)}, bf16[4,128,128]{2,1,0:T(8,128)(2,1)S(1)}, u32[]{:S(2)}, u32[]{:S(2)}) collective-permute-start(bf16[4,128,128]{2,1,0:T(8,128)(2,1)S(1)} %get-tuple-element.47), channel_id=1, source_target_pairs={{0,32},{32,64},{64,96},{96,0},{1,33},{33,65},{65,97},{97,1},{2,34}... | collective-permute-start | bytes 393224 | tf_op jit(solution)/shard_map/ppermute | solution.py:36
  15.8 8.2 %collective-permute-start.4 = (bf16[4,128,128]{2,1,0:T(8,128)(2,1)S(1)}, bf16[4,128,128]{2,1,0:T(8,128)(2,1)S(1)}, u32[]{:S(2)}, u32[]{:S(2)}) collective-permute-start(bf16[4,128,128]{2,1,0:T(8,128)(2,1)S(1)} %get-tuple-element.47), channel_id=1, source_target_pairs={{0,64},{32,96},{64,0},{96,32},{1,65},{33,97},{65,1},{97,33},{2,66}... | collective-permute-start | bytes 393224 | tf_op jit(solution)/shard_map/ppermute | solution.py:36
  18.2 5.8 %collective-permute-start.5 = (bf16[4,128,128]{2,1,0:T(8,128)(2,1)S(1)}, bf16[4,128,128]{2,1,0:T(8,128)(2,1)S(1)}, u32[]{:S(2)}, u32[]{:S(2)}) collective-permute-start(bf16[4,128,128]{2,1,0:T(8,128)(2,1)S(1)} %get-tuple-element.47), channel_id=1, source_target_pairs={{0,96},{32,0},{64,32},{96,64},{1,97},{33,1},{65,33},{97,65},{2,98}... | collective-permute-start | bytes 393224 | tf_op jit(solution)/shard_map/ppermute | solution.py:36
  20.2 7.8 %collective-permute-start.12 = (bf16[512,256]{1,0:T(8,128)(2,1)S(1)}, bf16[512,256]{1,0:T(8,128)(2,1)S(1)}, u32[]{:S(2)}, u32[]{:S(2)}) collective-permute-start(bf16[512,256]{1,0:T(8,128)(2,1)S(1)} %copy-done.6), channel_id=1, source_target_pairs={{0,8},{8,16},{16,24},{24,0},{1,9},{9,17},{17,25},{25,1},{2,10},{10... | collective-permute-start | bytes 786440 | tf_op jit(solution)/shard_map/ppermute | solution.py:36
  25.0 7.2 %collective-permute-start.7 = (bf16[256,512]{1,0:T(8,128)(2,1)S(1)}, bf16[256,512]{1,0:T(8,128)(2,1)S(1)}, u32[]{:S(2)}, u32[]{:S(2)}) collective-permute-start(bf16[256,512]{1,0:T(8,128)(2,1)S(1)} %shard_map.127.refs_0_), channel_id=1, source_target_pairs={{0,96},{32,0},{64,32},{96,64},{1,97},{33,1},{65,33},{97,65},{2,98}... | collective-permute-start | bytes 786440 | tf_op jit(solution)/shard_map/ppermute | solution.py:36
  27.2 7.8 %collective-permute-start.8 = (bf16[256,512]{1,0:T(8,128)(2,1)S(1)}, bf16[256,512]{1,0:T(8,128)(2,1)S(1)}, u32[]{:S(2)}, u32[]{:S(2)}) collective-permute-start(bf16[256,512]{1,0:T(8,128)(2,1)S(1)} %shard_map.127.refs_0_), channel_id=1, source_target_pairs={{0,64},{32,96},{64,0},{96,32},{1,65},{33,97},{65,1},{97,33},{2,66}... | collective-permute-start | bytes 786440 | tf_op jit(solution)/shard_map/ppermute | solution.py:36
  28.0 14.5 %collective-permute-start.9 = (bf16[256,512]{1,0:T(8,128)(2,1)S(1)}, bf16[256,512]{1,0:T(8,128)(2,1)S(1)}, u32[]{:S(2)}, u32[]{:S(2)}) collective-permute-start(bf16[256,512]{1,0:T(8,128)(2,1)S(1)} %shard_map.127.refs_0_), channel_id=1, source_target_pairs={{0,32},{32,64},{64,96},{96,0},{1,33},{33,65},{65,97},{97,1},{2,34}... | collective-permute-start | bytes 786440 | tf_op jit(solution)/shard_map/ppermute | solution.py:36
  48.1 10.2 %collective-permute-start.14 = (bf16[4,32,1024]{2,1,0:T(8,128)(2,1)S(1)}, bf16[4,32,1024]{2,1,0:T(8,128)(2,1)S(1)}, u32[]{:S(2)}, u32[]{:S(2)}) collective-permute-start(bf16[4,32,1024]{2,1,0:T(8,128)(2,1)S(1)} %get-tuple-element.31), channel_id=1, source_target_pairs={{0,2},{2,4},{4,6},{6,0},{1,3},{3,5},{5,7},{7,1},{8,10},{10,12},{12... | collective-permute-start | bytes 786440 | tf_op jit(solution)/shard_map/ppermute | solution.py:36
  49.8 15.0 %collective-permute-start.15 = (bf16[4,32,1024]{2,1,0:T(8,128)(2,1)S(1)}, bf16[4,32,1024]{2,1,0:T(8,128)(2,1)S(1)}, u32[]{:S(2)}, u32[]{:S(2)}) collective-permute-start(bf16[4,32,1024]{2,1,0:T(8,128)(2,1)S(1)} %get-tuple-element.37), channel_id=1, source_target_pairs={{0,4},{2,6},{4,0},{6,2},{1,5},{3,7},{5,1},{7,3},{8,12},{10,14},{12... | collective-permute-start | bytes 786440 | tf_op jit(solution)/shard_map/ppermute | solution.py:36
  53.1 11.7 %collective-permute-start.16 = (bf16[4,32,1024]{2,1,0:T(8,128)(2,1)S(1)}, bf16[4,32,1024]{2,1,0:T(8,128)(2,1)S(1)}, u32[]{:S(2)}, u32[]{:S(2)}) collective-permute-start(bf16[4,32,1024]{2,1,0:T(8,128)(2,1)S(1)} %get-tuple-element.38), channel_id=1, source_target_pairs={{0,6},{2,0},{4,2},{6,4},{1,7},{3,1},{5,3},{7,5},{8,14},{10,8},{12,... | collective-permute-start | bytes 786440 | tf_op jit(solution)/shard_map/ppermute | solution.py:36
  58.3 6.5 %collective-permute-start.17 = (bf16[32,1152]{1,0:T(8,128)(2,1)S(1)}, bf16[32,1152]{1,0:T(8,128)(2,1)S(1)}, u32[]{:S(2)}, u32[]{:S(2)}) collective-permute-start(bf16[32,1152]{1,0:T(8,128)(2,1)S(1)} %get-tuple-element.40), channel_id=1, source_target_pairs={{0,96},{32,0},{64,32},{96,64},{1,97},{33,1},{65,33},{97,65},{2,98}... | collective-permute-start | bytes 221192 | tf_op jit(solution)/shard_map/ppermute | solution.py:36
  58.6 6.2 %collective-permute-start.18 = (bf16[32,1152]{1,0:T(8,128)(2,1)S(1)}, bf16[32,1152]{1,0:T(8,128)(2,1)S(1)}, u32[]{:S(2)}, u32[]{:S(2)}) collective-permute-start(bf16[32,1152]{1,0:T(8,128)(2,1)S(1)} %get-tuple-element.41), channel_id=1, source_target_pairs={{0,64},{32,96},{64,0},{96,32},{1,65},{33,97},{65,1},{97,33},{2,66}... | collective-permute-start | bytes 221192 | tf_op jit(solution)/shard_map/ppermute | solution.py:36
  59.5 5.3 %collective-permute-start.19 = (bf16[32,1152]{1,0:T(8,128)(2,1)S(1)}, bf16[32,1152]{1,0:T(8,128)(2,1)S(1)}, u32[]{:S(2)}, u32[]{:S(2)}) collective-permute-start(bf16[32,1152]{1,0:T(8,128)(2,1)S(1)} %get-tuple-element.42), channel_id=1, source_target_pairs={{0,32},{32,64},{64,96},{96,0},{1,33},{33,65},{65,97},{97,1},{2,34}... | collective-permute-start | bytes 221192 | tf_op jit(solution)/shard_map/ppermute | solution.py:36
  65.5 7.1 %collective-permute-start.20 = (bf16[4,32,1024]{2,1,0:T(8,128)(2,1)S(1)}, bf16[4,32,1024]{2,1,0:T(8,128)(2,1)S(1)}, u32[]{:S(2)}, u32[]{:S(2)}) collective-permute-start(bf16[4,32,1024]{2,1,0:T(8,128)(2,1)S(1)} %shard_map.130.refs_0_), channel_id=1, source_target_pairs={{0,32},{32,64},{64,96},{96,0},{1,33},{33,65},{65,97},{97,1},{2,34}... | collective-permute-start | bytes 786440 | tf_op jit(solution)/shard_map/ppermute | solution.py:36
  65.6 8.1 %collective-permute-start.21 = (bf16[4,32,1024]{2,1,0:T(8,128)(2,1)S(1)}, bf16[4,32,1024]{2,1,0:T(8,128)(2,1)S(1)}, u32[]{:S(2)}, u32[]{:S(2)}) collective-permute-start(bf16[4,32,1024]{2,1,0:T(8,128)(2,1)S(1)} %shard_map.130.refs_0_), channel_id=1, source_target_pairs={{0,96},{32,0},{64,32},{96,64},{1,97},{33,1},{65,33},{97,65},{2,98}... | collective-permute-start | bytes 786440 | tf_op jit(solution)/shard_map/ppermute | solution.py:36
  68.3 10.4 %collective-permute-start.22 = (bf16[4,32,1024]{2,1,0:T(8,128)(2,1)S(1)}, bf16[4,32,1024]{2,1,0:T(8,128)(2,1)S(1)}, u32[]{:S(2)}, u32[]{:S(2)}) collective-permute-start(bf16[4,32,1024]{2,1,0:T(8,128)(2,1)S(1)} %shard_map.130.refs_0_), channel_id=1, source_target_pairs={{0,64},{32,96},{64,0},{96,32},{1,65},{33,97},{65,1},{97,33},{2,66}... | collective-permute-start | bytes 786440 | tf_op jit(solution)/shard_map/ppermute | solution.py:36
  80.3 4.8 %collective-permute-start.23 = (bf16[128,4096]{1,0:T(8,128)(2,1)S(1)}, bf16[128,4096]{1,0:T(8,128)(2,1)S(1)}, u32[]{:S(2)}, u32[]{:S(2)}) collective-permute-start(bf16[128,4096]{1,0:T(8,128)(2,1)S(1)} %get-tuple-element.45.own), channel_id=1, source_target_pairs={{0,1},{1,0},{2,3},{3,2},{4,5},{5,4},{6,7},{7,6},{8,9},{9,8},{10,11... | collective-permute-start | bytes 3145736 | tf_op jit(solution)/shard_map/ppermute | solution.py:36
  148.9 49.2 %all-to-all-start.1 = ((bf16[128,96,128]{2,1,0:T(8,128)(2,1)}), bf16[128,96,128]{2,1,0:T(8,128)(2,1)S(1)}, u32[]{:S(2)}, u32[]{:S(2)}) async-start(bf16[128,96,128]{2,1,0:T(8,128)(2,1)} %bitcast.48), calls=%async_computation.1 | async-start | bytes 6291456 | tf_op jit(solution)/shard_map/all_to_all | solution.py:413
  (10 other events, 116.1 us)

commit v8 on v4

--- a/solution.py
+++ b/solution.py
@@ -12,7 +12,7 @@
 NX, NY, NZ, NC = 4, 4, 4, 2
 LANES = 128
 BLOCKS = D // LANES
-WIDE = 256
+DEEP = 512
 OUT = 1024
 BF = jnp.bfloat16
 F32 = jnp.float32
@@ -125,6 +125,25 @@
         compiler_params=params(16),
         cost_estimate=cost(1 << 20, 5 << 20),
     )(pos, keep, got)
+
+
+def sum_kernel(own, one, two, three, *outs):
+    for dx, out in enumerate(outs):
+        total = own[dx] + one[dx].astype(F32) + two[dx].astype(F32) + three[dx].astype(F32)
+        out[...] = total.astype(out.dtype)
+
+
+def sum_z(own, parts):
+    shape = own.shape[1:]
+    low = jax.ShapeDtypeStruct(shape, BF)
+    return pl.pallas_call(
+        sum_kernel,
+        out_shape=(jax.ShapeDtypeStruct(shape, F32), low, low, low),
+        in_specs=[VMEM] * NZ,
+        out_specs=(VMEM,) * NX,
+        compiler_params=params(16),
+        cost_estimate=cost(1 << 20, 2 << 20),
+    )(own, *parts)
 
 
 def place_kernel(pos, target, own, one, two, three, stream, gain, res, message, total, scaled):
@@ -178,46 +197,75 @@
     )(pos, target, *parts, stream, gain)
 
 
-def expert_kernel(scale, rows, gate, up, down, out, act):
-    step = pl.program_id(0)
-    wide = act.shape[0]
-
-    @pl.when(step < wide)
-    def _():
-        x = rows[...]
-        gate_part = jnp.dot(x, gate[...], preferred_element_type=F32) * scale[0, 0]
-        up_part = jnp.dot(x, up[...], preferred_element_type=F32) * scale[0, 1]
-        act[step] = (gate_part / (1.0 + jnp.exp(-gate_part)) * up_part).astype(BF)
-
-    @pl.when(step >= wide)
-    def _():
-        total = jnp.dot(act[0], down[0:WIDE], preferred_element_type=F32)
-        for j in range(1, wide):
-            total += jnp.dot(act[j], down[j * WIDE : (j + 1) * WIDE], preferred_element_type=F32)
-        out[...] = (total * scale[0, 2]).astype(BF)
+def expert_kernel(scale, rows, gate, up, down, out, x, wg, wu, wd, gates, ups, act, part, done, in_sem, down_sem, out_sem):
+    depth, hidden = wg.shape
+    groups = OUT // LANES
+    loads, downs, stores = [], [], []
+    for i, j in enumerate(range(0, depth, DEEP)):
+        at = pl.ds(j, DEEP)
+        for k, (source, into) in enumerate(((rows, x), (gate, wg), (up, wu))):
+            view = (source.at[:, at], into.at[:, at]) if k == 0 else (source.at[at], into.at[at])
+            loads.append(pltpu.make_async_copy(*view, in_sem.at[3 * i + k]))
+            loads[-1].start()
+    for i, j in enumerate(range(0, depth, OUT)):
+        at = pl.ds(j, OUT)
+        downs.append(pltpu.make_async_copy(down.at[:, at], wd.at[:, at], down_sem.at[i]))
+        downs[-1].start()
+    for i, j in enumerate(range(0, depth, DEEP)):
+        for load in loads[3 * i : 3 * i + 3]:
+            load.wait()
+        cut = x[:, j : j + DEEP]
+        gate_part = jnp.dot(cut, wg[j : j + DEEP], preferred_element_type=F32)
+        up_part = jnp.dot(cut, wu[j : j + DEEP], preferred_element_type=F32)
+        if i == 0:
+            gates[...] = gate_part
+            ups[...] = up_part
+        else:
+            gates[...] += gate_part
+            ups[...] += up_part
+    gate_part = gates[...] * scale[0, 0]
+    act[...] = (gate_part / (1.0 + jnp.exp(-gate_part)) * (ups[...] * scale[0, 1])).astype(BF)
+    for load in downs:
+        load.wait()
+    for i, j in enumerate(range(0, depth, OUT)):
+        total = jnp.dot(act[...], wd[:, j : j + OUT], preferred_element_type=F32) * scale[0, 2]
+        two, first = i // 2, i % 2 * groups
+        for g in range(groups):
+            part[two % 2, :, first + g, :] = total[:, g * LANES : (g + 1) * LANES]
+        if first:
+            at = pl.ds(two * 2 * groups, 2 * groups)
+            done[:, at, :] = part[two % 2].astype(BF)
+            stores.append(pltpu.make_async_copy(done.at[:, at, :], out.at[:, at, :], out_sem.at[two]))
+            stores[-1].start()
+    for store in stores:
+        store.wait()
 
 
 def run_expert(scale, rows, gate, up, down):
     count, depth = rows.shape
     hidden = gate.shape[1]
-    wide = hidden // WIDE
+    anywhere = pl.BlockSpec(memory_space=pl.ANY)
     return pl.pallas_call(
         expert_kernel,
-        out_shape=jax.ShapeDtypeStruct((count, depth), BF),
-        grid=(wide + depth // OUT,),
-        in_specs=[
-            pl.BlockSpec(memory_space=pltpu.SMEM),
-            pl.BlockSpec((count, depth), lambda i: (0, 0)),
-            pl.BlockSpec((depth, WIDE), lambda i: (0, jnp.minimum(i, wide - 1))),
-            pl.BlockSpec((depth, WIDE), lambda i: (0, jnp.minimum(i, wide - 1))),
-            pl.BlockSpec((hidden, OUT), lambda i: (0, jnp.maximum(i - wide, 0))),
+        out_shape=jax.ShapeDtypeStruct((count, BLOCKS, LANES), BF),
+        in_specs=[SMEM] + [anywhere] * 4,
+        out_specs=anywhere,
+        scratch_shapes=[
+            pltpu.VMEM((count, depth), BF),
+            pltpu.VMEM((depth, hidden), BF),
+            pltpu.VMEM((depth, hidden), BF),
+            pltpu.VMEM((hidden, depth), BF),
+            pltpu.VMEM((count, hidden), F32),
+            pltpu.VMEM((count, hidden), F32),
+            pltpu.VMEM((count, hidden), BF),
+            pltpu.VMEM((2, count, 2 * OUT // LANES, LANES), F32),
+            pltpu.VMEM((count, BLOCKS, LANES), BF),
+            pltpu.SemaphoreType.DMA((3 * depth // DEEP,)),
+            pltpu.SemaphoreType.DMA((depth // OUT,)),
+            pltpu.SemaphoreType.DMA((depth // (2 * OUT),)),
         ],
-        out_specs=pl.BlockSpec((count, OUT), lambda i: (0, jnp.maximum(i - wide, 0))),
-        scratch_shapes=[pltpu.VMEM((wide, count, WIDE), BF)],
-        compiler_params=pltpu.CompilerParams(vmem_limit_bytes=60 << 20),
-        cost_estimate=pl.CostEstimate(
-            flops=6 * count * depth * hidden, bytes_accessed=6 * depth * hidden, transcendentals=count * hidden
-        ),
+        compiler_params=params(58),
+        cost_estimate=cost(6 * count * depth * hidden, 6 * depth * hidden),
     )(scale, rows, gate, up, down)
 
 
@@ -309,13 +357,12 @@
     tokens = [head_normed] + [to_x(head_normed, NX - d) for d in range(1, NX)]
     keep, give = project(pos, tokens, weights, tok_rows)
     own, *low = pair_sums(pos, keep, swap_core(give))
-    for d in range(1, NZ):
-        own = own + to_z(low[d - 1], d).astype(F32)
-    parts = [own[0]] + [to_x(own[d].astype(BF), d) for d in range(1, NX)]
+    sums = sum_z(own, [to_z(low[d - 1], d) for d in range(1, NZ)])
+    parts = [sums[0]] + [to_x(sums[d], d) for d in range(1, NX)]
     res, message = place(pos, target, parts, stream, model_gain[None], slots)
     slot_rows = exchange(message).reshape(slots, D)
     produced = run_expert(weight_scales, slot_rows, gate_weight[0], up_weight[0], down_weight[0])
-    results = exchange(produced.reshape(slots, BLOCKS, LANES))
+    results = exchange(produced)
     return mix(target, expert_gates, results, res)
 
 

time: 205 us -> 193 us (0.941)
  local copies, waits for them, and re-layouts: 14.6 us -> 6.85 us
    another operation x1 -> x0, local copies, waits for them, and re-layouts: 5.89 us -> none  [exchange(): message = rows.reshape(experts, CAP * BLOCKS, LANES)]
    pallas_call x1 -> x2, Pallas kernels: 16 us -> 15.7 us  [the longest x1 15.6 us: run_expert(): pl.pallas_call(expert_kernel, out_shape=jax.ShapeDtypeStruct((count, BLOC...]
  transfers between devices with their start and end apart: 20 -> 20, of which waited for: 14 -> 13; matrix products, arithmetic and copies ran while one was open for 1% -> 1% of each run, Pallas kernels for 0% -> 0%
where the time goes in v8:
time: 193 us
  waiting for transfers between devices  74 us (38%)
  blocking collectives  52.6 us (27%)
  starting transfers between devices  31.9 us (17%)
  Pallas kernels  25.3 us (13%)
  local copies, waits for them, and re-layouts  6.85 us (4%)
    all_to_all x1, blocking collectives, exchange(): lax.all_to_all(message, ('seq', 'head'), split_axis=0, concat_axis=0, til...  52.6 us
    all_to_all x1, waiting for transfers between devices, exchange(): lax.all_to_all(message, ('seq', 'head'), split_axis=0, concat_axis=0, til...  41.9 us
    pallas_call x1, Pallas kernels, run_expert(): pl.pallas_call(expert_kernel, out_shape=jax.ShapeDtypeStruct((count, BLOC...  15.6 us
    ppermute x9, waiting for transfers between devices, to_x(): return lax.ppermute(a, 'seq', pairs)  15.1 us
    ppermute x3, waiting for transfers between devices, to_z(): return lax.ppermute(a, 'head', pairs)  10.5 us
    ppermute x9, starting transfers between devices, to_x(): return lax.ppermute(a, 'seq', pairs)  10 us
    ppermute x6, starting transfers between devices, to_y(): return lax.ppermute(a, 'seq', pairs)  8.66 us
    ppermute x3, starting transfers between devices, to_z(): return lax.ppermute(a, 'head', pairs)  5.74 us
  transfers between devices with their start and end apart: 20, of which 13 were waited for; matrix products, arithmetic and copies ran while one was open for 1% of the time, Pallas kernels for 0%

profile of v8, /device:TPU:1, one launch (start us, length us, event | category | flops | bytes accessed | tf_op | source)
XLA Modules:
  0.0 192.9 jit_solution(12575692049343804841)
XLA Ops:
  1.5 2.2 %collective-permute-start = (bf16[4,128,128]{2,1,0:T(8,128)(2,1)S(1)}, bf16[4,128,128]{2,1,0:T(8,128)(2,1)S(1)}, u32[]{:S(2)}, u32[]{:S(2)}) collective-permute-start(bf16[4,128,128]{2,1,0:T(8,128)(2,1)S(1)} %get-tuple-element.31), channel_id=1, source_target_pairs={{0,8},{8,16},{16,24},{24,0},{32,40},{40,48},{48,56},{56,32},{64,72... | collective-permute-start | bytes 393224 | tf_op jit(solution)/shard_map/ppermute | solution.py:40
  3.7 2.6 %collective-permute-start.1 = (bf16[4,128,128]{2,1,0:T(8,128)(2,1)S(1)}, bf16[4,128,128]{2,1,0:T(8,128)(2,1)S(1)}, u32[]{:S(2)}, u32[]{:S(2)}) collective-permute-start(bf16[4,128,128]{2,1,0:T(8,128)(2,1)S(1)} %get-tuple-element.31), channel_id=1, source_target_pairs={{0,16},{8,24},{16,0},{24,8},{32,48},{40,56},{48,32},{56,40},{64,80... | collective-permute-start | bytes 393224 | tf_op jit(solution)/shard_map/ppermute | solution.py:40
  8.2 3.8 %collective-permute-done.1 = bf16[4,128,128]{2,1,0:T(8,128)(2,1)S(1)} collective-permute-done((bf16[4,128,128]{2,1,0:T(8,128)(2,1)S(1)}, bf16[4,128,128]{2,1,0:T(8,128)(2,1)S(1)}, u32[]{:S(2)}, u32[]{:S(2)}) %collective-permute-start.1) | collective-permute-done | bytes 131104 | tf_op jit(solution)/shard_map/ppermute | solution.py:40
  13.4 2.4 %collective-permute-start.4 = (bf16[4,128,128]{2,1,0:T(8,128)(2,1)S(1)}, bf16[4,128,128]{2,1,0:T(8,128)(2,1)S(1)}, u32[]{:S(2)}, u32[]{:S(2)}) collective-permute-start(bf16[4,128,128]{2,1,0:T(8,128)(2,1)S(1)} %get-tuple-element.29), channel_id=1, source_target_pairs={{0,64},{8,72},{16,80},{24,88},{32,96},{40,104},{48,112},{56,120},{... | collective-permute-start | bytes 393224 | tf_op jit(solution)/shard_map/ppermute | solution.py:35
  18.7 2.2 %collective-permute-start.9 = (bf16[512,256]{1,0:T(8,128)(2,1)S(1)}, bf16[512,256]{1,0:T(8,128)(2,1)S(1)}, u32[]{:S(2)}, u32[]{:S(2)}) collective-permute-start(bf16[512,256]{1,0:T(8,128)(2,1)S(1)} %copy-done.7), channel_id=1, source_target_pairs={{0,24},{8,0},{16,8},{24,16},{32,56},{40,32},{48,40},{56,48},{64,88... | collective-permute-start | bytes 786440 | tf_op jit(solution)/shard_map/ppermute | solution.py:40
  24.3 3.2 %collective-permute-done.6.refs_1_ = bf16[256,512]{1,0:T(8,128)(2,1)S(1)} collective-permute-done((bf16[256,512]{1,0:T(8,128)(2,1)S(1)}, bf16[256,512]{1,0:T(8,128)(2,1)S(1)}, u32[]{:S(2)}, u32[]{:S(2)}) %collective-permute-start.6) | collective-permute-done | bytes 262176 | tf_op jit(solution)/shard_map/ppermute | solution.py:35
  27.5 2.7 %collective-permute-done.7.refs_2_ = bf16[256,512]{1,0:T(8,128)(2,1)S(1)} collective-permute-done((bf16[256,512]{1,0:T(8,128)(2,1)S(1)}, bf16[256,512]{1,0:T(8,128)(2,1)S(1)}, u32[]{:S(2)}, u32[]{:S(2)}) %collective-permute-start.7) | collective-permute-done | bytes 262176 | tf_op jit(solution)/shard_map/ppermute | solution.py:35
  30.2 6.2 %collective-permute-done.8.refs_3_ = bf16[256,512]{1,0:T(8,128)(2,1)S(1)} collective-permute-done((bf16[256,512]{1,0:T(8,128)(2,1)S(1)}, bf16[256,512]{1,0:T(8,128)(2,1)S(1)}, u32[]{:S(2)}, u32[]{:S(2)}) %collective-permute-start.8) | collective-permute-done | bytes 262176 | tf_op jit(solution)/shard_map/ppermute | solution.py:35
  36.4 2.0 %shard_map.128 = (f32[16,32,1024]{2,1,0:T(8,128)S(1)}, bf16[16,32,1024]{2,1,0:T(8,128)(2,1)S(1)}) custom-call(s32[4]{0:T(128)S(1)} %pad_add_fusion.pos, bf16[256,512]{1,0:T(8,128)(2,1)S(1)} %shard_map.127.refs_0_, bf16[256,512]{1,0:T(8,128)(2,1)S(1)} %collective-permute-done.6.refs_1_, bf16[256,512]{1,0:T(8,128)(2,1)S(1)} %collective-permute-done.7.refs_2_, ...), custom_call_target="tpu_custom_call" | custom-call | flops 1073741824 | bytes 5242880 | tf_op jit(solution)/shard_map/pallas_call | solution.py:96
  38.4 2.9 %collective-permute-start.12 = (bf16[16,32,1024]{2,1,0:T(8,128)(2,1)S(1)}, bf16[16,32,1024]{2,1,0:T(8,128)(2,1)S(1)}, u32[]{:S(2)}, u32[]{:S(2)}) collective-permute-start(bf16[16,32,1024]{2,1,0:T(8,128)(2,1)S(1)} %get-tuple-element.18), channel_id=1, source_target_pairs={{0,1},{1,0},{2,3},{3,2},{4,5},{5,4},{6,7},{7,6},{8,9},{9,8},{10,11... | collective-permute-start | bytes 3145736 | tf_op jit(solution)/shard_map/ppermute | solution.py:50
  41.3 2.3 %collective-permute-done.12.got = bf16[16,32,1024]{2,1,0:T(8,128)(2,1)S(1)} collective-permute-done((bf16[16,32,1024]{2,1,0:T(8,128)(2,1)S(1)}, bf16[16,32,1024]{2,1,0:T(8,128)(2,1)S(1)}, u32[]{:S(2)}, u32[]{:S(2)}) %collective-permute-start.12) | collective-permute-done | bytes 1048608 | tf_op jit(solution)/shard_map/ppermute | solution.py:50
  44.3 1.7 collective-permute-start.13
  46.0 3.3 %collective-permute-start.14 = (bf16[4,32,1024]{2,1,0:T(8,128)(2,1)S(1)}, bf16[4,32,1024]{2,1,0:T(8,128)(2,1)S(1)}, u32[]{:S(2)}, u32[]{:S(2)}) collective-permute-start(bf16[4,32,1024]{2,1,0:T(8,128)(2,1)S(1)} %get-tuple-element.21), channel_id=1, source_target_pairs={{0,4},{1,5},{2,6},{3,7},{4,0},{5,1},{6,2},{7,3},{8,12},{9,13},{10,... | collective-permute-start | bytes 786440 | tf_op jit(solution)/shard_map/ppermute | solution.py:45
  50.5 4.0 %collective-permute-done.13.one = bf16[4,32,1024]{2,1,0:T(8,128)(2,1)S(1)} collective-permute-done((bf16[4,32,1024]{2,1,0:T(8,128)(2,1)S(1)}, bf16[4,32,1024]{2,1,0:T(8,128)(2,1)S(1)}, u32[]{:S(2)}, u32[]{:S(2)}) %collective-permute-start.13) | collective-permute-done | bytes 262176 | tf_op jit(solution)/shard_map/ppermute | solution.py:45
  54.5 6.5 %collective-permute-done.14.two = bf16[4,32,1024]{2,1,0:T(8,128)(2,1)S(1)} collective-permute-done((bf16[4,32,1024]{2,1,0:T(8,128)(2,1)S(1)}, bf16[4,32,1024]{2,1,0:T(8,128)(2,1)S(1)}, u32[]{:S(2)}, u32[]{:S(2)}) %collective-permute-start.14) | collective-permute-done | bytes 262176 | tf_op jit(solution)/shard_map/ppermute | solution.py:45
  61.2 1.5 collective-permute-start.17
  64.0 2.0 %collective-permute-done.16.one = bf16[32,1024]{1,0:T(8,128)(2,1)S(1)} collective-permute-done((bf16[32,1024]{1,0:T(8,128)(2,1)S(1)}, bf16[32,1024]{1,0:T(8,128)(2,1)S(1)}, u32[]{:S(2)}, u32[]{:S(2)}) %collective-permute-start.16) | collective-permute-done | bytes 65568 | tf_op jit(solution)/shard_map/ppermute | solution.py:35
  67.1 2.8 %shard_map.131 = (f32[32,32,128]{2,1,0:T(8,128)S(1)}, bf16[384,32,128]{2,1,0:T(8,128)(2,1)S(1)}) custom-call(s32[4]{0:T(128)S(1)} %pad_add_fusion.pos, s32[32,8]{1,0:T(8,128)S(1)} %multiply_add_fusion.target, f32[32,1024]{1,0:T(8,128)S(1)} %get-tuple-element.23.own, bf16[32,1024]{1,0:T(8,128)(2,1)S(1)} %collective-permute-done.16.one, ...), custom_call_target="tpu_custom_call" | custom-call | flops 1048576 | bytes 5242880 | tf_op jit(solution)/shard_map/pallas_call | solution.py:186
  70.7 52.6 %all_to_all.10 = bf16[128,96,128]{2,1,0:T(8,128)(2,1)S(1)} all-to-all(bf16[128,96,128]{2,1,0:T(8,128)(2,1)S(1)} %bitcast.44), channel_id=1, replica_groups=mesh['seq'=16,'head'=8] {'seq','head'}, dimensions={0} | all-to-all | bytes 6291456 | tf_op jit(solution)/shard_map/all_to_all | solution.py:354
  123.3 3.3 %reshape_reshape.3.rows = bf16[384,4096]{1,0:T(8,128)(2,1)} reshape(bf16[128,96,128]{2,1,0:T(8,128)(2,1)S(1)} %all_to_all.10) | data formatting | bytes 6291456 | tf_op jit(solution)/shard_map/reshape;reshape | solution.py:363
  126.6 15.6 %shard_map.132 = bf16[384,32,128]{2,1,0:T(8,128)(2,1)} custom-call(f32[1,3]{1,0:T(1,128)} %scale.1, bf16[384,4096]{1,0:T(8,128)(2,1)} %reshape_reshape.3.rows, bf16[4096,768]{1,0:T(8,128)(2,1)} %bitcast.51, bf16[4096,768]{1,0:T(8,128)(2,1)} %bitcast.52, bf16[768,4096]{1,0:T(8,128)(2,1)} %bitcast.53), custom_call_target="tpu_custom_call" | custom-call | flops 7247757312 | bytes 18874368 | tf_op jit(solution)/shard_map/pallas_call | solution.py:248
  142.2 4.6 %all-to-all-start.1 = ((bf16[128,96,128]{2,1,0:T(8,128)(2,1)}), bf16[128,96,128]{2,1,0:T(8,128)(2,1)S(1)}, u32[]{:S(2)}, u32[]{:S(2)}) async-start(bf16[128,96,128]{2,1,0:T(8,128)(2,1)} %bitcast.47), calls=%async_computation.1 | async-start | bytes 6291456 | tf_op jit(solution)/shard_map/all_to_all | solution.py:354
  146.9 41.9 %all-to-all-done.1 = bf16[128,96,128]{2,1,0:T(8,128)(2,1)S(1)} async-done(((bf16[128,96,128]{2,1,0:T(8,128)(2,1)}), bf16[128,96,128]{2,1,0:T(8,128)(2,1)S(1)}, u32[]{:S(2)}, u32[]{:S(2)}) %all-to-all-start.1) | async-done | bytes 3145760 | tf_op jit(solution)/shard_map/all_to_all | solution.py:354
  189.8 3.1 %shard_map.133 = bf16[32,4096]{1,0:T(8,128)(2,1)} custom-call(s32[32,8]{1,0:T(8,128)S(1)} %multiply_add_fusion.target, f32[32,8]{1,0:T(8,128)S(1)} %copy.35.gates, bf16[384,32,128]{2,1,0:T(8,128)(2,1)S(1)} %bitcast.43, f32[32,32,128]{2,1,0:T(8,128)S(1)} %copy-done.2), custom_call_target="tpu_custom_call" | custom-call | flops 1048576 | bytes 4194304 | tf_op jit(solution)/shard_map/pallas_call | solution.py:289
  (58 shorter events, 17.3 us)
Async XLA Ops:
  0.0 21.0 %copy-start.3 = (bf16[256,512]{1,0:T(8,128)(2,1)S(1)}, bf16[256,512]{1,0:T(8,128)(2,1)}, u32[]{:S(2)}) copy-start(bf16[256,512]{1,0:T(8,128)(2,1)} %query.1) | copy-start | bytes 786436
  1.5 6.7 %collective-permute-start = (bf16[4,128,128]{2,1,0:T(8,128)(2,1)S(1)}, bf16[4,128,128]{2,1,0:T(8,128)(2,1)S(1)}, u32[]{:S(2)}, u32[]{:S(2)}) collective-permute-start(bf16[4,128,128]{2,1,0:T(8,128)(2,1)S(1)} %get-tuple-element.31), channel_id=1, source_target_pairs={{0,8},{8,16},{16,24},{24,0},{32,40},{40,48},{48,56},{56,32},{64,72... | collective-permute-start | bytes 393224 | tf_op jit(solution)/shard_map/ppermute | solution.py:40
  3.7 8.3 %collective-permute-start.1 = (bf16[4,128,128]{2,1,0:T(8,128)(2,1)S(1)}, bf16[4,128,128]{2,1,0:T(8,128)(2,1)S(1)}, u32[]{:S(2)}, u32[]{:S(2)}) collective-permute-start(bf16[4,128,128]{2,1,0:T(8,128)(2,1)S(1)} %get-tuple-element.31), channel_id=1, source_target_pairs={{0,16},{8,24},{16,0},{24,8},{32,48},{40,56},{48,32},{56,40},{64,80... | collective-permute-start | bytes 393224 | tf_op jit(solution)/shard_map/ppermute | solution.py:40
  6.3 5.7 %collective-permute-start.2 = (bf16[4,128,128]{2,1,0:T(8,128)(2,1)S(1)}, bf16[4,128,128]{2,1,0:T(8,128)(2,1)S(1)}, u32[]{:S(2)}, u32[]{:S(2)}) collective-permute-start(bf16[4,128,128]{2,1,0:T(8,128)(2,1)S(1)} %get-tuple-element.31), channel_id=1, source_target_pairs={{0,24},{8,0},{16,8},{24,16},{32,56},{40,32},{48,40},{56,48},{64,88... | collective-permute-start | bytes 393224 | tf_op jit(solution)/shard_map/ppermute | solution.py:40
  7.3 16.8 %collective-permute-start.10 = (bf16[512,256]{1,0:T(8,128)(2,1)}, bf16[512,256]{1,0:T(8,128)(2,1)S(1)}, u32[]{:S(2)}, u32[]{:S(2)}) collective-permute-start(bf16[512,256]{1,0:T(8,128)(2,1)} %refs_4_.1), channel_id=1, source_target_pairs={{0,16},{8,24},{16,0},{24,8},{32,48},{40,56},{48,32},{56,40},{64,80... | collective-permute-start | bytes 786440 | tf_op jit(solution)/shard_map/ppermute | solution.py:40
  7.6 16.7 %collective-permute-start.11 = (bf16[512,256]{1,0:T(8,128)(2,1)}, bf16[512,256]{1,0:T(8,128)(2,1)S(1)}, u32[]{:S(2)}, u32[]{:S(2)}) collective-permute-start(bf16[512,256]{1,0:T(8,128)(2,1)} %refs_4_.1), channel_id=1, source_target_pairs={{0,8},{8,16},{16,24},{24,0},{32,40},{40,48},{48,56},{56,32},{64,72... | collective-permute-start | bytes 786440 | tf_op jit(solution)/shard_map/ppermute | solution.py:40
  12.1 6.6 %collective-permute-start.3 = (bf16[4,128,128]{2,1,0:T(8,128)(2,1)S(1)}, bf16[4,128,128]{2,1,0:T(8,128)(2,1)S(1)}, u32[]{:S(2)}, u32[]{:S(2)}) collective-permute-start(bf16[4,128,128]{2,1,0:T(8,128)(2,1)S(1)} %get-tuple-element.29), channel_id=1, source_target_pairs={{0,32},{8,40},{16,48},{24,56},{32,64},{40,72},{48,80},{56,88},{64,... | collective-permute-start | bytes 393224 | tf_op jit(solution)/shard_map/ppermute | solution.py:35
  13.4 7.6 %collective-permute-start.4 = (bf16[4,128,128]{2,1,0:T(8,128)(2,1)S(1)}, bf16[4,128,128]{2,1,0:T(8,128)(2,1)S(1)}, u32[]{:S(2)}, u32[]{:S(2)}) collective-permute-start(bf16[4,128,128]{2,1,0:T(8,128)(2,1)S(1)} %get-tuple-element.29), channel_id=1, source_target_pairs={{0,64},{8,72},{16,80},{24,88},{32,96},{40,104},{48,112},{56,120},{... | collective-permute-start | bytes 393224 | tf_op jit(solution)/shard_map/ppermute | solution.py:35
  15.8 5.1 %collective-permute-start.5 = (bf16[4,128,128]{2,1,0:T(8,128)(2,1)S(1)}, bf16[4,128,128]{2,1,0:T(8,128)(2,1)S(1)}, u32[]{:S(2)}, u32[]{:S(2)}) collective-permute-start(bf16[4,128,128]{2,1,0:T(8,128)(2,1)S(1)} %get-tuple-element.29), channel_id=1, source_target_pairs={{0,96},{8,104},{16,112},{24,120},{32,0},{40,8},{48,16},{56,24},{64... | collective-permute-start | bytes 393224 | tf_op jit(solution)/shard_map/ppermute | solution.py:35
  18.7 5.6 %collective-permute-start.9 = (bf16[512,256]{1,0:T(8,128)(2,1)S(1)}, bf16[512,256]{1,0:T(8,128)(2,1)S(1)}, u32[]{:S(2)}, u32[]{:S(2)}) collective-permute-start(bf16[512,256]{1,0:T(8,128)(2,1)S(1)} %copy-done.7), channel_id=1, source_target_pairs={{0,24},{8,0},{16,8},{24,16},{32,56},{40,32},{48,40},{56,48},{64,88... | collective-permute-start | bytes 786440 | tf_op jit(solution)/shard_map/ppermute | solution.py:40
  21.9 28.1 %copy-start.8 = (s32[32,8]{0,1:T(8,128)S(1)}, s32[32,8]{0,1:T(8,128)}, u32[]{:S(2)}) copy-start(s32[32,8]{0,1:T(8,128)} %param.20) | copy-start | bytes 3076
  21.9 5.6 %collective-permute-start.6 = (bf16[256,512]{1,0:T(8,128)(2,1)S(1)}, bf16[256,512]{1,0:T(8,128)(2,1)S(1)}, u32[]{:S(2)}, u32[]{:S(2)}) collective-permute-start(bf16[256,512]{1,0:T(8,128)(2,1)S(1)} %shard_map.127.refs_0_), channel_id=1, source_target_pairs={{0,96},{8,104},{16,112},{24,120},{32,0},{40,8},{48,16},{56,24},{64... | collective-permute-start | bytes 786440 | tf_op jit(solution)/shard_map/ppermute | solution.py:35
  23.4 6.8 %collective-permute-start.7 = (bf16[256,512]{1,0:T(8,128)(2,1)S(1)}, bf16[256,512]{1,0:T(8,128)(2,1)S(1)}, u32[]{:S(2)}, u32[]{:S(2)}) collective-permute-start(bf16[256,512]{1,0:T(8,128)(2,1)S(1)} %shard_map.127.refs_0_), channel_id=1, source_target_pairs={{0,64},{8,72},{16,80},{24,88},{32,96},{40,104},{48,112},{56,120},{... | collective-permute-start | bytes 786440 | tf_op jit(solution)/shard_map/ppermute | solution.py:35
  24.1 12.2 %collective-permute-start.8 = (bf16[256,512]{1,0:T(8,128)(2,1)S(1)}, bf16[256,512]{1,0:T(8,128)(2,1)S(1)}, u32[]{:S(2)}, u32[]{:S(2)}) collective-permute-start(bf16[256,512]{1,0:T(8,128)(2,1)S(1)} %shard_map.127.refs_0_), channel_id=1, source_target_pairs={{0,32},{8,40},{16,48},{24,56},{32,64},{40,72},{48,80},{56,88},{64,... | collective-permute-start | bytes 786440 | tf_op jit(solution)/shard_map/ppermute | solution.py:35
  38.3 28.7 %copy-start.4 = (bf16[32,4096]{1,0:T(8,128)(2,1)S(1)}, bf16[32,4096]{1,0:T(8,128)(2,1)}, u32[]{:S(2)}) copy-start(bf16[32,4096]{1,0:T(8,128)(2,1)} %stream.1) | copy-start | bytes 786436
  38.3 28.7 %copy-start.5 = (f32[4096]{0:T(1024)S(1)}, f32[4096]{0:T(1024)}, u32[]{:S(2)}) copy-start(f32[4096]{0:T(1024)} %param.19) | copy-start | bytes 49156
  38.4 5.2 %collective-permute-start.12 = (bf16[16,32,1024]{2,1,0:T(8,128)(2,1)S(1)}, bf16[16,32,1024]{2,1,0:T(8,128)(2,1)S(1)}, u32[]{:S(2)}, u32[]{:S(2)}) collective-permute-start(bf16[16,32,1024]{2,1,0:T(8,128)(2,1)S(1)} %get-tuple-element.18), channel_id=1, source_target_pairs={{0,1},{1,0},{2,3},{3,2},{4,5},{5,4},{6,7},{7,6},{8,9},{9,8},{10,11... | collective-permute-start | bytes 3145736 | tf_op jit(solution)/shard_map/ppermute | solution.py:50
  44.3 10.2 %collective-permute-start.13 = (bf16[4,32,1024]{2,1,0:T(8,128)(2,1)S(1)}, bf16[4,32,1024]{2,1,0:T(8,128)(2,1)S(1)}, u32[]{:S(2)}, u32[]{:S(2)}) collective-permute-start(bf16[4,32,1024]{2,1,0:T(8,128)(2,1)S(1)} %get-tuple-element.20), channel_id=1, source_target_pairs={{0,2},{1,3},{2,4},{3,5},{4,6},{5,7},{6,0},{7,1},{8,10},{9,11},{10,... | collective-permute-start | bytes 786440 | tf_op jit(solution)/shard_map/ppermute | solution.py:45
  46.0 15.0 %collective-permute-start.14 = (bf16[4,32,1024]{2,1,0:T(8,128)(2,1)S(1)}, bf16[4,32,1024]{2,1,0:T(8,128)(2,1)S(1)}, u32[]{:S(2)}, u32[]{:S(2)}) collective-permute-start(bf16[4,32,1024]{2,1,0:T(8,128)(2,1)S(1)} %get-tuple-element.21), channel_id=1, source_target_pairs={{0,4},{1,5},{2,6},{3,7},{4,0},{5,1},{6,2},{7,3},{8,12},{9,13},{10,... | collective-permute-start | bytes 786440 | tf_op jit(solution)/shard_map/ppermute | solution.py:45
  49.3 11.7 %collective-permute-start.15 = (bf16[4,32,1024]{2,1,0:T(8,128)(2,1)S(1)}, bf16[4,32,1024]{2,1,0:T(8,128)(2,1)S(1)}, u32[]{:S(2)}, u32[]{:S(2)}) collective-permute-start(bf16[4,32,1024]{2,1,0:T(8,128)(2,1)S(1)} %get-tuple-element.22), channel_id=1, source_target_pairs={{0,6},{1,7},{2,0},{3,1},{4,2},{5,3},{6,4},{7,5},{8,14},{9,15},{10,... | collective-permute-start | bytes 786440 | tf_op jit(solution)/shard_map/ppermute | solution.py:45
  61.1 4.9 %collective-permute-start.16 = (bf16[32,1024]{1,0:T(8,128)(2,1)S(1)}, bf16[32,1024]{1,0:T(8,128)(2,1)S(1)}, u32[]{:S(2)}, u32[]{:S(2)}) collective-permute-start(bf16[32,1024]{1,0:T(8,128)(2,1)S(1)} %get-tuple-element.24), channel_id=1, source_target_pairs={{0,32},{8,40},{16,48},{24,56},{32,64},{40,72},{48,80},{56,88},{64,... | collective-permute-start | bytes 196616 | tf_op jit(solution)/shard_map/ppermute | solution.py:35
  61.2 5.3 %collective-permute-start.17 = (bf16[32,1024]{1,0:T(8,128)(2,1)S(1)}, bf16[32,1024]{1,0:T(8,128)(2,1)S(1)}, u32[]{:S(2)}, u32[]{:S(2)}) collective-permute-start(bf16[32,1024]{1,0:T(8,128)(2,1)S(1)} %get-tuple-element.25), channel_id=1, source_target_pairs={{0,64},{8,72},{16,80},{24,88},{32,96},{40,104},{48,112},{56,120},{... | collective-permute-start | bytes 196616 | tf_op jit(solution)/shard_map/ppermute | solution.py:35
  62.7 4.4 %collective-permute-start.18 = (bf16[32,1024]{1,0:T(8,128)(2,1)S(1)}, bf16[32,1024]{1,0:T(8,128)(2,1)S(1)}, u32[]{:S(2)}, u32[]{:S(2)}) collective-permute-start(bf16[32,1024]{1,0:T(8,128)(2,1)S(1)} %get-tuple-element.26), channel_id=1, source_target_pairs={{0,96},{8,104},{16,112},{24,120},{32,0},{40,8},{48,16},{56,24},{64... | collective-permute-start | bytes 196616 | tf_op jit(solution)/shard_map/ppermute | solution.py:35
  142.2 46.5 %all-to-all-start.1 = ((bf16[128,96,128]{2,1,0:T(8,128)(2,1)}), bf16[128,96,128]{2,1,0:T(8,128)(2,1)S(1)}, u32[]{:S(2)}, u32[]{:S(2)}) async-start(bf16[128,96,128]{2,1,0:T(8,128)(2,1)} %bitcast.47), calls=%async_computation.1 | async-start | bytes 6291456 | tf_op jit(solution)/shard_map/all_to_all | solution.py:354
  (6 other events, 47.3 us)

commit v9 on v8

--- a/solution.py
+++ b/solution.py
@@ -160,10 +160,10 @@
             value = value.astype(BF).astype(F32)
             j = dx * NY + dy
             total[:, j * wide : (j + 1) * wide] = value
+            res[:, pl.ds(at, wide)] = value.astype(BF)
             for half in range(2):
                 cut = value[:, half * LANES : (half + 1) * LANES]
                 squares += cut * cut
-                res[:, pl.ds(seq * 2 + half, 1), :] = cut[:, None, :]
             places.append((j, seq, at))
     factor = lax.rsqrt(jnp.sum(squares, axis=1, keepdims=True) * (1.0 / D) + 1e-06)
     for j, seq, at in places:
@@ -186,7 +186,7 @@
     return pl.pallas_call(
         place_kernel,
         out_shape=(
-            jax.ShapeDtypeStruct((tok, BLOCKS, LANES), F32),
+            jax.ShapeDtypeStruct((tok, D), BF),
             jax.ShapeDtypeStruct((slots, BLOCKS, LANES), BF),
         ),
         in_specs=[SMEM, SMEM] + [VMEM] * 6,
@@ -264,7 +264,7 @@
             pltpu.SemaphoreType.DMA((depth // OUT,)),
             pltpu.SemaphoreType.DMA((depth // (2 * OUT),)),
         ],
-        compiler_params=params(58),
+        compiler_params=params(56),
         cost_estimate=cost(6 * count * depth * hidden, 6 * depth * hidden),
     )(scale, rows, gate, up, down)
 
@@ -276,12 +276,13 @@
         add = gates[t, 0] * results[target[t, 0]].astype(F32)
         for k in range(1, TOPK):
             add += gates[t, k] * results[target[t, k]].astype(F32)
-        mixed[t] = res[t] + add
+        mixed[t] = add
         return carry
 
     lax.fori_loop(0, tok, one_token, 0)
     for block in range(BLOCKS):
-        out[:, block * LANES : (block + 1) * LANES] = mixed[:, block, :].astype(BF)
+        lanes = slice(block * LANES, (block + 1) * LANES)
+        out[:, lanes] = (res[:, lanes].astype(F32) + mixed[:, block, :]).astype(BF)
 
 
 def mix(target, gates, results, res):
@@ -291,7 +292,7 @@
         out_shape=jax.ShapeDtypeStruct((tok, D), BF),
         in_specs=[SMEM, SMEM, VMEM, VMEM],
         out_specs=VMEM,
-        scratch_shapes=[pltpu.VMEM(res.shape, F32)],
+        scratch_shapes=[pltpu.VMEM((tok, BLOCKS, LANES), F32)],
         compiler_params=params(16),
         cost_estimate=cost(1 << 20, 4 << 20),
     )(target, gates, results, res)

time: 193 us -> 192 us (level)
  no operation moved by 1% of the time
where the time goes in v9:
time: 192 us
  waiting for transfers between devices  74 us (39%)
  blocking collectives  52.6 us (27%)
  starting transfers between devices  31.9 us (17%)
  Pallas kernels  24.6 us (13%)
  local copies, waits for them, and re-layouts  6.66 us (3%)
    all_to_all x1, blocking collectives, exchange(): lax.all_to_all(message, ('seq', 'head'), split_axis=0, concat_axis=0, til...  52.6 us
    all_to_all x1, waiting for transfers between devices, exchange(): lax.all_to_all(message, ('seq', 'head'), split_axis=0, concat_axis=0, til...  41.9 us
    pallas_call x1, Pallas kernels, run_expert(): pl.pallas_call(expert_kernel, out_shape=jax.ShapeDtypeStruct((count, BLOC...  15.6 us
    ppermute x9, waiting for transfers between devices, to_x(): return lax.ppermute(a, 'seq', pairs)  15.1 us
    ppermute x3, waiting for transfers between devices, to_z(): return lax.ppermute(a, 'head', pairs)  10.5 us
    ppermute x9, starting transfers between devices, to_x(): return lax.ppermute(a, 'seq', pairs)  10 us
    ppermute x6, starting transfers between devices, to_y(): return lax.ppermute(a, 'seq', pairs)  8.66 us
    ppermute x3, starting transfers between devices, to_z(): return lax.ppermute(a, 'head', pairs)  5.74 us
  transfers between devices with their start and end apart: 20, of which 13 were waited for; matrix products, arithmetic and copies ran while one was open for 1% of the time, Pallas kernels for 0%

profile of v9, /device:TPU:1, one launch (start us, length us, event | category | flops | bytes accessed | tf_op | source)
XLA Modules:
  0.0 192.0 jit_solution(12354812251688122019)
XLA Ops:
  1.5 2.2 %collective-permute-start = (bf16[4,128,128]{2,1,0:T(8,128)(2,1)S(1)}, bf16[4,128,128]{2,1,0:T(8,128)(2,1)S(1)}, u32[]{:S(2)}, u32[]{:S(2)}) collective-permute-start(bf16[4,128,128]{2,1,0:T(8,128)(2,1)S(1)} %get-tuple-element.31), channel_id=1, source_target_pairs={{0,8},{8,16},{16,24},{24,0},{32,40},{40,48},{48,56},{56,32},{64,72... | collective-permute-start | bytes 393224 | tf_op jit(solution)/shard_map/ppermute | solution.py:40
  3.7 2.6 %collective-permute-start.1 = (bf16[4,128,128]{2,1,0:T(8,128)(2,1)S(1)}, bf16[4,128,128]{2,1,0:T(8,128)(2,1)S(1)}, u32[]{:S(2)}, u32[]{:S(2)}) collective-permute-start(bf16[4,128,128]{2,1,0:T(8,128)(2,1)S(1)} %get-tuple-element.31), channel_id=1, source_target_pairs={{0,16},{8,24},{16,0},{24,8},{32,48},{40,56},{48,32},{56,40},{64,80... | collective-permute-start | bytes 393224 | tf_op jit(solution)/shard_map/ppermute | solution.py:40
  8.2 3.8 %collective-permute-done.1 = bf16[4,128,128]{2,1,0:T(8,128)(2,1)S(1)} collective-permute-done((bf16[4,128,128]{2,1,0:T(8,128)(2,1)S(1)}, bf16[4,128,128]{2,1,0:T(8,128)(2,1)S(1)}, u32[]{:S(2)}, u32[]{:S(2)}) %collective-permute-start.1) | collective-permute-done | bytes 131104 | tf_op jit(solution)/shard_map/ppermute | solution.py:40
  13.4 2.4 %collective-permute-start.4 = (bf16[4,128,128]{2,1,0:T(8,128)(2,1)S(1)}, bf16[4,128,128]{2,1,0:T(8,128)(2,1)S(1)}, u32[]{:S(2)}, u32[]{:S(2)}) collective-permute-start(bf16[4,128,128]{2,1,0:T(8,128)(2,1)S(1)} %get-tuple-element.29), channel_id=1, source_target_pairs={{0,64},{8,72},{16,80},{24,88},{32,96},{40,104},{48,112},{56,120},{... | collective-permute-start | bytes 393224 | tf_op jit(solution)/shard_map/ppermute | solution.py:35
  18.7 2.2 %collective-permute-start.9 = (bf16[512,256]{1,0:T(8,128)(2,1)S(1)}, bf16[512,256]{1,0:T(8,128)(2,1)S(1)}, u32[]{:S(2)}, u32[]{:S(2)}) collective-permute-start(bf16[512,256]{1,0:T(8,128)(2,1)S(1)} %copy-done.7), channel_id=1, source_target_pairs={{0,24},{8,0},{16,8},{24,16},{32,56},{40,32},{48,40},{56,48},{64,88... | collective-permute-start | bytes 786440 | tf_op jit(solution)/shard_map/ppermute | solution.py:40
  24.3 3.2 %collective-permute-done.6.refs_1_ = bf16[256,512]{1,0:T(8,128)(2,1)S(1)} collective-permute-done((bf16[256,512]{1,0:T(8,128)(2,1)S(1)}, bf16[256,512]{1,0:T(8,128)(2,1)S(1)}, u32[]{:S(2)}, u32[]{:S(2)}) %collective-permute-start.6) | collective-permute-done | bytes 262176 | tf_op jit(solution)/shard_map/ppermute | solution.py:35
  27.5 2.7 %collective-permute-done.7.refs_2_ = bf16[256,512]{1,0:T(8,128)(2,1)S(1)} collective-permute-done((bf16[256,512]{1,0:T(8,128)(2,1)S(1)}, bf16[256,512]{1,0:T(8,128)(2,1)S(1)}, u32[]{:S(2)}, u32[]{:S(2)}) %collective-permute-start.7) | collective-permute-done | bytes 262176 | tf_op jit(solution)/shard_map/ppermute | solution.py:35
  30.2 6.2 %collective-permute-done.8.refs_3_ = bf16[256,512]{1,0:T(8,128)(2,1)S(1)} collective-permute-done((bf16[256,512]{1,0:T(8,128)(2,1)S(1)}, bf16[256,512]{1,0:T(8,128)(2,1)S(1)}, u32[]{:S(2)}, u32[]{:S(2)}) %collective-permute-start.8) | collective-permute-done | bytes 262176 | tf_op jit(solution)/shard_map/ppermute | solution.py:35
  36.4 2.0 %shard_map.128 = (f32[16,32,1024]{2,1,0:T(8,128)S(1)}, bf16[16,32,1024]{2,1,0:T(8,128)(2,1)S(1)}) custom-call(s32[4]{0:T(128)S(1)} %pad_add_fusion.pos, bf16[256,512]{1,0:T(8,128)(2,1)S(1)} %shard_map.127.refs_0_, bf16[256,512]{1,0:T(8,128)(2,1)S(1)} %collective-permute-done.6.refs_1_, bf16[256,512]{1,0:T(8,128)(2,1)S(1)} %collective-permute-done.7.refs_2_, ...), custom_call_target="tpu_custom_call" | custom-call | flops 1073741824 | bytes 5242880 | tf_op jit(solution)/shard_map/pallas_call | solution.py:96
  38.4 2.9 %collective-permute-start.12 = (bf16[16,32,1024]{2,1,0:T(8,128)(2,1)S(1)}, bf16[16,32,1024]{2,1,0:T(8,128)(2,1)S(1)}, u32[]{:S(2)}, u32[]{:S(2)}) collective-permute-start(bf16[16,32,1024]{2,1,0:T(8,128)(2,1)S(1)} %get-tuple-element.18), channel_id=1, source_target_pairs={{0,1},{1,0},{2,3},{3,2},{4,5},{5,4},{6,7},{7,6},{8,9},{9,8},{10,11... | collective-permute-start | bytes 3145736 | tf_op jit(solution)/shard_map/ppermute | solution.py:50
  41.3 2.3 %collective-permute-done.12.got = bf16[16,32,1024]{2,1,0:T(8,128)(2,1)S(1)} collective-permute-done((bf16[16,32,1024]{2,1,0:T(8,128)(2,1)S(1)}, bf16[16,32,1024]{2,1,0:T(8,128)(2,1)S(1)}, u32[]{:S(2)}, u32[]{:S(2)}) %collective-permute-start.12) | collective-permute-done | bytes 1048608 | tf_op jit(solution)/shard_map/ppermute | solution.py:50
  44.3 1.7 collective-permute-start.13
  46.0 3.3 %collective-permute-start.14 = (bf16[4,32,1024]{2,1,0:T(8,128)(2,1)S(1)}, bf16[4,32,1024]{2,1,0:T(8,128)(2,1)S(1)}, u32[]{:S(2)}, u32[]{:S(2)}) collective-permute-start(bf16[4,32,1024]{2,1,0:T(8,128)(2,1)S(1)} %get-tuple-element.21), channel_id=1, source_target_pairs={{0,4},{1,5},{2,6},{3,7},{4,0},{5,1},{6,2},{7,3},{8,12},{9,13},{10,... | collective-permute-start | bytes 786440 | tf_op jit(solution)/shard_map/ppermute | solution.py:45
  50.5 4.0 %collective-permute-done.13.one = bf16[4,32,1024]{2,1,0:T(8,128)(2,1)S(1)} collective-permute-done((bf16[4,32,1024]{2,1,0:T(8,128)(2,1)S(1)}, bf16[4,32,1024]{2,1,0:T(8,128)(2,1)S(1)}, u32[]{:S(2)}, u32[]{:S(2)}) %collective-permute-start.13) | collective-permute-done | bytes 262176 | tf_op jit(solution)/shard_map/ppermute | solution.py:45
  54.5 6.5 %collective-permute-done.14.two = bf16[4,32,1024]{2,1,0:T(8,128)(2,1)S(1)} collective-permute-done((bf16[4,32,1024]{2,1,0:T(8,128)(2,1)S(1)}, bf16[4,32,1024]{2,1,0:T(8,128)(2,1)S(1)}, u32[]{:S(2)}, u32[]{:S(2)}) %collective-permute-start.14) | collective-permute-done | bytes 262176 | tf_op jit(solution)/shard_map/ppermute | solution.py:45
  61.2 1.5 collective-permute-start.17
  64.0 2.0 %collective-permute-done.16.one = bf16[32,1024]{1,0:T(8,128)(2,1)S(1)} collective-permute-done((bf16[32,1024]{1,0:T(8,128)(2,1)S(1)}, bf16[32,1024]{1,0:T(8,128)(2,1)S(1)}, u32[]{:S(2)}, u32[]{:S(2)}) %collective-permute-start.16) | collective-permute-done | bytes 65568 | tf_op jit(solution)/shard_map/ppermute | solution.py:35
  67.1 2.3 %shard_map.131 = (bf16[32,4096]{1,0:T(8,128)(2,1)S(1)}, bf16[384,32,128]{2,1,0:T(8,128)(2,1)S(1)}) custom-call(s32[4]{0:T(128)S(1)} %pad_add_fusion.pos, s32[32,8]{1,0:T(8,128)S(1)} %multiply_add_fusion.target, f32[32,1024]{1,0:T(8,128)S(1)} %get-tuple-element.23.own, bf16[32,1024]{1,0:T(8,128)(2,1)S(1)} %collective-permute-done.16.one, ...), custom_call_target="tpu_custom_call" | custom-call | flops 1048576 | bytes 5242880 | tf_op jit(solution)/shard_map/pallas_call | solution.py:186
  70.1 52.6 %all_to_all.10 = bf16[128,96,128]{2,1,0:T(8,128)(2,1)S(1)} all-to-all(bf16[128,96,128]{2,1,0:T(8,128)(2,1)S(1)} %bitcast.44), channel_id=1, replica_groups=mesh['seq'=16,'head'=8] {'seq','head'}, dimensions={0} | all-to-all | bytes 6291456 | tf_op jit(solution)/shard_map/all_to_all | solution.py:355
  122.7 3.3 %reshape_reshape.3.rows = bf16[384,4096]{1,0:T(8,128)(2,1)} reshape(bf16[128,96,128]{2,1,0:T(8,128)(2,1)S(1)} %all_to_all.10) | data formatting | bytes 6291456 | tf_op jit(solution)/shard_map/reshape;reshape | solution.py:364
  126.0 15.6 %shard_map.132 = bf16[384,32,128]{2,1,0:T(8,128)(2,1)} custom-call(f32[1,3]{1,0:T(1,128)} %scale.1, bf16[384,4096]{1,0:T(8,128)(2,1)} %reshape_reshape.3.rows, bf16[4096,768]{1,0:T(8,128)(2,1)} %bitcast.51, bf16[4096,768]{1,0:T(8,128)(2,1)} %bitcast.52, bf16[768,4096]{1,0:T(8,128)(2,1)} %bitcast.53), custom_call_target="tpu_custom_call" | custom-call | flops 7247757312 | bytes 18874368 | tf_op jit(solution)/shard_map/pallas_call | solution.py:248
  141.6 4.6 %all-to-all-start.1 = ((bf16[128,96,128]{2,1,0:T(8,128)(2,1)}), bf16[128,96,128]{2,1,0:T(8,128)(2,1)S(1)}, u32[]{:S(2)}, u32[]{:S(2)}) async-start(bf16[128,96,128]{2,1,0:T(8,128)(2,1)} %bitcast.47), calls=%async_computation.1 | async-start | bytes 6291456 | tf_op jit(solution)/shard_map/all_to_all | solution.py:355
  146.3 41.9 %all-to-all-done.1 = bf16[128,96,128]{2,1,0:T(8,128)(2,1)S(1)} async-done(((bf16[128,96,128]{2,1,0:T(8,128)(2,1)}), bf16[128,96,128]{2,1,0:T(8,128)(2,1)S(1)}, u32[]{:S(2)}, u32[]{:S(2)}) %all-to-all-start.1) | async-done | bytes 3145760 | tf_op jit(solution)/shard_map/all_to_all | solution.py:355
  189.1 2.9 %shard_map.133 = bf16[32,4096]{1,0:T(8,128)(2,1)} custom-call(s32[32,8]{1,0:T(8,128)S(1)} %multiply_add_fusion.target, f32[32,8]{1,0:T(8,128)S(1)} %copy.35.gates, bf16[384,32,128]{2,1,0:T(8,128)(2,1)S(1)} %bitcast.43, bf16[32,4096]{1,0:T(8,128)(2,1)S(1)} %copy-done.2), custom_call_target="tpu_custom_call" | custom-call | flops 1048576 | bytes 4194304 | tf_op jit(solution)/shard_map/pallas_call | solution.py:290
  (58 shorter events, 17.1 us)
Async XLA Ops:
  0.0 21.0 %copy-start.3 = (bf16[256,512]{1,0:T(8,128)(2,1)S(1)}, bf16[256,512]{1,0:T(8,128)(2,1)}, u32[]{:S(2)}) copy-start(bf16[256,512]{1,0:T(8,128)(2,1)} %query.1) | copy-start | bytes 786436
  1.5 6.7 %collective-permute-start = (bf16[4,128,128]{2,1,0:T(8,128)(2,1)S(1)}, bf16[4,128,128]{2,1,0:T(8,128)(2,1)S(1)}, u32[]{:S(2)}, u32[]{:S(2)}) collective-permute-start(bf16[4,128,128]{2,1,0:T(8,128)(2,1)S(1)} %get-tuple-element.31), channel_id=1, source_target_pairs={{0,8},{8,16},{16,24},{24,0},{32,40},{40,48},{48,56},{56,32},{64,72... | collective-permute-start | bytes 393224 | tf_op jit(solution)/shard_map/ppermute | solution.py:40
  3.7 8.3 %collective-permute-start.1 = (bf16[4,128,128]{2,1,0:T(8,128)(2,1)S(1)}, bf16[4,128,128]{2,1,0:T(8,128)(2,1)S(1)}, u32[]{:S(2)}, u32[]{:S(2)}) collective-permute-start(bf16[4,128,128]{2,1,0:T(8,128)(2,1)S(1)} %get-tuple-element.31), channel_id=1, source_target_pairs={{0,16},{8,24},{16,0},{24,8},{32,48},{40,56},{48,32},{56,40},{64,80... | collective-permute-start | bytes 393224 | tf_op jit(solution)/shard_map/ppermute | solution.py:40
  6.3 5.7 %collective-permute-start.2 = (bf16[4,128,128]{2,1,0:T(8,128)(2,1)S(1)}, bf16[4,128,128]{2,1,0:T(8,128)(2,1)S(1)}, u32[]{:S(2)}, u32[]{:S(2)}) collective-permute-start(bf16[4,128,128]{2,1,0:T(8,128)(2,1)S(1)} %get-tuple-element.31), channel_id=1, source_target_pairs={{0,24},{8,0},{16,8},{24,16},{32,56},{40,32},{48,40},{56,48},{64,88... | collective-permute-start | bytes 393224 | tf_op jit(solution)/shard_map/ppermute | solution.py:40
  7.3 16.8 %collective-permute-start.10 = (bf16[512,256]{1,0:T(8,128)(2,1)}, bf16[512,256]{1,0:T(8,128)(2,1)S(1)}, u32[]{:S(2)}, u32[]{:S(2)}) collective-permute-start(bf16[512,256]{1,0:T(8,128)(2,1)} %refs_4_.1), channel_id=1, source_target_pairs={{0,16},{8,24},{16,0},{24,8},{32,48},{40,56},{48,32},{56,40},{64,80... | collective-permute-start | bytes 786440 | tf_op jit(solution)/shard_map/ppermute | solution.py:40
  7.6 16.7 %collective-permute-start.11 = (bf16[512,256]{1,0:T(8,128)(2,1)}, bf16[512,256]{1,0:T(8,128)(2,1)S(1)}, u32[]{:S(2)}, u32[]{:S(2)}) collective-permute-start(bf16[512,256]{1,0:T(8,128)(2,1)} %refs_4_.1), channel_id=1, source_target_pairs={{0,8},{8,16},{16,24},{24,0},{32,40},{40,48},{48,56},{56,32},{64,72... | collective-permute-start | bytes 786440 | tf_op jit(solution)/shard_map/ppermute | solution.py:40
  12.1 6.6 %collective-permute-start.3 = (bf16[4,128,128]{2,1,0:T(8,128)(2,1)S(1)}, bf16[4,128,128]{2,1,0:T(8,128)(2,1)S(1)}, u32[]{:S(2)}, u32[]{:S(2)}) collective-permute-start(bf16[4,128,128]{2,1,0:T(8,128)(2,1)S(1)} %get-tuple-element.29), channel_id=1, source_target_pairs={{0,32},{8,40},{16,48},{24,56},{32,64},{40,72},{48,80},{56,88},{64,... | collective-permute-start | bytes 393224 | tf_op jit(solution)/shard_map/ppermute | solution.py:35
  13.4 7.6 %collective-permute-start.4 = (bf16[4,128,128]{2,1,0:T(8,128)(2,1)S(1)}, bf16[4,128,128]{2,1,0:T(8,128)(2,1)S(1)}, u32[]{:S(2)}, u32[]{:S(2)}) collective-permute-start(bf16[4,128,128]{2,1,0:T(8,128)(2,1)S(1)} %get-tuple-element.29), channel_id=1, source_target_pairs={{0,64},{8,72},{16,80},{24,88},{32,96},{40,104},{48,112},{56,120},{... | collective-permute-start | bytes 393224 | tf_op jit(solution)/shard_map/ppermute | solution.py:35
  15.8 5.1 %collective-permute-start.5 = (bf16[4,128,128]{2,1,0:T(8,128)(2,1)S(1)}, bf16[4,128,128]{2,1,0:T(8,128)(2,1)S(1)}, u32[]{:S(2)}, u32[]{:S(2)}) collective-permute-start(bf16[4,128,128]{2,1,0:T(8,128)(2,1)S(1)} %get-tuple-element.29), channel_id=1, source_target_pairs={{0,96},{8,104},{16,112},{24,120},{32,0},{40,8},{48,16},{56,24},{64... | collective-permute-start | bytes 393224 | tf_op jit(solution)/shard_map/ppermute | solution.py:35
  18.7 5.6 %collective-permute-start.9 = (bf16[512,256]{1,0:T(8,128)(2,1)S(1)}, bf16[512,256]{1,0:T(8,128)(2,1)S(1)}, u32[]{:S(2)}, u32[]{:S(2)}) collective-permute-start(bf16[512,256]{1,0:T(8,128)(2,1)S(1)} %copy-done.7), channel_id=1, source_target_pairs={{0,24},{8,0},{16,8},{24,16},{32,56},{40,32},{48,40},{56,48},{64,88... | collective-permute-start | bytes 786440 | tf_op jit(solution)/shard_map/ppermute | solution.py:40
  21.9 28.1 %copy-start.8 = (s32[32,8]{0,1:T(8,128)S(1)}, s32[32,8]{0,1:T(8,128)}, u32[]{:S(2)}) copy-start(s32[32,8]{0,1:T(8,128)} %param.20) | copy-start | bytes 3076
  21.9 5.6 %collective-permute-start.6 = (bf16[256,512]{1,0:T(8,128)(2,1)S(1)}, bf16[256,512]{1,0:T(8,128)(2,1)S(1)}, u32[]{:S(2)}, u32[]{:S(2)}) collective-permute-start(bf16[256,512]{1,0:T(8,128)(2,1)S(1)} %shard_map.127.refs_0_), channel_id=1, source_target_pairs={{0,96},{8,104},{16,112},{24,120},{32,0},{40,8},{48,16},{56,24},{64... | collective-permute-start | bytes 786440 | tf_op jit(solution)/shard_map/ppermute | solution.py:35
  23.4 6.8 %collective-permute-start.7 = (bf16[256,512]{1,0:T(8,128)(2,1)S(1)}, bf16[256,512]{1,0:T(8,128)(2,1)S(1)}, u32[]{:S(2)}, u32[]{:S(2)}) collective-permute-start(bf16[256,512]{1,0:T(8,128)(2,1)S(1)} %shard_map.127.refs_0_), channel_id=1, source_target_pairs={{0,64},{8,72},{16,80},{24,88},{32,96},{40,104},{48,112},{56,120},{... | collective-permute-start | bytes 786440 | tf_op jit(solution)/shard_map/ppermute | solution.py:35
  24.1 12.2 %collective-permute-start.8 = (bf16[256,512]{1,0:T(8,128)(2,1)S(1)}, bf16[256,512]{1,0:T(8,128)(2,1)S(1)}, u32[]{:S(2)}, u32[]{:S(2)}) collective-permute-start(bf16[256,512]{1,0:T(8,128)(2,1)S(1)} %shard_map.127.refs_0_), channel_id=1, source_target_pairs={{0,32},{8,40},{16,48},{24,56},{32,64},{40,72},{48,80},{56,88},{64,... | collective-permute-start | bytes 786440 | tf_op jit(solution)/shard_map/ppermute | solution.py:35
  38.3 28.7 %copy-start.4 = (bf16[32,4096]{1,0:T(8,128)(2,1)S(1)}, bf16[32,4096]{1,0:T(8,128)(2,1)}, u32[]{:S(2)}) copy-start(bf16[32,4096]{1,0:T(8,128)(2,1)} %stream.1) | copy-start | bytes 786436
  38.3 28.7 %copy-start.5 = (f32[4096]{0:T(1024)S(1)}, f32[4096]{0:T(1024)}, u32[]{:S(2)}) copy-start(f32[4096]{0:T(1024)} %param.19) | copy-start | bytes 49156
  38.4 5.2 %collective-permute-start.12 = (bf16[16,32,1024]{2,1,0:T(8,128)(2,1)S(1)}, bf16[16,32,1024]{2,1,0:T(8,128)(2,1)S(1)}, u32[]{:S(2)}, u32[]{:S(2)}) collective-permute-start(bf16[16,32,1024]{2,1,0:T(8,128)(2,1)S(1)} %get-tuple-element.18), channel_id=1, source_target_pairs={{0,1},{1,0},{2,3},{3,2},{4,5},{5,4},{6,7},{7,6},{8,9},{9,8},{10,11... | collective-permute-start | bytes 3145736 | tf_op jit(solution)/shard_map/ppermute | solution.py:50
  44.3 10.2 %collective-permute-start.13 = (bf16[4,32,1024]{2,1,0:T(8,128)(2,1)S(1)}, bf16[4,32,1024]{2,1,0:T(8,128)(2,1)S(1)}, u32[]{:S(2)}, u32[]{:S(2)}) collective-permute-start(bf16[4,32,1024]{2,1,0:T(8,128)(2,1)S(1)} %get-tuple-element.20), channel_id=1, source_target_pairs={{0,2},{1,3},{2,4},{3,5},{4,6},{5,7},{6,0},{7,1},{8,10},{9,11},{10,... | collective-permute-start | bytes 786440 | tf_op jit(solution)/shard_map/ppermute | solution.py:45
  46.0 15.0 %collective-permute-start.14 = (bf16[4,32,1024]{2,1,0:T(8,128)(2,1)S(1)}, bf16[4,32,1024]{2,1,0:T(8,128)(2,1)S(1)}, u32[]{:S(2)}, u32[]{:S(2)}) collective-permute-start(bf16[4,32,1024]{2,1,0:T(8,128)(2,1)S(1)} %get-tuple-element.21), channel_id=1, source_target_pairs={{0,4},{1,5},{2,6},{3,7},{4,0},{5,1},{6,2},{7,3},{8,12},{9,13},{10,... | collective-permute-start | bytes 786440 | tf_op jit(solution)/shard_map/ppermute | solution.py:45
  49.3 11.7 %collective-permute-start.15 = (bf16[4,32,1024]{2,1,0:T(8,128)(2,1)S(1)}, bf16[4,32,1024]{2,1,0:T(8,128)(2,1)S(1)}, u32[]{:S(2)}, u32[]{:S(2)}) collective-permute-start(bf16[4,32,1024]{2,1,0:T(8,128)(2,1)S(1)} %get-tuple-element.22), channel_id=1, source_target_pairs={{0,6},{1,7},{2,0},{3,1},{4,2},{5,3},{6,4},{7,5},{8,14},{9,15},{10,... | collective-permute-start | bytes 786440 | tf_op jit(solution)/shard_map/ppermute | solution.py:45
  61.1 4.9 %collective-permute-start.16 = (bf16[32,1024]{1,0:T(8,128)(2,1)S(1)}, bf16[32,1024]{1,0:T(8,128)(2,1)S(1)}, u32[]{:S(2)}, u32[]{:S(2)}) collective-permute-start(bf16[32,1024]{1,0:T(8,128)(2,1)S(1)} %get-tuple-element.24), channel_id=1, source_target_pairs={{0,32},{8,40},{16,48},{24,56},{32,64},{40,72},{48,80},{56,88},{64,... | collective-permute-start | bytes 196616 | tf_op jit(solution)/shard_map/ppermute | solution.py:35
  61.2 5.3 %collective-permute-start.17 = (bf16[32,1024]{1,0:T(8,128)(2,1)S(1)}, bf16[32,1024]{1,0:T(8,128)(2,1)S(1)}, u32[]{:S(2)}, u32[]{:S(2)}) collective-permute-start(bf16[32,1024]{1,0:T(8,128)(2,1)S(1)} %get-tuple-element.25), channel_id=1, source_target_pairs={{0,64},{8,72},{16,80},{24,88},{32,96},{40,104},{48,112},{56,120},{... | collective-permute-start | bytes 196616 | tf_op jit(solution)/shard_map/ppermute | solution.py:35
  62.7 4.4 %collective-permute-start.18 = (bf16[32,1024]{1,0:T(8,128)(2,1)S(1)}, bf16[32,1024]{1,0:T(8,128)(2,1)S(1)}, u32[]{:S(2)}, u32[]{:S(2)}) collective-permute-start(bf16[32,1024]{1,0:T(8,128)(2,1)S(1)} %get-tuple-element.26), channel_id=1, source_target_pairs={{0,96},{8,104},{16,112},{24,120},{32,0},{40,8},{48,16},{56,24},{64... | collective-permute-start | bytes 196616 | tf_op jit(solution)/shard_map/ppermute | solution.py:35
  141.6 46.6 %all-to-all-start.1 = ((bf16[128,96,128]{2,1,0:T(8,128)(2,1)}), bf16[128,96,128]{2,1,0:T(8,128)(2,1)S(1)}, u32[]{:S(2)}, u32[]{:S(2)}) async-start(bf16[128,96,128]{2,1,0:T(8,128)(2,1)} %bitcast.47), calls=%async_computation.1 | async-start | bytes 6291456 | tf_op jit(solution)/shard_map/all_to_all | solution.py:355
  (6 other events, 47.1 us)

commit v10 on v9

--- a/solution.py
+++ b/solution.py
@@ -75,11 +75,12 @@
 
 
 def project_kernel(pos, *refs):
-    tokens, weights, (keep, give, rows) = refs[:NX], refs[NX : NX + NY], refs[NX + NY :]
+    blocks = len(refs) - NY - 3
+    tokens, weights, (keep, give, rows) = refs[:blocks], refs[blocks : blocks + NY], refs[blocks + NY :]
     tok, wide = keep.shape[1], weights[0].shape[1]
     mine = pl.multiple_of(pos[3] * tok, tok)
     other = pl.multiple_of(tok - pos[3] * tok, tok)
-    for dx in range(NX):
+    for dx in range(blocks):
         for dy in range(NY):
             rows[:, dy * wide : (dy + 1) * wide] = jnp.dot(
                 tokens[dx][...], weights[dy][...], preferred_element_type=F32
@@ -91,22 +92,22 @@
 
 def project(pos, tokens, weights, tok):
     wide = NY * weights[0].shape[1]
-    shape = (NX * NZ, tok, wide)
+    shape = (len(tokens) * NZ, tok, wide)
     count, depth = tokens[0].shape
     return pl.pallas_call(
         project_kernel,
         out_shape=(jax.ShapeDtypeStruct(shape, F32), jax.ShapeDtypeStruct(shape, BF)),
-        in_specs=[SMEM] + [VMEM] * (NX + NY),
+        in_specs=[SMEM] + [VMEM] * (len(tokens) + NY),
         out_specs=(VMEM, VMEM),
         scratch_shapes=[pltpu.VMEM((count, wide), F32)],
         compiler_params=params(24),
-        cost_estimate=cost(2 * NX * count * depth * wide, 5 << 20),
+        cost_estimate=cost(2 * len(tokens) * count * depth * wide, 5 << 20),
     )(pos, *tokens, *weights)
 
 
 def pair_kernel(pos, keep, got, own, one, two, three):
     z = pos[2]
-    for dx in range(NX):
+    for dx in range(own.shape[0]):
         at = dx * NZ + z
         own[dx] = keep[at] + got[at].astype(F32)
         for d, out in ((1, one), (2, two), (3, three)):
@@ -115,7 +116,7 @@
 
 
 def pair_sums(pos, keep, got):
-    shape = (NX, *keep.shape[1:])
+    shape = (keep.shape[0] // NZ, *keep.shape[1:])
     low = jax.ShapeDtypeStruct(shape, BF)
     return pl.pallas_call(
         pair_kernel,
@@ -133,14 +134,12 @@
         out[...] = total.astype(out.dtype)
 
 
-def sum_z(own, parts):
-    shape = own.shape[1:]
-    low = jax.ShapeDtypeStruct(shape, BF)
+def sum_z(own, parts, kinds):
     return pl.pallas_call(
         sum_kernel,
-        out_shape=(jax.ShapeDtypeStruct(shape, F32), low, low, low),
+        out_shape=tuple(jax.ShapeDtypeStruct(own.shape[1:], kind) for kind in kinds),
         in_specs=[VMEM] * NZ,
-        out_specs=(VMEM,) * NX,
+        out_specs=(VMEM,) * len(kinds),
         compiler_params=params(16),
         cost_estimate=cost(1 << 20, 2 << 20),
     )(own, *parts)
@@ -356,10 +355,17 @@
         return got.reshape(slots, BLOCKS, LANES)
 
     tokens = [head_normed] + [to_x(head_normed, NX - d) for d in range(1, NX)]
-    keep, give = project(pos, tokens, weights, tok_rows)
-    own, *low = pair_sums(pos, keep, swap_core(give))
-    sums = sum_z(own, [to_z(low[d - 1], d) for d in range(1, NZ)])
-    parts = [sums[0]] + [to_x(sums[d], d) for d in range(1, NX)]
+    parts, later = [], tokens[2:]
+    for group in range(2):
+        keep, give = project(pos, later if group else tokens[:2], weights, tok_rows)
+        own, *low = pair_sums(pos, keep, swap_core(give))
+        along_z = [to_z(low[d - 1], d) for d in range(1, NZ)]
+        if group == 0:
+            along_z[:2], later = lax.optimization_barrier((along_z[:2], later))
+        kinds = (BF, BF) if parts else (F32, BF)
+        sums = sum_z(own, along_z, kinds)
+        for block in sums:
+            parts.append(to_x(block, len(parts)) if parts else block)
     res, message = place(pos, target, parts, stream, model_gain[None], slots)
     slot_rows = exchange(message).reshape(slots, D)
     produced = run_expert(weight_scales, slot_rows, gate_weight[0], up_weight[0], down_weight[0])

time: 192 us -> 194 us (1.010)
  starting transfers between devices: 31.9 us -> 46.3 us
  waiting for transfers between devices: 74 us -> 60.5 us
    ppermute x3 -> x6, waiting for transfers between devices: 10.5 us -> 4.58 us  [to_z(): return lax.ppermute(a, 'head', pairs)]
    ppermute x9, waiting for transfers between devices: 15.1 us -> 9.38 us  [to_x(): return lax.ppermute(a, 'seq', pairs)]
    ppermute x3 -> x6, starting transfers between devices: 5.74 us -> 11.2 us  [to_z(): return lax.ppermute(a, 'head', pairs)]
    ppermute x9, starting transfers between devices: 10 us -> 14.4 us  [to_x(): return lax.ppermute(a, 'seq', pairs)]
    ppermute x1 -> x2, starting transfers between devices: 2.93 us -> 6.93 us  [swap_core(): return lax.ppermute(a, 'head', pairs)]
    ppermute x1 -> x2, waiting for transfers between devices: 2.29 us -> 0.01 us  [swap_core(): return lax.ppermute(a, 'head', pairs)]
  transfers between devices with their start and end apart: 20 -> 24, of which waited for: 13 -> 11; matrix products, arithmetic and copies ran while one was open for 1% -> 1% of each run, Pallas kernels for 0% -> 1%
where the time goes in v10:
time: 194 us
  waiting for transfers between devices  60.5 us (31%)
  blocking collectives  52.5 us (27%)
  starting transfers between devices  46.3 us (24%)
  Pallas kernels  25.8 us (13%)
  local copies, waits for them, and re-layouts  6.69 us (3%)
    all_to_all x1, blocking collectives, exchange(): lax.all_to_all(message, ('seq', 'head'), split_axis=0, concat_axis=0, til...  52.5 us
    all_to_all x1, waiting for transfers between devices, exchange(): lax.all_to_all(message, ('seq', 'head'), split_axis=0, concat_axis=0, til...  41.9 us
    pallas_call x1, Pallas kernels, run_expert(): pl.pallas_call(expert_kernel, out_shape=jax.ShapeDtypeStruct((count, BLOC...  15.6 us
    ppermute x9, starting transfers between devices, to_x(): return lax.ppermute(a, 'seq', pairs)  14.4 us
    ppermute x6, starting transfers between devices, to_z(): return lax.ppermute(a, 'head', pairs)  11.2 us
    ppermute x9, waiting for transfers between devices, to_x(): return lax.ppermute(a, 'seq', pairs)  9.38 us
    ppermute x6, starting transfers between devices, to_y(): return lax.ppermute(a, 'seq', pairs)  9.14 us
    ppermute x2, starting transfers between devices, swap_core(): return lax.ppermute(a, 'head', pairs)  6.93 us
  transfers between devices with their start and end apart: 24, of which 11 were waited for; matrix products, arithmetic and copies ran while one was open for 1% of the time, Pallas kernels for 1%

profile of v10, /device:TPU:1, one launch (start us, length us, event | category | flops | bytes accessed | tf_op | source)
XLA Modules:
  0.0 194.1 jit_solution(10300699520679038543)
XLA Ops:
  1.5 2.2 %collective-permute-start = (bf16[4,128,128]{2,1,0:T(8,128)(2,1)S(1)}, bf16[4,128,128]{2,1,0:T(8,128)(2,1)S(1)}, u32[]{:S(2)}, u32[]{:S(2)}) collective-permute-start(bf16[4,128,128]{2,1,0:T(8,128)(2,1)S(1)} %get-tuple-element.51), channel_id=1, source_target_pairs={{0,8},{8,16},{16,24},{24,0},{32,40},{40,48},{48,56},{56,32},{64,72... | collective-permute-start | bytes 393224 | tf_op jit(solution)/shard_map/ppermute | solution.py:40
  3.7 2.6 %collective-permute-start.1 = (bf16[4,128,128]{2,1,0:T(8,128)(2,1)S(1)}, bf16[4,128,128]{2,1,0:T(8,128)(2,1)S(1)}, u32[]{:S(2)}, u32[]{:S(2)}) collective-permute-start(bf16[4,128,128]{2,1,0:T(8,128)(2,1)S(1)} %get-tuple-element.51), channel_id=1, source_target_pairs={{0,16},{8,24},{16,0},{24,8},{32,48},{40,56},{48,32},{56,40},{64,80... | collective-permute-start | bytes 393224 | tf_op jit(solution)/shard_map/ppermute | solution.py:40
  7.4 2.2 %collective-permute-start.8 = (bf16[512,256]{1,0:T(8,128)(2,1)}, bf16[512,256]{1,0:T(8,128)(2,1)S(1)}, u32[]{:S(2)}, u32[]{:S(2)}) collective-permute-start(bf16[512,256]{1,0:T(8,128)(2,1)} %refs_2_.3), channel_id=1, source_target_pairs={{0,16},{8,24},{16,0},{24,8},{32,48},{40,56},{48,32},{56,40},{64,80... | collective-permute-start | bytes 786440 | tf_op jit(solution)/shard_map/ppermute | solution.py:40
  9.6 2.4 %collective-permute-done.1 = bf16[4,128,128]{2,1,0:T(8,128)(2,1)S(1)} collective-permute-done((bf16[4,128,128]{2,1,0:T(8,128)(2,1)S(1)}, bf16[4,128,128]{2,1,0:T(8,128)(2,1)S(1)}, u32[]{:S(2)}, u32[]{:S(2)}) %collective-permute-start.1) | collective-permute-done | bytes 131104 | tf_op jit(solution)/shard_map/ppermute | solution.py:40
  13.4 2.4 %collective-permute-start.4 = (bf16[4,128,128]{2,1,0:T(8,128)(2,1)S(1)}, bf16[4,128,128]{2,1,0:T(8,128)(2,1)S(1)}, u32[]{:S(2)}, u32[]{:S(2)}) collective-permute-start(bf16[4,128,128]{2,1,0:T(8,128)(2,1)S(1)} %get-tuple-element.49), channel_id=1, source_target_pairs={{0,64},{8,72},{16,80},{24,88},{32,96},{40,104},{48,112},{56,120},{... | collective-permute-start | bytes 393224 | tf_op jit(solution)/shard_map/ppermute | solution.py:35
  20.9 2.1 %collective-permute-start.6 = (bf16[256,512]{1,0:T(8,128)(2,1)S(1)}, bf16[256,512]{1,0:T(8,128)(2,1)S(1)}, u32[]{:S(2)}, u32[]{:S(2)}) collective-permute-start(bf16[256,512]{1,0:T(8,128)(2,1)S(1)} %shard_map.127.refs_0_), channel_id=1, source_target_pairs={{0,96},{8,104},{16,112},{24,120},{32,0},{40,8},{48,16},{56,24},{64... | collective-permute-start | bytes 786440 | tf_op jit(solution)/shard_map/ppermute | solution.py:35
  23.1 2.2 %collective-permute-done.9.refs_5_ = bf16[512,256]{1,0:T(8,128)(2,1)S(1)} collective-permute-done((bf16[512,256]{1,0:T(8,128)(2,1)S(1)}, bf16[512,256]{1,0:T(8,128)(2,1)S(1)}, u32[]{:S(2)}, u32[]{:S(2)}) %collective-permute-start.9) | collective-permute-done | bytes 262176 | tf_op jit(solution)/shard_map/ppermute | solution.py:40
  27.7 5.3 %collective-permute-start.10 = (bf16[8,32,1024]{2,1,0:T(8,128)(2,1)S(1)}, bf16[8,32,1024]{2,1,0:T(8,128)(2,1)S(1)}, u32[]{:S(2)}, u32[]{:S(2)}) collective-permute-start(bf16[8,32,1024]{2,1,0:T(8,128)(2,1)S(1)} %get-tuple-element.28), channel_id=1, source_target_pairs={{0,1},{1,0},{2,3},{3,2},{4,5},{5,4},{6,7},{7,6},{8,9},{9,8},{10,11... | collective-permute-start | bytes 1572872 | tf_op jit(solution)/shard_map/ppermute | solution.py:50
  33.1 1.9 collective-permute-start.13
  35.0 2.1 %collective-permute-start.14 = (bf16[256,512]{1,0:T(8,128)(2,1)S(1)}, bf16[256,512]{1,0:T(8,128)(2,1)S(1)}, u32[]{:S(2)}, u32[]{:S(2)}) collective-permute-start(bf16[256,512]{1,0:T(8,128)(2,1)S(1)} %shard_map.127.refs_0_), channel_id=1, source_target_pairs={{0,32},{8,40},{16,48},{24,56},{32,64},{40,72},{48,80},{56,88},{64,... | collective-permute-start | bytes 786440 | tf_op jit(solution)/shard_map/ppermute | solution.py:35
  39.4 3.3 %collective-permute-start.12 = (bf16[2,32,1024]{2,1,0:T(8,128)(2,1)S(1)}, bf16[2,32,1024]{2,1,0:T(8,128)(2,1)S(1)}, u32[]{:S(2)}, u32[]{:S(2)}) collective-permute-start(bf16[2,32,1024]{2,1,0:T(8,128)(2,1)S(1)} %get-tuple-element.31), channel_id=1, source_target_pairs={{0,4},{1,5},{2,6},{3,7},{4,0},{5,1},{6,2},{7,3},{8,12},{9,13},{10,... | collective-permute-start | bytes 393224 | tf_op jit(solution)/shard_map/ppermute | solution.py:45
  42.7 5.7 %collective-permute-done.14.refs_1_ = bf16[256,512]{1,0:T(8,128)(2,1)S(1)} collective-permute-done((bf16[256,512]{1,0:T(8,128)(2,1)S(1)}, bf16[256,512]{1,0:T(8,128)(2,1)S(1)}, u32[]{:S(2)}, u32[]{:S(2)}) %collective-permute-start.14) | collective-permute-done | bytes 262176 | tf_op jit(solution)/shard_map/ppermute | solution.py:35
  51.4 2.7 %collective-permute-start.15 = (bf16[2,32,1024]{2,1,0:T(8,128)(2,1)S(1)}, bf16[2,32,1024]{2,1,0:T(8,128)(2,1)S(1)}, u32[]{:S(2)}, u32[]{:S(2)}) collective-permute-start(bf16[2,32,1024]{2,1,0:T(8,128)(2,1)S(1)} %get-tuple-element.34), channel_id=1, source_target_pairs={{0,6},{1,7},{2,0},{3,1},{4,2},{5,3},{6,4},{7,5},{8,14},{9,15},{10,... | collective-permute-start | bytes 393224 | tf_op jit(solution)/shard_map/ppermute | solution.py:45
  54.9 2.7 %collective-permute-start.19 = (bf16[2,32,1024]{2,1,0:T(8,128)(2,1)S(1)}, bf16[2,32,1024]{2,1,0:T(8,128)(2,1)S(1)}, u32[]{:S(2)}, u32[]{:S(2)}) collective-permute-start(bf16[2,32,1024]{2,1,0:T(8,128)(2,1)S(1)} %get-tuple-element.43), channel_id=1, source_target_pairs={{0,4},{1,5},{2,6},{3,7},{4,0},{5,1},{6,2},{7,3},{8,12},{9,13},{10,... | collective-permute-start | bytes 393224 | tf_op jit(solution)/shard_map/ppermute | solution.py:45
  60.8 2.8 %collective-permute-done.19.two = bf16[2,32,1024]{2,1,0:T(8,128)(2,1)S(1)} collective-permute-done((bf16[2,32,1024]{2,1,0:T(8,128)(2,1)S(1)}, bf16[2,32,1024]{2,1,0:T(8,128)(2,1)S(1)}, u32[]{:S(2)}, u32[]{:S(2)}) %collective-permute-start.19) | collective-permute-done | bytes 131104 | tf_op jit(solution)/shard_map/ppermute | solution.py:45
  63.9 2.0 %collective-permute-start.21 = (bf16[32,1024]{1,0:T(8,128)(2,1)S(1)}, bf16[32,1024]{1,0:T(8,128)(2,1)S(1)}, u32[]{:S(2)}, u32[]{:S(2)}) collective-permute-start(bf16[32,1024]{1,0:T(8,128)(2,1)S(1)} %get-tuple-element.45), channel_id=1, source_target_pairs={{0,64},{8,72},{16,80},{24,88},{32,96},{40,104},{48,112},{56,120},{... | collective-permute-start | bytes 196616 | tf_op jit(solution)/shard_map/ppermute | solution.py:35
  66.8 1.8 collective-permute-done.21.two
  69.2 2.3 %shard_map.134 = (bf16[32,4096]{1,0:T(8,128)(2,1)S(1)}, bf16[384,32,128]{2,1,0:T(8,128)(2,1)S(1)}) custom-call(s32[4]{0:T(128)S(1)} %pad_add_fusion.pos, s32[32,8]{1,0:T(8,128)S(1)} %multiply_add_fusion.target, f32[32,1024]{1,0:T(8,128)S(1)} %get-tuple-element.35.own, bf16[32,1024]{1,0:T(8,128)(2,1)S(1)} %collective-permute-done.16.one, ...), custom_call_target="tpu_custom_call" | custom-call | flops 1048576 | bytes 5242880 | tf_op jit(solution)/shard_map/pallas_call | solution.py:185
  72.3 52.5 %all_to_all.10 = bf16[128,96,128]{2,1,0:T(8,128)(2,1)S(1)} all-to-all(bf16[128,96,128]{2,1,0:T(8,128)(2,1)S(1)} %bitcast.44), channel_id=1, replica_groups=mesh['seq'=16,'head'=8] {'seq','head'}, dimensions={0} | all-to-all | bytes 6291456 | tf_op jit(solution)/shard_map/all_to_all | solution.py:354
  124.8 3.3 %reshape_reshape.3.rows = bf16[384,4096]{1,0:T(8,128)(2,1)} reshape(bf16[128,96,128]{2,1,0:T(8,128)(2,1)S(1)} %all_to_all.10) | data formatting | bytes 6291456 | tf_op jit(solution)/shard_map/reshape;reshape | solution.py:370
  128.1 15.6 %shard_map.135 = bf16[384,32,128]{2,1,0:T(8,128)(2,1)} custom-call(f32[1,3]{1,0:T(1,128)} %scale.1, bf16[384,4096]{1,0:T(8,128)(2,1)} %reshape_reshape.3.rows, bf16[4096,768]{1,0:T(8,128)(2,1)} %bitcast.51, bf16[4096,768]{1,0:T(8,128)(2,1)} %bitcast.52, bf16[768,4096]{1,0:T(8,128)(2,1)} %bitcast.53), custom_call_target="tpu_custom_call" | custom-call | flops 7247757312 | bytes 18874368 | tf_op jit(solution)/shard_map/pallas_call | solution.py:247
  143.7 4.6 %all-to-all-start.1 = ((bf16[128,96,128]{2,1,0:T(8,128)(2,1)}), bf16[128,96,128]{2,1,0:T(8,128)(2,1)S(1)}, u32[]{:S(2)}, u32[]{:S(2)}) async-start(bf16[128,96,128]{2,1,0:T(8,128)(2,1)} %bitcast.47), calls=%async_computation.1 | async-start | bytes 6291456 | tf_op jit(solution)/shard_map/all_to_all | solution.py:354
  148.3 41.9 %all-to-all-done.1 = bf16[128,96,128]{2,1,0:T(8,128)(2,1)S(1)} async-done(((bf16[128,96,128]{2,1,0:T(8,128)(2,1)}), bf16[128,96,128]{2,1,0:T(8,128)(2,1)S(1)}, u32[]{:S(2)}, u32[]{:S(2)}) %all-to-all-start.1) | async-done | bytes 3145760 | tf_op jit(solution)/shard_map/all_to_all | solution.py:354
  191.2 2.9 %shard_map.136 = bf16[32,4096]{1,0:T(8,128)(2,1)} custom-call(s32[32,8]{1,0:T(8,128)S(1)} %multiply_add_fusion.target, f32[32,8]{1,0:T(8,128)S(1)} %copy.35.gates, bf16[384,32,128]{2,1,0:T(8,128)(2,1)S(1)} %bitcast.43, bf16[32,4096]{1,0:T(8,128)(2,1)S(1)} %copy-done.2), custom_call_target="tpu_custom_call" | custom-call | flops 1048576 | bytes 4194304 | tf_op jit(solution)/shard_map/pallas_call | solution.py:289
  (69 shorter events, 24.3 us)
Async XLA Ops:
  1.5 8.1 %collective-permute-start = (bf16[4,128,128]{2,1,0:T(8,128)(2,1)S(1)}, bf16[4,128,128]{2,1,0:T(8,128)(2,1)S(1)}, u32[]{:S(2)}, u32[]{:S(2)}) collective-permute-start(bf16[4,128,128]{2,1,0:T(8,128)(2,1)S(1)} %get-tuple-element.51), channel_id=1, source_target_pairs={{0,8},{8,16},{16,24},{24,0},{32,40},{40,48},{48,56},{56,32},{64,72... | collective-permute-start | bytes 393224 | tf_op jit(solution)/shard_map/ppermute | solution.py:40
  3.7 8.3 %collective-permute-start.1 = (bf16[4,128,128]{2,1,0:T(8,128)(2,1)S(1)}, bf16[4,128,128]{2,1,0:T(8,128)(2,1)S(1)}, u32[]{:S(2)}, u32[]{:S(2)}) collective-permute-start(bf16[4,128,128]{2,1,0:T(8,128)(2,1)S(1)} %get-tuple-element.51), channel_id=1, source_target_pairs={{0,16},{8,24},{16,0},{24,8},{32,48},{40,56},{48,32},{56,40},{64,80... | collective-permute-start | bytes 393224 | tf_op jit(solution)/shard_map/ppermute | solution.py:40
  6.3 5.7 %collective-permute-start.2 = (bf16[4,128,128]{2,1,0:T(8,128)(2,1)S(1)}, bf16[4,128,128]{2,1,0:T(8,128)(2,1)S(1)}, u32[]{:S(2)}, u32[]{:S(2)}) collective-permute-start(bf16[4,128,128]{2,1,0:T(8,128)(2,1)S(1)} %get-tuple-element.51), channel_id=1, source_target_pairs={{0,24},{8,0},{16,8},{24,16},{32,56},{40,32},{48,40},{56,48},{64,88... | collective-permute-start | bytes 393224 | tf_op jit(solution)/shard_map/ppermute | solution.py:40
  7.3 15.7 %collective-permute-start.7 = (bf16[512,256]{1,0:T(8,128)(2,1)}, bf16[512,256]{1,0:T(8,128)(2,1)S(1)}, u32[]{:S(2)}, u32[]{:S(2)}) collective-permute-start(bf16[512,256]{1,0:T(8,128)(2,1)} %refs_2_.3), channel_id=1, source_target_pairs={{0,24},{8,0},{16,8},{24,16},{32,56},{40,32},{48,40},{56,48},{64,88... | collective-permute-start | bytes 786440 | tf_op jit(solution)/shard_map/ppermute | solution.py:40
  7.4 15.7 %collective-permute-start.8 = (bf16[512,256]{1,0:T(8,128)(2,1)}, bf16[512,256]{1,0:T(8,128)(2,1)S(1)}, u32[]{:S(2)}, u32[]{:S(2)}) collective-permute-start(bf16[512,256]{1,0:T(8,128)(2,1)} %refs_2_.3), channel_id=1, source_target_pairs={{0,16},{8,24},{16,0},{24,8},{32,48},{40,56},{48,32},{56,40},{64,80... | collective-permute-start | bytes 786440 | tf_op jit(solution)/shard_map/ppermute | solution.py:40
  12.1 6.6 %collective-permute-start.3 = (bf16[4,128,128]{2,1,0:T(8,128)(2,1)S(1)}, bf16[4,128,128]{2,1,0:T(8,128)(2,1)S(1)}, u32[]{:S(2)}, u32[]{:S(2)}) collective-permute-start(bf16[4,128,128]{2,1,0:T(8,128)(2,1)S(1)} %get-tuple-element.49), channel_id=1, source_target_pairs={{0,32},{8,40},{16,48},{24,56},{32,64},{40,72},{48,80},{56,88},{64,... | collective-permute-start | bytes 393224 | tf_op jit(solution)/shard_map/ppermute | solution.py:35
  13.4 6.4 %collective-permute-start.4 = (bf16[4,128,128]{2,1,0:T(8,128)(2,1)S(1)}, bf16[4,128,128]{2,1,0:T(8,128)(2,1)S(1)}, u32[]{:S(2)}, u32[]{:S(2)}) collective-permute-start(bf16[4,128,128]{2,1,0:T(8,128)(2,1)S(1)} %get-tuple-element.49), channel_id=1, source_target_pairs={{0,64},{8,72},{16,80},{24,88},{32,96},{40,104},{48,112},{56,120},{... | collective-permute-start | bytes 393224 | tf_op jit(solution)/shard_map/ppermute | solution.py:35
  15.8 4.1 %collective-permute-start.5 = (bf16[4,128,128]{2,1,0:T(8,128)(2,1)S(1)}, bf16[4,128,128]{2,1,0:T(8,128)(2,1)S(1)}, u32[]{:S(2)}, u32[]{:S(2)}) collective-permute-start(bf16[4,128,128]{2,1,0:T(8,128)(2,1)S(1)} %get-tuple-element.49), channel_id=1, source_target_pairs={{0,96},{8,104},{16,112},{24,120},{32,0},{40,8},{48,16},{56,24},{64... | collective-permute-start | bytes 393224 | tf_op jit(solution)/shard_map/ppermute | solution.py:35
  18.7 6.5 %collective-permute-start.9 = (bf16[512,256]{1,0:T(8,128)(2,1)S(1)}, bf16[512,256]{1,0:T(8,128)(2,1)S(1)}, u32[]{:S(2)}, u32[]{:S(2)}) collective-permute-start(bf16[512,256]{1,0:T(8,128)(2,1)S(1)} %copy-done.7), channel_id=1, source_target_pairs={{0,8},{8,16},{16,24},{24,0},{32,40},{40,48},{48,56},{56,32},{64,72... | collective-permute-start | bytes 786440 | tf_op jit(solution)/shard_map/ppermute | solution.py:40
  20.9 5.5 %collective-permute-start.6 = (bf16[256,512]{1,0:T(8,128)(2,1)S(1)}, bf16[256,512]{1,0:T(8,128)(2,1)S(1)}, u32[]{:S(2)}, u32[]{:S(2)}) collective-permute-start(bf16[256,512]{1,0:T(8,128)(2,1)S(1)} %shard_map.127.refs_0_), channel_id=1, source_target_pairs={{0,96},{8,104},{16,112},{24,120},{32,0},{40,8},{48,16},{56,24},{64... | collective-permute-start | bytes 786440 | tf_op jit(solution)/shard_map/ppermute | solution.py:35
  27.7 9.3 %collective-permute-start.10 = (bf16[8,32,1024]{2,1,0:T(8,128)(2,1)S(1)}, bf16[8,32,1024]{2,1,0:T(8,128)(2,1)S(1)}, u32[]{:S(2)}, u32[]{:S(2)}) collective-permute-start(bf16[8,32,1024]{2,1,0:T(8,128)(2,1)S(1)} %get-tuple-element.28), channel_id=1, source_target_pairs={{0,1},{1,0},{2,3},{3,2},{4,5},{5,4},{6,7},{7,6},{8,9},{9,8},{10,11... | collective-permute-start | bytes 1572872 | tf_op jit(solution)/shard_map/ppermute | solution.py:50
  33.1 9.7 %collective-permute-start.13 = (bf16[256,512]{1,0:T(8,128)(2,1)S(1)}, bf16[256,512]{1,0:T(8,128)(2,1)S(1)}, u32[]{:S(2)}, u32[]{:S(2)}) collective-permute-start(bf16[256,512]{1,0:T(8,128)(2,1)S(1)} %shard_map.127.refs_0_), channel_id=1, source_target_pairs={{0,64},{8,72},{16,80},{24,88},{32,96},{40,104},{48,112},{56,120},{... | collective-permute-start | bytes 786440 | tf_op jit(solution)/shard_map/ppermute | solution.py:35
  35.0 13.5 %collective-permute-start.14 = (bf16[256,512]{1,0:T(8,128)(2,1)S(1)}, bf16[256,512]{1,0:T(8,128)(2,1)S(1)}, u32[]{:S(2)}, u32[]{:S(2)}) collective-permute-start(bf16[256,512]{1,0:T(8,128)(2,1)S(1)} %shard_map.127.refs_0_), channel_id=1, source_target_pairs={{0,32},{8,40},{16,48},{24,56},{32,64},{40,72},{48,80},{56,88},{64,... | collective-permute-start | bytes 786440 | tf_op jit(solution)/shard_map/ppermute | solution.py:35
  37.7 10.7 %collective-permute-start.11 = (bf16[2,32,1024]{2,1,0:T(8,128)(2,1)S(1)}, bf16[2,32,1024]{2,1,0:T(8,128)(2,1)S(1)}, u32[]{:S(2)}, u32[]{:S(2)}) collective-permute-start(bf16[2,32,1024]{2,1,0:T(8,128)(2,1)S(1)} %get-tuple-element.30), channel_id=1, source_target_pairs={{0,2},{1,3},{2,4},{3,5},{4,6},{5,7},{6,0},{7,1},{8,10},{9,11},{10,... | collective-permute-start | bytes 393224 | tf_op jit(solution)/shard_map/ppermute | solution.py:45
  39.4 9.0 %collective-permute-start.12 = (bf16[2,32,1024]{2,1,0:T(8,128)(2,1)S(1)}, bf16[2,32,1024]{2,1,0:T(8,128)(2,1)S(1)}, u32[]{:S(2)}, u32[]{:S(2)}) collective-permute-start(bf16[2,32,1024]{2,1,0:T(8,128)(2,1)S(1)} %get-tuple-element.31), channel_id=1, source_target_pairs={{0,4},{1,5},{2,6},{3,7},{4,0},{5,1},{6,2},{7,3},{8,12},{9,13},{10,... | collective-permute-start | bytes 393224 | tf_op jit(solution)/shard_map/ppermute | solution.py:45
  49.8 4.3 %collective-permute-start.17 = (bf16[8,32,1024]{2,1,0:T(8,128)(2,1)S(1)}, bf16[8,32,1024]{2,1,0:T(8,128)(2,1)S(1)}, u32[]{:S(2)}, u32[]{:S(2)}) collective-permute-start(bf16[8,32,1024]{2,1,0:T(8,128)(2,1)S(1)} %get-tuple-element.40), channel_id=1, source_target_pairs={{0,1},{1,0},{2,3},{3,2},{4,5},{5,4},{6,7},{7,6},{8,9},{9,8},{10,11... | collective-permute-start | bytes 1572872 | tf_op jit(solution)/shard_map/ppermute | solution.py:50
  51.4 7.3 %collective-permute-start.15 = (bf16[2,32,1024]{2,1,0:T(8,128)(2,1)S(1)}, bf16[2,32,1024]{2,1,0:T(8,128)(2,1)S(1)}, u32[]{:S(2)}, u32[]{:S(2)}) collective-permute-start(bf16[2,32,1024]{2,1,0:T(8,128)(2,1)S(1)} %get-tuple-element.34), channel_id=1, source_target_pairs={{0,6},{1,7},{2,0},{3,1},{4,2},{5,3},{6,4},{7,5},{8,14},{9,15},{10,... | collective-permute-start | bytes 393224 | tf_op jit(solution)/shard_map/ppermute | solution.py:45
  54.8 6.0 %collective-permute-start.18 = (bf16[2,32,1024]{2,1,0:T(8,128)(2,1)S(1)}, bf16[2,32,1024]{2,1,0:T(8,128)(2,1)S(1)}, u32[]{:S(2)}, u32[]{:S(2)}) collective-permute-start(bf16[2,32,1024]{2,1,0:T(8,128)(2,1)S(1)} %get-tuple-element.42), channel_id=1, source_target_pairs={{0,2},{1,3},{2,4},{3,5},{4,6},{5,7},{6,0},{7,1},{8,10},{9,11},{10,... | collective-permute-start | bytes 393224 | tf_op jit(solution)/shard_map/ppermute | solution.py:45
  54.9 8.7 %collective-permute-start.19 = (bf16[2,32,1024]{2,1,0:T(8,128)(2,1)S(1)}, bf16[2,32,1024]{2,1,0:T(8,128)(2,1)S(1)}, u32[]{:S(2)}, u32[]{:S(2)}) collective-permute-start(bf16[2,32,1024]{2,1,0:T(8,128)(2,1)S(1)} %get-tuple-element.43), channel_id=1, source_target_pairs={{0,4},{1,5},{2,6},{3,7},{4,0},{5,1},{6,2},{7,3},{8,12},{9,13},{10,... | collective-permute-start | bytes 393224 | tf_op jit(solution)/shard_map/ppermute | solution.py:45
  57.6 6.3 %collective-permute-start.20 = (bf16[2,32,1024]{2,1,0:T(8,128)(2,1)S(1)}, bf16[2,32,1024]{2,1,0:T(8,128)(2,1)S(1)}, u32[]{:S(2)}, u32[]{:S(2)}) collective-permute-start(bf16[2,32,1024]{2,1,0:T(8,128)(2,1)S(1)} %get-tuple-element.44), channel_id=1, source_target_pairs={{0,6},{1,7},{2,0},{3,1},{4,2},{5,3},{6,4},{7,5},{8,14},{9,15},{10,... | collective-permute-start | bytes 393224 | tf_op jit(solution)/shard_map/ppermute | solution.py:45
  58.8 8.0 %collective-permute-start.16 = (bf16[32,1024]{1,0:T(8,128)(2,1)S(1)}, bf16[32,1024]{1,0:T(8,128)(2,1)S(1)}, u32[]{:S(2)}, u32[]{:S(2)}) collective-permute-start(bf16[32,1024]{1,0:T(8,128)(2,1)S(1)} %get-tuple-element.36), channel_id=1, source_target_pairs={{0,32},{8,40},{16,48},{24,56},{32,64},{40,72},{48,80},{56,88},{64,... | collective-permute-start | bytes 196616 | tf_op jit(solution)/shard_map/ppermute | solution.py:35
  63.9 4.7 %collective-permute-start.21 = (bf16[32,1024]{1,0:T(8,128)(2,1)S(1)}, bf16[32,1024]{1,0:T(8,128)(2,1)S(1)}, u32[]{:S(2)}, u32[]{:S(2)}) collective-permute-start(bf16[32,1024]{1,0:T(8,128)(2,1)S(1)} %get-tuple-element.45), channel_id=1, source_target_pairs={{0,64},{8,72},{16,80},{24,88},{32,96},{40,104},{48,112},{56,120},{... | collective-permute-start | bytes 196616 | tf_op jit(solution)/shard_map/ppermute | solution.py:35
  65.9 3.3 %collective-permute-start.22 = (bf16[32,1024]{1,0:T(8,128)(2,1)S(1)}, bf16[32,1024]{1,0:T(8,128)(2,1)S(1)}, u32[]{:S(2)}, u32[]{:S(2)}) collective-permute-start(bf16[32,1024]{1,0:T(8,128)(2,1)S(1)} %get-tuple-element.46), channel_id=1, source_target_pairs={{0,96},{8,104},{16,112},{24,120},{32,0},{40,8},{48,16},{56,24},{64... | collective-permute-start | bytes 196616 | tf_op jit(solution)/shard_map/ppermute | solution.py:35
  143.7 46.5 %all-to-all-start.1 = ((bf16[128,96,128]{2,1,0:T(8,128)(2,1)}), bf16[128,96,128]{2,1,0:T(8,128)(2,1)S(1)}, u32[]{:S(2)}, u32[]{:S(2)}) async-start(bf16[128,96,128]{2,1,0:T(8,128)(2,1)} %bitcast.47), calls=%async_computation.1 | async-start | bytes 6291456 | tf_op jit(solution)/shard_map/all_to_all | solution.py:354
  (10 other events, 167.7 us)

commit v11 on v10

--- a/solution.py
+++ b/solution.py
@@ -355,15 +355,12 @@
         return got.reshape(slots, BLOCKS, LANES)
 
     tokens = [head_normed] + [to_x(head_normed, NX - d) for d in range(1, NX)]
-    parts, later = [], tokens[2:]
-    for group in range(2):
-        keep, give = project(pos, later if group else tokens[:2], weights, tok_rows)
+    parts = []
+    for group in (tokens[:2], tokens[2:]):
+        keep, give = project(pos, group, weights, tok_rows)
         own, *low = pair_sums(pos, keep, swap_core(give))
-        along_z = [to_z(low[d - 1], d) for d in range(1, NZ)]
-        if group == 0:
-            along_z[:2], later = lax.optimization_barrier((along_z[:2], later))
         kinds = (BF, BF) if parts else (F32, BF)
-        sums = sum_z(own, along_z, kinds)
+        sums = sum_z(own, [to_z(low[d - 1], d) for d in range(1, NZ)], kinds)
         for block in sums:
             parts.append(to_x(block, len(parts)) if parts else block)
     res, message = place(pos, target, parts, stream, model_gain[None], slots)

time: 194 us -> 184 us (0.948)
  starting transfers between devices: 46.3 us -> 42.3 us
  waiting for transfers between devices: 60.5 us -> 56.8 us
  blocking collectives: 52.5 us -> 49.6 us
    all_to_all x1, blocking collectives: 52.5 us -> 49.6 us  [exchange(): lax.all_to_all(message, ('seq', 'head'), split_axis=0, concat_axis=0, til...]
    ppermute x6, starting transfers between devices: 11.2 us -> 9.03 us  [to_z(): return lax.ppermute(a, 'head', pairs)]
    ppermute x6, waiting for transfers between devices: 4.59 us -> 2.42 us  [to_y(): return lax.ppermute(a, 'seq', pairs)]
  transfers between devices with their start and end apart: 24 -> 24, of which waited for: 11 -> 9; matrix products, arithmetic and copies ran while one was open for 1% -> 1% of each run, Pallas kernels for 1% -> 3%
where the time goes in v11:
time: 184 us
  waiting for transfers between devices  56.8 us (31%)
  blocking collectives  49.6 us (27%)
  starting transfers between devices  42.3 us (23%)
  Pallas kernels  25.8 us (14%)
  local copies, waits for them, and re-layouts  6.69 us (4%)
    all_to_all x1, blocking collectives, exchange(): lax.all_to_all(message, ('seq', 'head'), split_axis=0, concat_axis=0, til...  49.6 us
    all_to_all x1, waiting for transfers between devices, exchange(): lax.all_to_all(message, ('seq', 'head'), split_axis=0, concat_axis=0, til...  41.9 us
    pallas_call x1, Pallas kernels, run_expert(): pl.pallas_call(expert_kernel, out_shape=jax.ShapeDtypeStruct((count, BLOC...  15.6 us
    ppermute x9, starting transfers between devices, to_x(): return lax.ppermute(a, 'seq', pairs)  14.3 us
    ppermute x9, waiting for transfers between devices, to_x(): return lax.ppermute(a, 'seq', pairs)  9.32 us
    ppermute x6, starting transfers between devices, to_y(): return lax.ppermute(a, 'seq', pairs)  9.14 us
    ppermute x6, starting transfers between devices, to_z(): return lax.ppermute(a, 'head', pairs)  9.03 us
    ppermute x2, starting transfers between devices, swap_core(): return lax.ppermute(a, 'head', pairs)  5.22 us
  transfers between devices with their start and end apart: 24, of which 9 were waited for; matrix products, arithmetic and copies ran while one was open for 1% of the time, Pallas kernels for 3%

profile of v11, /device:TPU:1, one launch (start us, length us, event | category | flops | bytes accessed | tf_op | source)
XLA Modules:
  0.0 183.6 jit_solution(1007806888598219337)
XLA Ops:
  1.5 2.2 %collective-permute-start = (bf16[4,128,128]{2,1,0:T(8,128)(2,1)S(1)}, bf16[4,128,128]{2,1,0:T(8,128)(2,1)S(1)}, u32[]{:S(2)}, u32[]{:S(2)}) collective-permute-start(bf16[4,128,128]{2,1,0:T(8,128)(2,1)S(1)} %get-tuple-element.43), channel_id=1, source_target_pairs={{0,8},{8,16},{16,24},{24,0},{32,40},{40,48},{48,56},{56,32},{64,72... | collective-permute-start | bytes 393224 | tf_op jit(solution)/shard_map/ppermute | solution.py:40
  3.7 2.6 %collective-permute-start.1 = (bf16[4,128,128]{2,1,0:T(8,128)(2,1)S(1)}, bf16[4,128,128]{2,1,0:T(8,128)(2,1)S(1)}, u32[]{:S(2)}, u32[]{:S(2)}) collective-permute-start(bf16[4,128,128]{2,1,0:T(8,128)(2,1)S(1)} %get-tuple-element.43), channel_id=1, source_target_pairs={{0,16},{8,24},{16,0},{24,8},{32,48},{40,56},{48,32},{56,40},{64,80... | collective-permute-start | bytes 393224 | tf_op jit(solution)/shard_map/ppermute | solution.py:40
  7.4 2.2 %collective-permute-start.8 = (bf16[512,256]{1,0:T(8,128)(2,1)}, bf16[512,256]{1,0:T(8,128)(2,1)S(1)}, u32[]{:S(2)}, u32[]{:S(2)}) collective-permute-start(bf16[512,256]{1,0:T(8,128)(2,1)} %refs_2_.3), channel_id=1, source_target_pairs={{0,16},{8,24},{16,0},{24,8},{32,48},{40,56},{48,32},{56,40},{64,80... | collective-permute-start | bytes 786440 | tf_op jit(solution)/shard_map/ppermute | solution.py:40
  9.6 2.4 %collective-permute-done.1 = bf16[4,128,128]{2,1,0:T(8,128)(2,1)S(1)} collective-permute-done((bf16[4,128,128]{2,1,0:T(8,128)(2,1)S(1)}, bf16[4,128,128]{2,1,0:T(8,128)(2,1)S(1)}, u32[]{:S(2)}, u32[]{:S(2)}) %collective-permute-start.1) | collective-permute-done | bytes 131104 | tf_op jit(solution)/shard_map/ppermute | solution.py:40
  13.4 2.4 %collective-permute-start.4 = (bf16[4,128,128]{2,1,0:T(8,128)(2,1)S(1)}, bf16[4,128,128]{2,1,0:T(8,128)(2,1)S(1)}, u32[]{:S(2)}, u32[]{:S(2)}) collective-permute-start(bf16[4,128,128]{2,1,0:T(8,128)(2,1)S(1)} %get-tuple-element.41), channel_id=1, source_target_pairs={{0,64},{8,72},{16,80},{24,88},{32,96},{40,104},{48,112},{56,120},{... | collective-permute-start | bytes 393224 | tf_op jit(solution)/shard_map/ppermute | solution.py:35
  20.9 2.4 %collective-permute-start.15 = (bf16[256,512]{1,0:T(8,128)(2,1)S(1)}, bf16[256,512]{1,0:T(8,128)(2,1)S(1)}, u32[]{:S(2)}, u32[]{:S(2)}) collective-permute-start(bf16[256,512]{1,0:T(8,128)(2,1)S(1)} %shard_map.127.refs_0_), channel_id=1, source_target_pairs={{0,64},{8,72},{16,80},{24,88},{32,96},{40,104},{48,112},{56,120},{... | collective-permute-start | bytes 786440 | tf_op jit(solution)/shard_map/ppermute | solution.py:35
  23.6 2.3 %collective-permute-start.6 = (bf16[256,512]{1,0:T(8,128)(2,1)S(1)}, bf16[256,512]{1,0:T(8,128)(2,1)S(1)}, u32[]{:S(2)}, u32[]{:S(2)}) collective-permute-start(bf16[256,512]{1,0:T(8,128)(2,1)S(1)} %shard_map.127.refs_0_), channel_id=1, source_target_pairs={{0,96},{8,104},{16,112},{24,120},{32,0},{40,8},{48,16},{56,24},{64... | collective-permute-start | bytes 786440 | tf_op jit(solution)/shard_map/ppermute | solution.py:35
  26.0 1.8 collective-permute-done.15.refs_0_
  27.8 4.0 %collective-permute-done.16.refs_1_ = bf16[256,512]{1,0:T(8,128)(2,1)S(1)} collective-permute-done((bf16[256,512]{1,0:T(8,128)(2,1)S(1)}, bf16[256,512]{1,0:T(8,128)(2,1)S(1)}, u32[]{:S(2)}, u32[]{:S(2)}) %collective-permute-start.16) | collective-permute-done | bytes 262176 | tf_op jit(solution)/shard_map/ppermute | solution.py:35
  33.2 5.1 %collective-permute-start.17 = (bf16[8,32,1024]{2,1,0:T(8,128)(2,1)S(1)}, bf16[8,32,1024]{2,1,0:T(8,128)(2,1)S(1)}, u32[]{:S(2)}, u32[]{:S(2)}) collective-permute-start(bf16[8,32,1024]{2,1,0:T(8,128)(2,1)S(1)} %get-tuple-element.32), channel_id=1, source_target_pairs={{0,1},{1,0},{2,3},{3,2},{4,5},{5,4},{6,7},{7,6},{8,9},{9,8},{10,11... | collective-permute-start | bytes 1572872 | tf_op jit(solution)/shard_map/ppermute | solution.py:50
  40.5 1.7 collective-permute-start.18
  42.2 3.3 %collective-permute-start.19 = (bf16[2,32,1024]{2,1,0:T(8,128)(2,1)S(1)}, bf16[2,32,1024]{2,1,0:T(8,128)(2,1)S(1)}, u32[]{:S(2)}, u32[]{:S(2)}) collective-permute-start(bf16[2,32,1024]{2,1,0:T(8,128)(2,1)S(1)} %get-tuple-element.35), channel_id=1, source_target_pairs={{0,4},{1,5},{2,6},{3,7},{4,0},{5,1},{6,2},{7,3},{8,12},{9,13},{10,... | collective-permute-start | bytes 393224 | tf_op jit(solution)/shard_map/ppermute | solution.py:45
  48.1 2.0 %collective-permute-start.13 = (bf16[2,32,1024]{2,1,0:T(8,128)(2,1)S(1)}, bf16[2,32,1024]{2,1,0:T(8,128)(2,1)S(1)}, u32[]{:S(2)}, u32[]{:S(2)}) collective-permute-start(bf16[2,32,1024]{2,1,0:T(8,128)(2,1)S(1)} %get-tuple-element.28), channel_id=1, source_target_pairs={{0,6},{1,7},{2,0},{3,1},{4,2},{5,3},{6,4},{7,5},{8,14},{9,15},{10,... | collective-permute-start | bytes 393224 | tf_op jit(solution)/shard_map/ppermute | solution.py:45
  51.5 1.5 collective-permute-start.21
  53.1 1.8 collective-permute-start.22
  54.9 2.2 %collective-permute-done.12.two = bf16[2,32,1024]{2,1,0:T(8,128)(2,1)S(1)} collective-permute-done((bf16[2,32,1024]{2,1,0:T(8,128)(2,1)S(1)}, bf16[2,32,1024]{2,1,0:T(8,128)(2,1)S(1)}, u32[]{:S(2)}, u32[]{:S(2)}) %collective-permute-start.12) | collective-permute-done | bytes 131104 | tf_op jit(solution)/shard_map/ppermute | solution.py:45
  58.2 3.4 %collective-permute-done.14.one = bf16[32,1024]{1,0:T(8,128)(2,1)S(1)} collective-permute-done((bf16[32,1024]{1,0:T(8,128)(2,1)S(1)}, bf16[32,1024]{1,0:T(8,128)(2,1)S(1)}, u32[]{:S(2)}, u32[]{:S(2)}) %collective-permute-start.14) | collective-permute-done | bytes 65568 | tf_op jit(solution)/shard_map/ppermute | solution.py:35
  61.6 2.3 %shard_map.134 = (bf16[32,4096]{1,0:T(8,128)(2,1)S(1)}, bf16[384,32,128]{2,1,0:T(8,128)(2,1)S(1)}) custom-call(s32[4]{0:T(128)S(1)} %pad_add_fusion.pos, s32[32,8]{1,0:T(8,128)S(1)} %multiply_add_fusion.target, f32[32,1024]{1,0:T(8,128)S(1)} %get-tuple-element.29.own, bf16[32,1024]{1,0:T(8,128)(2,1)S(1)} %collective-permute-done.14.one, ...), custom_call_target="tpu_custom_call" | custom-call | flops 1048576 | bytes 5242880 | tf_op jit(solution)/shard_map/pallas_call | solution.py:185
  64.6 49.6 %all_to_all.10 = bf16[128,96,128]{2,1,0:T(8,128)(2,1)S(1)} all-to-all(bf16[128,96,128]{2,1,0:T(8,128)(2,1)S(1)} %bitcast.44), channel_id=1, replica_groups=mesh['seq'=16,'head'=8] {'seq','head'}, dimensions={0} | all-to-all | bytes 6291456 | tf_op jit(solution)/shard_map/all_to_all | solution.py:354
  114.3 3.3 %reshape_reshape.3.rows = bf16[384,4096]{1,0:T(8,128)(2,1)} reshape(bf16[128,96,128]{2,1,0:T(8,128)(2,1)S(1)} %all_to_all.10) | data formatting | bytes 6291456 | tf_op jit(solution)/shard_map/reshape;reshape | solution.py:367
  117.6 15.6 %shard_map.135 = bf16[384,32,128]{2,1,0:T(8,128)(2,1)} custom-call(f32[1,3]{1,0:T(1,128)} %scale.1, bf16[384,4096]{1,0:T(8,128)(2,1)} %reshape_reshape.3.rows, bf16[4096,768]{1,0:T(8,128)(2,1)} %bitcast.51, bf16[4096,768]{1,0:T(8,128)(2,1)} %bitcast.52, bf16[768,4096]{1,0:T(8,128)(2,1)} %bitcast.53), custom_call_target="tpu_custom_call" | custom-call | flops 7247757312 | bytes 18874368 | tf_op jit(solution)/shard_map/pallas_call | solution.py:247
  133.2 4.6 %all-to-all-start.1 = ((bf16[128,96,128]{2,1,0:T(8,128)(2,1)}), bf16[128,96,128]{2,1,0:T(8,128)(2,1)S(1)}, u32[]{:S(2)}, u32[]{:S(2)}) async-start(bf16[128,96,128]{2,1,0:T(8,128)(2,1)} %bitcast.47), calls=%async_computation.1 | async-start | bytes 6291456 | tf_op jit(solution)/shard_map/all_to_all | solution.py:354
  137.8 41.9 %all-to-all-done.1 = bf16[128,96,128]{2,1,0:T(8,128)(2,1)S(1)} async-done(((bf16[128,96,128]{2,1,0:T(8,128)(2,1)}), bf16[128,96,128]{2,1,0:T(8,128)(2,1)S(1)}, u32[]{:S(2)}, u32[]{:S(2)}) %all-to-all-start.1) | async-done | bytes 3145760 | tf_op jit(solution)/shard_map/all_to_all | solution.py:354
  180.7 2.9 %shard_map.136 = bf16[32,4096]{1,0:T(8,128)(2,1)} custom-call(s32[32,8]{1,0:T(8,128)S(1)} %multiply_add_fusion.target, f32[32,8]{1,0:T(8,128)S(1)} %copy.35.gates, bf16[384,32,128]{2,1,0:T(8,128)(2,1)S(1)} %bitcast.43, bf16[32,4096]{1,0:T(8,128)(2,1)S(1)} %copy-done.2), custom_call_target="tpu_custom_call" | custom-call | flops 1048576 | bytes 4194304 | tf_op jit(solution)/shard_map/pallas_call | solution.py:289
  (69 shorter events, 19.6 us)
Async XLA Ops:
  1.5 8.1 %collective-permute-start = (bf16[4,128,128]{2,1,0:T(8,128)(2,1)S(1)}, bf16[4,128,128]{2,1,0:T(8,128)(2,1)S(1)}, u32[]{:S(2)}, u32[]{:S(2)}) collective-permute-start(bf16[4,128,128]{2,1,0:T(8,128)(2,1)S(1)} %get-tuple-element.43), channel_id=1, source_target_pairs={{0,8},{8,16},{16,24},{24,0},{32,40},{40,48},{48,56},{56,32},{64,72... | collective-permute-start | bytes 393224 | tf_op jit(solution)/shard_map/ppermute | solution.py:40
  3.7 8.3 %collective-permute-start.1 = (bf16[4,128,128]{2,1,0:T(8,128)(2,1)S(1)}, bf16[4,128,128]{2,1,0:T(8,128)(2,1)S(1)}, u32[]{:S(2)}, u32[]{:S(2)}) collective-permute-start(bf16[4,128,128]{2,1,0:T(8,128)(2,1)S(1)} %get-tuple-element.43), channel_id=1, source_target_pairs={{0,16},{8,24},{16,0},{24,8},{32,48},{40,56},{48,32},{56,40},{64,80... | collective-permute-start | bytes 393224 | tf_op jit(solution)/shard_map/ppermute | solution.py:40
  6.3 5.7 %collective-permute-start.2 = (bf16[4,128,128]{2,1,0:T(8,128)(2,1)S(1)}, bf16[4,128,128]{2,1,0:T(8,128)(2,1)S(1)}, u32[]{:S(2)}, u32[]{:S(2)}) collective-permute-start(bf16[4,128,128]{2,1,0:T(8,128)(2,1)S(1)} %get-tuple-element.43), channel_id=1, source_target_pairs={{0,24},{8,0},{16,8},{24,16},{32,56},{40,32},{48,40},{56,48},{64,88... | collective-permute-start | bytes 393224 | tf_op jit(solution)/shard_map/ppermute | solution.py:40
  7.3 16.3 %collective-permute-start.7 = (bf16[512,256]{1,0:T(8,128)(2,1)}, bf16[512,256]{1,0:T(8,128)(2,1)S(1)}, u32[]{:S(2)}, u32[]{:S(2)}) collective-permute-start(bf16[512,256]{1,0:T(8,128)(2,1)} %refs_2_.3), channel_id=1, source_target_pairs={{0,24},{8,0},{16,8},{24,16},{32,56},{40,32},{48,40},{56,48},{64,88... | collective-permute-start | bytes 786440 | tf_op jit(solution)/shard_map/ppermute | solution.py:40
  7.4 18.6 %collective-permute-start.8 = (bf16[512,256]{1,0:T(8,128)(2,1)}, bf16[512,256]{1,0:T(8,128)(2,1)S(1)}, u32[]{:S(2)}, u32[]{:S(2)}) collective-permute-start(bf16[512,256]{1,0:T(8,128)(2,1)} %refs_2_.3), channel_id=1, source_target_pairs={{0,16},{8,24},{16,0},{24,8},{32,48},{40,56},{48,32},{56,40},{64,80... | collective-permute-start | bytes 786440 | tf_op jit(solution)/shard_map/ppermute | solution.py:40
  12.1 6.6 %collective-permute-start.3 = (bf16[4,128,128]{2,1,0:T(8,128)(2,1)S(1)}, bf16[4,128,128]{2,1,0:T(8,128)(2,1)S(1)}, u32[]{:S(2)}, u32[]{:S(2)}) collective-permute-start(bf16[4,128,128]{2,1,0:T(8,128)(2,1)S(1)} %get-tuple-element.41), channel_id=1, source_target_pairs={{0,32},{8,40},{16,48},{24,56},{32,64},{40,72},{48,80},{56,88},{64,... | collective-permute-start | bytes 393224 | tf_op jit(solution)/shard_map/ppermute | solution.py:35
  13.4 6.4 %collective-permute-start.4 = (bf16[4,128,128]{2,1,0:T(8,128)(2,1)S(1)}, bf16[4,128,128]{2,1,0:T(8,128)(2,1)S(1)}, u32[]{:S(2)}, u32[]{:S(2)}) collective-permute-start(bf16[4,128,128]{2,1,0:T(8,128)(2,1)S(1)} %get-tuple-element.41), channel_id=1, source_target_pairs={{0,64},{8,72},{16,80},{24,88},{32,96},{40,104},{48,112},{56,120},{... | collective-permute-start | bytes 393224 | tf_op jit(solution)/shard_map/ppermute | solution.py:35
  15.8 4.1 %collective-permute-start.5 = (bf16[4,128,128]{2,1,0:T(8,128)(2,1)S(1)}, bf16[4,128,128]{2,1,0:T(8,128)(2,1)S(1)}, u32[]{:S(2)}, u32[]{:S(2)}) collective-permute-start(bf16[4,128,128]{2,1,0:T(8,128)(2,1)S(1)} %get-tuple-element.41), channel_id=1, source_target_pairs={{0,96},{8,104},{16,112},{24,120},{32,0},{40,8},{48,16},{56,24},{64... | collective-permute-start | bytes 393224 | tf_op jit(solution)/shard_map/ppermute | solution.py:35
  18.7 7.3 %collective-permute-start.9 = (bf16[512,256]{1,0:T(8,128)(2,1)S(1)}, bf16[512,256]{1,0:T(8,128)(2,1)S(1)}, u32[]{:S(2)}, u32[]{:S(2)}) collective-permute-start(bf16[512,256]{1,0:T(8,128)(2,1)S(1)} %copy-done.7), channel_id=1, source_target_pairs={{0,8},{8,16},{16,24},{24,0},{32,40},{40,48},{48,56},{56,32},{64,72... | collective-permute-start | bytes 786440 | tf_op jit(solution)/shard_map/ppermute | solution.py:40
  20.9 6.9 %collective-permute-start.15 = (bf16[256,512]{1,0:T(8,128)(2,1)S(1)}, bf16[256,512]{1,0:T(8,128)(2,1)S(1)}, u32[]{:S(2)}, u32[]{:S(2)}) collective-permute-start(bf16[256,512]{1,0:T(8,128)(2,1)S(1)} %shard_map.127.refs_0_), channel_id=1, source_target_pairs={{0,64},{8,72},{16,80},{24,88},{32,96},{40,104},{48,112},{56,120},{... | collective-permute-start | bytes 786440 | tf_op jit(solution)/shard_map/ppermute | solution.py:35
  23.3 8.5 %collective-permute-start.16 = (bf16[256,512]{1,0:T(8,128)(2,1)S(1)}, bf16[256,512]{1,0:T(8,128)(2,1)S(1)}, u32[]{:S(2)}, u32[]{:S(2)}) collective-permute-start(bf16[256,512]{1,0:T(8,128)(2,1)S(1)} %shard_map.127.refs_0_), channel_id=1, source_target_pairs={{0,32},{8,40},{16,48},{24,56},{32,64},{40,72},{48,80},{56,88},{64,... | collective-permute-start | bytes 786440 | tf_op jit(solution)/shard_map/ppermute | solution.py:35
  23.6 14.7 %collective-permute-start.6 = (bf16[256,512]{1,0:T(8,128)(2,1)S(1)}, bf16[256,512]{1,0:T(8,128)(2,1)S(1)}, u32[]{:S(2)}, u32[]{:S(2)}) collective-permute-start(bf16[256,512]{1,0:T(8,128)(2,1)S(1)} %shard_map.127.refs_0_), channel_id=1, source_target_pairs={{0,96},{8,104},{16,112},{24,120},{32,0},{40,8},{48,16},{56,24},{64... | collective-permute-start | bytes 786440 | tf_op jit(solution)/shard_map/ppermute | solution.py:35
  33.2 6.7 %collective-permute-start.17 = (bf16[8,32,1024]{2,1,0:T(8,128)(2,1)S(1)}, bf16[8,32,1024]{2,1,0:T(8,128)(2,1)S(1)}, u32[]{:S(2)}, u32[]{:S(2)}) collective-permute-start(bf16[8,32,1024]{2,1,0:T(8,128)(2,1)S(1)} %get-tuple-element.32), channel_id=1, source_target_pairs={{0,1},{1,0},{2,3},{3,2},{4,5},{5,4},{6,7},{7,6},{8,9},{9,8},{10,11... | collective-permute-start | bytes 1572872 | tf_op jit(solution)/shard_map/ppermute | solution.py:50
  39.7 6.6 %collective-permute-start.10 = (bf16[8,32,1024]{2,1,0:T(8,128)(2,1)S(1)}, bf16[8,32,1024]{2,1,0:T(8,128)(2,1)S(1)}, u32[]{:S(2)}, u32[]{:S(2)}) collective-permute-start(bf16[8,32,1024]{2,1,0:T(8,128)(2,1)S(1)} %get-tuple-element.24), channel_id=1, source_target_pairs={{0,1},{1,0},{2,3},{3,2},{4,5},{5,4},{6,7},{7,6},{8,9},{9,8},{10,11... | collective-permute-start | bytes 1572872 | tf_op jit(solution)/shard_map/ppermute | solution.py:50
  40.5 7.6 %collective-permute-start.18 = (bf16[2,32,1024]{2,1,0:T(8,128)(2,1)S(1)}, bf16[2,32,1024]{2,1,0:T(8,128)(2,1)S(1)}, u32[]{:S(2)}, u32[]{:S(2)}) collective-permute-start(bf16[2,32,1024]{2,1,0:T(8,128)(2,1)S(1)} %get-tuple-element.34), channel_id=1, source_target_pairs={{0,2},{1,3},{2,4},{3,5},{4,6},{5,7},{6,0},{7,1},{8,10},{9,11},{10,... | collective-permute-start | bytes 393224 | tf_op jit(solution)/shard_map/ppermute | solution.py:45
  42.2 9.3 %collective-permute-start.19 = (bf16[2,32,1024]{2,1,0:T(8,128)(2,1)S(1)}, bf16[2,32,1024]{2,1,0:T(8,128)(2,1)S(1)}, u32[]{:S(2)}, u32[]{:S(2)}) collective-permute-start(bf16[2,32,1024]{2,1,0:T(8,128)(2,1)S(1)} %get-tuple-element.35), channel_id=1, source_target_pairs={{0,4},{1,5},{2,6},{3,7},{4,0},{5,1},{6,2},{7,3},{8,12},{9,13},{10,... | collective-permute-start | bytes 393224 | tf_op jit(solution)/shard_map/ppermute | solution.py:45
  45.5 6.0 %collective-permute-start.20 = (bf16[2,32,1024]{2,1,0:T(8,128)(2,1)S(1)}, bf16[2,32,1024]{2,1,0:T(8,128)(2,1)S(1)}, u32[]{:S(2)}, u32[]{:S(2)}) collective-permute-start(bf16[2,32,1024]{2,1,0:T(8,128)(2,1)S(1)} %get-tuple-element.36), channel_id=1, source_target_pairs={{0,6},{1,7},{2,0},{3,1},{4,2},{5,3},{6,4},{7,5},{8,14},{9,15},{10,... | collective-permute-start | bytes 393224 | tf_op jit(solution)/shard_map/ppermute | solution.py:45
  46.9 8.1 %collective-permute-start.11 = (bf16[2,32,1024]{2,1,0:T(8,128)(2,1)S(1)}, bf16[2,32,1024]{2,1,0:T(8,128)(2,1)S(1)}, u32[]{:S(2)}, u32[]{:S(2)}) collective-permute-start(bf16[2,32,1024]{2,1,0:T(8,128)(2,1)S(1)} %get-tuple-element.26), channel_id=1, source_target_pairs={{0,2},{1,3},{2,4},{3,5},{4,6},{5,7},{6,0},{7,1},{8,10},{9,11},{10,... | collective-permute-start | bytes 393224 | tf_op jit(solution)/shard_map/ppermute | solution.py:45
  47.7 9.4 %collective-permute-start.12 = (bf16[2,32,1024]{2,1,0:T(8,128)(2,1)S(1)}, bf16[2,32,1024]{2,1,0:T(8,128)(2,1)S(1)}, u32[]{:S(2)}, u32[]{:S(2)}) collective-permute-start(bf16[2,32,1024]{2,1,0:T(8,128)(2,1)S(1)} %get-tuple-element.27), channel_id=1, source_target_pairs={{0,4},{1,5},{2,6},{3,7},{4,0},{5,1},{6,2},{7,3},{8,12},{9,13},{10,... | collective-permute-start | bytes 393224 | tf_op jit(solution)/shard_map/ppermute | solution.py:45
  48.1 9.0 %collective-permute-start.13 = (bf16[2,32,1024]{2,1,0:T(8,128)(2,1)S(1)}, bf16[2,32,1024]{2,1,0:T(8,128)(2,1)S(1)}, u32[]{:S(2)}, u32[]{:S(2)}) collective-permute-start(bf16[2,32,1024]{2,1,0:T(8,128)(2,1)S(1)} %get-tuple-element.28), channel_id=1, source_target_pairs={{0,6},{1,7},{2,0},{3,1},{4,2},{5,3},{6,4},{7,5},{8,14},{9,15},{10,... | collective-permute-start | bytes 393224 | tf_op jit(solution)/shard_map/ppermute | solution.py:45
  51.5 6.6 %collective-permute-start.21 = (bf16[32,1024]{1,0:T(8,128)(2,1)S(1)}, bf16[32,1024]{1,0:T(8,128)(2,1)S(1)}, u32[]{:S(2)}, u32[]{:S(2)}) collective-permute-start(bf16[32,1024]{1,0:T(8,128)(2,1)S(1)} %get-tuple-element.37), channel_id=1, source_target_pairs={{0,64},{8,72},{16,80},{24,88},{32,96},{40,104},{48,112},{56,120},{... | collective-permute-start | bytes 196616 | tf_op jit(solution)/shard_map/ppermute | solution.py:35
  53.1 5.1 %collective-permute-start.22 = (bf16[32,1024]{1,0:T(8,128)(2,1)S(1)}, bf16[32,1024]{1,0:T(8,128)(2,1)S(1)}, u32[]{:S(2)}, u32[]{:S(2)}) collective-permute-start(bf16[32,1024]{1,0:T(8,128)(2,1)S(1)} %get-tuple-element.38), channel_id=1, source_target_pairs={{0,96},{8,104},{16,112},{24,120},{32,0},{40,8},{48,16},{56,24},{64... | collective-permute-start | bytes 196616 | tf_op jit(solution)/shard_map/ppermute | solution.py:35
  57.2 4.4 %collective-permute-start.14 = (bf16[32,1024]{1,0:T(8,128)(2,1)S(1)}, bf16[32,1024]{1,0:T(8,128)(2,1)S(1)}, u32[]{:S(2)}, u32[]{:S(2)}) collective-permute-start(bf16[32,1024]{1,0:T(8,128)(2,1)S(1)} %get-tuple-element.30), channel_id=1, source_target_pairs={{0,32},{8,40},{16,48},{24,56},{32,64},{40,72},{48,80},{56,88},{64,... | collective-permute-start | bytes 196616 | tf_op jit(solution)/shard_map/ppermute | solution.py:35
  133.2 46.5 %all-to-all-start.1 = ((bf16[128,96,128]{2,1,0:T(8,128)(2,1)}), bf16[128,96,128]{2,1,0:T(8,128)(2,1)S(1)}, u32[]{:S(2)}, u32[]{:S(2)}) async-start(bf16[128,96,128]{2,1,0:T(8,128)(2,1)} %bitcast.47), calls=%async_computation.1 | async-start | bytes 6291456 | tf_op jit(solution)/shard_map/all_to_all | solution.py:354
  (10 other events, 152.1 us)
